TPU v7x, 256 devices: a whole 4x4x8 slice. The times are simulated.
256 devices in a mesh: pts: 64 (over y, z, core), cols: 4 (over x).
Axes of the slice: x: 4, y: 4, z: 8, core: 2. Of those that a mesh axis runs over, the one named last changes fastest.
Arguments:
- start: float32 [65536, 512], P('pts', 'cols'), may hold values from -6 to 6
- cov_blocks: float32 [512, 8, 128, 128], P('pts')
- col_index: int32 [512, 8], P('pts'), may hold values from 0 to 511, as said below
- order: int32 [4], replicated, may hold values from 0 to 3, each once
Outputs:
- basis: float32 [65536, 512], P('pts', 'cols')
Inputs may be any that keep to these rules, and one draw needn't show every extreme that they name: col_index[i, 0] = i; every other entry lies within cycle distance 8 of i (taken modulo 512); repeats may occur.
All inputs are finite; a program needn't handle non-finite values.
Results may differ from a plain program's by a relative error of at most 0.0001.
Values sent between devices are 32-bit elements; how exact they have to be, the bound alone decides.
A program may use at most 64 MiB of HBM per device.

v0:
```python
import jax
import jax.numpy as jnp
from jax import lax
from jax.sharding import PartitionSpec as P


def broadcast(value, axis, source):
    kept = jnp.where(lax.axis_index(axis) == source, value, 0).astype(value.dtype)
    return lax.psum(kept, axis)


def with_halo(cells, sides, width):
    for axis, dim in sides:
        count = lax.axis_size(axis)
        head = lax.slice_in_dim(cells, 0, width, axis=dim)
        tail = lax.slice_in_dim(cells, cells.shape[dim] - width, cells.shape[dim], axis=dim)
        cells = jnp.concatenate(
            [
                lax.ppermute(tail, axis, [(i, (i + 1) % count) for i in range(count)]),
                cells,
                lax.ppermute(head, axis, [((i + 1) % count, i) for i in range(count)]),
            ],
            axis=dim,
        )
    return cells


def inner(left, right):
    return lax.dot_general(
        left,
        right,
        (((0,), (0,)), ((), ())),
        precision=lax.Precision.HIGHEST,
        preferred_element_type=jnp.float32,
    )


def times(left, right):
    return jnp.dot(left, right, precision=lax.Precision.HIGHEST, preferred_element_type=jnp.float32)


def factor_out(gram, current):
    lower = jnp.linalg.cholesky(gram)
    return lax.linalg.triangular_solve(
        lower, current, left_side=False, lower=True, transpose_a=True
    )


def gram_total(value):
    return lax.psum(value, "pts")


def coef_total(value):
    return lax.psum(value, "pts")


def orthonormalize(image, order, ranks, groups, group_size, mine):
    local = image
    column_group = jnp.zeros((group_size,), jnp.int32) + mine
    positions = jnp.arange(groups, dtype=jnp.int32)
    col_rank = jnp.sum(
        jnp.where(column_group[:, None] == positions[None, :], ranks[None, :], 0), axis=1
    )
    repeat = local.shape[1] // group_size
    for step in range(groups):
        owner = order[step]
        current = local
        gram = gram_total(inner(current, current))
        candidate = factor_out(gram, current)
        ortho = broadcast(candidate, "cols", owner)
        coef = coef_total(inner(ortho, local))
        updated = local - times(ortho, coef)
        tiled = jnp.tile(ortho, (1, repeat))
        local = jnp.where(
            (col_rank > step)[None, :],
            updated,
            jnp.where((column_group == owner)[None, :], tiled, local),
        )
    return local


def body(start, cov_blocks, col_index, order):
    rows, group_size = start.shape
    blocks_dev = cov_blocks.shape[0]
    block = cov_blocks.shape[2]
    total_blocks = blocks_dev * lax.axis_size("pts")
    groups = lax.axis_size("cols")
    mine = lax.axis_index("cols")
    positions = jnp.arange(groups, dtype=jnp.int32)
    ranks = jnp.sum(
        positions[:, None] * (order[:, None] == positions[None, :]).astype(jnp.int32), axis=0
    )
    first_block = lax.axis_index("pts") * blocks_dev - blocks_dev
    relative = jnp.mod(col_index - first_block, total_blocks)
    basis = start
    window = with_halo(basis, (("pts", 0),), rows)
    tiles = window.reshape(3 * blocks_dev, block, group_size)[relative]
    image = jnp.einsum(
        "rsab,rsbk->rak", cov_blocks, tiles, precision=lax.Precision.HIGHEST
    ).reshape(rows, group_size)
    basis = orthonormalize(image, order, ranks, groups, group_size, mine)
    return basis


def solution(mesh):
    placed = (P("pts", "cols"), P("pts", None, None, None), P("pts", None), P())
    return jax.shard_map(
        body, mesh=mesh, in_specs=placed, out_specs=P("pts", "cols"), check_vma=False
    )
```

profile of v0, /device:TPU:6, one launch (start us, length us, event | category | flops | bytes accessed | tf_op | source)
XLA Modules:
  0.0 1689.0 jit_solution(17694205134196288816)
XLA Ops:
  6.5 7.7 collective-permute-start.1
  15.1 6.3 collective-permute-done
  22.5 2.7 gather_fusion
  25.3 7.9 fusion.23
  36.5 164.5 %all-reduce.13.cloned.1.call-done = f32[128,128]{0,1:T(8,128)} async-done(((f32[128,128]{0,1:T(8,128)}), f32[128,128]{0,1:T(8,128)}) %all-reduce.13.cloned.1.call-update) | async-done | bytes 65552 | tf_op jit(solution)/shard_map/psum | solution.py:50
  202.8 11.7 cholesky.74
  215.9 9.8 custom-call.8
  227.4 44.1 %all-reduce.15.cloned.1.call-done = f32[1024,128]{0,1:T(8,128)} async-done(((f32[1024,128]{0,1:T(8,128)}), f32[1024,128]{0,1:T(8,128)}) %all-reduce.15.cloned.1.call-update) | async-done | bytes 524304 | tf_op jit(solution)/shard_map/psum | solution.py:9
  274.1 170.3 %all-reduce.17.cloned.1.call-done = f32[128,128]{1,0:T(8,128)} async-done(((f32[128,128]{1,0:T(8,128)}), f32[128,128]{1,0:T(8,128)}) %all-reduce.17.cloned.1.call-update) | async-done | bytes 65552 | tf_op jit(solution)/shard_map/psum | solution.py:54
  448.8 163.9 %all-reduce.19.cloned.1.call-done = f32[128,128]{0,1:T(8,128)} async-done(((f32[128,128]{0,1:T(8,128)}), f32[128,128]{0,1:T(8,128)}) %all-reduce.19.cloned.1.call-update) | async-done | bytes 65552 | tf_op jit(solution)/shard_map/psum | solution.py:50
  614.4 11.7 cholesky.85
  627.5 9.8 custom-call.9
  638.8 44.3 %all-reduce.21.cloned.1.call-done = f32[1024,128]{0,1:T(8,128)} async-done(((f32[1024,128]{0,1:T(8,128)}), f32[1024,128]{0,1:T(8,128)}) %all-reduce.21.cloned.1.call-update) | async-done | bytes 524304 | tf_op jit(solution)/shard_map/psum | solution.py:9
  685.5 170.4 %all-reduce.23.cloned.1.call-done = f32[128,128]{1,0:T(8,128)} async-done(((f32[128,128]{1,0:T(8,128)}), f32[128,128]{1,0:T(8,128)}) %all-reduce.23.cloned.1.call-update) | async-done | bytes 65552 | tf_op jit(solution)/shard_map/psum | solution.py:54
  859.9 164.4 %all-reduce.25.cloned.1.call-done = f32[128,128]{0,1:T(8,128)} async-done(((f32[128,128]{0,1:T(8,128)}), f32[128,128]{0,1:T(8,128)}) %all-reduce.25.cloned.1.call-update) | async-done | bytes 65552 | tf_op jit(solution)/shard_map/psum | solution.py:50
  1026.1 11.7 cholesky.96
  1039.1 9.8 custom-call.10
  1050.4 44.3 %all-reduce.27.cloned.1.call-done = f32[1024,128]{0,1:T(8,128)} async-done(((f32[1024,128]{0,1:T(8,128)}), f32[1024,128]{0,1:T(8,128)}) %all-reduce.27.cloned.1.call-update) | async-done | bytes 524304 | tf_op jit(solution)/shard_map/psum | solution.py:9
  1097.1 170.5 %all-reduce.29.cloned.1.call-done = f32[128,128]{1,0:T(8,128)} async-done(((f32[128,128]{1,0:T(8,128)}), f32[128,128]{1,0:T(8,128)}) %all-reduce.29.cloned.1.call-update) | async-done | bytes 65552 | tf_op jit(solution)/shard_map/psum | solution.py:54
  1271.6 164.3 %all-reduce.31.cloned.1.call-done = f32[128,128]{0,1:T(8,128)} async-done(((f32[128,128]{0,1:T(8,128)}), f32[128,128]{0,1:T(8,128)}) %all-reduce.31.cloned.1.call-update) | async-done | bytes 65552 | tf_op jit(solution)/shard_map/psum | solution.py:50
  1437.7 11.7 cholesky.107
  1450.7 9.8 custom-call.11
  1462.0 44.3 %all-reduce.33.cloned.1.call-done = f32[1024,128]{0,1:T(8,128)} async-done(((f32[1024,128]{0,1:T(8,128)}), f32[1024,128]{0,1:T(8,128)}) %all-reduce.33.cloned.1.call-update) | async-done | bytes 524304 | tf_op jit(solution)/shard_map/psum | solution.py:9
  1508.6 170.4 %all-reduce.35.cloned.1.call-done = f32[128,128]{1,0:T(8,128)} async-done(((f32[128,128]{1,0:T(8,128)}), f32[128,128]{1,0:T(8,128)}) %all-reduce.35.cloned.1.call-update) | async-done | bytes 65552 | tf_op jit(solution)/shard_map/psum | solution.py:54
  (75 shorter events, 45.9 us)
Async XLA Ops:
  6.5 194.5 %all-reduce.13.cloned.1.call-start = ((), (), s32[]{:S(2)}) async-start(), calls=%async_computation | async-start | bytes 131072 | tf_op jit(solution)/shard_map/psum | solution.py:50
  6.5 14.8 collective-permute-start
  6.5 14.8 collective-permute-start.1
  25.3 10.0 copy-start
  34.9 236.7 %all-reduce.15.cloned.1.call-start = ((), (), s32[]{:S(2)}) async-start(), calls=%async_computation.1 | async-start | bytes 1048576 | tf_op jit(solution)/shard_map/psum | solution.py:9
  227.2 217.2 %all-reduce.17.cloned.1.call-start = ((), (), s32[]{:S(2)}) async-start(), calls=%async_computation.2 | async-start | bytes 131072 | tf_op jit(solution)/shard_map/psum | solution.py:54
  273.9 338.8 %all-reduce.19.cloned.1.call-start = ((), (), s32[]{:S(2)}) async-start(), calls=%async_computation.3 | async-start | bytes 131072 | tf_op jit(solution)/shard_map/psum | solution.py:50
  447.5 235.6 %all-reduce.21.cloned.1.call-start = ((), (), s32[]{:S(2)}) async-start(), calls=%async_computation.4 | async-start | bytes 1048576 | tf_op jit(solution)/shard_map/psum | solution.py:9
  638.8 217.1 %all-reduce.23.cloned.1.call-start = ((), (), s32[]{:S(2)}) async-start(), calls=%async_computation.5 | async-start | bytes 131072 | tf_op jit(solution)/shard_map/psum | solution.py:54
  685.4 338.9 %all-reduce.25.cloned.1.call-start = ((), (), s32[]{:S(2)}) async-start(), calls=%async_computation.6 | async-start | bytes 131072 | tf_op jit(solution)/shard_map/psum | solution.py:50
  859.0 235.8 %all-reduce.27.cloned.1.call-start = ((), (), s32[]{:S(2)}) async-start(), calls=%async_computation.7 | async-start | bytes 1048576 | tf_op jit(solution)/shard_map/psum | solution.py:9
  1050.4 217.2 %all-reduce.29.cloned.1.call-start = ((), (), s32[]{:S(2)}) async-start(), calls=%async_computation.8 | async-start | bytes 131072 | tf_op jit(solution)/shard_map/psum | solution.py:54
  1097.0 338.8 %all-reduce.31.cloned.1.call-start = ((), (), s32[]{:S(2)}) async-start(), calls=%async_computation.9 | async-start | bytes 131072 | tf_op jit(solution)/shard_map/psum | solution.py:50
  1270.7 235.6 %all-reduce.33.cloned.1.call-start = ((), (), s32[]{:S(2)}) async-start(), calls=%async_computation.10 | async-start | bytes 1048576 | tf_op jit(solution)/shard_map/psum | solution.py:9
  1462.0 217.1 %all-reduce.35.cloned.1.call-start = ((), (), s32[]{:S(2)}) async-start(), calls=%async_computation.11 | async-start | bytes 131072 | tf_op jit(solution)/shard_map/psum | solution.py:54
Sparse Core Ops, SparseCore 0:
  35.0 165.9 all-reduce.12
  227.3 44.2 all-reduce.14
  275.0 169.3 all-reduce.16
  447.7 164.8 all-reduce.18
  638.9 44.2 all-reduce.20
  686.5 169.3 all-reduce.22
  859.3 164.9 all-reduce.24
  1050.5 44.2 all-reduce.26
  1098.2 169.3 all-reduce.28
  1270.9 164.8 all-reduce.30
  1462.1 44.2 all-reduce.32
  1509.7 169.3 all-reduce.34
where the time goes:
time: 1700 us; the launch traced here: 1690 us
  waiting for transfers between devices  1520 us (89%)
  other arithmetic  96.9 us (6%)
  matrix products  35.6 us (2%)
    psum x4, waiting for transfers between devices, coef_total(): return lax.psum(value, 'pts')  682 us
    psum x4, waiting for transfers between devices, gram_total(): return lax.psum(value, 'pts')  657 us
    psum x4, waiting for transfers between devices, broadcast(): return lax.psum(kept, axis)  177 us
    another operation x12, other arithmetic, factor_out(): lower = jnp.linalg.cholesky(gram)  49.6 us
    another operation x8, other arithmetic, factor_out(): lax.linalg.triangular_solve(lower, current, left_side=False, lower=True,...  41.9 us
  transfers between devices with their start and end apart: 14, of which 13 were waited for; matrix products, arithmetic and copies ran while one was open for 0% of the time, Pallas kernels for 0%

commit v1 on v0

v1 whole, which is shorter than its diff:
```python
import jax
import jax.numpy as jnp
from jax import lax
from jax.experimental import pallas as pl
from jax.experimental.pallas import tpu as pltpu
from jax.sharding import PartitionSpec as P

MESH = pl.DeviceIdType.MESH
F32 = jnp.float32
BF16 = jnp.bfloat16
GROUPS = 4
WIDTH = 128
BLOCK = 128
ROW_BLOCKS = 8
SLOTS = 8
NBLK = 512
YS, ZS, CORES = 4, 8, 2
COLS = GROUPS * WIDTH
ROWS = ROW_BLOCKS * BLOCK
HALF = ROW_BLOCKS // 2
PIECE = 3 * WIDTH // CORES // ZS
TOLERANCE = 1e-4


def broadcast(value, axis, source):
    kept = jnp.where(lax.axis_index(axis) == source, value, 0).astype(value.dtype)
    return lax.psum(kept, axis)


def with_halo(cells, axis, width):
    count = lax.axis_size(axis)
    head = lax.slice_in_dim(cells, 0, width, axis=0)
    tail = lax.slice_in_dim(cells, cells.shape[0] - width, cells.shape[0], axis=0)
    return jnp.concatenate(
        [
            lax.ppermute(tail, axis, [(i, (i + 1) % count) for i in range(count)]),
            cells,
            lax.ppermute(head, axis, [((i + 1) % count, i) for i in range(count)]),
        ],
        axis=0,
    )


def inner(left, right):
    return lax.dot_general(
        left,
        right,
        (((0,), (0,)), ((), ())),
        precision=lax.Precision.HIGHEST,
        preferred_element_type=F32,
    )


def careful(start, cov_blocks, col_index, order):
    rows, group_size = start.shape
    blocks_dev = cov_blocks.shape[0]
    block = cov_blocks.shape[2]
    total_blocks = blocks_dev * lax.axis_size("pts")
    groups = lax.axis_size("cols")
    mine = lax.axis_index("cols")
    positions = jnp.arange(groups, dtype=jnp.int32)
    rank = jnp.sum(jnp.where(order == mine, positions, 0))
    first_block = lax.axis_index("pts") * blocks_dev - blocks_dev
    relative = jnp.mod(col_index - first_block, total_blocks)
    tiles = with_halo(start, "pts", rows).reshape(3 * blocks_dev, block, group_size)[relative]
    local = jnp.einsum(
        "rsab,rsbk->rak", cov_blocks, tiles, precision=lax.Precision.HIGHEST
    ).reshape(rows, group_size)

    def step(t, local):
        owner = order[t]
        gram = lax.psum(inner(local, local), "pts")
        lower = jnp.linalg.cholesky(gram)
        candidate = lax.linalg.triangular_solve(
            lower, local, left_side=False, lower=True, transpose_a=True
        )
        ortho = broadcast(candidate, "cols", owner)
        coef = lax.psum(inner(ortho, local), "pts")
        updated = local - jnp.dot(
            ortho, coef, precision=lax.Precision.HIGHEST, preferred_element_type=F32
        )
        return jnp.where(rank > t, updated, jnp.where(mine == owner, ortho, local))

    return lax.fori_loop(0, groups, step, local)


def split(x):
    high = x.astype(BF16)
    return high, (x - high.astype(F32)).astype(BF16)


def quarters(q, m, n):
    return (q[:m, :n] + q[m:, n:]) + (q[:m, n:] + q[m:, :n])


def dot(a, b):
    return jnp.dot(a, b, preferred_element_type=F32)


def dot_t(a, b):
    return lax.dot_general(a, b, (((0,), (0,)), ((), ())), preferred_element_type=F32)


def kernel(
    start, cov, col_index, order, out, residual,
    win, win_hl, covv, cov_hl, vall, vhl, tb, r1, s1, r2, r3, gb,
    e0, w, b, u, mk, e0_h, e0_l, w_h, w_l, b_h, b_l, u_h, x_hl, res, scol,
    c_sem, l_sem, o_sem, f_sem,
    halo_s, halo_r, left_s, right_s, fwdr_s, fwdl_s, next_r, prev_r, opp_r,
    p1_s, p1_r, p2_s, p2_r, p3_s, p3_r, p4_s, p4_r, p5_s, p5_r, p6_s, p6_r,
):
    p = lax.axis_index("pts")
    g = lax.axis_index("cols")
    npts = YS * ZS * CORES
    c = lax.rem(p, CORES)
    z = lax.rem(lax.div(p, CORES), ZS)
    y = lax.div(p, CORES * ZS)
    before, after = lax.rem(p + npts - 1, npts), lax.rem(p + 1, npts)
    sibling = p + 1 - 2 * c
    g_next, g_prev, g_opp = (lax.rem(g + k, GROUPS) for k in (1, 3, 2))

    def at_z(k):
        return p + (lax.rem(z + k, ZS) - z) * CORES

    def at_y(k):
        return p + (lax.rem(y + k, YS) - y) * (CORES * ZS)

    def remote(src, dst, send, recv, **where):
        return pltpu.make_async_remote_copy(
            src_ref=src, dst_ref=dst, send_sem=send, recv_sem=recv,
            device_id=where, device_id_type=MESH,
        )

    def cov_copy(r):
        return pltpu.make_async_copy(cov.at[r], covv.at[r], c_sem.at[r])

    own_copy = pltpu.make_async_copy(start, win.at[1], l_sem)
    own_copy.start()

    def start_cov(r, carry):
        cov_copy(r).start()
        return carry

    lax.fori_loop(0, ROW_BLOCKS, start_cov, 0)

    barrier = pltpu.get_barrier_semaphore()
    peers = [dict(pts=before), dict(pts=after)]
    peers += [dict(cols=h) for h in (g_next, g_prev, g_opp)]
    peers += [dict(pts=at_z(k)) for k in range(1, ZS)]
    peers += [dict(pts=at_y(k)) for k in range(1, YS)]
    for peer in peers:
        pl.semaphore_signal(barrier, inc=1, device_id=peer, device_id_type=MESH)
    pl.semaphore_wait(barrier, len(peers))

    to_after = remote(start, win.at[0], halo_s.at[0], halo_r.at[0], pts=after)
    to_before = remote(start, win.at[2], halo_s.at[1], halo_r.at[1], pts=before)
    to_after.start()
    to_before.start()

    ranks = []
    for a in range(GROUPS):
        rank = jnp.int32(0)
        for t in range(1, GROUPS):
            rank += jnp.where(order[t] == a, t, 0)
        ranks.append(rank)
    row_id = lax.broadcasted_iota(jnp.int32, (WIDTH, WIDTH), 0)
    col_id = lax.broadcasted_iota(jnp.int32, (WIDTH, WIDTH), 1)
    eye = (row_id == col_id).astype(F32)
    upper = (row_id < col_id).astype(F32) + 0.5 * eye
    for a in range(GROUPS):
        for h in range(GROUPS):
            rows, cols = slice(a * WIDTH, (a + 1) * WIDTH), slice(h * WIDTH, (h + 1) * WIDTH)
            if a == h:
                mk[rows, cols] = upper
            else:
                ahead = jnp.where(ranks[a] < ranks[h], 1.0, 0.0).astype(F32)
                mk[rows, cols] = jnp.full((WIDTH, WIDTH), ahead, F32)

    def split_cov(r, carry):
        cov_copy(r).wait()
        for s in range(SLOTS):
            high, low = split(covv[r, s])
            cov_hl[r, :BLOCK, s * BLOCK:(s + 1) * BLOCK] = high
            cov_hl[r, BLOCK:, s * BLOCK:(s + 1) * BLOCK] = low
        return carry

    lax.fori_loop(0, ROW_BLOCKS, split_cov, 0)

    def split_window(side):
        def one(k, carry):
            rows = pl.ds(pl.multiple_of(k * BLOCK, BLOCK), BLOCK)
            high, low = split(win[side, rows, :])
            win_hl[side * ROW_BLOCKS + k, :, :WIDTH] = high
            win_hl[side * ROW_BLOCKS + k, :, WIDTH:] = low
            return carry

        lax.fori_loop(0, ROW_BLOCKS, one, 0)

    own_copy.wait()
    split_window(1)
    to_after.wait_recv()
    split_window(0)
    to_before.wait_recv()
    split_window(2)

    base = p * ROW_BLOCKS - ROW_BLOCKS - NBLK

    def rows_of(src, i):
        r = lax.rem(i + HALF * (1 - lax.div(src, 2)), ROW_BLOCKS)
        return r, pl.ds(pl.multiple_of(r * BLOCK, BLOCK), BLOCK)

    def xcopy(src, i, send, recv, to):
        ref = vall.at[src, rows_of(src, i)[1], :]
        return remote(ref, ref, send.at[i], recv.at[i], cols=to)

    def own_left(i):
        return xcopy(g, i, left_s, next_r, g_prev)

    def own_right(i):
        return xcopy(g, i, right_s, prev_r, g_next)

    def forward_right(i):
        return xcopy(g_prev, i, fwdr_s, opp_r, g_next)

    def forward_left(i):
        return xcopy(g_next, i, fwdl_s, opp_r, g_prev)

    def from_opp(i):
        return xcopy(g_opp, i, fwdr_s, opp_r, g_next)

    def keep_split(src, i):
        rows = rows_of(src, i)[1]
        high, low = split(vall[src, rows, :])
        vhl[src, rows, :WIDTH] = high
        vhl[src, rows, WIDTH:] = low

    def image(i, carry):
        r, rows = rows_of(g, i)
        tiles = []
        for s in range(SLOTS):
            rel = lax.rem(col_index[r, s] - base, NBLK)
            tiles.append(win_hl[lax.min(rel, 3 * ROW_BLOCKS - 1)])
        quad = dot(cov_hl[r], jnp.concatenate(tiles, axis=0))
        vall[g, rows, :] = quarters(quad, BLOCK, WIDTH)
        own_left(i).start()

        @pl.when(i < HALF)
        def _():
            own_right(i).start()

        keep_split(g, i)
        return carry

    lax.fori_loop(0, ROW_BLOCKS, image, 0)

    def pass_right(i, carry):
        own_copy_in = xcopy(g_prev, i, right_s, prev_r, g_next)
        own_copy_in.wait_recv()
        forward_right(i).start()
        keep_split(g_prev, i)
        return carry

    lax.fori_loop(0, HALF, pass_right, 0)

    def rest_right(i, carry):
        own_right(i).start()
        return carry

    lax.fori_loop(HALF, ROW_BLOCKS, rest_right, 0)

    def half_of(src, k):
        return pl.ds(pl.multiple_of(lax.rem(k + 1 - lax.div(src, 2), 2) * (HALF * BLOCK), HALF * BLOCK), HALF * BLOCK)

    def gram_half(src, k):
        rows = half_of(src, k)
        return quarters(dot_t(vhl[g, rows, :], vhl[src, rows, :]), WIDTH, WIDTH)

    gram_own = gram_half(g, 0) + gram_half(g, 1)
    tb[0, :WIDTH, :] = gram_own

    def take_next(i, carry):
        xcopy(g_next, i, left_s, next_r, g_prev).wait_recv()

        @pl.when(i >= HALF)
        def _():
            forward_left(i).start()

        keep_split(g_next, i)
        return carry

    lax.fori_loop(0, HALF, take_next, 0)
    first = gram_half(g_next, 0)

    def take_opp(i, carry):
        from_opp(i).wait_recv()
        keep_split(g_opp, i)
        return carry

    lax.fori_loop(HALF, ROW_BLOCKS, take_next, 0)
    gram_next = first + gram_half(g_next, 1)
    lax.fori_loop(0, HALF, take_opp, 0)
    gram_opp = gram_half(g_opp, 0)
    edge = 3 * WIDTH // 2 - WIDTH
    tb[0, WIDTH:, :] = gram_next[:edge]
    tb[1, :WIDTH - edge, :] = gram_next[edge:]
    tb[1, WIDTH - edge:, :] = gram_opp

    to_core = remote(tb.at[1 - c], r1, p1_s, p1_r, pts=sibling)
    to_core.start()
    to_core.wait_recv()
    s1[...] = (tb[c] + r1[...]).reshape(ZS, PIECE, WIDTH)

    def z_send(k):
        to = lax.rem(z + k, ZS)
        return remote(s1.at[to], r2.at[z], p2_s.at[k], p2_r.at[z], pts=at_z(k))

    def z_recv(k):
        source = lax.rem(z + k, ZS)
        return remote(s1.at[source], r2.at[source], p2_s.at[k], p2_r.at[source], pts=at_z(k))

    for k in range(1, ZS):
        z_send(k).start()
    total = s1[z]
    for k in range(1, ZS):
        z_recv(k).wait_recv()
        total += r2[lax.rem(z + k, ZS)]
    r3[y] = total

    def y_send(k):
        return remote(r3.at[y], r3.at[y], p3_s.at[k], p3_r.at[y], pts=at_y(k))

    def y_recv(k):
        source = lax.rem(y + k, YS)
        return remote(r3.at[source], r3.at[source], p3_s.at[k], p3_r.at[source], pts=at_y(k))

    for k in range(1, YS):
        y_send(k).start()
    for k in range(1, YS):
        y_recv(k).wait_recv()
    gb[g, c, z] = (r3[0] + r3[1]) + (r3[2] + r3[3])

    def z_share(k):
        ref = gb.at[g, c, z]
        return remote(ref, ref, p4_s.at[k], p4_r.at[z], pts=at_z(k))

    def z_shared(k):
        source = lax.rem(z + k, ZS)
        ref = gb.at[g, c, source]
        return remote(ref, ref, p4_s.at[k], p4_r.at[source], pts=at_z(k))

    for k in range(1, ZS):
        z_share(k).start()

    def rest(i, carry):
        xcopy(g_prev, i, right_s, prev_r, g_next).wait_recv()
        keep_split(g_prev, i)
        return carry

    for k in range(1, ZS):
        z_shared(k).wait_recv()

    def x_share(k):
        ref = gb.at[g, c]
        return remote(ref, ref, p5_s.at[k], p5_r.at[g], cols=lax.rem(g + k, GROUPS))

    def x_shared(k):
        source = lax.rem(g + k, GROUPS)
        ref = gb.at[source, c]
        return remote(ref, ref, p5_s.at[k], p5_r.at[source], cols=source)

    def core_share(k):
        source = lax.rem(g + k, GROUPS)
        ref = gb.at[source, c]
        return remote(ref, ref, p6_s.at[source], p6_r.at[source], pts=sibling)

    def core_shared(k):
        source = lax.rem(g + k, GROUPS)
        ref = gb.at[source, 1 - c]
        return remote(ref, ref, p6_s.at[source], p6_r.at[source], pts=sibling)

    for k in range(1, GROUPS):
        x_share(k).start()
    core_share(0).start()
    lax.fori_loop(HALF, ROW_BLOCKS, rest, 0)
    lax.fori_loop(HALF, ROW_BLOCKS, take_opp, 0)
    for k in range(1, GROUPS):
        x_shared(k).wait_recv()
        core_share(k).start()
    for k in range(GROUPS):
        core_shared(k).wait_recv()

    parts = [gb[a].reshape(3 * WIDTH, WIDTH) for a in range(GROUPS)]
    diag = [parts[a][:WIDTH] for a in range(GROUPS)]
    down = [lax.rsqrt(jnp.sum(d * eye, axis=1, keepdims=True)) for d in diag]
    across = [lax.rsqrt(jnp.sum(d * eye, axis=0, keepdims=True)) for d in diag]

    def put(a, h, block):
        rows, cols = slice(a * WIDTH, (a + 1) * WIDTH), slice(h * WIDTH, (h + 1) * WIDTH)
        block = block * down[a] * across[h]
        if a == h:
            block = block - eye
        high, low = split(block)
        e0[rows, cols] = block
        e0_h[rows, cols] = high
        e0_l[rows, cols] = low
        block = -(mk[rows, cols] * block)
        w[rows, cols] = block
        high, low = split(block)
        w_h[rows, cols] = high
        w_l[rows, cols] = low

    for a in range(GROUPS):
        scol[a * WIDTH:(a + 1) * WIDTH, :] = jnp.broadcast_to(down[a], (WIDTH, WIDTH))
        put(a, a, diag[a])
        h = (a + 1) % GROUPS
        block = parts[a][WIDTH:2 * WIDTH]
        put(a, h, block)
        put(h, a, block.T)
    for a in range(GROUPS // 2):
        h = a + GROUPS // 2
        block = parts[a][2 * WIDTH:] + parts[h][2 * WIDTH:].T
        put(a, h, block)
        put(h, a, block.T)

    def tile(m):
        return pl.ds(pl.multiple_of(m * WIDTH, WIDTH), WIDTH)

    def newton(fine):
        def first(m, carry):
            rows = tile(m)
            prod = dot(e0_h[rows, :], w_h[...])
            if fine:
                prod += dot(e0_l[rows, :], w_h[...]) + dot(e0_h[rows, :], w_l[...])
            value = (e0[rows, :] + w[rows, :]) + prod
            b[rows, :] = value
            high, low = split(value)
            b_h[rows, :] = high
            if fine:
                b_l[rows, :] = low
            return carry

        def second(m, carry):
            rows = tile(m)
            prod = dot_t(w_h[:, rows], b_h[...])
            if fine:
                prod += dot_t(w_l[:, rows], b_h[...]) + dot_t(w_h[:, rows], b_l[...])
            here = lax.broadcasted_iota(jnp.int32, (WIDTH, COLS), 0) + m * WIDTH
            there = lax.broadcasted_iota(jnp.int32, (WIDTH, COLS), 1)
            own = jnp.where(here == there, w[rows, :], 0.0)
            value = mk[rows, :] * ((b[rows, :] + own) + prod)
            u[rows, :] = value
            u_h[rows, :] = value.astype(BF16)
            if fine:
                res[...] += jnp.sum((value * value).reshape(WIDTH // 8, 8, COLS), axis=0)
            return carry

        def third(m, carry):
            rows = tile(m)
            value = (w[rows, :] - u[rows, :]) - dot(w_h[rows, :], u_h[...])
            w[rows, :] = value
            high, low = split(value)
            w_h[rows, :] = high
            w_l[rows, :] = low
            return carry

        lax.fori_loop(0, GROUPS, first, 0)
        lax.fori_loop(0, GROUPS, second, 0)
        lax.fori_loop(0, GROUPS, third, 0)

    res[...] = jnp.zeros_like(res)
    newton(False)
    newton(False)
    newton(True)
    residual[...] = jnp.full(residual.shape, jnp.sum(res[...]), F32)

    mine = pl.ds(pl.multiple_of(g * WIDTH, WIDTH), WIDTH)
    for a in range(GROUPS):
        rows = slice(a * WIDTH, (a + 1) * WIDTH)
        same = jnp.where(g == a, 1.0, 0.0).astype(F32)
        high, low = split(scol[rows, :] * (w[rows, mine] + same * eye))
        x_hl[rows, :WIDTH] = high
        x_hl[rows, WIDTH:] = low

    outv = win

    def result(k):
        rows = pl.ds(pl.multiple_of(k * 2 * BLOCK, 2 * BLOCK), 2 * BLOCK)
        return pltpu.make_async_copy(outv.at[1, rows, :], out.at[rows, :], f_sem.at[k])

    def finish(k, carry):
        rows = pl.ds(pl.multiple_of(k * 2 * BLOCK, 2 * BLOCK), 2 * BLOCK)
        high = jnp.concatenate([vhl[h, rows, :WIDTH] for h in range(GROUPS)], axis=1)
        low = jnp.concatenate([vhl[h, rows, WIDTH:] for h in range(GROUPS)], axis=1)
        q = dot(jnp.concatenate([high, low], axis=0), x_hl[...])
        outv[1, rows, :] = quarters(q, 2 * BLOCK, WIDTH)
        result(k).start()
        return carry

    lax.fori_loop(0, ROW_BLOCKS // 2, finish, 0)

    to_after.wait_send()
    to_before.wait_send()

    def sent(i, carry):
        own_left(i).wait_send()
        own_right(i).wait_send()
        return carry

    def sent_on(i, carry):
        forward_right(i).wait_send()
        forward_left(i + HALF).wait_send()
        return carry

    lax.fori_loop(0, ROW_BLOCKS, sent, 0)
    lax.fori_loop(0, HALF, sent_on, 0)
    to_core.wait_send()
    for k in range(1, ZS):
        z_send(k).wait_send()
        z_share(k).wait_send()
    for k in range(1, YS):
        y_send(k).wait_send()
    for k in range(1, GROUPS):
        x_share(k).wait_send()
    for k in range(GROUPS):
        core_share(k).wait_send()

    def written(k, carry):
        result(k).wait()
        return carry

    lax.fori_loop(0, ROW_BLOCKS // 2, written, 0)


def fast(start, cov_blocks, col_index, order):
    dma = pltpu.SemaphoreType.DMA
    square = (COLS, COLS)
    hbm = pl.BlockSpec(memory_space=pl.ANY)
    smem = pl.BlockSpec(memory_space=pltpu.SMEM)
    return pl.pallas_call(
        kernel,
        out_shape=(
            jax.ShapeDtypeStruct((ROWS, WIDTH), F32),
            jax.ShapeDtypeStruct((8, 128), F32),
        ),
        in_specs=[hbm, hbm, smem, smem],
        out_specs=(hbm, pl.BlockSpec(memory_space=pltpu.VMEM)),
        scratch_shapes=[
            pltpu.VMEM((3, ROWS, WIDTH), F32),
            pltpu.VMEM((3 * ROW_BLOCKS, BLOCK, 2 * WIDTH), BF16),
            pltpu.VMEM((ROW_BLOCKS, SLOTS, BLOCK, BLOCK), F32),
            pltpu.VMEM((ROW_BLOCKS, 2 * BLOCK, SLOTS * BLOCK), BF16),
            pltpu.VMEM((GROUPS, ROWS, WIDTH), F32),
            pltpu.VMEM((GROUPS, ROWS, 2 * WIDTH), BF16),
            pltpu.VMEM((CORES, ZS * PIECE, WIDTH), F32),
            pltpu.VMEM((ZS * PIECE, WIDTH), F32),
            pltpu.VMEM((ZS, PIECE, WIDTH), F32),
            pltpu.VMEM((ZS, PIECE, WIDTH), F32),
            pltpu.VMEM((YS, PIECE, WIDTH), F32),
            pltpu.VMEM((GROUPS, CORES, ZS, PIECE, WIDTH), F32),
            pltpu.VMEM(square, F32),
            pltpu.VMEM(square, F32),
            pltpu.VMEM(square, F32),
            pltpu.VMEM(square, F32),
            pltpu.VMEM(square, F32),
            pltpu.VMEM(square, BF16),
            pltpu.VMEM(square, BF16),
            pltpu.VMEM(square, BF16),
            pltpu.VMEM(square, BF16),
            pltpu.VMEM(square, BF16),
            pltpu.VMEM(square, BF16),
            pltpu.VMEM(square, BF16),
            pltpu.VMEM((COLS, 2 * WIDTH), BF16),
            pltpu.VMEM((8, COLS), F32),
            pltpu.VMEM((COLS, WIDTH), F32),
            dma((ROW_BLOCKS,)),
            dma,
            dma,
            dma((ROW_BLOCKS // 2,)),
            dma((2,)), dma((2,)),
            dma((ROW_BLOCKS,)), dma((ROW_BLOCKS,)),
            dma((ROW_BLOCKS,)), dma((ROW_BLOCKS,)),
            dma((ROW_BLOCKS,)), dma((ROW_BLOCKS,)), dma((ROW_BLOCKS,)),
            dma, dma,
            dma((ZS,)), dma((ZS,)),
            dma((YS,)), dma((YS,)),
            dma((ZS,)), dma((ZS,)),
            dma((GROUPS,)), dma((GROUPS,)),
            dma((GROUPS,)), dma((GROUPS,)),
        ],
        compiler_params=pltpu.CompilerParams(
            collective_id=0, has_side_effects=True, vmem_limit_bytes=56 * 1024 * 1024
        ),
    )(start, cov_blocks, col_index, order)


def body(start, cov_blocks, col_index, order):
    result, residual = fast(start, cov_blocks, col_index, order)
    return lax.cond(
        residual[0, 0] < TOLERANCE,
        lambda: result,
        lambda: careful(start, cov_blocks, col_index, order),
    )


def solution(mesh):
    placed = (P("pts", "cols"), P("pts", None, None, None), P("pts", None), P())
    return jax.shard_map(
        body, mesh=mesh, in_specs=placed, out_specs=P("pts", "cols"), check_vma=False
    )
```

time: 1700 us -> 1770 us (1.041)
  Pallas kernels: 0 us -> 67.2 us
    pallas_call x0 -> x1, Pallas kernels: none -> 67.2 us  [fast(): pl.pallas_call(kernel, out_shape=(jax.ShapeDtypeStruct((ROWS, WIDTH), F32...]
where the time goes in v1:
time: 1770 us
  waiting for transfers between devices  1530 us (86%)
  other arithmetic  95.6 us (5%)
  Pallas kernels  67.2 us (4%)
  matrix products  35.4 us (2%)
    psum x4, waiting for transfers between devices, step(): coef = lax.psum(inner(ortho, local), 'pts')  677 us
    psum x4, waiting for transfers between devices, step(): gram = lax.psum(inner(local, local), 'pts')  666 us
    psum x4, waiting for transfers between devices, broadcast(): return lax.psum(kept, axis)  177 us
    pallas_call x1, Pallas kernels, fast(): pl.pallas_call(kernel, out_shape=(jax.ShapeDtypeStruct((ROWS, WIDTH), F32...  67.2 us
    another operation x12, other arithmetic, step(): lower = jnp.linalg.cholesky(gram)  49.6 us
    another operation x8, other arithmetic, step(): lax.linalg.triangular_solve(lower, local, left_side=False, lower=True, tr...  41.9 us
  transfers between devices with their start and end apart: 14, of which 13 were waited for; matrix products, arithmetic and copies ran while one was open for 0% of the time, Pallas kernels for 0%

profile of v1, /device:TPU:6, one launch (start us, length us, event | category | flops | bytes accessed | tf_op | source)
XLA Modules:
  0.0 1765.1 jit_solution(17948929930217522207)
XLA Ops:
  6.5 67.2 %shard_map.48 = (f32[1024,128]{1,0:T(8,128)S(1)}, f32[8,128]{1,0:T(8,128)}) custom-call(f32[1024,128]{1,0:T(8,128)} %start.1, f32[8,8,128,128]{3,2,1,0:T(8,128)} %cov.1, s32[8,8]{1,0:T(8,128)} %col_index.1, s32[4]{0:T(128)} %order.1), custom_call_target="tpu_custom_call" | custom-call | tf_op jit(solution)/shard_map/pallas_call | solution.py:539
  75.7 1681.8 %conditional.1 = (f32[1024,128]{1,0:T(8,128)S(1)}) conditional(s32[]{:T(128)} %bitcast.11, (f32[1024,128]{1,0:T(8,128)S(1)}, s32[8,8]{1,0:T(8,128)S(1)}, f32[8,8,128,128]{3,2,1,0:T(8,128)}, s32[4]{0:T(128)S(1)}) %tuple.61, f32[1024,128]{1,0:T(8,128)S(1)} %get-tuple-element.156), branch_computations={%region_0.9_spmd, %region_9.10_spmd} | conditional | flops 2417543168 | bytes 35658756 | solution.py:598
  90.5 7.9 fusion.9
  98.7 1658.3 %while.14 = (s32[]{:T(128)}, f32[1024,128]{0,1:T(8,128)S(1)}, s32[]{:T(128)}, s32[4]{0:T(128)S(1)}, s32[]{:T(128)}, /*index=5*/s32[]{:T(128)}, u32[]{:T(128)}) while((s32[]{:T(128)}, f32[1024,128]{0,1:T(8,128)S(1)}, s32[]{:T(128)}, s32[4]{0:T(128)S(1)}, s32[]{:T(128)}, /*index=5*/s32[]{:T(128)}, u32[]{:T(128)}) %tuple.48), condition=%wide.region_8.8_spmd, body=%wide.region_2.7_spmd.sunk | while | flops 806142080 | bytes 8914181 | solution.py:84
  101.5 167.4 %all-reduce.4.cloned.1.call-done = f32[128,128]{0,1:T(8,128)} async-done(((f32[128,128]{0,1:T(8,128)}), f32[128,128]{0,1:T(8,128)}) %all-reduce.4.cloned.1.call-update) | async-done | bytes 65552 | tf_op jit(solution)/shard_map/cond/branch_0_fun/while/body/eval_jaxpr/psum | solution.py:72
  270.7 11.7 cholesky.58
  283.8 9.8 custom-call.23
  295.1 44.3 %all-reduce.6.cloned.1.call-done = f32[1024,128]{0,1:T(8,128)} async-done(((f32[1024,128]{0,1:T(8,128)}), f32[1024,128]{0,1:T(8,128)}) %all-reduce.6.cloned.1.call-update) | async-done | bytes 524304 | tf_op jit(solution)/shard_map/cond/branch_0_fun/while/body/eval_jaxpr/psum | solution.py:27
  342.9 169.3 %all-reduce.8.cloned.1.call-done = f32[128,128]{1,0:T(8,128)} async-done(((f32[128,128]{1,0:T(8,128)}), f32[128,128]{1,0:T(8,128)}) %all-reduce.8.cloned.1.call-update) | async-done | bytes 65552 | tf_op jit(solution)/shard_map/cond/branch_0_fun/while/body/eval_jaxpr/psum | solution.py:78
  516.9 166.3 %all-reduce.4.cloned.1.call-done = f32[128,128]{0,1:T(8,128)} async-done(((f32[128,128]{0,1:T(8,128)}), f32[128,128]{0,1:T(8,128)}) %all-reduce.4.cloned.1.call-update) | async-done | bytes 65552 | tf_op jit(solution)/shard_map/cond/branch_0_fun/while/body/eval_jaxpr/psum | solution.py:72
  685.0 11.7 cholesky.58
  698.0 9.8 custom-call.23
  709.3 44.3 %all-reduce.6.cloned.1.call-done = f32[1024,128]{0,1:T(8,128)} async-done(((f32[1024,128]{0,1:T(8,128)}), f32[1024,128]{0,1:T(8,128)}) %all-reduce.6.cloned.1.call-update) | async-done | bytes 524304 | tf_op jit(solution)/shard_map/cond/branch_0_fun/while/body/eval_jaxpr/psum | solution.py:27
  757.2 169.2 %all-reduce.8.cloned.1.call-done = f32[128,128]{1,0:T(8,128)} async-done(((f32[128,128]{1,0:T(8,128)}), f32[128,128]{1,0:T(8,128)}) %all-reduce.8.cloned.1.call-update) | async-done | bytes 65552 | tf_op jit(solution)/shard_map/cond/branch_0_fun/while/body/eval_jaxpr/psum | solution.py:78
  931.0 166.5 %all-reduce.4.cloned.1.call-done = f32[128,128]{0,1:T(8,128)} async-done(((f32[128,128]{0,1:T(8,128)}), f32[128,128]{0,1:T(8,128)}) %all-reduce.4.cloned.1.call-update) | async-done | bytes 65552 | tf_op jit(solution)/shard_map/cond/branch_0_fun/while/body/eval_jaxpr/psum | solution.py:72
  1099.4 11.7 cholesky.58
  1112.4 9.8 custom-call.23
  1123.7 44.3 %all-reduce.6.cloned.1.call-done = f32[1024,128]{0,1:T(8,128)} async-done(((f32[1024,128]{0,1:T(8,128)}), f32[1024,128]{0,1:T(8,128)}) %all-reduce.6.cloned.1.call-update) | async-done | bytes 524304 | tf_op jit(solution)/shard_map/cond/branch_0_fun/while/body/eval_jaxpr/psum | solution.py:27
  1171.6 169.3 %all-reduce.8.cloned.1.call-done = f32[128,128]{1,0:T(8,128)} async-done(((f32[128,128]{1,0:T(8,128)}), f32[128,128]{1,0:T(8,128)}) %all-reduce.8.cloned.1.call-update) | async-done | bytes 65552 | tf_op jit(solution)/shard_map/cond/branch_0_fun/while/body/eval_jaxpr/psum | solution.py:78
  1345.6 166.3 %all-reduce.4.cloned.1.call-done = f32[128,128]{0,1:T(8,128)} async-done(((f32[128,128]{0,1:T(8,128)}), f32[128,128]{0,1:T(8,128)}) %all-reduce.4.cloned.1.call-update) | async-done | bytes 65552 | tf_op jit(solution)/shard_map/cond/branch_0_fun/while/body/eval_jaxpr/psum | solution.py:72
  1513.6 11.7 cholesky.58
  1526.7 9.8 custom-call.23
  1538.0 44.3 %all-reduce.6.cloned.1.call-done = f32[1024,128]{0,1:T(8,128)} async-done(((f32[1024,128]{0,1:T(8,128)}), f32[1024,128]{0,1:T(8,128)}) %all-reduce.6.cloned.1.call-update) | async-done | bytes 524304 | tf_op jit(solution)/shard_map/cond/branch_0_fun/while/body/eval_jaxpr/psum | solution.py:27
  1585.8 169.2 %all-reduce.8.cloned.1.call-done = f32[128,128]{1,0:T(8,128)} async-done(((f32[128,128]{1,0:T(8,128)}), f32[128,128]{1,0:T(8,128)}) %all-reduce.8.cloned.1.call-update) | async-done | bytes 65552 | tf_op jit(solution)/shard_map/cond/branch_0_fun/while/body/eval_jaxpr/psum | solution.py:78
  (84 shorter events, 60.4 us)
Async XLA Ops:
  6.5 69.1 %copy-start.1 = (s32[8,8]{1,0:T(8,128)S(1)}, s32[8,8]{1,0:T(8,128)}, u32[]{:S(2)}) copy-start(s32[8,8]{1,0:T(8,128)} %col_index.1) | copy-start | bytes 772
  6.5 69.1 %copy-start.2 = (s32[4]{0:T(128)S(1)}, s32[4]{0:T(128)}, u32[]{:S(2)}) copy-start(s32[4]{0:T(128)} %order.1) | copy-start | bytes 52
  6.5 69.1 %copy-start = (f32[1024,128]{1,0:T(8,128)S(1)}, f32[1024,128]{1,0:T(8,128)}, u32[]{:S(2)}) copy-start(f32[1024,128]{1,0:T(8,128)} %start.1) | copy-start | bytes 1572868
  75.7 12.0 collective-permute-start
  77.3 10.4 collective-permute-start.1
  98.9 170.1 %all-reduce.4.cloned.1.call-start = ((), (), s32[]{:S(2)}) async-start(), calls=%async_computation | async-start | bytes 131072 | tf_op jit(solution)/shard_map/cond/branch_0_fun/while/body/eval_jaxpr/psum | solution.py:72
  100.2 239.2 %all-reduce.6.cloned.1.call-start = ((), (), s32[]{:S(2)}) async-start(), calls=%async_computation.1 | async-start | bytes 1048576 | tf_op jit(solution)/shard_map/cond/branch_0_fun/while/body/eval_jaxpr/psum | solution.py:27
  295.0 217.2 %all-reduce.8.cloned.1.call-start = ((), (), s32[]{:S(2)}) async-start(), calls=%async_computation.2 | async-start | bytes 131072 | tf_op jit(solution)/shard_map/cond/branch_0_fun/while/body/eval_jaxpr/psum | solution.py:78
  514.2 168.9 %all-reduce.4.cloned.1.call-start = ((), (), s32[]{:S(2)}) async-start(), calls=%async_computation | async-start | bytes 131072 | tf_op jit(solution)/shard_map/cond/branch_0_fun/while/body/eval_jaxpr/psum | solution.py:72
  515.5 238.1 %all-reduce.6.cloned.1.call-start = ((), (), s32[]{:S(2)}) async-start(), calls=%async_computation.1 | async-start | bytes 1048576 | tf_op jit(solution)/shard_map/cond/branch_0_fun/while/body/eval_jaxpr/psum | solution.py:27
  709.3 217.1 %all-reduce.8.cloned.1.call-start = ((), (), s32[]{:S(2)}) async-start(), calls=%async_computation.2 | async-start | bytes 131072 | tf_op jit(solution)/shard_map/cond/branch_0_fun/while/body/eval_jaxpr/psum | solution.py:78
  928.4 169.2 %all-reduce.4.cloned.1.call-start = ((), (), s32[]{:S(2)}) async-start(), calls=%async_computation | async-start | bytes 131072 | tf_op jit(solution)/shard_map/cond/branch_0_fun/while/body/eval_jaxpr/psum | solution.py:72
  929.6 238.4 %all-reduce.6.cloned.1.call-start = ((), (), s32[]{:S(2)}) async-start(), calls=%async_computation.1 | async-start | bytes 1048576 | tf_op jit(solution)/shard_map/cond/branch_0_fun/while/body/eval_jaxpr/psum | solution.py:27
  1123.7 217.2 %all-reduce.8.cloned.1.call-start = ((), (), s32[]{:S(2)}) async-start(), calls=%async_computation.2 | async-start | bytes 131072 | tf_op jit(solution)/shard_map/cond/branch_0_fun/while/body/eval_jaxpr/psum | solution.py:78
  1342.9 168.9 %all-reduce.4.cloned.1.call-start = ((), (), s32[]{:S(2)}) async-start(), calls=%async_computation | async-start | bytes 131072 | tf_op jit(solution)/shard_map/cond/branch_0_fun/while/body/eval_jaxpr/psum | solution.py:72
  1344.2 238.1 %all-reduce.6.cloned.1.call-start = ((), (), s32[]{:S(2)}) async-start(), calls=%async_computation.1 | async-start | bytes 1048576 | tf_op jit(solution)/shard_map/cond/branch_0_fun/while/body/eval_jaxpr/psum | solution.py:27
  1538.0 217.1 %all-reduce.8.cloned.1.call-start = ((), (), s32[]{:S(2)}) async-start(), calls=%async_computation.2 | async-start | bytes 131072 | tf_op jit(solution)/shard_map/cond/branch_0_fun/while/body/eval_jaxpr/psum | solution.py:78
Sparse Core Ops, SparseCore 0:
  103.2 165.6 all-reduce.3
  295.2 44.2 all-reduce.5
  342.9 169.3 all-reduce.7
  518.2 164.8 all-reduce.3
  709.4 44.2 all-reduce.5
  757.0 169.3 all-reduce.7
  932.7 164.8 all-reduce.3
  1123.8 44.2 all-reduce.5
  1171.5 169.3 all-reduce.7
  1346.9 164.8 all-reduce.3
  1538.1 44.2 all-reduce.5
  1585.6 169.3 all-reduce.7

commit v2 on v1

--- a/solution.py
+++ b/solution.py
@@ -22,9 +22,18 @@
 TOLERANCE = 1e-4
 
 
+def total(value, axis):
+    distance = 1
+    while distance < lax.axis_size(axis):
+        pairs = [(i, i ^ distance) for i in range(lax.axis_size(axis))]
+        value = value + lax.ppermute(value, axis, pairs)
+        distance *= 2
+    return value
+
+
 def broadcast(value, axis, source):
     kept = jnp.where(lax.axis_index(axis) == source, value, 0).astype(value.dtype)
-    return lax.psum(kept, axis)
+    return total(kept, axis)
 
 
 def with_halo(cells, axis, width):
@@ -69,13 +78,13 @@
 
     def step(t, local):
         owner = order[t]
-        gram = lax.psum(inner(local, local), "pts")
+        gram = total(inner(local, local), "pts")
         lower = jnp.linalg.cholesky(gram)
         candidate = lax.linalg.triangular_solve(
             lower, local, left_side=False, lower=True, transpose_a=True
         )
         ortho = broadcast(candidate, "cols", owner)
-        coef = lax.psum(inner(ortho, local), "pts")
+        coef = total(inner(ortho, local), "pts")
         updated = local - jnp.dot(
             ortho, coef, precision=lax.Precision.HIGHEST, preferred_element_type=F32
         )
@@ -320,11 +329,11 @@
 
     for k in range(1, ZS):
         z_send(k).start()
-    total = s1[z]
+    summed = s1[z]
     for k in range(1, ZS):
         z_recv(k).wait_recv()
-        total += r2[lax.rem(z + k, ZS)]
-    r3[y] = total
+        summed += r2[lax.rem(z + k, ZS)]
+    r3[y] = summed
 
     def y_send(k):
         return remote(r3.at[y], r3.at[y], p3_s.at[k], p3_r.at[y], pts=at_y(k))

time: 1770 us -> 538 us (0.30)
  waiting for transfers between devices: 1530 us -> 265 us
  starting transfers between devices: 5.64 us -> 77.2 us
    psum x12 -> x0, waiting for transfers between devices: 1520 us -> none  [the longest x4 677 us: step(): coef = lax.psum(inner(ortho, local), 'pts')]
    ppermute x0 -> x56, waiting for transfers between devices: none -> 258 us  [total(): value = value + lax.ppermute(value, axis, pairs)]
    ppermute x0 -> x56, starting transfers between devices: none -> 72 us  [total(): value = value + lax.ppermute(value, axis, pairs)]
  transfers between devices with their start and end apart: 14 -> 58, of which waited for: 13 -> 57; matrix products, arithmetic and copies ran while one was open for 0% -> 1% of each run, Pallas kernels for 0% -> 0%
where the time goes in v2:
time: 538 us
  waiting for transfers between devices  265 us (49%)
  other arithmetic  93.2 us (17%)
  starting transfers between devices  77.2 us (14%)
  Pallas kernels  67.4 us (13%)
  matrix products  18.2 us (3%)
  loops' own time  8.6 us (2%)
  local copies, waits for them, and re-layouts  8.04 us (1%)
    ppermute x56, waiting for transfers between devices, total(): value = value + lax.ppermute(value, axis, pairs)  258 us
    ppermute x56, starting transfers between devices, total(): value = value + lax.ppermute(value, axis, pairs)  72 us
    pallas_call x1, Pallas kernels, fast(): pl.pallas_call(kernel, out_shape=(jax.ShapeDtypeStruct((ROWS, WIDTH), F32...  67.4 us
    another operation x12, other arithmetic, step(): lower = jnp.linalg.cholesky(gram)  49.8 us
    another operation x8, other arithmetic, step(): lax.linalg.triangular_solve(lower, local, left_side=False, lower=True, tr...  41.8 us
  transfers between devices with their start and end apart: 58, of which 57 were waited for; matrix products, arithmetic and copies ran while one was open for 1% of the time, Pallas kernels for 0%

profile of v2, /device:TPU:6, one launch (start us, length us, event | category | flops | bytes accessed | tf_op | source)
XLA Modules:
  0.0 537.9 jit_solution(6623471512688319217)
XLA Ops:
  0.0 67.4 %shard_map.48 = (f32[1024,128]{1,0:T(8,128)S(1)}, f32[8,128]{1,0:T(8,128)}) custom-call(f32[1024,128]{1,0:T(8,128)} %start.1, f32[8,8,128,128]{3,2,1,0:T(8,128)} %cov.1, s32[8,8]{1,0:T(8,128)} %col_index.1, s32[4]{0:T(128)} %order.1), custom_call_target="tpu_custom_call" | custom-call | tf_op jit(solution)/shard_map/pallas_call | solution.py:548
  69.3 467.8 %conditional.1 = (f32[1024,128]{1,0:T(8,128)S(1)}) conditional(s32[]{:T(128)} %bitcast.11, (f32[1024,128]{1,0:T(8,128)S(1)}, s32[8,8]{1,0:T(8,128)S(1)}, f32[8,8,128,128]{3,2,1,0:T(8,128)}, s32[4]{0:T(128)S(1)}) %tuple.55, f32[1024,128]{1,0:T(8,128)S(1)} %get-tuple-element.156), branch_computations={%region_0.6_spmd, %region_6.7_spmd} | conditional | flops 2417838080 | bytes 44441020 | solution.py:607
  75.2 6.1 %collective-permute-done.14 = f32[1024,128]{1,0:T(8,128)S(1)} collective-permute-done((f32[1024,128]{1,0:T(8,128)S(1)}, f32[1024,128]{1,0:T(8,128)S(1)}, u32[]{:S(2)}, u32[]{:S(2)}) %collective-permute-start.14) | collective-permute-done | bytes 524320 | tf_op jit(solution)/shard_map/cond/branch_0_fun/ppermute | solution.py:45
  84.2 7.9 %fusion.10 = f32[8,128,128,1]{1,2,3,0:T(8,128)S(1)} fusion(f32[8,8,128,128]{3,2,1,0:T(8,128)} %bitcast.52, f32[8,8,128,128]{3,2,1,0:T(8,128)} %get-tuple-element.150), kind=kOutput, calls=%fused_computation.26 | convolution fusion | flops 1610612736 | bytes 8912896 | tf_op jit(solution)/shard_map/cond/branch_0_fun/rsab,rsbk->rak/dot_general | solution.py:75
  92.3 444.3 %while.14 = (s32[]{:T(128)}, f32[1024,128]{0,1:T(8,128)S(1)}, s32[]{:T(128)}, s32[4]{0:T(128)S(1)}, s32[]{:T(128)}, /*index=5*/s32[]{:T(128)}, u32[]{:T(128)}) while((s32[]{:T(128)}, f32[1024,128]{0,1:T(8,128)S(1)}, s32[]{:T(128)}, s32[4]{0:T(128)S(1)}, s32[]{:T(128)}, /*index=5*/s32[]{:T(128)}, u32[]{:T(128)}) %tuple.48), condition=%wide.region_5.5_spmd, body=%wide.region_2.4_spmd.sunk | while | flops 806436992 | bytes 17696444 | solution.py:93
  107.5 5.5 %collective-permute-done.3 = f32[128,128]{0,1:T(8,128)S(1)} collective-permute-done((f32[128,128]{0,1:T(8,128)S(1)}, f32[128,128]{0,1:T(8,128)S(1)}, u32[]{:S(2)}, u32[]{:S(2)}) %collective-permute-start.3) | collective-permute-done | bytes 65568 | tf_op jit(solution)/shard_map/cond/branch_0_fun/while/body/eval_jaxpr/ppermute | solution.py:29
  123.9 11.7 %cholesky.58 = f32[128,128]{1,0:T(8,128)S(1)} custom-call(f32[128,128]{1,0:T(8,128)S(1)} %fusion.42), custom_call_target="Cholesky" | custom-call | tf_op jit(solution)/shard_map/cond/branch_0_fun/while/body/eval_jaxpr/jit(cholesky)/cholesky | solution.py:82
  137.0 9.8 %custom-call.23 = f32[1,128,128]{1,2,0:T(8,128)S(1)} custom-call(f32[1,128,128]{2,1,0:T(8,128)S(1)} %fusion.43), custom_call_target="InvertDiagBlocksLowerTriangular" | custom-call | tf_op jit(solution)/shard_map/cond/branch_0_fun/while/body/eval_jaxpr/triangular_solve | solution.py:83
  147.5 12.5 %collective-permute-done.6 = f32[1024,128]{0,1:T(8,128)S(1)} collective-permute-done((f32[1024,128]{0,1:T(8,128)S(1)}, f32[1024,128]{0,1:T(8,128)S(1)}, u32[]{:S(2)}, u32[]{:S(2)}) %collective-permute-start.6) | collective-permute-done | bytes 524320 | tf_op jit(solution)/shard_map/cond/branch_0_fun/while/body/eval_jaxpr/ppermute | solution.py:29
  160.3 10.6 %collective-permute-done.7 = f32[1024,128]{0,1:T(8,128)S(1)} collective-permute-done((f32[1024,128]{0,1:T(8,128)S(1)}, f32[1024,128]{0,1:T(8,128)S(1)}, u32[]{:S(2)}, u32[]{:S(2)}) %collective-permute-start.7) | collective-permute-done | bytes 524320 | tf_op jit(solution)/shard_map/cond/branch_0_fun/while/body/eval_jaxpr/ppermute | solution.py:29
  234.2 11.7 %cholesky.58 = f32[128,128]{1,0:T(8,128)S(1)} custom-call(f32[128,128]{1,0:T(8,128)S(1)} %fusion.42), custom_call_target="Cholesky" | custom-call | tf_op jit(solution)/shard_map/cond/branch_0_fun/while/body/eval_jaxpr/jit(cholesky)/cholesky | solution.py:82
  247.3 9.8 %custom-call.23 = f32[1,128,128]{1,2,0:T(8,128)S(1)} custom-call(f32[1,128,128]{2,1,0:T(8,128)S(1)} %fusion.43), custom_call_target="InvertDiagBlocksLowerTriangular" | custom-call | tf_op jit(solution)/shard_map/cond/branch_0_fun/while/body/eval_jaxpr/triangular_solve | solution.py:83
  257.9 14.5 %collective-permute-done.6 = f32[1024,128]{0,1:T(8,128)S(1)} collective-permute-done((f32[1024,128]{0,1:T(8,128)S(1)}, f32[1024,128]{0,1:T(8,128)S(1)}, u32[]{:S(2)}, u32[]{:S(2)}) %collective-permute-start.6) | collective-permute-done | bytes 524320 | tf_op jit(solution)/shard_map/cond/branch_0_fun/while/body/eval_jaxpr/ppermute | solution.py:29
  272.5 10.7 %collective-permute-done.7 = f32[1024,128]{0,1:T(8,128)S(1)} collective-permute-done((f32[1024,128]{0,1:T(8,128)S(1)}, f32[1024,128]{0,1:T(8,128)S(1)}, u32[]{:S(2)}, u32[]{:S(2)}) %collective-permute-start.7) | collective-permute-done | bytes 524320 | tf_op jit(solution)/shard_map/cond/branch_0_fun/while/body/eval_jaxpr/ppermute | solution.py:29
  321.0 5.5 %collective-permute-done.2 = f32[128,128]{0,1:T(8,128)S(1)} collective-permute-done((f32[128,128]{0,1:T(8,128)S(1)}, f32[128,128]{0,1:T(8,128)S(1)}, u32[]{:S(2)}, u32[]{:S(2)}) %collective-permute-start.2) | collective-permute-done | bytes 65568 | tf_op jit(solution)/shard_map/cond/branch_0_fun/while/body/eval_jaxpr/ppermute | solution.py:29
  345.4 11.7 %cholesky.58 = f32[128,128]{1,0:T(8,128)S(1)} custom-call(f32[128,128]{1,0:T(8,128)S(1)} %fusion.42), custom_call_target="Cholesky" | custom-call | tf_op jit(solution)/shard_map/cond/branch_0_fun/while/body/eval_jaxpr/jit(cholesky)/cholesky | solution.py:82
  358.5 9.8 %custom-call.23 = f32[1,128,128]{1,2,0:T(8,128)S(1)} custom-call(f32[1,128,128]{2,1,0:T(8,128)S(1)} %fusion.43), custom_call_target="InvertDiagBlocksLowerTriangular" | custom-call | tf_op jit(solution)/shard_map/cond/branch_0_fun/while/body/eval_jaxpr/triangular_solve | solution.py:83
  369.0 14.1 %collective-permute-done.6 = f32[1024,128]{0,1:T(8,128)S(1)} collective-permute-done((f32[1024,128]{0,1:T(8,128)S(1)}, f32[1024,128]{0,1:T(8,128)S(1)}, u32[]{:S(2)}, u32[]{:S(2)}) %collective-permute-start.6) | collective-permute-done | bytes 524320 | tf_op jit(solution)/shard_map/cond/branch_0_fun/while/body/eval_jaxpr/ppermute | solution.py:29
  383.3 10.7 %collective-permute-done.7 = f32[1024,128]{0,1:T(8,128)S(1)} collective-permute-done((f32[1024,128]{0,1:T(8,128)S(1)}, f32[1024,128]{0,1:T(8,128)S(1)}, u32[]{:S(2)}, u32[]{:S(2)}) %collective-permute-start.7) | collective-permute-done | bytes 524320 | tf_op jit(solution)/shard_map/cond/branch_0_fun/while/body/eval_jaxpr/ppermute | solution.py:29
  457.2 11.7 %cholesky.58 = f32[128,128]{1,0:T(8,128)S(1)} custom-call(f32[128,128]{1,0:T(8,128)S(1)} %fusion.42), custom_call_target="Cholesky" | custom-call | tf_op jit(solution)/shard_map/cond/branch_0_fun/while/body/eval_jaxpr/jit(cholesky)/cholesky | solution.py:82
  470.3 9.8 %custom-call.23 = f32[1,128,128]{1,2,0:T(8,128)S(1)} custom-call(f32[1,128,128]{2,1,0:T(8,128)S(1)} %fusion.43), custom_call_target="InvertDiagBlocksLowerTriangular" | custom-call | tf_op jit(solution)/shard_map/cond/branch_0_fun/while/body/eval_jaxpr/triangular_solve | solution.py:83
  480.8 13.1 %collective-permute-done.6 = f32[1024,128]{0,1:T(8,128)S(1)} collective-permute-done((f32[1024,128]{0,1:T(8,128)S(1)}, f32[1024,128]{0,1:T(8,128)S(1)}, u32[]{:S(2)}, u32[]{:S(2)}) %collective-permute-start.6) | collective-permute-done | bytes 524320 | tf_op jit(solution)/shard_map/cond/branch_0_fun/while/body/eval_jaxpr/ppermute | solution.py:29
  494.1 10.7 %collective-permute-done.7 = f32[1024,128]{0,1:T(8,128)S(1)} collective-permute-done((f32[1024,128]{0,1:T(8,128)S(1)}, f32[1024,128]{0,1:T(8,128)S(1)}, u32[]{:S(2)}, u32[]{:S(2)}) %collective-permute-start.7) | collective-permute-done | bytes 524320 | tf_op jit(solution)/shard_map/cond/branch_0_fun/while/body/eval_jaxpr/ppermute | solution.py:29
  516.4 6.0 %collective-permute-start.11 = (f32[128,128]{1,0:T(8,128)S(1)}, f32[128,128]{1,0:T(8,128)S(1)}, u32[]{:S(2)}, u32[]{:S(2)}) collective-permute-start(f32[128,128]{1,0:T(8,128)S(1)} %add.236), channel_id=1, source_target_pairs={{0,32},{4,36},{8,40},{12,44},{16,48},{20,52},{24,56},{28,60},{32,0... | collective-permute-start | bytes 196616 | tf_op jit(solution)/shard_map/cond/branch_0_fun/while/body/eval_jaxpr/ppermute | solution.py:29
  (212 shorter events, 247.2 us)
Async XLA Ops:
  69.3 12.0 %collective-permute-start.14 = (f32[1024,128]{1,0:T(8,128)S(1)}, f32[1024,128]{1,0:T(8,128)S(1)}, u32[]{:S(2)}, u32[]{:S(2)}) collective-permute-start(f32[1024,128]{1,0:T(8,128)S(1)} %get-tuple-element.148), channel_id=1, source_target_pairs={{0,4},{4,8},{8,12},{12,16},{16,20},{20,24},{24,28},{28,32},{32,36}... | collective-permute-start | bytes 1572872 | tf_op jit(solution)/shard_map/cond/branch_0_fun/ppermute | solution.py:45
  70.9 10.4 %collective-permute-start.15 = (f32[1024,128]{1,0:T(8,128)S(1)}, f32[1024,128]{1,0:T(8,128)S(1)}, u32[]{:S(2)}, u32[]{:S(2)}) collective-permute-start(f32[1024,128]{1,0:T(8,128)S(1)} %get-tuple-element.148), channel_id=1, source_target_pairs={{4,0},{8,4},{12,8},{16,12},{20,16},{24,20},{28,24},{32,28},{36,32}... | collective-permute-start | bytes 1572872 | tf_op jit(solution)/shard_map/cond/branch_0_fun/ppermute | solution.py:47
  98.8 6.0 %collective-permute-start.2 = (f32[128,128]{0,1:T(8,128)S(1)}, f32[128,128]{0,1:T(8,128)S(1)}, u32[]{:S(2)}, u32[]{:S(2)}) collective-permute-start(f32[128,128]{0,1:T(8,128)S(1)} %add.227), channel_id=1, source_target_pairs={{0,16},{4,20},{8,24},{12,28},{16,0},{20,4},{24,8},{28,12},{32,48},... | collective-permute-start | bytes 196616 | tf_op jit(solution)/shard_map/cond/branch_0_fun/while/body/eval_jaxpr/ppermute | solution.py:29
  104.8 8.3 %collective-permute-start.3 = (f32[128,128]{0,1:T(8,128)S(1)}, f32[128,128]{0,1:T(8,128)S(1)}, u32[]{:S(2)}, u32[]{:S(2)}) collective-permute-start(f32[128,128]{0,1:T(8,128)S(1)} %add.228), channel_id=1, source_target_pairs={{0,32},{4,36},{8,40},{12,44},{16,48},{20,52},{24,56},{28,60},{32,0... | collective-permute-start | bytes 196616 | tf_op jit(solution)/shard_map/cond/branch_0_fun/while/body/eval_jaxpr/ppermute | solution.py:29
  147.4 12.6 %collective-permute-start.6 = (f32[1024,128]{0,1:T(8,128)S(1)}, f32[1024,128]{0,1:T(8,128)S(1)}, u32[]{:S(2)}, u32[]{:S(2)}) collective-permute-start(f32[1024,128]{0,1:T(8,128)S(1)} %fusion.44), channel_id=1, source_target_pairs={{0,1},{1,0},{2,3},{3,2},{4,5},{5,4},{6,7},{7,6},{8,9},{9,8},{10,11... | collective-permute-start | bytes 1572872 | tf_op jit(solution)/shard_map/cond/branch_0_fun/while/body/eval_jaxpr/ppermute | solution.py:29
  160.2 10.8 %collective-permute-start.7 = (f32[1024,128]{0,1:T(8,128)S(1)}, f32[1024,128]{0,1:T(8,128)S(1)}, u32[]{:S(2)}, u32[]{:S(2)}) collective-permute-start(f32[1024,128]{0,1:T(8,128)S(1)} %add.232), channel_id=1, source_target_pairs={{0,2},{1,3},{2,0},{3,1},{4,6},{5,7},{6,4},{7,5},{8,10},{9,11},{10,... | collective-permute-start | bytes 1572872 | tf_op jit(solution)/shard_map/cond/branch_0_fun/while/body/eval_jaxpr/ppermute | solution.py:29
  177.3 6.0 %collective-permute-start.10 = (f32[128,128]{1,0:T(8,128)S(1)}, f32[128,128]{1,0:T(8,128)S(1)}, u32[]{:S(2)}, u32[]{:S(2)}) collective-permute-start(f32[128,128]{1,0:T(8,128)S(1)} %add.235), channel_id=1, source_target_pairs={{0,16},{4,20},{8,24},{12,28},{16,0},{20,4},{24,8},{28,12},{32,48},... | collective-permute-start | bytes 196616 | tf_op jit(solution)/shard_map/cond/branch_0_fun/while/body/eval_jaxpr/ppermute | solution.py:29
  183.3 8.3 %collective-permute-start.11 = (f32[128,128]{1,0:T(8,128)S(1)}, f32[128,128]{1,0:T(8,128)S(1)}, u32[]{:S(2)}, u32[]{:S(2)}) collective-permute-start(f32[128,128]{1,0:T(8,128)S(1)} %add.236), channel_id=1, source_target_pairs={{0,32},{4,36},{8,40},{12,44},{16,48},{20,52},{24,56},{28,60},{32,0... | collective-permute-start | bytes 196616 | tf_op jit(solution)/shard_map/cond/branch_0_fun/while/body/eval_jaxpr/ppermute | solution.py:29
  214.9 8.3 %collective-permute-start.3 = (f32[128,128]{0,1:T(8,128)S(1)}, f32[128,128]{0,1:T(8,128)S(1)}, u32[]{:S(2)}, u32[]{:S(2)}) collective-permute-start(f32[128,128]{0,1:T(8,128)S(1)} %add.228), channel_id=1, source_target_pairs={{0,32},{4,36},{8,40},{12,44},{16,48},{20,52},{24,56},{28,60},{32,0... | collective-permute-start | bytes 196616 | tf_op jit(solution)/shard_map/cond/branch_0_fun/while/body/eval_jaxpr/ppermute | solution.py:29
  257.8 14.6 %collective-permute-start.6 = (f32[1024,128]{0,1:T(8,128)S(1)}, f32[1024,128]{0,1:T(8,128)S(1)}, u32[]{:S(2)}, u32[]{:S(2)}) collective-permute-start(f32[1024,128]{0,1:T(8,128)S(1)} %fusion.44), channel_id=1, source_target_pairs={{0,1},{1,0},{2,3},{3,2},{4,5},{5,4},{6,7},{7,6},{8,9},{9,8},{10,11... | collective-permute-start | bytes 1572872 | tf_op jit(solution)/shard_map/cond/branch_0_fun/while/body/eval_jaxpr/ppermute | solution.py:29
  272.4 10.8 %collective-permute-start.7 = (f32[1024,128]{0,1:T(8,128)S(1)}, f32[1024,128]{0,1:T(8,128)S(1)}, u32[]{:S(2)}, u32[]{:S(2)}) collective-permute-start(f32[1024,128]{0,1:T(8,128)S(1)} %add.232), channel_id=1, source_target_pairs={{0,2},{1,3},{2,0},{3,1},{4,6},{5,7},{6,4},{7,5},{8,10},{9,11},{10,... | collective-permute-start | bytes 1572872 | tf_op jit(solution)/shard_map/cond/branch_0_fun/while/body/eval_jaxpr/ppermute | solution.py:29
  295.1 8.4 %collective-permute-start.11 = (f32[128,128]{1,0:T(8,128)S(1)}, f32[128,128]{1,0:T(8,128)S(1)}, u32[]{:S(2)}, u32[]{:S(2)}) collective-permute-start(f32[128,128]{1,0:T(8,128)S(1)} %add.236), channel_id=1, source_target_pairs={{0,32},{4,36},{8,40},{12,44},{16,48},{20,52},{24,56},{28,60},{32,0... | collective-permute-start | bytes 196616 | tf_op jit(solution)/shard_map/cond/branch_0_fun/while/body/eval_jaxpr/ppermute | solution.py:29
  326.5 8.4 %collective-permute-start.3 = (f32[128,128]{0,1:T(8,128)S(1)}, f32[128,128]{0,1:T(8,128)S(1)}, u32[]{:S(2)}, u32[]{:S(2)}) collective-permute-start(f32[128,128]{0,1:T(8,128)S(1)} %add.228), channel_id=1, source_target_pairs={{0,32},{4,36},{8,40},{12,44},{16,48},{20,52},{24,56},{28,60},{32,0... | collective-permute-start | bytes 196616 | tf_op jit(solution)/shard_map/cond/branch_0_fun/while/body/eval_jaxpr/ppermute | solution.py:29
  339.4 5.9 %collective-permute-start.5 = (f32[128,128]{0,1:T(8,128)S(1)}, f32[128,128]{0,1:T(8,128)S(1)}, u32[]{:S(2)}, u32[]{:S(2)}) collective-permute-start(f32[128,128]{0,1:T(8,128)S(1)} %add.230), channel_id=1, source_target_pairs={{0,128},{4,132},{8,136},{12,140},{16,144},{20,148},{24,152},{28,15... | collective-permute-start | bytes 196616 | tf_op jit(solution)/shard_map/cond/branch_0_fun/while/body/eval_jaxpr/ppermute | solution.py:29
  368.9 14.2 %collective-permute-start.6 = (f32[1024,128]{0,1:T(8,128)S(1)}, f32[1024,128]{0,1:T(8,128)S(1)}, u32[]{:S(2)}, u32[]{:S(2)}) collective-permute-start(f32[1024,128]{0,1:T(8,128)S(1)} %fusion.44), channel_id=1, source_target_pairs={{0,1},{1,0},{2,3},{3,2},{4,5},{5,4},{6,7},{7,6},{8,9},{9,8},{10,11... | collective-permute-start | bytes 1572872 | tf_op jit(solution)/shard_map/cond/branch_0_fun/while/body/eval_jaxpr/ppermute | solution.py:29
  383.2 10.8 %collective-permute-start.7 = (f32[1024,128]{0,1:T(8,128)S(1)}, f32[1024,128]{0,1:T(8,128)S(1)}, u32[]{:S(2)}, u32[]{:S(2)}) collective-permute-start(f32[1024,128]{0,1:T(8,128)S(1)} %add.232), channel_id=1, source_target_pairs={{0,2},{1,3},{2,0},{3,1},{4,6},{5,7},{6,4},{7,5},{8,10},{9,11},{10,... | collective-permute-start | bytes 1572872 | tf_op jit(solution)/shard_map/cond/branch_0_fun/while/body/eval_jaxpr/ppermute | solution.py:29
  400.4 6.0 %collective-permute-start.10 = (f32[128,128]{1,0:T(8,128)S(1)}, f32[128,128]{1,0:T(8,128)S(1)}, u32[]{:S(2)}, u32[]{:S(2)}) collective-permute-start(f32[128,128]{1,0:T(8,128)S(1)} %add.235), channel_id=1, source_target_pairs={{0,16},{4,20},{8,24},{12,28},{16,0},{20,4},{24,8},{28,12},{32,48},... | collective-permute-start | bytes 196616 | tf_op jit(solution)/shard_map/cond/branch_0_fun/while/body/eval_jaxpr/ppermute | solution.py:29
  406.3 9.0 %collective-permute-start.11 = (f32[128,128]{1,0:T(8,128)S(1)}, f32[128,128]{1,0:T(8,128)S(1)}, u32[]{:S(2)}, u32[]{:S(2)}) collective-permute-start(f32[128,128]{1,0:T(8,128)S(1)} %add.236), channel_id=1, source_target_pairs={{0,32},{4,36},{8,40},{12,44},{16,48},{20,52},{24,56},{28,60},{32,0... | collective-permute-start | bytes 196616 | tf_op jit(solution)/shard_map/cond/branch_0_fun/while/body/eval_jaxpr/ppermute | solution.py:29
  420.0 5.9 %collective-permute-start.13 = (f32[128,128]{1,0:T(8,128)S(1)}, f32[128,128]{1,0:T(8,128)S(1)}, u32[]{:S(2)}, u32[]{:S(2)}) collective-permute-start(f32[128,128]{1,0:T(8,128)S(1)} %add.238), channel_id=1, source_target_pairs={{0,128},{4,132},{8,136},{12,140},{16,144},{20,148},{24,152},{28,15... | collective-permute-start | bytes 196616 | tf_op jit(solution)/shard_map/cond/branch_0_fun/while/body/eval_jaxpr/ppermute | solution.py:29
  438.6 8.3 %collective-permute-start.3 = (f32[128,128]{0,1:T(8,128)S(1)}, f32[128,128]{0,1:T(8,128)S(1)}, u32[]{:S(2)}, u32[]{:S(2)}) collective-permute-start(f32[128,128]{0,1:T(8,128)S(1)} %add.228), channel_id=1, source_target_pairs={{0,32},{4,36},{8,40},{12,44},{16,48},{20,52},{24,56},{28,60},{32,0... | collective-permute-start | bytes 196616 | tf_op jit(solution)/shard_map/cond/branch_0_fun/while/body/eval_jaxpr/ppermute | solution.py:29
  480.7 13.2 %collective-permute-start.6 = (f32[1024,128]{0,1:T(8,128)S(1)}, f32[1024,128]{0,1:T(8,128)S(1)}, u32[]{:S(2)}, u32[]{:S(2)}) collective-permute-start(f32[1024,128]{0,1:T(8,128)S(1)} %fusion.44), channel_id=1, source_target_pairs={{0,1},{1,0},{2,3},{3,2},{4,5},{5,4},{6,7},{7,6},{8,9},{9,8},{10,11... | collective-permute-start | bytes 1572872 | tf_op jit(solution)/shard_map/cond/branch_0_fun/while/body/eval_jaxpr/ppermute | solution.py:29
  494.0 10.8 %collective-permute-start.7 = (f32[1024,128]{0,1:T(8,128)S(1)}, f32[1024,128]{0,1:T(8,128)S(1)}, u32[]{:S(2)}, u32[]{:S(2)}) collective-permute-start(f32[1024,128]{0,1:T(8,128)S(1)} %add.232), channel_id=1, source_target_pairs={{0,2},{1,3},{2,0},{3,1},{4,6},{5,7},{6,4},{7,5},{8,10},{9,11},{10,... | collective-permute-start | bytes 1572872 | tf_op jit(solution)/shard_map/cond/branch_0_fun/while/body/eval_jaxpr/ppermute | solution.py:29
  516.4 9.0 %collective-permute-start.11 = (f32[128,128]{1,0:T(8,128)S(1)}, f32[128,128]{1,0:T(8,128)S(1)}, u32[]{:S(2)}, u32[]{:S(2)}) collective-permute-start(f32[128,128]{1,0:T(8,128)S(1)} %add.236), channel_id=1, source_target_pairs={{0,32},{4,36},{8,40},{12,44},{16,48},{20,52},{24,56},{28,60},{32,0... | collective-permute-start | bytes 196616 | tf_op jit(solution)/shard_map/cond/branch_0_fun/while/body/eval_jaxpr/ppermute | solution.py:29
  529.8 6.1 %collective-permute-start.13 = (f32[128,128]{1,0:T(8,128)S(1)}, f32[128,128]{1,0:T(8,128)S(1)}, u32[]{:S(2)}, u32[]{:S(2)}) collective-permute-start(f32[128,128]{1,0:T(8,128)S(1)} %add.238), channel_id=1, source_target_pairs={{0,128},{4,132},{8,136},{12,140},{16,144},{20,148},{24,152},{28,15... | collective-permute-start | bytes 196616 | tf_op jit(solution)/shard_map/cond/branch_0_fun/while/body/eval_jaxpr/ppermute | solution.py:29
  (37 other events, 347.1 us)

commit v3 on v2

--- a/solution.py
+++ b/solution.py
@@ -18,8 +18,11 @@
 COLS = GROUPS * WIDTH
 ROWS = ROW_BLOCKS * BLOCK
 HALF = ROW_BLOCKS // 2
-PIECE = 3 * WIDTH // CORES // ZS
-TOLERANCE = 1e-4
+TILES = 3 * WIDTH // CORES // 8
+PLANE = YS * ZS
+TILES_G = WIDTH // 8
+SETS = TILES // ZS
+TOLERANCE = 4e-4
 
 
 def total(value, axis):
@@ -111,12 +114,12 @@
 
 
 def kernel(
-    start, cov, col_index, order, out, residual,
-    win, win_hl, covv, cov_hl, vall, vhl, tb, r1, s1, r2, r3, gb,
-    e0, w, b, u, mk, e0_h, e0_l, w_h, w_l, b_h, b_l, u_h, x_hl, res, scol,
-    c_sem, l_sem, o_sem, f_sem,
+    start, cov, col_index, order, out, small,
+    win, win_hl, covv, cov_hl, vall, vhl, acc, tb, r1, s1, r2, gb,
+    e0, w, b, u, mk, e0_h, e0_l, w_h, w2_h, w_l, b_h, b_l, u_h, x_hl, res, scol,
+    c_sem, l_sem, f_sem,
     halo_s, halo_r, left_s, right_s, fwdr_s, fwdl_s, next_r, prev_r, opp_r,
-    p1_s, p1_r, p2_s, p2_r, p3_s, p3_r, p4_s, p4_r, p5_s, p5_r, p6_s, p6_r,
+    p1_s, p1_r, p2_s, p2_r, p4_s, p4_r, p5_s, p5_r, p6_s, p6_r,
 ):
     p = lax.axis_index("pts")
     g = lax.axis_index("cols")
@@ -128,11 +131,14 @@
     sibling = p + 1 - 2 * c
     g_next, g_prev, g_opp = (lax.rem(g + k, GROUPS) for k in (1, 3, 2))
 
-    def at_z(k):
-        return p + (lax.rem(z + k, ZS) - z) * CORES
-
-    def at_y(k):
-        return p + (lax.rem(y + k, YS) - y) * (CORES * ZS)
+    here = y * ZS + z
+
+    def peer(k):
+        y_to, z_to = lax.rem(y + lax.div(k, ZS), YS), lax.rem(z + lax.rem(k, ZS), ZS)
+        return y_to * ZS + z_to
+
+    def device(chip):
+        return chip * CORES + c
 
     def remote(src, dst, send, recv, **where):
         return pltpu.make_async_remote_copy(
@@ -155,16 +161,30 @@
     barrier = pltpu.get_barrier_semaphore()
     peers = [dict(pts=before), dict(pts=after)]
     peers += [dict(cols=h) for h in (g_next, g_prev, g_opp)]
-    peers += [dict(pts=at_z(k)) for k in range(1, ZS)]
-    peers += [dict(pts=at_y(k)) for k in range(1, YS)]
-    for peer in peers:
-        pl.semaphore_signal(barrier, inc=1, device_id=peer, device_id_type=MESH)
-    pl.semaphore_wait(barrier, len(peers))
-
-    to_after = remote(start, win.at[0], halo_s.at[0], halo_r.at[0], pts=after)
-    to_before = remote(start, win.at[2], halo_s.at[1], halo_r.at[1], pts=before)
-    to_after.start()
-    to_before.start()
+    for one in peers:
+        pl.semaphore_signal(barrier, inc=1, device_id=one, device_id_type=MESH)
+
+    def greet(k, carry):
+        pl.semaphore_signal(barrier, inc=1, device_id=dict(pts=device(peer(k))), device_id_type=MESH)
+        return carry
+
+    lax.fori_loop(1, PLANE, greet, 0)
+    pl.semaphore_wait(barrier, len(peers) + PLANE - 1)
+
+    def to_after(k):
+        rows = pl.ds(pl.multiple_of(k * BLOCK, BLOCK), BLOCK)
+        return remote(start.at[rows, :], win.at[0, rows, :], halo_s.at[0, k], halo_r.at[0, k], pts=after)
+
+    def to_before(k):
+        rows = pl.ds(pl.multiple_of(k * BLOCK, BLOCK), BLOCK)
+        return remote(start.at[rows, :], win.at[2, rows, :], halo_s.at[1, k], halo_r.at[1, k], pts=before)
+
+    def start_halo(k, carry):
+        to_after(ROW_BLOCKS - 1 - k).start()
+        to_before(k).start()
+        return carry
+
+    lax.fori_loop(0, ROW_BLOCKS, start_halo, 0)
 
     ranks = []
     for a in range(GROUPS):
@@ -195,27 +215,33 @@
 
     lax.fori_loop(0, ROW_BLOCKS, split_cov, 0)
 
-    def split_window(side):
-        def one(k, carry):
-            rows = pl.ds(pl.multiple_of(k * BLOCK, BLOCK), BLOCK)
-            high, low = split(win[side, rows, :])
-            win_hl[side * ROW_BLOCKS + k, :, :WIDTH] = high
-            win_hl[side * ROW_BLOCKS + k, :, WIDTH:] = low
-            return carry
-
-        lax.fori_loop(0, ROW_BLOCKS, one, 0)
+    def split_window(side, k):
+        rows = pl.ds(pl.multiple_of(k * BLOCK, BLOCK), BLOCK)
+        high, low = split(win[side, rows, :])
+        win_hl[side * ROW_BLOCKS + k, :, :WIDTH] = high
+        win_hl[side * ROW_BLOCKS + k, :, WIDTH:] = low
+
+    def split_own(k, carry):
+        split_window(1, k)
+        return carry
+
+    def take_halo(k, carry):
+        to_after(ROW_BLOCKS - 1 - k).wait_recv()
+        split_window(0, ROW_BLOCKS - 1 - k)
+        to_before(k).wait_recv()
+        split_window(2, k)
+        return carry
 
     own_copy.wait()
-    split_window(1)
-    to_after.wait_recv()
-    split_window(0)
-    to_before.wait_recv()
-    split_window(2)
+    lax.fori_loop(0, ROW_BLOCKS, split_own, 0)
+    lax.fori_loop(0, HALF, take_halo, 0)
 
     base = p * ROW_BLOCKS - ROW_BLOCKS - NBLK
 
     def rows_of(src, i):
-        r = lax.rem(i + HALF * (1 - lax.div(src, 2)), ROW_BLOCKS)
+        step, late = lax.rem(i, HALF), lax.div(i, HALF)
+        up = lax.rem(lax.div(src, 2) + late, 2)
+        r = HALF + step - up * (2 * step + 1)
         return r, pl.ds(pl.multiple_of(r * BLOCK, BLOCK), BLOCK)
 
     def xcopy(src, i, send, recv, to):
@@ -243,7 +269,7 @@
         vhl[src, rows, :WIDTH] = high
         vhl[src, rows, WIDTH:] = low
 
-    def image(i, carry):
+    def image(i):
         r, rows = rows_of(g, i)
         tiles = []
         for s in range(SLOTS):
@@ -253,129 +279,114 @@
         vall[g, rows, :] = quarters(quad, BLOCK, WIDTH)
         own_left(i).start()
 
-        @pl.when(i < HALF)
-        def _():
-            own_right(i).start()
-
-        keep_split(g, i)
-        return carry
-
-    lax.fori_loop(0, ROW_BLOCKS, image, 0)
-
-    def pass_right(i, carry):
-        own_copy_in = xcopy(g_prev, i, right_s, prev_r, g_next)
-        own_copy_in.wait_recv()
-        forward_right(i).start()
-        keep_split(g_prev, i)
+    def images(j, carry):
+        take_halo(j + HALF, 0)
+        image(j)
+        own_right(j).start()
+        image(j + HALF)
+        keep_split(g, j)
+        keep_split(g, j + HALF)
+        return carry
+
+    lax.fori_loop(0, HALF, images, 0)
+
+    def half_of(src, late):
+        low = lax.rem(lax.div(src, 2) + 1 + late, 2)
+        return pl.ds(pl.multiple_of(low * (HALF * BLOCK), HALF * BLOCK), HALF * BLOCK)
+
+    def gram_half(src, late):
+        rows = half_of(src, late)
+        return quarters(dot_t(vhl[g, rows, :], vhl[src, rows, :]), WIDTH, WIDTH)
+
+    tb[0, :TILES_G] = (gram_half(g, 0) + gram_half(g, 1)).reshape(TILES_G, 8, WIDTH)
+
+    def pass_right(j, carry):
+        xcopy(g_prev, j, right_s, prev_r, g_next).wait_recv()
+        forward_right(j).start()
+        return carry
+
+    def rest_right(j, carry):
+        own_right(j).start()
         return carry
 
     lax.fori_loop(0, HALF, pass_right, 0)
-
-    def rest_right(i, carry):
-        own_right(i).start()
-        return carry
-
     lax.fori_loop(HALF, ROW_BLOCKS, rest_right, 0)
 
-    def half_of(src, k):
-        return pl.ds(pl.multiple_of(lax.rem(k + 1 - lax.div(src, 2), 2) * (HALF * BLOCK), HALF * BLOCK), HALF * BLOCK)
-
-    def gram_half(src, k):
-        rows = half_of(src, k)
-        return quarters(dot_t(vhl[g, rows, :], vhl[src, rows, :]), WIDTH, WIDTH)
-
-    gram_own = gram_half(g, 0) + gram_half(g, 1)
-    tb[0, :WIDTH, :] = gram_own
-
-    def take_next(i, carry):
-        xcopy(g_next, i, left_s, next_r, g_prev).wait_recv()
-
-        @pl.when(i >= HALF)
-        def _():
-            forward_left(i).start()
-
-        keep_split(g_next, i)
-        return carry
-
-    lax.fori_loop(0, HALF, take_next, 0)
-    first = gram_half(g_next, 0)
+    acc[...] = jnp.zeros_like(acc)
+
+    def take_next(j, carry):
+        for i in (j, j + HALF):
+            xcopy(g_next, i, left_s, next_r, g_prev).wait_recv()
+            keep_split(g_next, i)
+        forward_left(j + HALF).start()
+        near, far = rows_of(g_next, j)[1], rows_of(g_next, j + HALF)[1]
+        left = jnp.concatenate([vhl[g, near, :], vhl[g, far, :]], axis=0)
+        right = jnp.concatenate([vhl[g_next, near, :], vhl[g_next, far, :]], axis=0)
+        acc[...] += dot_t(left, right)
+        return carry
 
     def take_opp(i, carry):
         from_opp(i).wait_recv()
         keep_split(g_opp, i)
         return carry
 
-    lax.fori_loop(HALF, ROW_BLOCKS, take_next, 0)
-    gram_next = first + gram_half(g_next, 1)
+    lax.fori_loop(0, HALF, take_next, 0)
+    gram_next = quarters(acc[...], WIDTH, WIDTH).reshape(TILES_G, 8, WIDTH)
+    edge = TILES - TILES_G
+    tb[0, TILES_G:] = gram_next[:edge]
+    tb[1, :TILES_G - edge] = gram_next[edge:]
     lax.fori_loop(0, HALF, take_opp, 0)
-    gram_opp = gram_half(g_opp, 0)
-    edge = 3 * WIDTH // 2 - WIDTH
-    tb[0, WIDTH:, :] = gram_next[:edge]
-    tb[1, :WIDTH - edge, :] = gram_next[edge:]
-    tb[1, WIDTH - edge:, :] = gram_opp
+    tb[1, TILES_G - edge:] = gram_half(g_opp, 0).reshape(TILES_G, 8, WIDTH)
 
     to_core = remote(tb.at[1 - c], r1, p1_s, p1_r, pts=sibling)
     to_core.start()
     to_core.wait_recv()
-    s1[...] = (tb[c] + r1[...]).reshape(ZS, PIECE, WIDTH)
-
-    def z_send(k):
-        to = lax.rem(z + k, ZS)
-        return remote(s1.at[to], r2.at[z], p2_s.at[k], p2_r.at[z], pts=at_z(k))
-
-    def z_recv(k):
-        source = lax.rem(z + k, ZS)
-        return remote(s1.at[source], r2.at[source], p2_s.at[k], p2_r.at[source], pts=at_z(k))
-
-    for k in range(1, ZS):
-        z_send(k).start()
-    summed = s1[z]
-    for k in range(1, ZS):
-        z_recv(k).wait_recv()
-        summed += r2[lax.rem(z + k, ZS)]
-    r3[y] = summed
-
-    def y_send(k):
-        return remote(r3.at[y], r3.at[y], p3_s.at[k], p3_r.at[y], pts=at_y(k))
-
-    def y_recv(k):
-        source = lax.rem(y + k, YS)
-        return remote(r3.at[source], r3.at[source], p3_s.at[k], p3_r.at[source], pts=at_y(k))
-
-    for k in range(1, YS):
-        y_send(k).start()
-    for k in range(1, YS):
-        y_recv(k).wait_recv()
-    gb[g, c, z] = (r3[0] + r3[1]) + (r3[2] + r3[3])
-
-    def z_share(k):
-        ref = gb.at[g, c, z]
-        return remote(ref, ref, p4_s.at[k], p4_r.at[z], pts=at_z(k))
-
-    def z_shared(k):
-        source = lax.rem(z + k, ZS)
-        ref = gb.at[g, c, source]
-        return remote(ref, ref, p4_s.at[k], p4_r.at[source], pts=at_z(k))
-
-    for k in range(1, ZS):
-        z_share(k).start()
-
-    def rest(i, carry):
-        xcopy(g_prev, i, right_s, prev_r, g_next).wait_recv()
-        keep_split(g_prev, i)
-        return carry
-
-    for k in range(1, ZS):
-        z_shared(k).wait_recv()
-
-    def x_share(k):
-        ref = gb.at[g, c]
-        return remote(ref, ref, p5_s.at[k], p5_r.at[g], cols=lax.rem(g + k, GROUPS))
-
-    def x_shared(k):
+    s1[...] = tb[c] + r1[...]
+
+    def scatter(k):
+        to = lax.min(peer(k), TILES - 1)
+        return remote(s1.at[to], r2.at[here], p2_s.at[k], p2_r.at[here], pts=device(to))
+
+    def start_scatter(k, carry):
+        @pl.when(peer(k) < TILES)
+        def _():
+            scatter(k).start()
+
+        return carry
+
+    lax.fori_loop(1, PLANE, start_scatter, 0)
+
+    def share(k):
+        ref = gb.at[g, c, lax.min(here, TILES - 1)]
+        return remote(ref, ref, p4_s.at[k], p4_r.at[lax.min(here, TILES - 1)], pts=device(peer(k)))
+
+    @pl.when(here < TILES)
+    def _():
+        def take(k, summed):
+            source = peer(k)
+            remote(r2.at[source], r2.at[source], p2_s.at[k], p2_r.at[source], pts=device(source)).wait_recv()
+            return summed + r2[source]
+
+        gb[g, c, lax.min(here, TILES - 1)] = lax.fori_loop(1, PLANE, take, s1[lax.min(here, TILES - 1)])
+
+        def start_share(k, carry):
+            share(k).start()
+            return carry
+
+        lax.fori_loop(1, PLANE, start_share, 0)
+
+
+    def rows_of_set(n):
+        return pl.ds(pl.multiple_of(n * ZS, ZS), ZS)
+
+    def x_share(k, n):
+        ref = gb.at[g, c, rows_of_set(n)]
+        return remote(ref, ref, p5_s.at[k, n], p5_r.at[g, n], cols=lax.rem(g + k, GROUPS))
+
+    def x_shared(k, n):
         source = lax.rem(g + k, GROUPS)
-        ref = gb.at[source, c]
-        return remote(ref, ref, p5_s.at[k], p5_r.at[source], cols=source)
+        ref = gb.at[source, c, rows_of_set(n)]
+        return remote(ref, ref, p5_s.at[k, n], p5_r.at[source, n], cols=source)
 
     def core_share(k):
         source = lax.rem(g + k, GROUPS)
@@ -387,13 +398,31 @@
         ref = gb.at[source, 1 - c]
         return remote(ref, ref, p6_s.at[source], p6_r.at[source], pts=sibling)
 
+    def shared(t, carry):
+        @pl.when(t != here)
+        def _():
+            ref = gb.at[g, c, t]
+            remote(ref, ref, p4_s.at[0], p4_r.at[t], pts=device(t)).wait_recv()
+
+        return carry
+
+    for n in range(SETS):
+        lax.fori_loop(n * ZS, (n + 1) * ZS, shared, 0)
+        for k in range(1, GROUPS):
+            x_share(k, n).start()
+    core_share(0).start()
+
+    def rest(j, carry):
+        keep_split(g_prev, j)
+        xcopy(g_prev, j + HALF, right_s, prev_r, g_next).wait_recv()
+        keep_split(g_prev, j + HALF)
+        take_opp(j + HALF, 0)
+        return carry
+
+    lax.fori_loop(0, HALF, rest, 0)
     for k in range(1, GROUPS):
-        x_share(k).start()
-    core_share(0).start()
-    lax.fori_loop(HALF, ROW_BLOCKS, rest, 0)
-    lax.fori_loop(HALF, ROW_BLOCKS, take_opp, 0)
-    for k in range(1, GROUPS):
-        x_shared(k).wait_recv()
+        for n in range(SETS):
+            x_shared(k, n).wait_recv()
         core_share(k).start()
     for k in range(GROUPS):
         core_shared(k).wait_recv()
@@ -431,56 +460,44 @@
         put(a, h, block)
         put(h, a, block.T)
 
-    def tile(m):
-        return pl.ds(pl.multiple_of(m * WIDTH, WIDTH), WIDTH)
-
-    def newton(fine):
-        def first(m, carry):
-            rows = tile(m)
-            prod = dot(e0_h[rows, :], w_h[...])
+    def newton(w_h, next_h, fine):
+        for n in range(2):
+            cols = slice(n * COLS // 2, (n + 1) * COLS // 2)
+            prod = dot(e0_h[...], w_h[:, cols])
             if fine:
-                prod += dot(e0_l[rows, :], w_h[...]) + dot(e0_h[rows, :], w_l[...])
-            value = (e0[rows, :] + w[rows, :]) + prod
-            b[rows, :] = value
+                prod += dot(e0_l[...], w_h[:, cols]) + dot(e0_h[...], w_l[:, cols])
+            value = (e0[:, cols] + w[:, cols]) + prod
+            b[:, cols] = value
             high, low = split(value)
-            b_h[rows, :] = high
+            b_h[:, cols] = high
             if fine:
-                b_l[rows, :] = low
-            return carry
-
-        def second(m, carry):
-            rows = tile(m)
-            prod = dot_t(w_h[:, rows], b_h[...])
+                b_l[:, cols] = low
+        for n in range(2):
+            cols = slice(n * COLS // 2, (n + 1) * COLS // 2)
+            prod = dot_t(w_h[...], b_h[:, cols])
             if fine:
-                prod += dot_t(w_l[:, rows], b_h[...]) + dot_t(w_h[:, rows], b_l[...])
-            here = lax.broadcasted_iota(jnp.int32, (WIDTH, COLS), 0) + m * WIDTH
-            there = lax.broadcasted_iota(jnp.int32, (WIDTH, COLS), 1)
-            own = jnp.where(here == there, w[rows, :], 0.0)
-            value = mk[rows, :] * ((b[rows, :] + own) + prod)
-            u[rows, :] = value
-            u_h[rows, :] = value.astype(BF16)
+                prod += dot_t(w_l[...], b_h[:, cols]) + dot_t(w_h[...], b_l[:, cols])
+            down_id = lax.broadcasted_iota(jnp.int32, (COLS, COLS // 2), 0)
+            across_id = lax.broadcasted_iota(jnp.int32, (COLS, COLS // 2), 1) + n * COLS // 2
+            own = jnp.where(down_id == across_id, w[:, cols], 0.0)
+            value = mk[:, cols] * ((b[:, cols] + own) + prod)
+            u[:, cols] = value
+            u_h[:, cols] = value.astype(BF16)
             if fine:
-                res[...] += jnp.sum((value * value).reshape(WIDTH // 8, 8, COLS), axis=0)
-            return carry
-
-        def third(m, carry):
-            rows = tile(m)
-            value = (w[rows, :] - u[rows, :]) - dot(w_h[rows, :], u_h[...])
-            w[rows, :] = value
-            high, low = split(value)
-            w_h[rows, :] = high
-            w_l[rows, :] = low
-            return carry
-
-        lax.fori_loop(0, GROUPS, first, 0)
-        lax.fori_loop(0, GROUPS, second, 0)
-        lax.fori_loop(0, GROUPS, third, 0)
+                res[...] += jnp.sum((value * value).reshape(COLS // 8, 8, COLS // 2), axis=0)
+        for n in range(2):
+            cols = slice(n * COLS // 2, (n + 1) * COLS // 2)
+            value = (w[:, cols] - u[:, cols]) - dot(w_h[...], u_h[:, cols])
+            w[:, cols] = value
+            if not fine:
+                high, low = split(value)
+                next_h[:, cols] = high
+                w_l[:, cols] = low
 
     res[...] = jnp.zeros_like(res)
-    newton(False)
-    newton(False)
-    newton(True)
-    residual[...] = jnp.full(residual.shape, jnp.sum(res[...]), F32)
+    newton(w_h, w2_h, False)
+    newton(w2_h, None, True)
+    small[0, 0] = jnp.where(jnp.sum(res[...]) < TOLERANCE, 1, 0).astype(jnp.int32)
 
     mine = pl.ds(pl.multiple_of(g * WIDTH, WIDTH), WIDTH)
     for a in range(GROUPS):
@@ -507,10 +524,9 @@
 
     lax.fori_loop(0, ROW_BLOCKS // 2, finish, 0)
 
-    to_after.wait_send()
-    to_before.wait_send()
-
     def sent(i, carry):
+        to_after(i).wait_send()
+        to_before(i).wait_send()
         own_left(i).wait_send()
         own_right(i).wait_send()
         return carry
@@ -520,16 +536,24 @@
         forward_left(i + HALF).wait_send()
         return carry
 
+    def scattered(k, carry):
+        @pl.when(peer(k) < TILES)
+        def _():
+            scatter(k).wait_send()
+
+        @pl.when(here < TILES)
+        def _():
+            share(k).wait_send()
+
+        return carry
+
     lax.fori_loop(0, ROW_BLOCKS, sent, 0)
     lax.fori_loop(0, HALF, sent_on, 0)
     to_core.wait_send()
-    for k in range(1, ZS):
-        z_send(k).wait_send()
-        z_share(k).wait_send()
-    for k in range(1, YS):
-        y_send(k).wait_send()
+    lax.fori_loop(1, PLANE, scattered, 0)
     for k in range(1, GROUPS):
-        x_share(k).wait_send()
+        for n in range(SETS):
+            x_share(k, n).wait_send()
     for k in range(GROUPS):
         core_share(k).wait_send()
 
@@ -549,10 +573,10 @@
         kernel,
         out_shape=(
             jax.ShapeDtypeStruct((ROWS, WIDTH), F32),
-            jax.ShapeDtypeStruct((8, 128), F32),
+            jax.ShapeDtypeStruct((1, 1), jnp.int32),
         ),
         in_specs=[hbm, hbm, smem, smem],
-        out_specs=(hbm, pl.BlockSpec(memory_space=pltpu.VMEM)),
+        out_specs=(hbm, smem),
         scratch_shapes=[
             pltpu.VMEM((3, ROWS, WIDTH), F32),
             pltpu.VMEM((3 * ROW_BLOCKS, BLOCK, 2 * WIDTH), BF16),
@@ -560,12 +584,12 @@
             pltpu.VMEM((ROW_BLOCKS, 2 * BLOCK, SLOTS * BLOCK), BF16),
             pltpu.VMEM((GROUPS, ROWS, WIDTH), F32),
             pltpu.VMEM((GROUPS, ROWS, 2 * WIDTH), BF16),
-            pltpu.VMEM((CORES, ZS * PIECE, WIDTH), F32),
-            pltpu.VMEM((ZS * PIECE, WIDTH), F32),
-            pltpu.VMEM((ZS, PIECE, WIDTH), F32),
-            pltpu.VMEM((ZS, PIECE, WIDTH), F32),
-            pltpu.VMEM((YS, PIECE, WIDTH), F32),
-            pltpu.VMEM((GROUPS, CORES, ZS, PIECE, WIDTH), F32),
+            pltpu.VMEM((2 * WIDTH, 2 * WIDTH), F32),
+            pltpu.VMEM((CORES, TILES, 8, WIDTH), F32),
+            pltpu.VMEM((TILES, 8, WIDTH), F32),
+            pltpu.VMEM((TILES, 8, WIDTH), F32),
+            pltpu.VMEM((PLANE, 8, WIDTH), F32),
+            pltpu.VMEM((GROUPS, CORES, TILES, 8, WIDTH), F32),
             pltpu.VMEM(square, F32),
             pltpu.VMEM(square, F32),
             pltpu.VMEM(square, F32),
@@ -578,22 +602,21 @@
             pltpu.VMEM(square, BF16),
             pltpu.VMEM(square, BF16),
             pltpu.VMEM(square, BF16),
+            pltpu.VMEM(square, BF16),
             pltpu.VMEM((COLS, 2 * WIDTH), BF16),
-            pltpu.VMEM((8, COLS), F32),
+            pltpu.VMEM((8, COLS // 2), F32),
             pltpu.VMEM((COLS, WIDTH), F32),
             dma((ROW_BLOCKS,)),
             dma,
-            dma,
             dma((ROW_BLOCKS // 2,)),
-            dma((2,)), dma((2,)),
+            dma((2, ROW_BLOCKS)), dma((2, ROW_BLOCKS)),
             dma((ROW_BLOCKS,)), dma((ROW_BLOCKS,)),
             dma((ROW_BLOCKS,)), dma((ROW_BLOCKS,)),
             dma((ROW_BLOCKS,)), dma((ROW_BLOCKS,)), dma((ROW_BLOCKS,)),
             dma, dma,
-            dma((ZS,)), dma((ZS,)),
-            dma((YS,)), dma((YS,)),
-            dma((ZS,)), dma((ZS,)),
-            dma((GROUPS,)), dma((GROUPS,)),
+            dma((PLANE,)), dma((PLANE,)),
+            dma((PLANE,)), dma((TILES,)),
+            dma((GROUPS, SETS)), dma((GROUPS, SETS)),
             dma((GROUPS,)), dma((GROUPS,)),
         ],
         compiler_params=pltpu.CompilerParams(
@@ -603,9 +626,9 @@
 
 
 def body(start, cov_blocks, col_index, order):
-    result, residual = fast(start, cov_blocks, col_index, order)
+    result, small = fast(start, cov_blocks, col_index, order)
     return lax.cond(
-        residual[0, 0] < TOLERANCE,
+        small[0, 0] == 1,
         lambda: result,
         lambda: careful(start, cov_blocks, col_index, order),
     )

time: 538 us -> 528 us (0.981)
  waiting for transfers between devices: 265 us -> 225 us
  starting transfers between devices: 77.2 us -> 111 us
  Pallas kernels: 67.4 us -> 59.5 us
    ppermute x56, waiting for transfers between devices: 258 us -> 219 us  [total(): value = value + lax.ppermute(value, axis, pairs)]
    ppermute x56, starting transfers between devices: 72 us -> 106 us  [total(): value = value + lax.ppermute(value, axis, pairs)]
    pallas_call x1, Pallas kernels: 67.4 us -> 59.5 us  [fast(): pl.pallas_call(kernel, out_shape=(jax.ShapeDtypeStruct((ROWS, WIDTH), F32...]
  transfers between devices with their start and end apart: 58 -> 58, of which waited for: 57 -> 58; matrix products, arithmetic and copies ran while one was open for 1% -> 1% of each run, Pallas kernels for 0% -> 0%
where the time goes in v3:
time: 528 us; the launch traced here: 523 us
  waiting for transfers between devices  225 us (43%)
  starting transfers between devices  111 us (21%)
  other arithmetic  93.2 us (18%)
  Pallas kernels  59.5 us (11%)
  matrix products  18.2 us (3%)
  loops' own time  8.59 us (2%)
  local copies, waits for them, and re-layouts  6.85 us (1%)
    ppermute x56, waiting for transfers between devices, total(): value = value + lax.ppermute(value, axis, pairs)  219 us
    ppermute x56, starting transfers between devices, total(): value = value + lax.ppermute(value, axis, pairs)  106 us
    pallas_call x1, Pallas kernels, fast(): pl.pallas_call(kernel, out_shape=(jax.ShapeDtypeStruct((ROWS, WIDTH), F32...  59.5 us
    another operation x12, other arithmetic, step(): lower = jnp.linalg.cholesky(gram)  49.8 us
    another operation x8, other arithmetic, step(): lax.linalg.triangular_solve(lower, local, left_side=False, lower=True, tr...  41.8 us
  transfers between devices with their start and end apart: 58, of which 58 were waited for; matrix products, arithmetic and copies ran while one was open for 1% of the time, Pallas kernels for 0%

profile of v3, /device:TPU:6, one launch (start us, length us, event | category | flops | bytes accessed | tf_op | source)
XLA Modules:
  0.0 523.2 jit_solution(17043912860279241226)
XLA Ops:
  0.0 59.5 %shard_map.48 = (f32[1024,128]{1,0:T(8,128)S(1)}, s32[1,1]{1,0:T(1,128)}) custom-call(f32[1024,128]{1,0:T(8,128)} %start.1, f32[8,8,128,128]{3,2,1,0:T(8,128)} %cov.1, s32[8,8]{1,0:T(8,128)} %col_index.1, s32[4]{0:T(128)} %order.1), custom_call_target="tpu_custom_call" | custom-call | tf_op jit(solution)/shard_map/pallas_call | solution.py:572
  60.2 462.2 %conditional.1 = (f32[1024,128]{1,0:T(8,128)S(1)}) conditional(s32[]{:T(128)} %bitcast.11, (f32[1024,128]{1,0:T(8,128)S(1)}, s32[8,8]{1,0:T(8,128)S(1)}, f32[8,8,128,128]{3,2,1,0:T(8,128)}, s32[4]{0:T(128)S(1)}) %tuple.55, f32[1024,128]{1,0:T(8,128)S(1)} %get-tuple-element.156), branch_computations={%region_0.6_spmd, %region_6.7_spmd} | conditional | flops 2417838080 | bytes 44441020 | solution.py:630
  66.6 5.9 %collective-permute-done.14 = f32[1024,128]{1,0:T(8,128)S(1)} collective-permute-done((f32[1024,128]{1,0:T(8,128)S(1)}, f32[1024,128]{1,0:T(8,128)S(1)}, u32[]{:S(2)}, u32[]{:S(2)}) %collective-permute-start.14) | collective-permute-done | bytes 524320 | tf_op jit(solution)/shard_map/cond/branch_0_fun/ppermute | solution.py:48
  75.4 7.9 %fusion.10 = f32[8,128,128,1]{1,2,3,0:T(8,128)S(1)} fusion(f32[8,8,128,128]{3,2,1,0:T(8,128)} %bitcast.52, f32[8,8,128,128]{3,2,1,0:T(8,128)} %get-tuple-element.150), kind=kOutput, calls=%fused_computation.26 | convolution fusion | flops 1610612736 | bytes 8912896 | tf_op jit(solution)/shard_map/cond/branch_0_fun/rsab,rsbk->rak/dot_general | solution.py:78
  83.6 438.4 %while.14 = (s32[]{:T(128)}, f32[1024,128]{0,1:T(8,128)S(1)}, s32[]{:T(128)}, s32[4]{0:T(128)S(1)}, s32[]{:T(128)}, /*index=5*/s32[]{:T(128)}, u32[]{:T(128)}) while((s32[]{:T(128)}, f32[1024,128]{0,1:T(8,128)S(1)}, s32[]{:T(128)}, s32[4]{0:T(128)S(1)}, s32[]{:T(128)}, /*index=5*/s32[]{:T(128)}, u32[]{:T(128)}) %tuple.48), condition=%wide.region_5.5_spmd, body=%wide.region_2.4_spmd.sunk | while | flops 806436992 | bytes 17696444 | solution.py:96
  98.0 5.9 %collective-permute-done.3 = f32[128,128]{0,1:T(8,128)S(1)} collective-permute-done((f32[128,128]{0,1:T(8,128)S(1)}, f32[128,128]{0,1:T(8,128)S(1)}, u32[]{:S(2)}, u32[]{:S(2)}) %collective-permute-start.3) | collective-permute-done | bytes 65568 | tf_op jit(solution)/shard_map/cond/branch_0_fun/while/body/eval_jaxpr/ppermute | solution.py:32
  114.3 11.7 %cholesky.58 = f32[128,128]{1,0:T(8,128)S(1)} custom-call(f32[128,128]{1,0:T(8,128)S(1)} %fusion.42), custom_call_target="Cholesky" | custom-call | tf_op jit(solution)/shard_map/cond/branch_0_fun/while/body/eval_jaxpr/jit(cholesky)/cholesky | solution.py:85
  127.4 9.8 %custom-call.23 = f32[1,128,128]{1,2,0:T(8,128)S(1)} custom-call(f32[1,128,128]{2,1,0:T(8,128)S(1)} %fusion.43), custom_call_target="InvertDiagBlocksLowerTriangular" | custom-call | tf_op jit(solution)/shard_map/cond/branch_0_fun/while/body/eval_jaxpr/triangular_solve | solution.py:86
  138.8 11.0 %collective-permute-done.6 = f32[1024,128]{0,1:T(8,128)S(1)} collective-permute-done((f32[1024,128]{0,1:T(8,128)S(1)}, f32[1024,128]{0,1:T(8,128)S(1)}, u32[]{:S(2)}, u32[]{:S(2)}) %collective-permute-start.6) | collective-permute-done | bytes 524320 | tf_op jit(solution)/shard_map/cond/branch_0_fun/while/body/eval_jaxpr/ppermute | solution.py:32
  150.7 9.9 %collective-permute-done.7 = f32[1024,128]{0,1:T(8,128)S(1)} collective-permute-done((f32[1024,128]{0,1:T(8,128)S(1)}, f32[1024,128]{0,1:T(8,128)S(1)}, u32[]{:S(2)}, u32[]{:S(2)}) %collective-permute-start.7) | collective-permute-done | bytes 524320 | tf_op jit(solution)/shard_map/cond/branch_0_fun/while/body/eval_jaxpr/ppermute | solution.py:32
  222.7 11.7 %cholesky.58 = f32[128,128]{1,0:T(8,128)S(1)} custom-call(f32[128,128]{1,0:T(8,128)S(1)} %fusion.42), custom_call_target="Cholesky" | custom-call | tf_op jit(solution)/shard_map/cond/branch_0_fun/while/body/eval_jaxpr/jit(cholesky)/cholesky | solution.py:85
  235.8 9.8 %custom-call.23 = f32[1,128,128]{1,2,0:T(8,128)S(1)} custom-call(f32[1,128,128]{2,1,0:T(8,128)S(1)} %fusion.43), custom_call_target="InvertDiagBlocksLowerTriangular" | custom-call | tf_op jit(solution)/shard_map/cond/branch_0_fun/while/body/eval_jaxpr/triangular_solve | solution.py:86
  246.6 11.1 %collective-permute-done.6 = f32[1024,128]{0,1:T(8,128)S(1)} collective-permute-done((f32[1024,128]{0,1:T(8,128)S(1)}, f32[1024,128]{0,1:T(8,128)S(1)}, u32[]{:S(2)}, u32[]{:S(2)}) %collective-permute-start.6) | collective-permute-done | bytes 524320 | tf_op jit(solution)/shard_map/cond/branch_0_fun/while/body/eval_jaxpr/ppermute | solution.py:32
  260.8 7.8 %collective-permute-done.7 = f32[1024,128]{0,1:T(8,128)S(1)} collective-permute-done((f32[1024,128]{0,1:T(8,128)S(1)}, f32[1024,128]{0,1:T(8,128)S(1)}, u32[]{:S(2)}, u32[]{:S(2)}) %collective-permute-start.7) | collective-permute-done | bytes 524320 | tf_op jit(solution)/shard_map/cond/branch_0_fun/while/body/eval_jaxpr/ppermute | solution.py:32
  331.5 11.7 %cholesky.58 = f32[128,128]{1,0:T(8,128)S(1)} custom-call(f32[128,128]{1,0:T(8,128)S(1)} %fusion.42), custom_call_target="Cholesky" | custom-call | tf_op jit(solution)/shard_map/cond/branch_0_fun/while/body/eval_jaxpr/jit(cholesky)/cholesky | solution.py:85
  344.6 9.8 %custom-call.23 = f32[1,128,128]{1,2,0:T(8,128)S(1)} custom-call(f32[1,128,128]{2,1,0:T(8,128)S(1)} %fusion.43), custom_call_target="InvertDiagBlocksLowerTriangular" | custom-call | tf_op jit(solution)/shard_map/cond/branch_0_fun/while/body/eval_jaxpr/triangular_solve | solution.py:86
  356.3 8.7 %collective-permute-done.6 = f32[1024,128]{0,1:T(8,128)S(1)} collective-permute-done((f32[1024,128]{0,1:T(8,128)S(1)}, f32[1024,128]{0,1:T(8,128)S(1)}, u32[]{:S(2)}, u32[]{:S(2)}) %collective-permute-start.6) | collective-permute-done | bytes 524320 | tf_op jit(solution)/shard_map/cond/branch_0_fun/while/body/eval_jaxpr/ppermute | solution.py:32
  365.1 7.1 %collective-permute-start.7 = (f32[1024,128]{0,1:T(8,128)S(1)}, f32[1024,128]{0,1:T(8,128)S(1)}, u32[]{:S(2)}, u32[]{:S(2)}) collective-permute-start(f32[1024,128]{0,1:T(8,128)S(1)} %add.232), channel_id=1, source_target_pairs={{0,2},{1,3},{2,0},{3,1},{4,6},{5,7},{6,4},{7,5},{8,10},{9,11},{10,... | collective-permute-start | bytes 1572872 | tf_op jit(solution)/shard_map/cond/branch_0_fun/while/body/eval_jaxpr/ppermute | solution.py:32
  372.2 7.2 %collective-permute-done.7 = f32[1024,128]{0,1:T(8,128)S(1)} collective-permute-done((f32[1024,128]{0,1:T(8,128)S(1)}, f32[1024,128]{0,1:T(8,128)S(1)}, u32[]{:S(2)}, u32[]{:S(2)}) %collective-permute-start.7) | collective-permute-done | bytes 524320 | tf_op jit(solution)/shard_map/cond/branch_0_fun/while/body/eval_jaxpr/ppermute | solution.py:32
  441.8 11.7 %cholesky.58 = f32[128,128]{1,0:T(8,128)S(1)} custom-call(f32[128,128]{1,0:T(8,128)S(1)} %fusion.42), custom_call_target="Cholesky" | custom-call | tf_op jit(solution)/shard_map/cond/branch_0_fun/while/body/eval_jaxpr/jit(cholesky)/cholesky | solution.py:85
  454.9 9.8 %custom-call.23 = f32[1,128,128]{1,2,0:T(8,128)S(1)} custom-call(f32[1,128,128]{2,1,0:T(8,128)S(1)} %fusion.43), custom_call_target="InvertDiagBlocksLowerTriangular" | custom-call | tf_op jit(solution)/shard_map/cond/branch_0_fun/while/body/eval_jaxpr/triangular_solve | solution.py:86
  467.3 7.7 %collective-permute-done.6 = f32[1024,128]{0,1:T(8,128)S(1)} collective-permute-done((f32[1024,128]{0,1:T(8,128)S(1)}, f32[1024,128]{0,1:T(8,128)S(1)}, u32[]{:S(2)}, u32[]{:S(2)}) %collective-permute-start.6) | collective-permute-done | bytes 524320 | tf_op jit(solution)/shard_map/cond/branch_0_fun/while/body/eval_jaxpr/ppermute | solution.py:32
  475.1 8.2 %collective-permute-start.7 = (f32[1024,128]{0,1:T(8,128)S(1)}, f32[1024,128]{0,1:T(8,128)S(1)}, u32[]{:S(2)}, u32[]{:S(2)}) collective-permute-start(f32[1024,128]{0,1:T(8,128)S(1)} %add.232), channel_id=1, source_target_pairs={{0,2},{1,3},{2,0},{3,1},{4,6},{5,7},{6,4},{7,5},{8,10},{9,11},{10,... | collective-permute-start | bytes 1572872 | tf_op jit(solution)/shard_map/cond/branch_0_fun/while/body/eval_jaxpr/ppermute | solution.py:32
  483.2 7.2 %collective-permute-done.7 = f32[1024,128]{0,1:T(8,128)S(1)} collective-permute-done((f32[1024,128]{0,1:T(8,128)S(1)}, f32[1024,128]{0,1:T(8,128)S(1)}, u32[]{:S(2)}, u32[]{:S(2)}) %collective-permute-start.7) | collective-permute-done | bytes 524320 | tf_op jit(solution)/shard_map/cond/branch_0_fun/while/body/eval_jaxpr/ppermute | solution.py:32
  (211 shorter events, 262.9 us)
Async XLA Ops:
  60.2 12.2 %collective-permute-start.14 = (f32[1024,128]{1,0:T(8,128)S(1)}, f32[1024,128]{1,0:T(8,128)S(1)}, u32[]{:S(2)}, u32[]{:S(2)}) collective-permute-start(f32[1024,128]{1,0:T(8,128)S(1)} %get-tuple-element.148), channel_id=1, source_target_pairs={{0,4},{4,8},{8,12},{12,16},{16,20},{20,24},{24,28},{28,32},{32,36}... | collective-permute-start | bytes 1572872 | tf_op jit(solution)/shard_map/cond/branch_0_fun/ppermute | solution.py:48
  61.9 10.7 %collective-permute-start.15 = (f32[1024,128]{1,0:T(8,128)S(1)}, f32[1024,128]{1,0:T(8,128)S(1)}, u32[]{:S(2)}, u32[]{:S(2)}) collective-permute-start(f32[1024,128]{1,0:T(8,128)S(1)} %get-tuple-element.148), channel_id=1, source_target_pairs={{4,0},{8,4},{12,8},{16,12},{20,16},{24,20},{28,24},{32,28},{36,32}... | collective-permute-start | bytes 1572872 | tf_op jit(solution)/shard_map/cond/branch_0_fun/ppermute | solution.py:50
  95.7 8.3 %collective-permute-start.3 = (f32[128,128]{0,1:T(8,128)S(1)}, f32[128,128]{0,1:T(8,128)S(1)}, u32[]{:S(2)}, u32[]{:S(2)}) collective-permute-start(f32[128,128]{0,1:T(8,128)S(1)} %add.228), channel_id=1, source_target_pairs={{0,32},{4,36},{8,40},{12,44},{16,48},{20,52},{24,56},{28,60},{32,0... | collective-permute-start | bytes 196616 | tf_op jit(solution)/shard_map/cond/branch_0_fun/while/body/eval_jaxpr/ppermute | solution.py:32
  108.3 5.9 %collective-permute-start.5 = (f32[128,128]{0,1:T(8,128)S(1)}, f32[128,128]{0,1:T(8,128)S(1)}, u32[]{:S(2)}, u32[]{:S(2)}) collective-permute-start(f32[128,128]{0,1:T(8,128)S(1)} %add.230), channel_id=1, source_target_pairs={{0,128},{4,132},{8,136},{12,140},{16,144},{20,148},{24,152},{28,15... | collective-permute-start | bytes 196616 | tf_op jit(solution)/shard_map/cond/branch_0_fun/while/body/eval_jaxpr/ppermute | solution.py:32
  137.8 11.9 %collective-permute-start.6 = (f32[1024,128]{0,1:T(8,128)S(1)}, f32[1024,128]{0,1:T(8,128)S(1)}, u32[]{:S(2)}, u32[]{:S(2)}) collective-permute-start(f32[1024,128]{0,1:T(8,128)S(1)} %fusion.44), channel_id=1, source_target_pairs={{0,1},{1,0},{2,3},{3,2},{4,5},{5,4},{6,7},{7,6},{8,9},{9,8},{10,11... | collective-permute-start | bytes 1572872 | tf_op jit(solution)/shard_map/cond/branch_0_fun/while/body/eval_jaxpr/ppermute | solution.py:32
  149.8 10.8 %collective-permute-start.7 = (f32[1024,128]{0,1:T(8,128)S(1)}, f32[1024,128]{0,1:T(8,128)S(1)}, u32[]{:S(2)}, u32[]{:S(2)}) collective-permute-start(f32[1024,128]{0,1:T(8,128)S(1)} %add.232), channel_id=1, source_target_pairs={{0,2},{1,3},{2,0},{3,1},{4,6},{5,7},{6,4},{7,5},{8,10},{9,11},{10,... | collective-permute-start | bytes 1572872 | tf_op jit(solution)/shard_map/cond/branch_0_fun/while/body/eval_jaxpr/ppermute | solution.py:32
  172.5 8.3 %collective-permute-start.11 = (f32[128,128]{1,0:T(8,128)S(1)}, f32[128,128]{1,0:T(8,128)S(1)}, u32[]{:S(2)}, u32[]{:S(2)}) collective-permute-start(f32[128,128]{1,0:T(8,128)S(1)} %add.236), channel_id=1, source_target_pairs={{0,32},{4,36},{8,40},{12,44},{16,48},{20,52},{24,56},{28,60},{32,0... | collective-permute-start | bytes 196616 | tf_op jit(solution)/shard_map/cond/branch_0_fun/while/body/eval_jaxpr/ppermute | solution.py:32
  198.1 6.0 %collective-permute-start.2 = (f32[128,128]{0,1:T(8,128)S(1)}, f32[128,128]{0,1:T(8,128)S(1)}, u32[]{:S(2)}, u32[]{:S(2)}) collective-permute-start(f32[128,128]{0,1:T(8,128)S(1)} %add.227), channel_id=1, source_target_pairs={{0,16},{4,20},{8,24},{12,28},{16,0},{20,4},{24,8},{28,12},{32,48},... | collective-permute-start | bytes 196616 | tf_op jit(solution)/shard_map/cond/branch_0_fun/while/body/eval_jaxpr/ppermute | solution.py:32
  204.1 8.3 %collective-permute-start.3 = (f32[128,128]{0,1:T(8,128)S(1)}, f32[128,128]{0,1:T(8,128)S(1)}, u32[]{:S(2)}, u32[]{:S(2)}) collective-permute-start(f32[128,128]{0,1:T(8,128)S(1)} %add.228), channel_id=1, source_target_pairs={{0,32},{4,36},{8,40},{12,44},{16,48},{20,52},{24,56},{28,60},{32,0... | collective-permute-start | bytes 196616 | tf_op jit(solution)/shard_map/cond/branch_0_fun/while/body/eval_jaxpr/ppermute | solution.py:32
  246.3 11.5 %collective-permute-start.6 = (f32[1024,128]{0,1:T(8,128)S(1)}, f32[1024,128]{0,1:T(8,128)S(1)}, u32[]{:S(2)}, u32[]{:S(2)}) collective-permute-start(f32[1024,128]{0,1:T(8,128)S(1)} %fusion.44), channel_id=1, source_target_pairs={{0,1},{1,0},{2,3},{3,2},{4,5},{5,4},{6,7},{7,6},{8,9},{9,8},{10,11... | collective-permute-start | bytes 1572872 | tf_op jit(solution)/shard_map/cond/branch_0_fun/while/body/eval_jaxpr/ppermute | solution.py:32
  257.8 10.8 %collective-permute-start.7 = (f32[1024,128]{0,1:T(8,128)S(1)}, f32[1024,128]{0,1:T(8,128)S(1)}, u32[]{:S(2)}, u32[]{:S(2)}) collective-permute-start(f32[1024,128]{0,1:T(8,128)S(1)} %add.232), channel_id=1, source_target_pairs={{0,2},{1,3},{2,0},{3,1},{4,6},{5,7},{6,4},{7,5},{8,10},{9,11},{10,... | collective-permute-start | bytes 1572872 | tf_op jit(solution)/shard_map/cond/branch_0_fun/while/body/eval_jaxpr/ppermute | solution.py:32
  275.2 6.0 %collective-permute-start.10 = (f32[128,128]{1,0:T(8,128)S(1)}, f32[128,128]{1,0:T(8,128)S(1)}, u32[]{:S(2)}, u32[]{:S(2)}) collective-permute-start(f32[128,128]{1,0:T(8,128)S(1)} %add.235), channel_id=1, source_target_pairs={{0,16},{4,20},{8,24},{12,28},{16,0},{20,4},{24,8},{28,12},{32,48},... | collective-permute-start | bytes 196616 | tf_op jit(solution)/shard_map/cond/branch_0_fun/while/body/eval_jaxpr/ppermute | solution.py:32
  281.3 8.3 %collective-permute-start.11 = (f32[128,128]{1,0:T(8,128)S(1)}, f32[128,128]{1,0:T(8,128)S(1)}, u32[]{:S(2)}, u32[]{:S(2)}) collective-permute-start(f32[128,128]{1,0:T(8,128)S(1)} %add.236), channel_id=1, source_target_pairs={{0,32},{4,36},{8,40},{12,44},{16,48},{20,52},{24,56},{28,60},{32,0... | collective-permute-start | bytes 196616 | tf_op jit(solution)/shard_map/cond/branch_0_fun/while/body/eval_jaxpr/ppermute | solution.py:32
  312.8 8.3 %collective-permute-start.3 = (f32[128,128]{0,1:T(8,128)S(1)}, f32[128,128]{0,1:T(8,128)S(1)}, u32[]{:S(2)}, u32[]{:S(2)}) collective-permute-start(f32[128,128]{0,1:T(8,128)S(1)} %add.228), channel_id=1, source_target_pairs={{0,32},{4,36},{8,40},{12,44},{16,48},{20,52},{24,56},{28,60},{32,0... | collective-permute-start | bytes 196616 | tf_op jit(solution)/shard_map/cond/branch_0_fun/while/body/eval_jaxpr/ppermute | solution.py:32
  355.0 10.0 %collective-permute-start.6 = (f32[1024,128]{0,1:T(8,128)S(1)}, f32[1024,128]{0,1:T(8,128)S(1)}, u32[]{:S(2)}, u32[]{:S(2)}) collective-permute-start(f32[1024,128]{0,1:T(8,128)S(1)} %fusion.44), channel_id=1, source_target_pairs={{0,1},{1,0},{2,3},{3,2},{4,5},{5,4},{6,7},{7,6},{8,9},{9,8},{10,11... | collective-permute-start | bytes 1572872 | tf_op jit(solution)/shard_map/cond/branch_0_fun/while/body/eval_jaxpr/ppermute | solution.py:32
  365.1 14.2 %collective-permute-start.7 = (f32[1024,128]{0,1:T(8,128)S(1)}, f32[1024,128]{0,1:T(8,128)S(1)}, u32[]{:S(2)}, u32[]{:S(2)}) collective-permute-start(f32[1024,128]{0,1:T(8,128)S(1)} %add.232), channel_id=1, source_target_pairs={{0,2},{1,3},{2,0},{3,1},{4,6},{5,7},{6,4},{7,5},{8,10},{9,11},{10,... | collective-permute-start | bytes 1572872 | tf_op jit(solution)/shard_map/cond/branch_0_fun/while/body/eval_jaxpr/ppermute | solution.py:32
  385.7 6.0 %collective-permute-start.10 = (f32[128,128]{1,0:T(8,128)S(1)}, f32[128,128]{1,0:T(8,128)S(1)}, u32[]{:S(2)}, u32[]{:S(2)}) collective-permute-start(f32[128,128]{1,0:T(8,128)S(1)} %add.235), channel_id=1, source_target_pairs={{0,16},{4,20},{8,24},{12,28},{16,0},{20,4},{24,8},{28,12},{32,48},... | collective-permute-start | bytes 196616 | tf_op jit(solution)/shard_map/cond/branch_0_fun/while/body/eval_jaxpr/ppermute | solution.py:32
  391.7 8.3 %collective-permute-start.11 = (f32[128,128]{1,0:T(8,128)S(1)}, f32[128,128]{1,0:T(8,128)S(1)}, u32[]{:S(2)}, u32[]{:S(2)}) collective-permute-start(f32[128,128]{1,0:T(8,128)S(1)} %add.236), channel_id=1, source_target_pairs={{0,32},{4,36},{8,40},{12,44},{16,48},{20,52},{24,56},{28,60},{32,0... | collective-permute-start | bytes 196616 | tf_op jit(solution)/shard_map/cond/branch_0_fun/while/body/eval_jaxpr/ppermute | solution.py:32
  404.3 6.2 %collective-permute-start.13 = (f32[128,128]{1,0:T(8,128)S(1)}, f32[128,128]{1,0:T(8,128)S(1)}, u32[]{:S(2)}, u32[]{:S(2)}) collective-permute-start(f32[128,128]{1,0:T(8,128)S(1)} %add.238), channel_id=1, source_target_pairs={{0,128},{4,132},{8,136},{12,140},{16,144},{20,148},{24,152},{28,15... | collective-permute-start | bytes 196616 | tf_op jit(solution)/shard_map/cond/branch_0_fun/while/body/eval_jaxpr/ppermute | solution.py:32
  423.1 8.3 %collective-permute-start.3 = (f32[128,128]{0,1:T(8,128)S(1)}, f32[128,128]{0,1:T(8,128)S(1)}, u32[]{:S(2)}, u32[]{:S(2)}) collective-permute-start(f32[128,128]{0,1:T(8,128)S(1)} %add.228), channel_id=1, source_target_pairs={{0,32},{4,36},{8,40},{12,44},{16,48},{20,52},{24,56},{28,60},{32,0... | collective-permute-start | bytes 196616 | tf_op jit(solution)/shard_map/cond/branch_0_fun/while/body/eval_jaxpr/ppermute | solution.py:32
  465.3 9.7 %collective-permute-start.6 = (f32[1024,128]{0,1:T(8,128)S(1)}, f32[1024,128]{0,1:T(8,128)S(1)}, u32[]{:S(2)}, u32[]{:S(2)}) collective-permute-start(f32[1024,128]{0,1:T(8,128)S(1)} %fusion.44), channel_id=1, source_target_pairs={{0,1},{1,0},{2,3},{3,2},{4,5},{5,4},{6,7},{7,6},{8,9},{9,8},{10,11... | collective-permute-start | bytes 1572872 | tf_op jit(solution)/shard_map/cond/branch_0_fun/while/body/eval_jaxpr/ppermute | solution.py:32
  475.1 15.3 %collective-permute-start.7 = (f32[1024,128]{0,1:T(8,128)S(1)}, f32[1024,128]{0,1:T(8,128)S(1)}, u32[]{:S(2)}, u32[]{:S(2)}) collective-permute-start(f32[1024,128]{0,1:T(8,128)S(1)} %add.232), channel_id=1, source_target_pairs={{0,2},{1,3},{2,0},{3,1},{4,6},{5,7},{6,4},{7,5},{8,10},{9,11},{10,... | collective-permute-start | bytes 1572872 | tf_op jit(solution)/shard_map/cond/branch_0_fun/while/body/eval_jaxpr/ppermute | solution.py:32
  502.3 8.3 %collective-permute-start.11 = (f32[128,128]{1,0:T(8,128)S(1)}, f32[128,128]{1,0:T(8,128)S(1)}, u32[]{:S(2)}, u32[]{:S(2)}) collective-permute-start(f32[128,128]{1,0:T(8,128)S(1)} %add.236), channel_id=1, source_target_pairs={{0,32},{4,36},{8,40},{12,44},{16,48},{20,52},{24,56},{28,60},{32,0... | collective-permute-start | bytes 196616 | tf_op jit(solution)/shard_map/cond/branch_0_fun/while/body/eval_jaxpr/ppermute | solution.py:32
  515.0 6.2 %collective-permute-start.13 = (f32[128,128]{1,0:T(8,128)S(1)}, f32[128,128]{1,0:T(8,128)S(1)}, u32[]{:S(2)}, u32[]{:S(2)}) collective-permute-start(f32[128,128]{1,0:T(8,128)S(1)} %add.238), channel_id=1, source_target_pairs={{0,128},{4,132},{8,136},{12,140},{16,144},{20,148},{24,152},{28,15... | collective-permute-start | bytes 196616 | tf_op jit(solution)/shard_map/cond/branch_0_fun/while/body/eval_jaxpr/ppermute | solution.py:32
  (37 other events, 318.6 us)

commit v4 on v3

--- a/solution.py
+++ b/solution.py
@@ -117,8 +117,8 @@
     start, cov, col_index, order, out, small,
     win, win_hl, covv, cov_hl, vall, vhl, acc, tb, r1, s1, r2, gb,
     e0, w, b, u, mk, e0_h, e0_l, w_h, w2_h, w_l, b_h, b_l, u_h, x_hl, res, scol,
-    c_sem, l_sem, f_sem,
-    halo_s, halo_r, left_s, right_s, fwdr_s, fwdl_s, next_r, prev_r, opp_r,
+    word, c_sem, l_sem, f_sem,
+    halo_s, halo_r, v_s, next_r, prev_r, opp_r,
     p1_s, p1_r, p2_s, p2_r, p4_s, p4_r, p5_s, p5_r, p6_s, p6_r,
 ):
     p = lax.axis_index("pts")
@@ -146,45 +146,44 @@
             device_id=where, device_id_type=MESH,
         )
 
-    def cov_copy(r):
-        return pltpu.make_async_copy(cov.at[r], covv.at[r], c_sem.at[r])
-
+    cov_copy = pltpu.make_async_copy(cov, covv, c_sem)
     own_copy = pltpu.make_async_copy(start, win.at[1], l_sem)
     own_copy.start()
 
-    def start_cov(r, carry):
-        cov_copy(r).start()
-        return carry
-
-    lax.fori_loop(0, ROW_BLOCKS, start_cov, 0)
+    cov_copy.start()
 
     barrier = pltpu.get_barrier_semaphore()
-    peers = [dict(pts=before), dict(pts=after)]
-    peers += [dict(cols=h) for h in (g_next, g_prev, g_opp)]
-    for one in peers:
-        pl.semaphore_signal(barrier, inc=1, device_id=one, device_id_type=MESH)
-
-    def greet(k, carry):
-        pl.semaphore_signal(barrier, inc=1, device_id=dict(pts=device(peer(k))), device_id_type=MESH)
-        return carry
-
-    lax.fori_loop(1, PLANE, greet, 0)
-    pl.semaphore_wait(barrier, len(peers) + PLANE - 1)
+    near_x = [dict(cols=h) for h in (g_next, g_prev)]
+    near_z = [dict(pts=device(peer(k))) for k in (1, ZS - 1)]
+    near_y = [dict(pts=device(peer(k))) for k in (ZS, (YS - 1) * ZS)]
+    next_z = [dict(pts=device(peer(k))) for k in (2, ZS - 2)]
+    neighbours = [dict(pts=before), dict(pts=after)] + near_x + near_z + near_y
+
+    def tell(sem, devices):
+        for one in devices:
+            pl.semaphore_signal(sem, inc=1, device_id=one, device_id_type=MESH)
+
+    tell(barrier, neighbours)
+    pl.semaphore_wait(barrier, len(neighbours))
+    tell(word.at[0], near_z)
+    tell(word.at[1], near_x)
+
+    def halo_rows(side, k):
+        count = HALF + 1 if k == 0 else 1
+        low = HALF - 1 - k if side == 0 else (0 if k == 0 else HALF + k)
+        return slice(low * BLOCK, (low + count) * BLOCK)
 
     def to_after(k):
-        rows = pl.ds(pl.multiple_of(k * BLOCK, BLOCK), BLOCK)
-        return remote(start.at[rows, :], win.at[0, rows, :], halo_s.at[0, k], halo_r.at[0, k], pts=after)
+        rows = halo_rows(0, k)
+        return remote(start.at[rows, :], win.at[0, rows, :], halo_s.at[0], halo_r.at[0, k], pts=after)
 
     def to_before(k):
-        rows = pl.ds(pl.multiple_of(k * BLOCK, BLOCK), BLOCK)
-        return remote(start.at[rows, :], win.at[2, rows, :], halo_s.at[1, k], halo_r.at[1, k], pts=before)
-
-    def start_halo(k, carry):
-        to_after(ROW_BLOCKS - 1 - k).start()
+        rows = halo_rows(2, k)
+        return remote(start.at[rows, :], win.at[2, rows, :], halo_s.at[1], halo_r.at[1, k], pts=before)
+
+    for k in range(HALF):
+        to_after(k).start()
         to_before(k).start()
-        return carry
-
-    lax.fori_loop(0, ROW_BLOCKS, start_halo, 0)
 
     ranks = []
     for a in range(GROUPS):
@@ -205,8 +204,9 @@
                 ahead = jnp.where(ranks[a] < ranks[h], 1.0, 0.0).astype(F32)
                 mk[rows, cols] = jnp.full((WIDTH, WIDTH), ahead, F32)
 
+    cov_copy.wait()
+
     def split_cov(r, carry):
-        cov_copy(r).wait()
         for s in range(SLOTS):
             high, low = split(covv[r, s])
             cov_hl[r, :BLOCK, s * BLOCK:(s + 1) * BLOCK] = high
@@ -215,8 +215,10 @@
 
     lax.fori_loop(0, ROW_BLOCKS, split_cov, 0)
 
+    pl.semaphore_wait(word.at[0], 2)
+    tell(word.at[2], next_z)
     def split_window(side, k):
-        rows = pl.ds(pl.multiple_of(k * BLOCK, BLOCK), BLOCK)
+        rows = pl.ds(k * BLOCK if isinstance(k, int) else pl.multiple_of(k * BLOCK, BLOCK), BLOCK)
         high, low = split(win[side, rows, :])
         win_hl[side * ROW_BLOCKS + k, :, :WIDTH] = high
         win_hl[side * ROW_BLOCKS + k, :, WIDTH:] = low
@@ -225,16 +227,8 @@
         split_window(1, k)
         return carry
 
-    def take_halo(k, carry):
-        to_after(ROW_BLOCKS - 1 - k).wait_recv()
-        split_window(0, ROW_BLOCKS - 1 - k)
-        to_before(k).wait_recv()
-        split_window(2, k)
-        return carry
-
     own_copy.wait()
     lax.fori_loop(0, ROW_BLOCKS, split_own, 0)
-    lax.fori_loop(0, HALF, take_halo, 0)
 
     base = p * ROW_BLOCKS - ROW_BLOCKS - NBLK
 
@@ -244,24 +238,28 @@
         r = HALF + step - up * (2 * step + 1)
         return r, pl.ds(pl.multiple_of(r * BLOCK, BLOCK), BLOCK)
 
-    def xcopy(src, i, send, recv, to):
+    def xcopy(src, i, recv, to):
         ref = vall.at[src, rows_of(src, i)[1], :]
-        return remote(ref, ref, send.at[i], recv.at[i], cols=to)
+        return remote(ref, ref, v_s, recv, cols=to)
 
     def own_left(i):
-        return xcopy(g, i, left_s, next_r, g_prev)
+        return xcopy(g, i, next_r.at[lax.rem(i, HALF)], g_prev)
 
     def own_right(i):
-        return xcopy(g, i, right_s, prev_r, g_next)
+        return xcopy(g, i, prev_r.at[lax.min(i, HALF)], g_next)
 
     def forward_right(i):
-        return xcopy(g_prev, i, fwdr_s, opp_r, g_next)
+        return xcopy(g_prev, i, opp_r.at[0], g_next)
 
     def forward_left(i):
-        return xcopy(g_next, i, fwdl_s, opp_r, g_prev)
-
-    def from_opp(i):
-        return xcopy(g_opp, i, fwdr_s, opp_r, g_next)
+        return xcopy(g_next, i, opp_r.at[1], g_prev)
+
+    def arrived(sem, *like):
+        for ref in like:
+            pltpu.make_async_copy(ref, ref, sem).wait()
+
+    def several(src, count):
+        return vall.at[src, pl.ds(0, count * BLOCK), :]
 
     def keep_split(src, i):
         rows = rows_of(src, i)[1]
@@ -279,16 +277,26 @@
         vall[g, rows, :] = quarters(quad, BLOCK, WIDTH)
         own_left(i).start()
 
-    def images(j, carry):
-        take_halo(j + HALF, 0)
+    for j in range(HALF):
+        to_after(j).wait_recv()
+        to_before(j).wait_recv()
+        if j == 0:
+            for k in range(HALF):
+                split_window(0, ROW_BLOCKS - 1 - k)
+                split_window(2, k)
+        split_window(0, HALF - 1 - j)
+        split_window(2, HALF + j)
         image(j)
         own_right(j).start()
         image(j + HALF)
         keep_split(g, j)
         keep_split(g, j + HALF)
-        return carry
-
-    lax.fori_loop(0, HALF, images, 0)
+        if j == 0:
+            pl.semaphore_wait(word.at[2], 2)
+            tell(word.at[3], near_y)
+
+    pl.semaphore_wait(word.at[3], 2)
+    tell(word.at[4], near_y)
 
     def half_of(src, late):
         low = lax.rem(lax.div(src, 2) + 1 + late, 2)
@@ -301,7 +309,7 @@
     tb[0, :TILES_G] = (gram_half(g, 0) + gram_half(g, 1)).reshape(TILES_G, 8, WIDTH)
 
     def pass_right(j, carry):
-        xcopy(g_prev, j, right_s, prev_r, g_next).wait_recv()
+        arrived(prev_r.at[j], several(g_prev, 1))
         forward_right(j).start()
         return carry
 
@@ -315,9 +323,9 @@
     acc[...] = jnp.zeros_like(acc)
 
     def take_next(j, carry):
-        for i in (j, j + HALF):
-            xcopy(g_next, i, left_s, next_r, g_prev).wait_recv()
-            keep_split(g_next, i)
+        arrived(next_r.at[j], several(g_next, 2))
+        keep_split(g_next, j)
+        keep_split(g_next, j + HALF)
         forward_left(j + HALF).start()
         near, far = rows_of(g_next, j)[1], rows_of(g_next, j + HALF)[1]
         left = jnp.concatenate([vhl[g, near, :], vhl[g, far, :]], axis=0)
@@ -326,7 +334,6 @@
         return carry
 
     def take_opp(i, carry):
-        from_opp(i).wait_recv()
         keep_split(g_opp, i)
         return carry
 
@@ -335,7 +342,8 @@
     edge = TILES - TILES_G
     tb[0, TILES_G:] = gram_next[:edge]
     tb[1, :TILES_G - edge] = gram_next[edge:]
-    lax.fori_loop(0, HALF, take_opp, 0)
+    arrived(opp_r.at[0], several(g_opp, HALF))
+    lax.fori_loop(0, HALF, take_opp, 0, unroll=True)
     tb[1, TILES_G - edge:] = gram_half(g_opp, 0).reshape(TILES_G, 8, WIDTH)
 
     to_core = remote(tb.at[1 - c], r1, p1_s, p1_r, pts=sibling)
@@ -343,9 +351,11 @@
     to_core.wait_recv()
     s1[...] = tb[c] + r1[...]
 
+    pl.semaphore_wait(word.at[4], 2)
+    pl.semaphore_wait(word.at[1], 2)
     def scatter(k):
         to = lax.min(peer(k), TILES - 1)
-        return remote(s1.at[to], r2.at[here], p2_s.at[k], p2_r.at[here], pts=device(to))
+        return remote(s1.at[to], r2.at[here], p2_s, p2_r, pts=device(to))
 
     def start_scatter(k, carry):
         @pl.when(peer(k) < TILES)
@@ -358,16 +368,13 @@
 
     def share(k):
         ref = gb.at[g, c, lax.min(here, TILES - 1)]
-        return remote(ref, ref, p4_s.at[k], p4_r.at[lax.min(here, TILES - 1)], pts=device(peer(k)))
+        return remote(ref, ref, p4_s, p4_r.at[lax.div(lax.min(here, TILES - 1), ZS)], pts=device(peer(k)))
 
     @pl.when(here < TILES)
     def _():
-        def take(k, summed):
-            source = peer(k)
-            remote(r2.at[source], r2.at[source], p2_s.at[k], p2_r.at[source], pts=device(source)).wait_recv()
-            return summed + r2[source]
-
-        gb[g, c, lax.min(here, TILES - 1)] = lax.fori_loop(1, PLANE, take, s1[lax.min(here, TILES - 1)])
+        arrived(p2_r, r2.at[pl.ds(1, PLANE - 1)])
+        r2[here] = s1[lax.min(here, TILES - 1)]
+        gb[g, c, lax.min(here, TILES - 1)] = jnp.sum(r2[...], axis=0)
 
         def start_share(k, carry):
             share(k).start()
@@ -381,51 +388,40 @@
 
     def x_share(k, n):
         ref = gb.at[g, c, rows_of_set(n)]
-        return remote(ref, ref, p5_s.at[k, n], p5_r.at[g, n], cols=lax.rem(g + k, GROUPS))
-
-    def x_shared(k, n):
-        source = lax.rem(g + k, GROUPS)
-        ref = gb.at[source, c, rows_of_set(n)]
-        return remote(ref, ref, p5_s.at[k, n], p5_r.at[source, n], cols=source)
-
-    def core_share(k):
-        source = lax.rem(g + k, GROUPS)
-        ref = gb.at[source, c]
-        return remote(ref, ref, p6_s.at[source], p6_r.at[source], pts=sibling)
-
-    def core_shared(k):
-        source = lax.rem(g + k, GROUPS)
-        ref = gb.at[source, 1 - c]
-        return remote(ref, ref, p6_s.at[source], p6_r.at[source], pts=sibling)
-
-    def shared(t, carry):
-        @pl.when(t != here)
+        return remote(ref, ref, p5_s, p5_r.at[GROUPS - k, n], cols=lax.rem(g + k, GROUPS))
+
+    def core_share(k, n):
+        ref = gb.at[lax.rem(g + k, GROUPS), c, rows_of_set(n)]
+        return remote(ref, ref, p6_s, p6_r, pts=sibling)
+
+    for n in range(SETS):
+        @pl.when(y == n)
         def _():
-            ref = gb.at[g, c, t]
-            remote(ref, ref, p4_s.at[0], p4_r.at[t], pts=device(t)).wait_recv()
-
-        return carry
-
-    for n in range(SETS):
-        lax.fori_loop(n * ZS, (n + 1) * ZS, shared, 0)
+            arrived(p4_r.at[n], gb.at[g, c, pl.ds(0, ZS - 1)])
+
+        @pl.when(y != n)
+        def _():
+            arrived(p4_r.at[n], gb.at[g, c, pl.ds(0, ZS)])
+
         for k in range(1, GROUPS):
             x_share(k, n).start()
-    core_share(0).start()
+        core_share(0, n).start()
+
+    arrived(prev_r.at[HALF], several(g_prev, HALF))
+    arrived(opp_r.at[1], several(g_opp, HALF))
 
     def rest(j, carry):
         keep_split(g_prev, j)
-        xcopy(g_prev, j + HALF, right_s, prev_r, g_next).wait_recv()
         keep_split(g_prev, j + HALF)
         take_opp(j + HALF, 0)
         return carry
 
     lax.fori_loop(0, HALF, rest, 0)
-    for k in range(1, GROUPS):
-        for n in range(SETS):
-            x_shared(k, n).wait_recv()
-        core_share(k).start()
-    for k in range(GROUPS):
-        core_shared(k).wait_recv()
+    for n in range(SETS):
+        for k in (1, 3, 2):
+            arrived(p5_r.at[k, n], gb.at[lax.rem(g + k, GROUPS), c, rows_of_set(n)])
+            core_share(k, n).start()
+    arrived(p6_r, gb.at[:, 1 - c])
 
     parts = [gb[a].reshape(3 * WIDTH, WIDTH) for a in range(GROUPS)]
     diag = [parts[a][:WIDTH] for a in range(GROUPS)]
@@ -510,58 +506,34 @@
     outv = win
 
     def result(k):
-        rows = pl.ds(pl.multiple_of(k * 2 * BLOCK, 2 * BLOCK), 2 * BLOCK)
-        return pltpu.make_async_copy(outv.at[1, rows, :], out.at[rows, :], f_sem.at[k])
-
-    def finish(k, carry):
-        rows = pl.ds(pl.multiple_of(k * 2 * BLOCK, 2 * BLOCK), 2 * BLOCK)
+        rows = slice(k * 2 * BLOCK, (k + 1) * 2 * BLOCK)
+        return pltpu.make_async_copy(outv.at[1, rows, :], out.at[rows, :], f_sem)
+
+    for k in range(ROW_BLOCKS // 2):
+        rows = slice(k * 2 * BLOCK, (k + 1) * 2 * BLOCK)
         high = jnp.concatenate([vhl[h, rows, :WIDTH] for h in range(GROUPS)], axis=1)
         low = jnp.concatenate([vhl[h, rows, WIDTH:] for h in range(GROUPS)], axis=1)
         q = dot(jnp.concatenate([high, low], axis=0), x_hl[...])
         outv[1, rows, :] = quarters(q, 2 * BLOCK, WIDTH)
         result(k).start()
-        return carry
-
-    lax.fori_loop(0, ROW_BLOCKS // 2, finish, 0)
-
-    def sent(i, carry):
-        to_after(i).wait_send()
-        to_before(i).wait_send()
-        own_left(i).wait_send()
-        own_right(i).wait_send()
-        return carry
-
-    def sent_on(i, carry):
-        forward_right(i).wait_send()
-        forward_left(i + HALF).wait_send()
-        return carry
-
-    def scattered(k, carry):
-        @pl.when(peer(k) < TILES)
-        def _():
-            scatter(k).wait_send()
-
-        @pl.when(here < TILES)
-        def _():
-            share(k).wait_send()
-
-        return carry
-
-    lax.fori_loop(0, ROW_BLOCKS, sent, 0)
-    lax.fori_loop(0, HALF, sent_on, 0)
+
+    arrived(halo_s.at[0], win.at[0])
+    arrived(halo_s.at[1], win.at[2])
+    arrived(v_s, vall.at[:3])
     to_core.wait_send()
-    lax.fori_loop(1, PLANE, scattered, 0)
-    for k in range(1, GROUPS):
-        for n in range(SETS):
-            x_share(k, n).wait_send()
-    for k in range(GROUPS):
-        core_share(k).wait_send()
-
-    def written(k, carry):
-        result(k).wait()
-        return carry
-
-    lax.fori_loop(0, ROW_BLOCKS // 2, written, 0)
+    arrived(p5_s, gb.at[:3, 0])
+    arrived(p6_s, gb.at[:, 0])
+
+    @pl.when(here < TILES)
+    def _():
+        arrived(p2_s, s1.at[pl.ds(0, TILES - 1)])
+        arrived(p4_s, r2.at[pl.ds(0, PLANE - 1)])
+
+    @pl.when(here >= TILES)
+    def _():
+        arrived(p2_s, s1)
+
+    arrived(f_sem, out)
 
 
 def fast(start, cov_blocks, col_index, order):
@@ -606,18 +578,15 @@
             pltpu.VMEM((COLS, 2 * WIDTH), BF16),
             pltpu.VMEM((8, COLS // 2), F32),
             pltpu.VMEM((COLS, WIDTH), F32),
-            dma((ROW_BLOCKS,)),
-            dma,
-            dma((ROW_BLOCKS // 2,)),
-            dma((2, ROW_BLOCKS)), dma((2, ROW_BLOCKS)),
-            dma((ROW_BLOCKS,)), dma((ROW_BLOCKS,)),
-            dma((ROW_BLOCKS,)), dma((ROW_BLOCKS,)),
-            dma((ROW_BLOCKS,)), dma((ROW_BLOCKS,)), dma((ROW_BLOCKS,)),
+            pltpu.SemaphoreType.REGULAR((5,)),
+            dma, dma, dma,
+            dma((2,)), dma((2, HALF)),
+            dma, dma((HALF,)), dma((HALF + 1,)), dma((2,)),
             dma, dma,
-            dma((PLANE,)), dma((PLANE,)),
-            dma((PLANE,)), dma((TILES,)),
-            dma((GROUPS, SETS)), dma((GROUPS, SETS)),
-            dma((GROUPS,)), dma((GROUPS,)),
+            dma, dma,
+            dma, dma((SETS,)),
+            dma, dma((GROUPS, SETS)),
+            dma, dma,
         ],
         compiler_params=pltpu.CompilerParams(
             collective_id=0, has_side_effects=True, vmem_limit_bytes=56 * 1024 * 1024

time: 528 us -> 524 us (level)
  waiting for transfers between devices: 225 us -> 306 us
  starting transfers between devices: 111 us -> 35.2 us
    ppermute x56, waiting for transfers between devices: 219 us -> 300 us  [total(): value = value + lax.ppermute(value, axis, pairs)]
    ppermute x56, starting transfers between devices: 106 us -> 29.2 us  [total(): value = value + lax.ppermute(value, axis, pairs)]
where the time goes in v4:
time: 524 us
  waiting for transfers between devices  306 us (58%)
  other arithmetic  93.2 us (18%)
  Pallas kernels  55.2 us (11%)
  starting transfers between devices  35.2 us (7%)
  matrix products  18.2 us (3%)
  loops' own time  8.46 us (2%)
  local copies, waits for them, and re-layouts  6.86 us (1%)
    ppermute x56, waiting for transfers between devices, total(): value = value + lax.ppermute(value, axis, pairs)  300 us
    pallas_call x1, Pallas kernels, fast(): pl.pallas_call(kernel, out_shape=(jax.ShapeDtypeStruct((ROWS, WIDTH), F32...  55.2 us
    another operation x12, other arithmetic, step(): lower = jnp.linalg.cholesky(gram)  49.8 us
    another operation x8, other arithmetic, step(): lax.linalg.triangular_solve(lower, local, left_side=False, lower=True, tr...  41.8 us
    ppermute x56, starting transfers between devices, total(): value = value + lax.ppermute(value, axis, pairs)  29.2 us
  transfers between devices with their start and end apart: 58, of which 58 were waited for; matrix products, arithmetic and copies ran while one was open for 1% of the time, Pallas kernels for 0%

profile of v4, /device:TPU:6, one launch (start us, length us, event | category | flops | bytes accessed | tf_op | source)
XLA Modules:
  0.0 524.0 jit_solution(15306525589886196946)
XLA Ops:
  0.0 55.2 %shard_map.48 = (f32[1024,128]{1,0:T(8,128)S(1)}, s32[1,1]{1,0:T(1,128)}) custom-call(f32[1024,128]{1,0:T(8,128)} %start.1, f32[8,8,128,128]{3,2,1,0:T(8,128)} %cov.1, s32[8,8]{1,0:T(8,128)} %col_index.1, s32[4]{0:T(128)} %order.1), custom_call_target="tpu_custom_call" | custom-call | tf_op jit(solution)/shard_map/pallas_call | solution.py:544
  55.9 467.4 %conditional.1 = (f32[1024,128]{1,0:T(8,128)S(1)}) conditional(s32[]{:T(128)} %bitcast.11, (f32[1024,128]{1,0:T(8,128)S(1)}, s32[8,8]{1,0:T(8,128)S(1)}, f32[8,8,128,128]{3,2,1,0:T(8,128)}, s32[4]{0:T(128)S(1)}) %tuple.55, f32[1024,128]{1,0:T(8,128)S(1)} %get-tuple-element.156), branch_computations={%region_0.6_spmd, %region_6.7_spmd} | conditional | flops 2417838080 | bytes 44441020 | solution.py:599
  71.5 7.9 %fusion.10 = f32[8,128,128,1]{1,2,3,0:T(8,128)S(1)} fusion(f32[8,8,128,128]{3,2,1,0:T(8,128)} %bitcast.52, f32[8,8,128,128]{3,2,1,0:T(8,128)} %get-tuple-element.150), kind=kOutput, calls=%fused_computation.26 | convolution fusion | flops 1610612736 | bytes 8912896 | tf_op jit(solution)/shard_map/cond/branch_0_fun/rsab,rsbk->rak/dot_general | solution.py:78
  79.6 443.2 %while.14 = (s32[]{:T(128)}, f32[1024,128]{0,1:T(8,128)S(1)}, s32[]{:T(128)}, s32[4]{0:T(128)S(1)}, s32[]{:T(128)}, /*index=5*/s32[]{:T(128)}, u32[]{:T(128)}) while((s32[]{:T(128)}, f32[1024,128]{0,1:T(8,128)S(1)}, s32[]{:T(128)}, s32[4]{0:T(128)S(1)}, s32[]{:T(128)}, /*index=5*/s32[]{:T(128)}, u32[]{:T(128)}) %tuple.48), condition=%wide.region_5.5_spmd, body=%wide.region_2.4_spmd.sunk | while | flops 806436992 | bytes 17696444 | solution.py:96
  110.9 11.7 %cholesky.58 = f32[128,128]{1,0:T(8,128)S(1)} custom-call(f32[128,128]{1,0:T(8,128)S(1)} %fusion.42), custom_call_target="Cholesky" | custom-call | tf_op jit(solution)/shard_map/cond/branch_0_fun/while/body/eval_jaxpr/jit(cholesky)/cholesky | solution.py:85
  124.0 9.8 %custom-call.23 = f32[1,128,128]{1,2,0:T(8,128)S(1)} custom-call(f32[1,128,128]{2,1,0:T(8,128)S(1)} %fusion.43), custom_call_target="InvertDiagBlocksLowerTriangular" | custom-call | tf_op jit(solution)/shard_map/cond/branch_0_fun/while/body/eval_jaxpr/triangular_solve | solution.py:86
  135.0 12.4 %collective-permute-done.6 = f32[1024,128]{0,1:T(8,128)S(1)} collective-permute-done((f32[1024,128]{0,1:T(8,128)S(1)}, f32[1024,128]{0,1:T(8,128)S(1)}, u32[]{:S(2)}, u32[]{:S(2)}) %collective-permute-start.6) | collective-permute-done | bytes 524320 | tf_op jit(solution)/shard_map/cond/branch_0_fun/while/body/eval_jaxpr/ppermute | solution.py:32
  147.9 10.3 %collective-permute-done.7 = f32[1024,128]{0,1:T(8,128)S(1)} collective-permute-done((f32[1024,128]{0,1:T(8,128)S(1)}, f32[1024,128]{0,1:T(8,128)S(1)}, u32[]{:S(2)}, u32[]{:S(2)}) %collective-permute-start.7) | collective-permute-done | bytes 524320 | tf_op jit(solution)/shard_map/cond/branch_0_fun/while/body/eval_jaxpr/ppermute | solution.py:32
  221.6 11.7 %cholesky.58 = f32[128,128]{1,0:T(8,128)S(1)} custom-call(f32[128,128]{1,0:T(8,128)S(1)} %fusion.42), custom_call_target="Cholesky" | custom-call | tf_op jit(solution)/shard_map/cond/branch_0_fun/while/body/eval_jaxpr/jit(cholesky)/cholesky | solution.py:85
  234.7 9.8 %custom-call.23 = f32[1,128,128]{1,2,0:T(8,128)S(1)} custom-call(f32[1,128,128]{2,1,0:T(8,128)S(1)} %fusion.43), custom_call_target="InvertDiagBlocksLowerTriangular" | custom-call | tf_op jit(solution)/shard_map/cond/branch_0_fun/while/body/eval_jaxpr/triangular_solve | solution.py:86
  245.2 14.1 %collective-permute-done.6 = f32[1024,128]{0,1:T(8,128)S(1)} collective-permute-done((f32[1024,128]{0,1:T(8,128)S(1)}, f32[1024,128]{0,1:T(8,128)S(1)}, u32[]{:S(2)}, u32[]{:S(2)}) %collective-permute-start.6) | collective-permute-done | bytes 524320 | tf_op jit(solution)/shard_map/cond/branch_0_fun/while/body/eval_jaxpr/ppermute | solution.py:32
  259.4 10.7 %collective-permute-done.7 = f32[1024,128]{0,1:T(8,128)S(1)} collective-permute-done((f32[1024,128]{0,1:T(8,128)S(1)}, f32[1024,128]{0,1:T(8,128)S(1)}, u32[]{:S(2)}, u32[]{:S(2)}) %collective-permute-start.7) | collective-permute-done | bytes 524320 | tf_op jit(solution)/shard_map/cond/branch_0_fun/while/body/eval_jaxpr/ppermute | solution.py:32
  283.0 7.3 %collective-permute-done.11 = f32[128,128]{1,0:T(8,128)S(1)} collective-permute-done((f32[128,128]{1,0:T(8,128)S(1)}, f32[128,128]{1,0:T(8,128)S(1)}, u32[]{:S(2)}, u32[]{:S(2)}) %collective-permute-start.11) | collective-permute-done | bytes 65568 | tf_op jit(solution)/shard_map/cond/branch_0_fun/while/body/eval_jaxpr/ppermute | solution.py:32
  314.6 7.4 %collective-permute-done.3 = f32[128,128]{0,1:T(8,128)S(1)} collective-permute-done((f32[128,128]{0,1:T(8,128)S(1)}, f32[128,128]{0,1:T(8,128)S(1)}, u32[]{:S(2)}, u32[]{:S(2)}) %collective-permute-start.3) | collective-permute-done | bytes 65568 | tf_op jit(solution)/shard_map/cond/branch_0_fun/while/body/eval_jaxpr/ppermute | solution.py:32
  332.4 11.7 %cholesky.58 = f32[128,128]{1,0:T(8,128)S(1)} custom-call(f32[128,128]{1,0:T(8,128)S(1)} %fusion.42), custom_call_target="Cholesky" | custom-call | tf_op jit(solution)/shard_map/cond/branch_0_fun/while/body/eval_jaxpr/jit(cholesky)/cholesky | solution.py:85
  345.4 9.8 %custom-call.23 = f32[1,128,128]{1,2,0:T(8,128)S(1)} custom-call(f32[1,128,128]{2,1,0:T(8,128)S(1)} %fusion.43), custom_call_target="InvertDiagBlocksLowerTriangular" | custom-call | tf_op jit(solution)/shard_map/cond/branch_0_fun/while/body/eval_jaxpr/triangular_solve | solution.py:86
  356.0 14.1 %collective-permute-done.6 = f32[1024,128]{0,1:T(8,128)S(1)} collective-permute-done((f32[1024,128]{0,1:T(8,128)S(1)}, f32[1024,128]{0,1:T(8,128)S(1)}, u32[]{:S(2)}, u32[]{:S(2)}) %collective-permute-start.6) | collective-permute-done | bytes 524320 | tf_op jit(solution)/shard_map/cond/branch_0_fun/while/body/eval_jaxpr/ppermute | solution.py:32
  370.3 10.7 %collective-permute-done.7 = f32[1024,128]{0,1:T(8,128)S(1)} collective-permute-done((f32[1024,128]{0,1:T(8,128)S(1)}, f32[1024,128]{0,1:T(8,128)S(1)}, u32[]{:S(2)}, u32[]{:S(2)}) %collective-permute-start.7) | collective-permute-done | bytes 524320 | tf_op jit(solution)/shard_map/cond/branch_0_fun/while/body/eval_jaxpr/ppermute | solution.py:32
  394.2 7.0 %collective-permute-done.11 = f32[128,128]{1,0:T(8,128)S(1)} collective-permute-done((f32[128,128]{1,0:T(8,128)S(1)}, f32[128,128]{1,0:T(8,128)S(1)}, u32[]{:S(2)}, u32[]{:S(2)}) %collective-permute-start.11) | collective-permute-done | bytes 65568 | tf_op jit(solution)/shard_map/cond/branch_0_fun/while/body/eval_jaxpr/ppermute | solution.py:32
  442.8 11.7 %cholesky.58 = f32[128,128]{1,0:T(8,128)S(1)} custom-call(f32[128,128]{1,0:T(8,128)S(1)} %fusion.42), custom_call_target="Cholesky" | custom-call | tf_op jit(solution)/shard_map/cond/branch_0_fun/while/body/eval_jaxpr/jit(cholesky)/cholesky | solution.py:85
  455.9 9.8 %custom-call.23 = f32[1,128,128]{1,2,0:T(8,128)S(1)} custom-call(f32[1,128,128]{2,1,0:T(8,128)S(1)} %fusion.43), custom_call_target="InvertDiagBlocksLowerTriangular" | custom-call | tf_op jit(solution)/shard_map/cond/branch_0_fun/while/body/eval_jaxpr/triangular_solve | solution.py:86
  466.4 14.3 %collective-permute-done.6 = f32[1024,128]{0,1:T(8,128)S(1)} collective-permute-done((f32[1024,128]{0,1:T(8,128)S(1)}, f32[1024,128]{0,1:T(8,128)S(1)}, u32[]{:S(2)}, u32[]{:S(2)}) %collective-permute-start.6) | collective-permute-done | bytes 524320 | tf_op jit(solution)/shard_map/cond/branch_0_fun/while/body/eval_jaxpr/ppermute | solution.py:32
  480.8 10.7 %collective-permute-done.7 = f32[1024,128]{0,1:T(8,128)S(1)} collective-permute-done((f32[1024,128]{0,1:T(8,128)S(1)}, f32[1024,128]{0,1:T(8,128)S(1)}, u32[]{:S(2)}, u32[]{:S(2)}) %collective-permute-start.7) | collective-permute-done | bytes 524320 | tf_op jit(solution)/shard_map/cond/branch_0_fun/while/body/eval_jaxpr/ppermute | solution.py:32
  503.7 8.1 %collective-permute-done.11 = f32[128,128]{1,0:T(8,128)S(1)} collective-permute-done((f32[128,128]{1,0:T(8,128)S(1)}, f32[128,128]{1,0:T(8,128)S(1)}, u32[]{:S(2)}, u32[]{:S(2)}) %collective-permute-start.11) | collective-permute-done | bytes 65568 | tf_op jit(solution)/shard_map/cond/branch_0_fun/while/body/eval_jaxpr/ppermute | solution.py:32
  (211 shorter events, 238.8 us)
Async XLA Ops:
  55.9 12.6 %collective-permute-start.14 = (f32[1024,128]{1,0:T(8,128)S(1)}, f32[1024,128]{1,0:T(8,128)S(1)}, u32[]{:S(2)}, u32[]{:S(2)}) collective-permute-start(f32[1024,128]{1,0:T(8,128)S(1)} %get-tuple-element.148), channel_id=1, source_target_pairs={{0,4},{4,8},{8,12},{12,16},{16,20},{20,24},{24,28},{28,32},{32,36}... | collective-permute-start | bytes 1572872 | tf_op jit(solution)/shard_map/cond/branch_0_fun/ppermute | solution.py:48
  57.3 11.4 %collective-permute-start.15 = (f32[1024,128]{1,0:T(8,128)S(1)}, f32[1024,128]{1,0:T(8,128)S(1)}, u32[]{:S(2)}, u32[]{:S(2)}) collective-permute-start(f32[1024,128]{1,0:T(8,128)S(1)} %get-tuple-element.148), channel_id=1, source_target_pairs={{4,0},{8,4},{12,8},{16,12},{20,16},{24,20},{28,24},{32,28},{36,32}... | collective-permute-start | bytes 1572872 | tf_op jit(solution)/shard_map/cond/branch_0_fun/ppermute | solution.py:50
  91.5 8.3 %collective-permute-start.3 = (f32[128,128]{0,1:T(8,128)S(1)}, f32[128,128]{0,1:T(8,128)S(1)}, u32[]{:S(2)}, u32[]{:S(2)}) collective-permute-start(f32[128,128]{0,1:T(8,128)S(1)} %add.228), channel_id=1, source_target_pairs={{0,32},{4,36},{8,40},{12,44},{16,48},{20,52},{24,56},{28,60},{32,0... | collective-permute-start | bytes 196616 | tf_op jit(solution)/shard_map/cond/branch_0_fun/while/body/eval_jaxpr/ppermute | solution.py:32
  104.9 5.9 %collective-permute-start.5 = (f32[128,128]{0,1:T(8,128)S(1)}, f32[128,128]{0,1:T(8,128)S(1)}, u32[]{:S(2)}, u32[]{:S(2)}) collective-permute-start(f32[128,128]{0,1:T(8,128)S(1)} %add.230), channel_id=1, source_target_pairs={{0,128},{4,132},{8,136},{12,140},{16,144},{20,148},{24,152},{28,15... | collective-permute-start | bytes 196616 | tf_op jit(solution)/shard_map/cond/branch_0_fun/while/body/eval_jaxpr/ppermute | solution.py:32
  134.4 13.0 %collective-permute-start.6 = (f32[1024,128]{0,1:T(8,128)S(1)}, f32[1024,128]{0,1:T(8,128)S(1)}, u32[]{:S(2)}, u32[]{:S(2)}) collective-permute-start(f32[1024,128]{0,1:T(8,128)S(1)} %fusion.44), channel_id=1, source_target_pairs={{0,1},{1,0},{2,3},{3,2},{4,5},{5,4},{6,7},{7,6},{8,9},{9,8},{10,11... | collective-permute-start | bytes 1572872 | tf_op jit(solution)/shard_map/cond/branch_0_fun/while/body/eval_jaxpr/ppermute | solution.py:32
  147.5 10.8 %collective-permute-start.7 = (f32[1024,128]{0,1:T(8,128)S(1)}, f32[1024,128]{0,1:T(8,128)S(1)}, u32[]{:S(2)}, u32[]{:S(2)}) collective-permute-start(f32[1024,128]{0,1:T(8,128)S(1)} %add.232), channel_id=1, source_target_pairs={{0,2},{1,3},{2,0},{3,1},{4,6},{5,7},{6,4},{7,5},{8,10},{9,11},{10,... | collective-permute-start | bytes 1572872 | tf_op jit(solution)/shard_map/cond/branch_0_fun/while/body/eval_jaxpr/ppermute | solution.py:32
  170.2 9.0 %collective-permute-start.11 = (f32[128,128]{1,0:T(8,128)S(1)}, f32[128,128]{1,0:T(8,128)S(1)}, u32[]{:S(2)}, u32[]{:S(2)}) collective-permute-start(f32[128,128]{1,0:T(8,128)S(1)} %add.236), channel_id=1, source_target_pairs={{0,32},{4,36},{8,40},{12,44},{16,48},{20,52},{24,56},{28,60},{32,0... | collective-permute-start | bytes 196616 | tf_op jit(solution)/shard_map/cond/branch_0_fun/while/body/eval_jaxpr/ppermute | solution.py:32
  183.7 5.9 %collective-permute-start.13 = (f32[128,128]{1,0:T(8,128)S(1)}, f32[128,128]{1,0:T(8,128)S(1)}, u32[]{:S(2)}, u32[]{:S(2)}) collective-permute-start(f32[128,128]{1,0:T(8,128)S(1)} %add.238), channel_id=1, source_target_pairs={{0,128},{4,132},{8,136},{12,140},{16,144},{20,148},{24,152},{28,15... | collective-permute-start | bytes 196616 | tf_op jit(solution)/shard_map/cond/branch_0_fun/while/body/eval_jaxpr/ppermute | solution.py:32
  202.2 9.0 %collective-permute-start.3 = (f32[128,128]{0,1:T(8,128)S(1)}, f32[128,128]{0,1:T(8,128)S(1)}, u32[]{:S(2)}, u32[]{:S(2)}) collective-permute-start(f32[128,128]{0,1:T(8,128)S(1)} %add.228), channel_id=1, source_target_pairs={{0,32},{4,36},{8,40},{12,44},{16,48},{20,52},{24,56},{28,60},{32,0... | collective-permute-start | bytes 196616 | tf_op jit(solution)/shard_map/cond/branch_0_fun/while/body/eval_jaxpr/ppermute | solution.py:32
  215.6 5.9 %collective-permute-start.5 = (f32[128,128]{0,1:T(8,128)S(1)}, f32[128,128]{0,1:T(8,128)S(1)}, u32[]{:S(2)}, u32[]{:S(2)}) collective-permute-start(f32[128,128]{0,1:T(8,128)S(1)} %add.230), channel_id=1, source_target_pairs={{0,128},{4,132},{8,136},{12,140},{16,144},{20,148},{24,152},{28,15... | collective-permute-start | bytes 196616 | tf_op jit(solution)/shard_map/cond/branch_0_fun/while/body/eval_jaxpr/ppermute | solution.py:32
  245.1 14.2 %collective-permute-start.6 = (f32[1024,128]{0,1:T(8,128)S(1)}, f32[1024,128]{0,1:T(8,128)S(1)}, u32[]{:S(2)}, u32[]{:S(2)}) collective-permute-start(f32[1024,128]{0,1:T(8,128)S(1)} %fusion.44), channel_id=1, source_target_pairs={{0,1},{1,0},{2,3},{3,2},{4,5},{5,4},{6,7},{7,6},{8,9},{9,8},{10,11... | collective-permute-start | bytes 1572872 | tf_op jit(solution)/shard_map/cond/branch_0_fun/while/body/eval_jaxpr/ppermute | solution.py:32
  259.3 10.8 %collective-permute-start.7 = (f32[1024,128]{0,1:T(8,128)S(1)}, f32[1024,128]{0,1:T(8,128)S(1)}, u32[]{:S(2)}, u32[]{:S(2)}) collective-permute-start(f32[1024,128]{0,1:T(8,128)S(1)} %add.232), channel_id=1, source_target_pairs={{0,2},{1,3},{2,0},{3,1},{4,6},{5,7},{6,4},{7,5},{8,10},{9,11},{10,... | collective-permute-start | bytes 1572872 | tf_op jit(solution)/shard_map/cond/branch_0_fun/while/body/eval_jaxpr/ppermute | solution.py:32
  282.1 8.3 %collective-permute-start.11 = (f32[128,128]{1,0:T(8,128)S(1)}, f32[128,128]{1,0:T(8,128)S(1)}, u32[]{:S(2)}, u32[]{:S(2)}) collective-permute-start(f32[128,128]{1,0:T(8,128)S(1)} %add.236), channel_id=1, source_target_pairs={{0,32},{4,36},{8,40},{12,44},{16,48},{20,52},{24,56},{28,60},{32,0... | collective-permute-start | bytes 196616 | tf_op jit(solution)/shard_map/cond/branch_0_fun/while/body/eval_jaxpr/ppermute | solution.py:32
  294.7 5.9 %collective-permute-start.13 = (f32[128,128]{1,0:T(8,128)S(1)}, f32[128,128]{1,0:T(8,128)S(1)}, u32[]{:S(2)}, u32[]{:S(2)}) collective-permute-start(f32[128,128]{1,0:T(8,128)S(1)} %add.238), channel_id=1, source_target_pairs={{0,128},{4,132},{8,136},{12,140},{16,144},{20,148},{24,152},{28,15... | collective-permute-start | bytes 196616 | tf_op jit(solution)/shard_map/cond/branch_0_fun/while/body/eval_jaxpr/ppermute | solution.py:32
  313.5 8.5 %collective-permute-start.3 = (f32[128,128]{0,1:T(8,128)S(1)}, f32[128,128]{0,1:T(8,128)S(1)}, u32[]{:S(2)}, u32[]{:S(2)}) collective-permute-start(f32[128,128]{0,1:T(8,128)S(1)} %add.228), channel_id=1, source_target_pairs={{0,32},{4,36},{8,40},{12,44},{16,48},{20,52},{24,56},{28,60},{32,0... | collective-permute-start | bytes 196616 | tf_op jit(solution)/shard_map/cond/branch_0_fun/while/body/eval_jaxpr/ppermute | solution.py:32
  326.4 5.9 %collective-permute-start.5 = (f32[128,128]{0,1:T(8,128)S(1)}, f32[128,128]{0,1:T(8,128)S(1)}, u32[]{:S(2)}, u32[]{:S(2)}) collective-permute-start(f32[128,128]{0,1:T(8,128)S(1)} %add.230), channel_id=1, source_target_pairs={{0,128},{4,132},{8,136},{12,140},{16,144},{20,148},{24,152},{28,15... | collective-permute-start | bytes 196616 | tf_op jit(solution)/shard_map/cond/branch_0_fun/while/body/eval_jaxpr/ppermute | solution.py:32
  355.9 14.2 %collective-permute-start.6 = (f32[1024,128]{0,1:T(8,128)S(1)}, f32[1024,128]{0,1:T(8,128)S(1)}, u32[]{:S(2)}, u32[]{:S(2)}) collective-permute-start(f32[1024,128]{0,1:T(8,128)S(1)} %fusion.44), channel_id=1, source_target_pairs={{0,1},{1,0},{2,3},{3,2},{4,5},{5,4},{6,7},{7,6},{8,9},{9,8},{10,11... | collective-permute-start | bytes 1572872 | tf_op jit(solution)/shard_map/cond/branch_0_fun/while/body/eval_jaxpr/ppermute | solution.py:32
  370.2 10.8 %collective-permute-start.7 = (f32[1024,128]{0,1:T(8,128)S(1)}, f32[1024,128]{0,1:T(8,128)S(1)}, u32[]{:S(2)}, u32[]{:S(2)}) collective-permute-start(f32[1024,128]{0,1:T(8,128)S(1)} %add.232), channel_id=1, source_target_pairs={{0,2},{1,3},{2,0},{3,1},{4,6},{5,7},{6,4},{7,5},{8,10},{9,11},{10,... | collective-permute-start | bytes 1572872 | tf_op jit(solution)/shard_map/cond/branch_0_fun/while/body/eval_jaxpr/ppermute | solution.py:32
  393.0 8.3 %collective-permute-start.11 = (f32[128,128]{1,0:T(8,128)S(1)}, f32[128,128]{1,0:T(8,128)S(1)}, u32[]{:S(2)}, u32[]{:S(2)}) collective-permute-start(f32[128,128]{1,0:T(8,128)S(1)} %add.236), channel_id=1, source_target_pairs={{0,32},{4,36},{8,40},{12,44},{16,48},{20,52},{24,56},{28,60},{32,0... | collective-permute-start | bytes 196616 | tf_op jit(solution)/shard_map/cond/branch_0_fun/while/body/eval_jaxpr/ppermute | solution.py:32
  405.6 5.9 %collective-permute-start.13 = (f32[128,128]{1,0:T(8,128)S(1)}, f32[128,128]{1,0:T(8,128)S(1)}, u32[]{:S(2)}, u32[]{:S(2)}) collective-permute-start(f32[128,128]{1,0:T(8,128)S(1)} %add.238), channel_id=1, source_target_pairs={{0,128},{4,132},{8,136},{12,140},{16,144},{20,148},{24,152},{28,15... | collective-permute-start | bytes 196616 | tf_op jit(solution)/shard_map/cond/branch_0_fun/while/body/eval_jaxpr/ppermute | solution.py:32
  424.1 8.3 %collective-permute-start.3 = (f32[128,128]{0,1:T(8,128)S(1)}, f32[128,128]{0,1:T(8,128)S(1)}, u32[]{:S(2)}, u32[]{:S(2)}) collective-permute-start(f32[128,128]{0,1:T(8,128)S(1)} %add.228), channel_id=1, source_target_pairs={{0,32},{4,36},{8,40},{12,44},{16,48},{20,52},{24,56},{28,60},{32,0... | collective-permute-start | bytes 196616 | tf_op jit(solution)/shard_map/cond/branch_0_fun/while/body/eval_jaxpr/ppermute | solution.py:32
  466.3 14.4 %collective-permute-start.6 = (f32[1024,128]{0,1:T(8,128)S(1)}, f32[1024,128]{0,1:T(8,128)S(1)}, u32[]{:S(2)}, u32[]{:S(2)}) collective-permute-start(f32[1024,128]{0,1:T(8,128)S(1)} %fusion.44), channel_id=1, source_target_pairs={{0,1},{1,0},{2,3},{3,2},{4,5},{5,4},{6,7},{7,6},{8,9},{9,8},{10,11... | collective-permute-start | bytes 1572872 | tf_op jit(solution)/shard_map/cond/branch_0_fun/while/body/eval_jaxpr/ppermute | solution.py:32
  480.7 10.8 %collective-permute-start.7 = (f32[1024,128]{0,1:T(8,128)S(1)}, f32[1024,128]{0,1:T(8,128)S(1)}, u32[]{:S(2)}, u32[]{:S(2)}) collective-permute-start(f32[1024,128]{0,1:T(8,128)S(1)} %add.232), channel_id=1, source_target_pairs={{0,2},{1,3},{2,0},{3,1},{4,6},{5,7},{6,4},{7,5},{8,10},{9,11},{10,... | collective-permute-start | bytes 1572872 | tf_op jit(solution)/shard_map/cond/branch_0_fun/while/body/eval_jaxpr/ppermute | solution.py:32
  503.5 8.3 %collective-permute-start.11 = (f32[128,128]{1,0:T(8,128)S(1)}, f32[128,128]{1,0:T(8,128)S(1)}, u32[]{:S(2)}, u32[]{:S(2)}) collective-permute-start(f32[128,128]{1,0:T(8,128)S(1)} %add.236), channel_id=1, source_target_pairs={{0,32},{4,36},{8,40},{12,44},{16,48},{20,52},{24,56},{28,60},{32,0... | collective-permute-start | bytes 196616 | tf_op jit(solution)/shard_map/cond/branch_0_fun/while/body/eval_jaxpr/ppermute | solution.py:32
  (37 other events, 305.4 us)

commit v5 on v4

--- a/solution.py
+++ b/solution.py
@@ -18,10 +18,12 @@
 COLS = GROUPS * WIDTH
 ROWS = ROW_BLOCKS * BLOCK
 HALF = ROW_BLOCKS // 2
-TILES = 3 * WIDTH // CORES // 8
 PLANE = YS * ZS
-TILES_G = WIDTH // 8
-SETS = TILES // ZS
+TILES_G = WIDTH // CORES // 8
+KINDS = 4
+TILES = KINDS * TILES_G
+LATE = TILES - TILES_G
+NEAR_LAST = (4, 3, 5, 2, 6, 1, 7, 0)
 TOLERANCE = 4e-4
 
 
@@ -115,10 +117,10 @@
 
 def kernel(
     start, cov, col_index, order, out, small,
-    win, win_hl, covv, cov_hl, vall, vhl, acc, tb, r1, s1, r2, gb,
+    win, win_hl, covv, cov_hl, vall, vhl, acc, acc2, tb, r1, s1, r2, gb,
     e0, w, b, u, mk, e0_h, e0_l, w_h, w2_h, w_l, b_h, b_l, u_h, x_hl, res, scol,
     word, c_sem, l_sem, f_sem,
-    halo_s, halo_r, v_s, next_r, prev_r, opp_r,
+    halo_s, halo_r, v_s, next_r, prev_r, rest_r,
     p1_s, p1_r, p2_s, p2_r, p4_s, p4_r, p5_s, p5_r, p6_s, p6_r,
 ):
     p = lax.axis_index("pts")
@@ -232,50 +234,66 @@
 
     base = p * ROW_BLOCKS - ROW_BLOCKS - NBLK
 
-    def rows_of(src, i):
-        step, late = lax.rem(i, HALF), lax.div(i, HALF)
-        up = lax.rem(lax.div(src, 2) + late, 2)
-        r = HALF + step - up * (2 * step + 1)
-        return r, pl.ds(pl.multiple_of(r * BLOCK, BLOCK), BLOCK)
-
-    def xcopy(src, i, recv, to):
-        ref = vall.at[src, rows_of(src, i)[1], :]
+    def rows(r):
+        return slice(r * BLOCK, (r + 1) * BLOCK)
+
+    def turn(r):
+        return lax.rem(g + GROUPS - r % GROUPS, GROUPS)
+
+    def goes_left(r):
+        t = turn(r)
+        return (t >= 2) | (t == 0) if r < HALF else t >= 2
+
+    def goes_right(r):
+        t = turn(r)
+        return t <= 1 if r < HALF else (t <= 1) | (t == 3)
+
+    def between(r):
+        t = turn(r)
+        return (t == 1) | (t == 2)
+
+    def has_next(r):
+        t = turn(r)
+        return t >= 1 if r < HALF else (t == 1) | (t == 2)
+
+    def has_prev(r):
+        t = turn(r)
+        return (t == 1) | (t == 2) if r < HALF else t <= 2
+
+    def prev_pair(r):
+        t = turn(r)
+        return t == 1 if r < HALF else t <= 1
+
+    def xcopy(src, r, recv, to):
+        ref = vall.at[src, rows(r), :]
         return remote(ref, ref, v_s, recv, cols=to)
 
-    def own_left(i):
-        return xcopy(g, i, next_r.at[lax.rem(i, HALF)], g_prev)
-
-    def own_right(i):
-        return xcopy(g, i, prev_r.at[lax.min(i, HALF)], g_next)
-
-    def forward_right(i):
-        return xcopy(g_prev, i, opp_r.at[0], g_next)
-
-    def forward_left(i):
-        return xcopy(g_next, i, opp_r.at[1], g_prev)
-
-    def arrived(sem, *like):
-        for ref in like:
-            pltpu.make_async_copy(ref, ref, sem).wait()
-
-    def several(src, count):
-        return vall.at[src, pl.ds(0, count * BLOCK), :]
-
-    def keep_split(src, i):
-        rows = rows_of(src, i)[1]
-        high, low = split(vall[src, rows, :])
-        vhl[src, rows, :WIDTH] = high
-        vhl[src, rows, WIDTH:] = low
-
-    def image(i):
-        r, rows = rows_of(g, i)
+    def arrived(sem, ref):
+        pltpu.make_async_copy(ref, ref, sem).wait()
+
+    def several(count):
+        return vall.at[0, :count * BLOCK, :]
+
+    def keep_split(src, r):
+        high, low = split(vall[src, rows(r), :])
+        vhl[src, rows(r), :WIDTH] = high
+        vhl[src, rows(r), WIDTH:] = low
+
+    def image(r):
         tiles = []
         for s in range(SLOTS):
             rel = lax.rem(col_index[r, s] - base, NBLK)
             tiles.append(win_hl[lax.min(rel, 3 * ROW_BLOCKS - 1)])
         quad = dot(cov_hl[r], jnp.concatenate(tiles, axis=0))
-        vall[g, rows, :] = quarters(quad, BLOCK, WIDTH)
-        own_left(i).start()
+        vall[g, rows(r), :] = quarters(quad, BLOCK, WIDTH)
+
+        @pl.when(goes_left(r))
+        def _():
+            xcopy(g, r, next_r.at[r], g_prev).start()
+
+        @pl.when(goes_right(r))
+        def _():
+            xcopy(g, r, prev_r.at[r], g_next).start()
 
     for j in range(HALF):
         to_after(j).wait_recv()
@@ -286,11 +304,9 @@
                 split_window(2, k)
         split_window(0, HALF - 1 - j)
         split_window(2, HALF + j)
-        image(j)
-        own_right(j).start()
-        image(j + HALF)
-        keep_split(g, j)
-        keep_split(g, j + HALF)
+        for r in (HALF + j, HALF - 1 - j):
+            image(r)
+            keep_split(g, r)
         if j == 0:
             pl.semaphore_wait(word.at[2], 2)
             tell(word.at[3], near_y)
@@ -298,133 +314,158 @@
     pl.semaphore_wait(word.at[3], 2)
     tell(word.at[4], near_y)
 
-    def half_of(src, late):
-        low = lax.rem(lax.div(src, 2) + 1 + late, 2)
-        return pl.ds(pl.multiple_of(low * (HALF * BLOCK), HALF * BLOCK), HALF * BLOCK)
-
-    def gram_half(src, late):
-        rows = half_of(src, late)
-        return quarters(dot_t(vhl[g, rows, :], vhl[src, rows, :]), WIDTH, WIDTH)
-
-    tb[0, :TILES_G] = (gram_half(g, 0) + gram_half(g, 1)).reshape(TILES_G, 8, WIDTH)
-
-    def pass_right(j, carry):
-        arrived(prev_r.at[j], several(g_prev, 1))
-        forward_right(j).start()
-        return carry
-
-    def rest_right(j, carry):
-        own_right(j).start()
-        return carry
-
-    lax.fori_loop(0, HALF, pass_right, 0)
-    lax.fori_loop(HALF, ROW_BLOCKS, rest_right, 0)
+    def place(kind, block):
+        for core in range(CORES):
+            part = block[core * WIDTH // CORES:(core + 1) * WIDTH // CORES]
+            tb[core, kind * TILES_G:(kind + 1) * TILES_G] = part.reshape(TILES_G, 8, WIDTH)
+
+    def core_sum(first, count, send, recv):
+        part = pl.ds(first, count)
+        copy = remote(tb.at[1 - c, part], r1.at[part], send, recv, pts=sibling)
+        return copy, part
+
+    def scatter(y_to, far):
+        to = y_to * ZS + lax.rem(z + far, ZS)
+        return remote(s1.at[to], r2.at[here], p2_s, p2_r, pts=device(to))
+
+    def scatter_rows(y_to):
+        for far in NEAR_LAST[:-1]:
+            scatter(y_to, far).start()
+
+        @pl.when(y != y_to)
+        def _():
+            scatter(y_to, 0).start()
+
+    def sum_tile():
+        arrived(p2_r, r2.at[pl.ds(1, PLANE - 1)])
+        r2[here] = s1[here]
+        gb[g, c, here] = jnp.sum(r2[...], axis=0)
+        ref = gb.at[g, c, here]
+        for over in (2, 1, 3, 0):
+            for far in NEAR_LAST:
+                if over or far:
+                    to = lax.rem(y + over, YS) * ZS + lax.rem(z + far, ZS)
+                    remote(ref, ref, p4_s, p4_r.at[y], pts=device(to)).start()
 
     acc[...] = jnp.zeros_like(acc)
-
-    def take_next(j, carry):
-        arrived(next_r.at[j], several(g_next, 2))
-        keep_split(g_next, j)
-        keep_split(g_next, j + HALF)
-        forward_left(j + HALF).start()
-        near, far = rows_of(g_next, j)[1], rows_of(g_next, j + HALF)[1]
-        left = jnp.concatenate([vhl[g, near, :], vhl[g, far, :]], axis=0)
-        right = jnp.concatenate([vhl[g_next, near, :], vhl[g_next, far, :]], axis=0)
-        acc[...] += dot_t(left, right)
-        return carry
-
-    def take_opp(i, carry):
-        keep_split(g_opp, i)
-        return carry
-
-    lax.fori_loop(0, HALF, take_next, 0)
-    gram_next = quarters(acc[...], WIDTH, WIDTH).reshape(TILES_G, 8, WIDTH)
-    edge = TILES - TILES_G
-    tb[0, TILES_G:] = gram_next[:edge]
-    tb[1, :TILES_G - edge] = gram_next[edge:]
-    arrived(opp_r.at[0], several(g_opp, HALF))
-    lax.fori_loop(0, HALF, take_opp, 0, unroll=True)
-    tb[1, TILES_G - edge:] = gram_half(g_opp, 0).reshape(TILES_G, 8, WIDTH)
-
-    to_core = remote(tb.at[1 - c], r1, p1_s, p1_r, pts=sibling)
-    to_core.start()
-    to_core.wait_recv()
-    s1[...] = tb[c] + r1[...]
-
-    pl.semaphore_wait(word.at[4], 2)
+    acc2[...] = jnp.zeros_like(acc2)
+    place(3, quarters(dot_t(vhl[g], vhl[g]), WIDTH, WIDTH))
+    own_core, own_part = core_sum(LATE, TILES_G, p1_s.at[0], p1_r.at[0])
+    own_core.start()
+
+    for j in range(HALF):
+        for r in (HALF + j, HALF - 1 - j):
+            @pl.when(has_next(r))
+            def _():
+                arrived(next_r.at[r], several(1))
+                keep_split(g_next, r)
+
+            @pl.when(has_prev(r))
+            def _():
+                arrived(prev_r.at[r], several(1))
+                keep_split(g_prev, r)
+
+            @pl.when(between(r))
+            def _():
+                left = jnp.concatenate([vhl[g, rows(r), :], vhl[g_prev, rows(r), :]], axis=1)
+                acc[...] += dot_t(left, vhl[g_next, rows(r), :])
+
+            if r < HALF:
+                @pl.when(turn(r) == 3)
+                def _():
+                    acc[:2 * WIDTH] += dot_t(vhl[g, rows(r), :], vhl[g_next, rows(r), :])
+
+            @pl.when(prev_pair(r))
+            def _():
+                acc2[...] += dot_t(vhl[g_prev, rows(r), :], vhl[g, rows(r), :])
+
+        if j == 1:
+            own_core.wait_recv()
+            s1[own_part] = tb[c, own_part] + r1[own_part]
+            pl.semaphore_wait(word.at[4], 2)
+            scatter_rows(YS - 1)
+
+    place(0, quarters(acc[:2 * WIDTH], WIDTH, WIDTH))
+    place(1, quarters(acc2[...], WIDTH, WIDTH))
+    place(2, quarters(acc[2 * WIDTH:], WIDTH, WIDTH))
+
+    late_core, late_part = core_sum(0, LATE, p1_s.at[1], p1_r.at[1])
+    late_core.start()
+    late_core.wait_recv()
+    s1[late_part] = tb[c, late_part] + r1[late_part]
+
+    for y_to in range(YS - 1):
+        scatter_rows(y_to)
+
+    for r in range(ROW_BLOCKS):
+        @pl.when(jnp.logical_not(goes_left(r)))
+        def _():
+            xcopy(g, r, rest_r.at[0], g_prev).start()
+
+        @pl.when(jnp.logical_not(goes_right(r)))
+        def _():
+            xcopy(g, r, rest_r.at[1], g_next).start()
+
+        @pl.when(between(r))
+        def _():
+            xcopy(g_prev, r, rest_r.at[2], g_next).start()
+            xcopy(g_next, r, rest_r.at[3], g_prev).start()
+
+    sum_tile()
+
     pl.semaphore_wait(word.at[1], 2)
-    def scatter(k):
-        to = lax.min(peer(k), TILES - 1)
-        return remote(s1.at[to], r2.at[here], p2_s, p2_r, pts=device(to))
-
-    def start_scatter(k, carry):
-        @pl.when(peer(k) < TILES)
-        def _():
-            scatter(k).start()
-
-        return carry
-
-    lax.fori_loop(1, PLANE, start_scatter, 0)
-
-    def share(k):
-        ref = gb.at[g, c, lax.min(here, TILES - 1)]
-        return remote(ref, ref, p4_s, p4_r.at[lax.div(lax.min(here, TILES - 1), ZS)], pts=device(peer(k)))
-
-    @pl.when(here < TILES)
-    def _():
-        arrived(p2_r, r2.at[pl.ds(1, PLANE - 1)])
-        r2[here] = s1[lax.min(here, TILES - 1)]
-        gb[g, c, lax.min(here, TILES - 1)] = jnp.sum(r2[...], axis=0)
-
-        def start_share(k, carry):
-            share(k).start()
-            return carry
-
-        lax.fori_loop(1, PLANE, start_share, 0)
-
-
-    def rows_of_set(n):
-        return pl.ds(pl.multiple_of(n * ZS, ZS), ZS)
+
+    def of_set(n):
+        return pl.ds(n * TILES_G, TILES_G)
 
     def x_share(k, n):
-        ref = gb.at[g, c, rows_of_set(n)]
+        ref = gb.at[g, c, of_set(n)]
         return remote(ref, ref, p5_s, p5_r.at[GROUPS - k, n], cols=lax.rem(g + k, GROUPS))
 
     def core_share(k, n):
-        ref = gb.at[lax.rem(g + k, GROUPS), c, rows_of_set(n)]
+        ref = gb.at[lax.rem(g + k, GROUPS), c, of_set(n)]
         return remote(ref, ref, p6_s, p6_r, pts=sibling)
 
-    for n in range(SETS):
+    for n in (3, 0, 1, 2):
         @pl.when(y == n)
         def _():
-            arrived(p4_r.at[n], gb.at[g, c, pl.ds(0, ZS - 1)])
+            arrived(p4_r.at[n], gb.at[g, c, pl.ds(0, TILES_G - 1)])
 
         @pl.when(y != n)
         def _():
-            arrived(p4_r.at[n], gb.at[g, c, pl.ds(0, ZS)])
-
-        for k in range(1, GROUPS):
+            arrived(p4_r.at[n], gb.at[g, c, pl.ds(0, TILES_G)])
+
+        for k in (2, 1, 3):
             x_share(k, n).start()
         core_share(0, n).start()
 
-    arrived(prev_r.at[HALF], several(g_prev, HALF))
-    arrived(opp_r.at[1], several(g_opp, HALF))
-
-    def rest(j, carry):
-        keep_split(g_prev, j)
-        keep_split(g_prev, j + HALF)
-        take_opp(j + HALF, 0)
-        return carry
-
-    lax.fori_loop(0, HALF, rest, 0)
-    for n in range(SETS):
+    arrived(rest_r.at[0], several(3))
+    arrived(rest_r.at[1], several(3))
+    arrived(rest_r.at[2], several(4))
+    arrived(rest_r.at[3], several(4))
+    for r in range(ROW_BLOCKS):
+        keep_split(g_opp, r)
+
+        @pl.when(jnp.logical_not(has_next(r)))
+        def _():
+            keep_split(g_next, r)
+
+        @pl.when(jnp.logical_not(has_prev(r)))
+        def _():
+            keep_split(g_prev, r)
+
+    for n in (3, 0, 1, 2):
         for k in (1, 3, 2):
-            arrived(p5_r.at[k, n], gb.at[lax.rem(g + k, GROUPS), c, rows_of_set(n)])
+            arrived(p5_r.at[k, n], gb.at[g, c, of_set(n)])
             core_share(k, n).start()
     arrived(p6_r, gb.at[:, 1 - c])
 
-    parts = [gb[a].reshape(3 * WIDTH, WIDTH) for a in range(GROUPS)]
-    diag = [parts[a][:WIDTH] for a in range(GROUPS)]
+    def part(a, kind):
+        return jnp.concatenate(
+            [gb[a, core, kind * TILES_G:(kind + 1) * TILES_G].reshape(WIDTH // CORES, WIDTH) for core in range(CORES)], axis=0
+        )
+
+    diag = [part(a, 3) for a in range(GROUPS)]
     down = [lax.rsqrt(jnp.sum(d * eye, axis=1, keepdims=True)) for d in diag]
     across = [lax.rsqrt(jnp.sum(d * eye, axis=0, keepdims=True)) for d in diag]
 
@@ -447,12 +488,12 @@
         scol[a * WIDTH:(a + 1) * WIDTH, :] = jnp.broadcast_to(down[a], (WIDTH, WIDTH))
         put(a, a, diag[a])
         h = (a + 1) % GROUPS
-        block = parts[a][WIDTH:2 * WIDTH]
+        block = part(a, 0) + part(h, 1)
         put(a, h, block)
         put(h, a, block.T)
     for a in range(GROUPS // 2):
         h = a + GROUPS // 2
-        block = parts[a][2 * WIDTH:] + parts[h][2 * WIDTH:].T
+        block = part((a + 1) % GROUPS, 2) + part((a + 3) % GROUPS, 2).T
         put(a, h, block)
         put(h, a, block.T)
 
@@ -520,19 +561,12 @@
     arrived(halo_s.at[0], win.at[0])
     arrived(halo_s.at[1], win.at[2])
     arrived(v_s, vall.at[:3])
-    to_core.wait_send()
+    own_core.wait_send()
+    late_core.wait_send()
+    arrived(p2_s, s1.at[pl.ds(0, TILES - 1)])
+    arrived(p4_s, r2.at[pl.ds(0, PLANE - 1)])
     arrived(p5_s, gb.at[:3, 0])
     arrived(p6_s, gb.at[:, 0])
-
-    @pl.when(here < TILES)
-    def _():
-        arrived(p2_s, s1.at[pl.ds(0, TILES - 1)])
-        arrived(p4_s, r2.at[pl.ds(0, PLANE - 1)])
-
-    @pl.when(here >= TILES)
-    def _():
-        arrived(p2_s, s1)
-
     arrived(f_sem, out)
 
 
@@ -556,6 +590,7 @@
             pltpu.VMEM((ROW_BLOCKS, 2 * BLOCK, SLOTS * BLOCK), BF16),
             pltpu.VMEM((GROUPS, ROWS, WIDTH), F32),
             pltpu.VMEM((GROUPS, ROWS, 2 * WIDTH), BF16),
+            pltpu.VMEM((4 * WIDTH, 2 * WIDTH), F32),
             pltpu.VMEM((2 * WIDTH, 2 * WIDTH), F32),
             pltpu.VMEM((CORES, TILES, 8, WIDTH), F32),
             pltpu.VMEM((TILES, 8, WIDTH), F32),
@@ -581,11 +616,11 @@
             pltpu.SemaphoreType.REGULAR((5,)),
             dma, dma, dma,
             dma((2,)), dma((2, HALF)),
-            dma, dma((HALF,)), dma((HALF + 1,)), dma((2,)),
+            dma, dma((ROW_BLOCKS,)), dma((ROW_BLOCKS,)), dma((4,)),
+            dma((2,)), dma((2,)),
             dma, dma,
-            dma, dma,
-            dma, dma((SETS,)),
-            dma, dma((GROUPS, SETS)),
+            dma, dma((KINDS,)),
+            dma, dma((GROUPS, KINDS)),
             dma, dma,
         ],
         compiler_params=pltpu.CompilerParams(

time: 524 us -> 521 us (level)
  waiting for transfers between devices: 306 us -> 226 us
  starting transfers between devices: 35.2 us -> 114 us
  Pallas kernels: 55.2 us -> 49.4 us
    ppermute x56, waiting for transfers between devices: 300 us -> 220 us  [total(): value = value + lax.ppermute(value, axis, pairs)]
    ppermute x56, starting transfers between devices: 29.2 us -> 109 us  [total(): value = value + lax.ppermute(value, axis, pairs)]
    pallas_call x1, Pallas kernels: 55.2 us -> 49.4 us  [fast(): pl.pallas_call(kernel, out_shape=(jax.ShapeDtypeStruct((ROWS, WIDTH), F32...]
  transfers between devices with their start and end apart: 58 -> 58, of which waited for: 58 -> 57; matrix products, arithmetic and copies ran while one was open for 1% -> 1% of each run, Pallas kernels for 0% -> 0%
where the time goes in v5:
time: 521 us; the launch traced here: 516 us
  waiting for transfers between devices  226 us (43%)
  starting transfers between devices  114 us (22%)
  other arithmetic  93.2 us (18%)
  Pallas kernels  49.4 us (9%)
  matrix products  18.2 us (3%)
  loops' own time  8.33 us (2%)
  local copies, waits for them, and re-layouts  6.85 us (1%)
    ppermute x56, waiting for transfers between devices, total(): value = value + lax.ppermute(value, axis, pairs)  220 us
    ppermute x56, starting transfers between devices, total(): value = value + lax.ppermute(value, axis, pairs)  109 us
    another operation x12, other arithmetic, step(): lower = jnp.linalg.cholesky(gram)  49.8 us
    pallas_call x1, Pallas kernels, fast(): pl.pallas_call(kernel, out_shape=(jax.ShapeDtypeStruct((ROWS, WIDTH), F32...  49.4 us
    another operation x8, other arithmetic, step(): lax.linalg.triangular_solve(lower, local, left_side=False, lower=True, tr...  41.8 us
  transfers between devices with their start and end apart: 58, of which 57 were waited for; matrix products, arithmetic and copies ran while one was open for 1% of the time, Pallas kernels for 0%

profile of v5, /device:TPU:6, one launch (start us, length us, event | category | flops | bytes accessed | tf_op | source)
XLA Modules:
  0.0 516.0 jit_solution(5432233884186100546)
XLA Ops:
  0.0 49.4 %shard_map.48 = (f32[1024,128]{1,0:T(8,128)S(1)}, s32[1,1]{1,0:T(1,128)}) custom-call(f32[1024,128]{1,0:T(8,128)} %start.1, f32[8,8,128,128]{3,2,1,0:T(8,128)} %cov.1, s32[8,8]{1,0:T(8,128)} %col_index.1, s32[4]{0:T(128)} %order.1), custom_call_target="tpu_custom_call" | custom-call | tf_op jit(solution)/shard_map/pallas_call | solution.py:578
  50.1 465.1 %conditional.1 = (f32[1024,128]{1,0:T(8,128)S(1)}) conditional(s32[]{:T(128)} %bitcast.11, (f32[1024,128]{1,0:T(8,128)S(1)}, s32[8,8]{1,0:T(8,128)S(1)}, f32[8,8,128,128]{3,2,1,0:T(8,128)}, s32[4]{0:T(128)S(1)}) %tuple.55, f32[1024,128]{1,0:T(8,128)S(1)} %get-tuple-element.156), branch_computations={%region_0.6_spmd, %region_6.7_spmd} | conditional | flops 2417838080 | bytes 44441020 | solution.py:634
  56.0 6.1 %collective-permute-done.14 = f32[1024,128]{1,0:T(8,128)S(1)} collective-permute-done((f32[1024,128]{1,0:T(8,128)S(1)}, f32[1024,128]{1,0:T(8,128)S(1)}, u32[]{:S(2)}, u32[]{:S(2)}) %collective-permute-start.14) | collective-permute-done | bytes 524320 | tf_op jit(solution)/shard_map/cond/branch_0_fun/ppermute | solution.py:50
  65.0 7.9 %fusion.10 = f32[8,128,128,1]{1,2,3,0:T(8,128)S(1)} fusion(f32[8,8,128,128]{3,2,1,0:T(8,128)} %bitcast.52, f32[8,8,128,128]{3,2,1,0:T(8,128)} %get-tuple-element.150), kind=kOutput, calls=%fused_computation.26 | convolution fusion | flops 1610612736 | bytes 8912896 | tf_op jit(solution)/shard_map/cond/branch_0_fun/rsab,rsbk->rak/dot_general | solution.py:80
  73.1 441.6 %while.14 = (s32[]{:T(128)}, f32[1024,128]{0,1:T(8,128)S(1)}, s32[]{:T(128)}, s32[4]{0:T(128)S(1)}, s32[]{:T(128)}, /*index=5*/s32[]{:T(128)}, u32[]{:T(128)}) while((s32[]{:T(128)}, f32[1024,128]{0,1:T(8,128)S(1)}, s32[]{:T(128)}, s32[4]{0:T(128)S(1)}, s32[]{:T(128)}, /*index=5*/s32[]{:T(128)}, u32[]{:T(128)}) %tuple.48), condition=%wide.region_5.5_spmd, body=%wide.region_2.4_spmd.sunk | while | flops 806436992 | bytes 17696444 | solution.py:98
  104.4 11.7 %cholesky.58 = f32[128,128]{1,0:T(8,128)S(1)} custom-call(f32[128,128]{1,0:T(8,128)S(1)} %fusion.42), custom_call_target="Cholesky" | custom-call | tf_op jit(solution)/shard_map/cond/branch_0_fun/while/body/eval_jaxpr/jit(cholesky)/cholesky | solution.py:87
  117.5 9.8 %custom-call.23 = f32[1,128,128]{1,2,0:T(8,128)S(1)} custom-call(f32[1,128,128]{2,1,0:T(8,128)S(1)} %fusion.43), custom_call_target="InvertDiagBlocksLowerTriangular" | custom-call | tf_op jit(solution)/shard_map/cond/branch_0_fun/while/body/eval_jaxpr/triangular_solve | solution.py:88
  128.9 10.6 %collective-permute-done.6 = f32[1024,128]{0,1:T(8,128)S(1)} collective-permute-done((f32[1024,128]{0,1:T(8,128)S(1)}, f32[1024,128]{0,1:T(8,128)S(1)}, u32[]{:S(2)}, u32[]{:S(2)}) %collective-permute-start.6) | collective-permute-done | bytes 524320 | tf_op jit(solution)/shard_map/cond/branch_0_fun/while/body/eval_jaxpr/ppermute | solution.py:34
  141.6 8.7 %collective-permute-done.7 = f32[1024,128]{0,1:T(8,128)S(1)} collective-permute-done((f32[1024,128]{0,1:T(8,128)S(1)}, f32[1024,128]{0,1:T(8,128)S(1)}, u32[]{:S(2)}, u32[]{:S(2)}) %collective-permute-start.7) | collective-permute-done | bytes 524320 | tf_op jit(solution)/shard_map/cond/branch_0_fun/while/body/eval_jaxpr/ppermute | solution.py:34
  214.7 11.7 %cholesky.58 = f32[128,128]{1,0:T(8,128)S(1)} custom-call(f32[128,128]{1,0:T(8,128)S(1)} %fusion.42), custom_call_target="Cholesky" | custom-call | tf_op jit(solution)/shard_map/cond/branch_0_fun/while/body/eval_jaxpr/jit(cholesky)/cholesky | solution.py:87
  227.8 9.8 %custom-call.23 = f32[1,128,128]{1,2,0:T(8,128)S(1)} custom-call(f32[1,128,128]{2,1,0:T(8,128)S(1)} %fusion.43), custom_call_target="InvertDiagBlocksLowerTriangular" | custom-call | tf_op jit(solution)/shard_map/cond/branch_0_fun/while/body/eval_jaxpr/triangular_solve | solution.py:88
  238.5 9.4 %collective-permute-done.6 = f32[1024,128]{0,1:T(8,128)S(1)} collective-permute-done((f32[1024,128]{0,1:T(8,128)S(1)}, f32[1024,128]{0,1:T(8,128)S(1)}, u32[]{:S(2)}, u32[]{:S(2)}) %collective-permute-start.6) | collective-permute-done | bytes 524320 | tf_op jit(solution)/shard_map/cond/branch_0_fun/while/body/eval_jaxpr/ppermute | solution.py:34
  253.1 8.1 %collective-permute-done.7 = f32[1024,128]{0,1:T(8,128)S(1)} collective-permute-done((f32[1024,128]{0,1:T(8,128)S(1)}, f32[1024,128]{0,1:T(8,128)S(1)}, u32[]{:S(2)}, u32[]{:S(2)}) %collective-permute-start.7) | collective-permute-done | bytes 524320 | tf_op jit(solution)/shard_map/cond/branch_0_fun/while/body/eval_jaxpr/ppermute | solution.py:34
  323.6 11.7 %cholesky.58 = f32[128,128]{1,0:T(8,128)S(1)} custom-call(f32[128,128]{1,0:T(8,128)S(1)} %fusion.42), custom_call_target="Cholesky" | custom-call | tf_op jit(solution)/shard_map/cond/branch_0_fun/while/body/eval_jaxpr/jit(cholesky)/cholesky | solution.py:87
  336.7 9.8 %custom-call.23 = f32[1,128,128]{1,2,0:T(8,128)S(1)} custom-call(f32[1,128,128]{2,1,0:T(8,128)S(1)} %fusion.43), custom_call_target="InvertDiagBlocksLowerTriangular" | custom-call | tf_op jit(solution)/shard_map/cond/branch_0_fun/while/body/eval_jaxpr/triangular_solve | solution.py:88
  349.2 7.7 %collective-permute-done.6 = f32[1024,128]{0,1:T(8,128)S(1)} collective-permute-done((f32[1024,128]{0,1:T(8,128)S(1)}, f32[1024,128]{0,1:T(8,128)S(1)}, u32[]{:S(2)}, u32[]{:S(2)}) %collective-permute-start.6) | collective-permute-done | bytes 524320 | tf_op jit(solution)/shard_map/cond/branch_0_fun/while/body/eval_jaxpr/ppermute | solution.py:34
  357.0 7.1 %collective-permute-start.7 = (f32[1024,128]{0,1:T(8,128)S(1)}, f32[1024,128]{0,1:T(8,128)S(1)}, u32[]{:S(2)}, u32[]{:S(2)}) collective-permute-start(f32[1024,128]{0,1:T(8,128)S(1)} %add.232), channel_id=1, source_target_pairs={{0,2},{1,3},{2,0},{3,1},{4,6},{5,7},{6,4},{7,5},{8,10},{9,11},{10,... | collective-permute-start | bytes 1572872 | tf_op jit(solution)/shard_map/cond/branch_0_fun/while/body/eval_jaxpr/ppermute | solution.py:34
  364.0 7.7 %collective-permute-done.7 = f32[1024,128]{0,1:T(8,128)S(1)} collective-permute-done((f32[1024,128]{0,1:T(8,128)S(1)}, f32[1024,128]{0,1:T(8,128)S(1)}, u32[]{:S(2)}, u32[]{:S(2)}) %collective-permute-start.7) | collective-permute-done | bytes 524320 | tf_op jit(solution)/shard_map/cond/branch_0_fun/while/body/eval_jaxpr/ppermute | solution.py:34
  410.3 5.8 %collective-permute-done.2 = f32[128,128]{0,1:T(8,128)S(1)} collective-permute-done((f32[128,128]{0,1:T(8,128)S(1)}, f32[128,128]{0,1:T(8,128)S(1)}, u32[]{:S(2)}, u32[]{:S(2)}) %collective-permute-start.2) | collective-permute-done | bytes 65568 | tf_op jit(solution)/shard_map/cond/branch_0_fun/while/body/eval_jaxpr/ppermute | solution.py:34
  434.7 11.7 %cholesky.58 = f32[128,128]{1,0:T(8,128)S(1)} custom-call(f32[128,128]{1,0:T(8,128)S(1)} %fusion.42), custom_call_target="Cholesky" | custom-call | tf_op jit(solution)/shard_map/cond/branch_0_fun/while/body/eval_jaxpr/jit(cholesky)/cholesky | solution.py:87
  447.8 9.8 %custom-call.23 = f32[1,128,128]{1,2,0:T(8,128)S(1)} custom-call(f32[1,128,128]{2,1,0:T(8,128)S(1)} %fusion.43), custom_call_target="InvertDiagBlocksLowerTriangular" | custom-call | tf_op jit(solution)/shard_map/cond/branch_0_fun/while/body/eval_jaxpr/triangular_solve | solution.py:88
  460.2 7.6 %collective-permute-done.6 = f32[1024,128]{0,1:T(8,128)S(1)} collective-permute-done((f32[1024,128]{0,1:T(8,128)S(1)}, f32[1024,128]{0,1:T(8,128)S(1)}, u32[]{:S(2)}, u32[]{:S(2)}) %collective-permute-start.6) | collective-permute-done | bytes 524320 | tf_op jit(solution)/shard_map/cond/branch_0_fun/while/body/eval_jaxpr/ppermute | solution.py:34
  467.9 8.2 %collective-permute-start.7 = (f32[1024,128]{0,1:T(8,128)S(1)}, f32[1024,128]{0,1:T(8,128)S(1)}, u32[]{:S(2)}, u32[]{:S(2)}) collective-permute-start(f32[1024,128]{0,1:T(8,128)S(1)} %add.232), channel_id=1, source_target_pairs={{0,2},{1,3},{2,0},{3,1},{4,6},{5,7},{6,4},{7,5},{8,10},{9,11},{10,... | collective-permute-start | bytes 1572872 | tf_op jit(solution)/shard_map/cond/branch_0_fun/while/body/eval_jaxpr/ppermute | solution.py:34
  476.1 7.2 %collective-permute-done.7 = f32[1024,128]{0,1:T(8,128)S(1)} collective-permute-done((f32[1024,128]{0,1:T(8,128)S(1)}, f32[1024,128]{0,1:T(8,128)S(1)}, u32[]{:S(2)}, u32[]{:S(2)}) %collective-permute-start.7) | collective-permute-done | bytes 524320 | tf_op jit(solution)/shard_map/cond/branch_0_fun/while/body/eval_jaxpr/ppermute | solution.py:34
  (211 shorter events, 269.5 us)
Async XLA Ops:
  50.1 12.0 %collective-permute-start.14 = (f32[1024,128]{1,0:T(8,128)S(1)}, f32[1024,128]{1,0:T(8,128)S(1)}, u32[]{:S(2)}, u32[]{:S(2)}) collective-permute-start(f32[1024,128]{1,0:T(8,128)S(1)} %get-tuple-element.148), channel_id=1, source_target_pairs={{0,4},{4,8},{8,12},{12,16},{16,20},{20,24},{24,28},{28,32},{32,36}... | collective-permute-start | bytes 1572872 | tf_op jit(solution)/shard_map/cond/branch_0_fun/ppermute | solution.py:50
  51.5 10.6 %collective-permute-start.15 = (f32[1024,128]{1,0:T(8,128)S(1)}, f32[1024,128]{1,0:T(8,128)S(1)}, u32[]{:S(2)}, u32[]{:S(2)}) collective-permute-start(f32[1024,128]{1,0:T(8,128)S(1)} %get-tuple-element.148), channel_id=1, source_target_pairs={{4,0},{8,4},{12,8},{16,12},{20,16},{24,20},{28,24},{32,28},{36,32}... | collective-permute-start | bytes 1572872 | tf_op jit(solution)/shard_map/cond/branch_0_fun/ppermute | solution.py:52
  85.0 9.0 %collective-permute-start.3 = (f32[128,128]{0,1:T(8,128)S(1)}, f32[128,128]{0,1:T(8,128)S(1)}, u32[]{:S(2)}, u32[]{:S(2)}) collective-permute-start(f32[128,128]{0,1:T(8,128)S(1)} %add.228), channel_id=1, source_target_pairs={{0,32},{4,36},{8,40},{12,44},{16,48},{20,52},{24,56},{28,60},{32,0... | collective-permute-start | bytes 196616 | tf_op jit(solution)/shard_map/cond/branch_0_fun/while/body/eval_jaxpr/ppermute | solution.py:34
  127.9 11.6 %collective-permute-start.6 = (f32[1024,128]{0,1:T(8,128)S(1)}, f32[1024,128]{0,1:T(8,128)S(1)}, u32[]{:S(2)}, u32[]{:S(2)}) collective-permute-start(f32[1024,128]{0,1:T(8,128)S(1)} %fusion.44), channel_id=1, source_target_pairs={{0,1},{1,0},{2,3},{3,2},{4,5},{5,4},{6,7},{7,6},{8,9},{9,8},{10,11... | collective-permute-start | bytes 1572872 | tf_op jit(solution)/shard_map/cond/branch_0_fun/while/body/eval_jaxpr/ppermute | solution.py:34
  139.6 10.8 %collective-permute-start.7 = (f32[1024,128]{0,1:T(8,128)S(1)}, f32[1024,128]{0,1:T(8,128)S(1)}, u32[]{:S(2)}, u32[]{:S(2)}) collective-permute-start(f32[1024,128]{0,1:T(8,128)S(1)} %add.232), channel_id=1, source_target_pairs={{0,2},{1,3},{2,0},{3,1},{4,6},{5,7},{6,4},{7,5},{8,10},{9,11},{10,... | collective-permute-start | bytes 1572872 | tf_op jit(solution)/shard_map/cond/branch_0_fun/while/body/eval_jaxpr/ppermute | solution.py:34
  156.7 6.0 %collective-permute-start.10 = (f32[128,128]{1,0:T(8,128)S(1)}, f32[128,128]{1,0:T(8,128)S(1)}, u32[]{:S(2)}, u32[]{:S(2)}) collective-permute-start(f32[128,128]{1,0:T(8,128)S(1)} %add.235), channel_id=1, source_target_pairs={{0,16},{4,20},{8,24},{12,28},{16,0},{20,4},{24,8},{28,12},{32,48},... | collective-permute-start | bytes 196616 | tf_op jit(solution)/shard_map/cond/branch_0_fun/while/body/eval_jaxpr/ppermute | solution.py:34
  162.7 8.5 %collective-permute-start.11 = (f32[128,128]{1,0:T(8,128)S(1)}, f32[128,128]{1,0:T(8,128)S(1)}, u32[]{:S(2)}, u32[]{:S(2)}) collective-permute-start(f32[128,128]{1,0:T(8,128)S(1)} %add.236), channel_id=1, source_target_pairs={{0,32},{4,36},{8,40},{12,44},{16,48},{20,52},{24,56},{28,60},{32,0... | collective-permute-start | bytes 196616 | tf_op jit(solution)/shard_map/cond/branch_0_fun/while/body/eval_jaxpr/ppermute | solution.py:34
  195.5 8.3 %collective-permute-start.3 = (f32[128,128]{0,1:T(8,128)S(1)}, f32[128,128]{0,1:T(8,128)S(1)}, u32[]{:S(2)}, u32[]{:S(2)}) collective-permute-start(f32[128,128]{0,1:T(8,128)S(1)} %add.228), channel_id=1, source_target_pairs={{0,32},{4,36},{8,40},{12,44},{16,48},{20,52},{24,56},{28,60},{32,0... | collective-permute-start | bytes 196616 | tf_op jit(solution)/shard_map/cond/branch_0_fun/while/body/eval_jaxpr/ppermute | solution.py:34
  238.2 9.7 %collective-permute-start.6 = (f32[1024,128]{0,1:T(8,128)S(1)}, f32[1024,128]{0,1:T(8,128)S(1)}, u32[]{:S(2)}, u32[]{:S(2)}) collective-permute-start(f32[1024,128]{0,1:T(8,128)S(1)} %fusion.44), channel_id=1, source_target_pairs={{0,1},{1,0},{2,3},{3,2},{4,5},{5,4},{6,7},{7,6},{8,9},{9,8},{10,11... | collective-permute-start | bytes 1572872 | tf_op jit(solution)/shard_map/cond/branch_0_fun/while/body/eval_jaxpr/ppermute | solution.py:34
  248.0 13.2 %collective-permute-start.7 = (f32[1024,128]{0,1:T(8,128)S(1)}, f32[1024,128]{0,1:T(8,128)S(1)}, u32[]{:S(2)}, u32[]{:S(2)}) collective-permute-start(f32[1024,128]{0,1:T(8,128)S(1)} %add.232), channel_id=1, source_target_pairs={{0,2},{1,3},{2,0},{3,1},{4,6},{5,7},{6,4},{7,5},{8,10},{9,11},{10,... | collective-permute-start | bytes 1572872 | tf_op jit(solution)/shard_map/cond/branch_0_fun/while/body/eval_jaxpr/ppermute | solution.py:34
  273.2 8.3 %collective-permute-start.11 = (f32[128,128]{1,0:T(8,128)S(1)}, f32[128,128]{1,0:T(8,128)S(1)}, u32[]{:S(2)}, u32[]{:S(2)}) collective-permute-start(f32[128,128]{1,0:T(8,128)S(1)} %add.236), channel_id=1, source_target_pairs={{0,32},{4,36},{8,40},{12,44},{16,48},{20,52},{24,56},{28,60},{32,0... | collective-permute-start | bytes 196616 | tf_op jit(solution)/shard_map/cond/branch_0_fun/while/body/eval_jaxpr/ppermute | solution.py:34
  285.8 6.4 %collective-permute-start.13 = (f32[128,128]{1,0:T(8,128)S(1)}, f32[128,128]{1,0:T(8,128)S(1)}, u32[]{:S(2)}, u32[]{:S(2)}) collective-permute-start(f32[128,128]{1,0:T(8,128)S(1)} %add.238), channel_id=1, source_target_pairs={{0,128},{4,132},{8,136},{12,140},{16,144},{20,148},{24,152},{28,15... | collective-permute-start | bytes 196616 | tf_op jit(solution)/shard_map/cond/branch_0_fun/while/body/eval_jaxpr/ppermute | solution.py:34
  304.9 8.3 %collective-permute-start.3 = (f32[128,128]{0,1:T(8,128)S(1)}, f32[128,128]{0,1:T(8,128)S(1)}, u32[]{:S(2)}, u32[]{:S(2)}) collective-permute-start(f32[128,128]{0,1:T(8,128)S(1)} %add.228), channel_id=1, source_target_pairs={{0,32},{4,36},{8,40},{12,44},{16,48},{20,52},{24,56},{28,60},{32,0... | collective-permute-start | bytes 196616 | tf_op jit(solution)/shard_map/cond/branch_0_fun/while/body/eval_jaxpr/ppermute | solution.py:34
  317.5 6.0 %collective-permute-start.5 = (f32[128,128]{0,1:T(8,128)S(1)}, f32[128,128]{0,1:T(8,128)S(1)}, u32[]{:S(2)}, u32[]{:S(2)}) collective-permute-start(f32[128,128]{0,1:T(8,128)S(1)} %add.230), channel_id=1, source_target_pairs={{0,128},{4,132},{8,136},{12,140},{16,144},{20,148},{24,152},{28,15... | collective-permute-start | bytes 196616 | tf_op jit(solution)/shard_map/cond/branch_0_fun/while/body/eval_jaxpr/ppermute | solution.py:34
  347.2 9.7 %collective-permute-start.6 = (f32[1024,128]{0,1:T(8,128)S(1)}, f32[1024,128]{0,1:T(8,128)S(1)}, u32[]{:S(2)}, u32[]{:S(2)}) collective-permute-start(f32[1024,128]{0,1:T(8,128)S(1)} %fusion.44), channel_id=1, source_target_pairs={{0,1},{1,0},{2,3},{3,2},{4,5},{5,4},{6,7},{7,6},{8,9},{9,8},{10,11... | collective-permute-start | bytes 1572872 | tf_op jit(solution)/shard_map/cond/branch_0_fun/while/body/eval_jaxpr/ppermute | solution.py:34
  357.0 14.8 %collective-permute-start.7 = (f32[1024,128]{0,1:T(8,128)S(1)}, f32[1024,128]{0,1:T(8,128)S(1)}, u32[]{:S(2)}, u32[]{:S(2)}) collective-permute-start(f32[1024,128]{0,1:T(8,128)S(1)} %add.232), channel_id=1, source_target_pairs={{0,2},{1,3},{2,0},{3,1},{4,6},{5,7},{6,4},{7,5},{8,10},{9,11},{10,... | collective-permute-start | bytes 1572872 | tf_op jit(solution)/shard_map/cond/branch_0_fun/while/body/eval_jaxpr/ppermute | solution.py:34
  383.4 8.3 %collective-permute-start.11 = (f32[128,128]{1,0:T(8,128)S(1)}, f32[128,128]{1,0:T(8,128)S(1)}, u32[]{:S(2)}, u32[]{:S(2)}) collective-permute-start(f32[128,128]{1,0:T(8,128)S(1)} %add.236), channel_id=1, source_target_pairs={{0,32},{4,36},{8,40},{12,44},{16,48},{20,52},{24,56},{28,60},{32,0... | collective-permute-start | bytes 196616 | tf_op jit(solution)/shard_map/cond/branch_0_fun/while/body/eval_jaxpr/ppermute | solution.py:34
  396.0 7.0 %collective-permute-start.13 = (f32[128,128]{1,0:T(8,128)S(1)}, f32[128,128]{1,0:T(8,128)S(1)}, u32[]{:S(2)}, u32[]{:S(2)}) collective-permute-start(f32[128,128]{1,0:T(8,128)S(1)} %add.238), channel_id=1, source_target_pairs={{0,128},{4,132},{8,136},{12,140},{16,144},{20,148},{24,152},{28,15... | collective-permute-start | bytes 196616 | tf_op jit(solution)/shard_map/cond/branch_0_fun/while/body/eval_jaxpr/ppermute | solution.py:34
  410.1 6.0 %collective-permute-start.2 = (f32[128,128]{0,1:T(8,128)S(1)}, f32[128,128]{0,1:T(8,128)S(1)}, u32[]{:S(2)}, u32[]{:S(2)}) collective-permute-start(f32[128,128]{0,1:T(8,128)S(1)} %add.227), channel_id=1, source_target_pairs={{0,16},{4,20},{8,24},{12,28},{16,0},{20,4},{24,8},{28,12},{32,48},... | collective-permute-start | bytes 196616 | tf_op jit(solution)/shard_map/cond/branch_0_fun/while/body/eval_jaxpr/ppermute | solution.py:34
  416.1 8.3 %collective-permute-start.3 = (f32[128,128]{0,1:T(8,128)S(1)}, f32[128,128]{0,1:T(8,128)S(1)}, u32[]{:S(2)}, u32[]{:S(2)}) collective-permute-start(f32[128,128]{0,1:T(8,128)S(1)} %add.228), channel_id=1, source_target_pairs={{0,32},{4,36},{8,40},{12,44},{16,48},{20,52},{24,56},{28,60},{32,0... | collective-permute-start | bytes 196616 | tf_op jit(solution)/shard_map/cond/branch_0_fun/while/body/eval_jaxpr/ppermute | solution.py:34
  458.3 9.6 %collective-permute-start.6 = (f32[1024,128]{0,1:T(8,128)S(1)}, f32[1024,128]{0,1:T(8,128)S(1)}, u32[]{:S(2)}, u32[]{:S(2)}) collective-permute-start(f32[1024,128]{0,1:T(8,128)S(1)} %fusion.44), channel_id=1, source_target_pairs={{0,1},{1,0},{2,3},{3,2},{4,5},{5,4},{6,7},{7,6},{8,9},{9,8},{10,11... | collective-permute-start | bytes 1572872 | tf_op jit(solution)/shard_map/cond/branch_0_fun/while/body/eval_jaxpr/ppermute | solution.py:34
  467.9 15.3 %collective-permute-start.7 = (f32[1024,128]{0,1:T(8,128)S(1)}, f32[1024,128]{0,1:T(8,128)S(1)}, u32[]{:S(2)}, u32[]{:S(2)}) collective-permute-start(f32[1024,128]{0,1:T(8,128)S(1)} %add.232), channel_id=1, source_target_pairs={{0,2},{1,3},{2,0},{3,1},{4,6},{5,7},{6,4},{7,5},{8,10},{9,11},{10,... | collective-permute-start | bytes 1572872 | tf_op jit(solution)/shard_map/cond/branch_0_fun/while/body/eval_jaxpr/ppermute | solution.py:34
  495.2 8.3 %collective-permute-start.11 = (f32[128,128]{1,0:T(8,128)S(1)}, f32[128,128]{1,0:T(8,128)S(1)}, u32[]{:S(2)}, u32[]{:S(2)}) collective-permute-start(f32[128,128]{1,0:T(8,128)S(1)} %add.236), channel_id=1, source_target_pairs={{0,32},{4,36},{8,40},{12,44},{16,48},{20,52},{24,56},{28,60},{32,0... | collective-permute-start | bytes 196616 | tf_op jit(solution)/shard_map/cond/branch_0_fun/while/body/eval_jaxpr/ppermute | solution.py:34
  507.9 6.1 %collective-permute-start.13 = (f32[128,128]{1,0:T(8,128)S(1)}, f32[128,128]{1,0:T(8,128)S(1)}, u32[]{:S(2)}, u32[]{:S(2)}) collective-permute-start(f32[128,128]{1,0:T(8,128)S(1)} %add.238), channel_id=1, source_target_pairs={{0,128},{4,132},{8,136},{12,140},{16,144},{20,148},{24,152},{28,15... | collective-permute-start | bytes 196616 | tf_op jit(solution)/shard_map/cond/branch_0_fun/while/body/eval_jaxpr/ppermute | solution.py:34
  (37 other events, 289.2 us)

commit v6 on v5

--- a/solution.py
+++ b/solution.py
@@ -116,10 +116,11 @@
 
 
 def kernel(
-    start, cov, col_index, order, out, small,
+    start, cov, col_in, order_in, out, small,
+    col_index, order,
     win, win_hl, covv, cov_hl, vall, vhl, acc, acc2, tb, r1, s1, r2, gb,
-    e0, w, b, u, mk, e0_h, e0_l, w_h, w2_h, w_l, b_h, b_l, u_h, x_hl, res, scol,
-    word, c_sem, l_sem, f_sem,
+    e0, w, b, u, mk, e0_h, e0_l, w_h, w2_h, w_l, b_h, b_l, u_h, w_by, u_by, x_hl, res, scol,
+    word, i_sem, c_sem, l_sem,
     halo_s, halo_r, v_s, next_r, prev_r, rest_r,
     p1_s, p1_r, p2_s, p2_r, p4_s, p4_r, p5_s, p5_r, p6_s, p6_r,
 ):
@@ -151,6 +152,10 @@
     cov_copy = pltpu.make_async_copy(cov, covv, c_sem)
     own_copy = pltpu.make_async_copy(start, win.at[1], l_sem)
     own_copy.start()
+    col_copy = pltpu.make_async_copy(col_in, col_index, i_sem.at[0])
+    col_copy.start()
+    order_copy = pltpu.make_async_copy(order_in, order, i_sem.at[1])
+    order_copy.start()
 
     cov_copy.start()
 
@@ -187,6 +192,8 @@
         to_after(k).start()
         to_before(k).start()
 
+    col_copy.wait()
+    order_copy.wait()
     ranks = []
     for a in range(GROUPS):
         rank = jnp.int32(0)
@@ -439,6 +446,10 @@
             x_share(k, n).start()
         core_share(0, n).start()
 
+    for n in (3, 0, 1, 2):
+        for k in (1, 3, 2):
+            arrived(p5_r.at[k, n], gb.at[g, c, of_set(n)])
+            core_share(k, n).start()
     arrived(rest_r.at[0], several(3))
     arrived(rest_r.at[1], several(3))
     arrived(rest_r.at[2], several(4))
@@ -454,10 +465,6 @@
         def _():
             keep_split(g_prev, r)
 
-    for n in (3, 0, 1, 2):
-        for k in (1, 3, 2):
-            arrived(p5_r.at[k, n], gb.at[g, c, of_set(n)])
-            core_share(k, n).start()
     arrived(p6_r, gb.at[:, 1 - c])
 
     def part(a, kind):
@@ -518,45 +525,46 @@
             across_id = lax.broadcasted_iota(jnp.int32, (COLS, COLS // 2), 1) + n * COLS // 2
             own = jnp.where(down_id == across_id, w[:, cols], 0.0)
             value = mk[:, cols] * ((b[:, cols] + own) + prod)
-            u[:, cols] = value
-            u_h[:, cols] = value.astype(BF16)
+            if fine:
+                for k in range(2):
+                    u_by[2 * n + k] = value[:, k * WIDTH:(k + 1) * WIDTH]
+            else:
+                u[:, cols] = value
+                u_h[:, cols] = value.astype(BF16)
             if fine:
                 res[...] += jnp.sum((value * value).reshape(COLS // 8, 8, COLS // 2), axis=0)
+        if fine:
+            return
         for n in range(2):
             cols = slice(n * COLS // 2, (n + 1) * COLS // 2)
             value = (w[:, cols] - u[:, cols]) - dot(w_h[...], u_h[:, cols])
             w[:, cols] = value
-            if not fine:
-                high, low = split(value)
-                next_h[:, cols] = high
-                w_l[:, cols] = low
+            for k in range(2):
+                w_by[2 * n + k] = value[:, k * WIDTH:(k + 1) * WIDTH]
+            high, low = split(value)
+            next_h[:, cols] = high
+            w_l[:, cols] = low
 
     res[...] = jnp.zeros_like(res)
     newton(w_h, w2_h, False)
     newton(w2_h, None, True)
     small[0, 0] = jnp.where(jnp.sum(res[...]) < TOLERANCE, 1, 0).astype(jnp.int32)
 
-    mine = pl.ds(pl.multiple_of(g * WIDTH, WIDTH), WIDTH)
+    step = u_by[g]
+    inverse = (w_by[g] - step) - dot(w2_h[...], step.astype(BF16))
     for a in range(GROUPS):
-        rows = slice(a * WIDTH, (a + 1) * WIDTH)
+        rows_a = slice(a * WIDTH, (a + 1) * WIDTH)
         same = jnp.where(g == a, 1.0, 0.0).astype(F32)
-        high, low = split(scol[rows, :] * (w[rows, mine] + same * eye))
-        x_hl[rows, :WIDTH] = high
-        x_hl[rows, WIDTH:] = low
-
-    outv = win
-
-    def result(k):
-        rows = slice(k * 2 * BLOCK, (k + 1) * 2 * BLOCK)
-        return pltpu.make_async_copy(outv.at[1, rows, :], out.at[rows, :], f_sem)
+        high, low = split(scol[rows_a, :] * (inverse[rows_a] + same * eye))
+        x_hl[rows_a, :WIDTH] = high
+        x_hl[rows_a, WIDTH:] = low
 
     for k in range(ROW_BLOCKS // 2):
-        rows = slice(k * 2 * BLOCK, (k + 1) * 2 * BLOCK)
-        high = jnp.concatenate([vhl[h, rows, :WIDTH] for h in range(GROUPS)], axis=1)
-        low = jnp.concatenate([vhl[h, rows, WIDTH:] for h in range(GROUPS)], axis=1)
+        rows_k = slice(k * 2 * BLOCK, (k + 1) * 2 * BLOCK)
+        high = jnp.concatenate([vhl[h, rows_k, :WIDTH] for h in range(GROUPS)], axis=1)
+        low = jnp.concatenate([vhl[h, rows_k, WIDTH:] for h in range(GROUPS)], axis=1)
         q = dot(jnp.concatenate([high, low], axis=0), x_hl[...])
-        outv[1, rows, :] = quarters(q, 2 * BLOCK, WIDTH)
-        result(k).start()
+        out[rows_k, :] = quarters(q, 2 * BLOCK, WIDTH)
 
     arrived(halo_s.at[0], win.at[0])
     arrived(halo_s.at[1], win.at[2])
@@ -567,7 +575,6 @@
     arrived(p4_s, r2.at[pl.ds(0, PLANE - 1)])
     arrived(p5_s, gb.at[:3, 0])
     arrived(p6_s, gb.at[:, 0])
-    arrived(f_sem, out)
 
 
 def fast(start, cov_blocks, col_index, order):
@@ -578,12 +585,14 @@
     return pl.pallas_call(
         kernel,
         out_shape=(
-            jax.ShapeDtypeStruct((ROWS, WIDTH), F32),
-            jax.ShapeDtypeStruct((1, 1), jnp.int32),
+            pltpu.VMEM((ROWS, WIDTH), F32),
+            pltpu.SMEM((1, 1), jnp.int32),
         ),
-        in_specs=[hbm, hbm, smem, smem],
-        out_specs=(hbm, smem),
+        in_specs=[hbm, hbm, hbm, hbm],
+        out_specs=(pl.BlockSpec(memory_space=pltpu.VMEM), smem),
         scratch_shapes=[
+            pltpu.SMEM((ROW_BLOCKS, SLOTS), jnp.int32),
+            pltpu.SMEM((GROUPS,), jnp.int32),
             pltpu.VMEM((3, ROWS, WIDTH), F32),
             pltpu.VMEM((3 * ROW_BLOCKS, BLOCK, 2 * WIDTH), BF16),
             pltpu.VMEM((ROW_BLOCKS, SLOTS, BLOCK, BLOCK), F32),
@@ -610,11 +619,14 @@
             pltpu.VMEM(square, BF16),
             pltpu.VMEM(square, BF16),
             pltpu.VMEM(square, BF16),
+            pltpu.VMEM((GROUPS, COLS, WIDTH), F32),
+            pltpu.VMEM((GROUPS, COLS, WIDTH), F32),
             pltpu.VMEM((COLS, 2 * WIDTH), BF16),
             pltpu.VMEM((8, COLS // 2), F32),
             pltpu.VMEM((COLS, WIDTH), F32),
             pltpu.SemaphoreType.REGULAR((5,)),
-            dma, dma, dma,
+            dma((2,)),
+            dma, dma,
             dma((2,)), dma((2, HALF)),
             dma, dma((ROW_BLOCKS,)), dma((ROW_BLOCKS,)), dma((4,)),
             dma((2,)), dma((2,)),

time: 521 us -> 519 us (level)
  waiting for transfers between devices: 226 us -> 247 us
  starting transfers between devices: 114 us -> 95.8 us
    ppermute x56, waiting for transfers between devices: 220 us -> 240 us  [total(): value = value + lax.ppermute(value, axis, pairs)]
    ppermute x56, starting transfers between devices: 109 us -> 90.6 us  [total(): value = value + lax.ppermute(value, axis, pairs)]
where the time goes in v6:
time: 519 us; the launch traced here: 515 us
  waiting for transfers between devices  247 us (48%)
  starting transfers between devices  95.8 us (18%)
  other arithmetic  93.3 us (18%)
  Pallas kernels  46.3 us (9%)
  matrix products  18.2 us (4%)
  loops' own time  8.37 us (2%)
  local copies, waits for them, and re-layouts  6.85 us (1%)
    ppermute x56, waiting for transfers between devices, total(): value = value + lax.ppermute(value, axis, pairs)  240 us
    ppermute x56, starting transfers between devices, total(): value = value + lax.ppermute(value, axis, pairs)  90.6 us
    another operation x12, other arithmetic, step(): lower = jnp.linalg.cholesky(gram)  49.8 us
    pallas_call x1, Pallas kernels, fast(): pl.pallas_call(kernel, out_shape=(pltpu.VMEM((ROWS, WIDTH), F32), pltpu.S...  46.3 us
    another operation x8, other arithmetic, step(): lax.linalg.triangular_solve(lower, local, left_side=False, lower=True, tr...  41.8 us
  transfers between devices with their start and end apart: 58, of which 57 were waited for; matrix products, arithmetic and copies ran while one was open for 1% of the time, Pallas kernels for 0%

profile of v6, /device:TPU:6, one launch (start us, length us, event | category | flops | bytes accessed | tf_op | source)
XLA Modules:
  0.0 515.5 jit_solution(11060817477796260897)
XLA Ops:
  0.0 46.3 %shard_map.48 = (f32[1024,128]{1,0:T(8,128)S(1)}, s32[1,1]{1,0:T(1,128)S(4)}) custom-call(f32[1024,128]{1,0:T(8,128)} %start.1, f32[8,8,128,128]{3,2,1,0:T(8,128)} %cov.1, s32[8,8]{1,0:T(8,128)} %col_in.1, s32[4]{0:T(128)} %order_in.1), custom_call_target="tpu_custom_call" | custom-call | tf_op jit(solution)/shard_map/pallas_call | solution.py:585
  46.4 468.3 %conditional.1 = (f32[1024,128]{1,0:T(8,128)S(1)}) conditional(s32[]{:T(128)} %bitcast.11, (f32[1024,128]{1,0:T(8,128)S(1)}, s32[8,8]{1,0:T(8,128)S(1)}, f32[8,8,128,128]{3,2,1,0:T(8,128)}, s32[4]{0:T(128)S(1)}) %tuple.55, f32[1024,128]{1,0:T(8,128)S(1)} %get-tuple-element.156), branch_computations={%region_0.6_spmd, %region_6.7_spmd} | conditional | flops 2417838080 | bytes 44441020 | solution.py:646
  61.3 7.9 %fusion.10 = f32[8,128,128,1]{1,2,3,0:T(8,128)S(1)} fusion(f32[8,8,128,128]{3,2,1,0:T(8,128)} %bitcast.52, f32[8,8,128,128]{3,2,1,0:T(8,128)} %get-tuple-element.150), kind=kOutput, calls=%fused_computation.26 | convolution fusion | flops 1610612736 | bytes 8912896 | tf_op jit(solution)/shard_map/cond/branch_0_fun/rsab,rsbk->rak/dot_general | solution.py:80
  69.4 444.9 %while.14 = (s32[]{:T(128)}, f32[1024,128]{0,1:T(8,128)S(1)}, s32[]{:T(128)}, s32[4]{0:T(128)S(1)}, s32[]{:T(128)}, /*index=5*/s32[]{:T(128)}, u32[]{:T(128)}) while((s32[]{:T(128)}, f32[1024,128]{0,1:T(8,128)S(1)}, s32[]{:T(128)}, s32[4]{0:T(128)S(1)}, s32[]{:T(128)}, /*index=5*/s32[]{:T(128)}, u32[]{:T(128)}) %tuple.48), condition=%wide.region_5.5_spmd, body=%wide.region_2.4_spmd.sunk | while | flops 806436992 | bytes 17696444 | solution.py:98
  100.6 11.7 %cholesky.58 = f32[128,128]{1,0:T(8,128)S(1)} custom-call(f32[128,128]{1,0:T(8,128)S(1)} %fusion.42), custom_call_target="Cholesky" | custom-call | tf_op jit(solution)/shard_map/cond/branch_0_fun/while/body/eval_jaxpr/jit(cholesky)/cholesky | solution.py:87
  113.7 9.8 %custom-call.23 = f32[1,128,128]{1,2,0:T(8,128)S(1)} custom-call(f32[1,128,128]{2,1,0:T(8,128)S(1)} %fusion.43), custom_call_target="InvertDiagBlocksLowerTriangular" | custom-call | tf_op jit(solution)/shard_map/cond/branch_0_fun/while/body/eval_jaxpr/triangular_solve | solution.py:88
  124.9 11.1 %collective-permute-done.6 = f32[1024,128]{0,1:T(8,128)S(1)} collective-permute-done((f32[1024,128]{0,1:T(8,128)S(1)}, f32[1024,128]{0,1:T(8,128)S(1)}, u32[]{:S(2)}, u32[]{:S(2)}) %collective-permute-start.6) | collective-permute-done | bytes 524320 | tf_op jit(solution)/shard_map/cond/branch_0_fun/while/body/eval_jaxpr/ppermute | solution.py:34
  137.9 8.9 %collective-permute-done.7 = f32[1024,128]{0,1:T(8,128)S(1)} collective-permute-done((f32[1024,128]{0,1:T(8,128)S(1)}, f32[1024,128]{0,1:T(8,128)S(1)}, u32[]{:S(2)}, u32[]{:S(2)}) %collective-permute-start.7) | collective-permute-done | bytes 524320 | tf_op jit(solution)/shard_map/cond/branch_0_fun/while/body/eval_jaxpr/ppermute | solution.py:34
  210.9 11.7 %cholesky.58 = f32[128,128]{1,0:T(8,128)S(1)} custom-call(f32[128,128]{1,0:T(8,128)S(1)} %fusion.42), custom_call_target="Cholesky" | custom-call | tf_op jit(solution)/shard_map/cond/branch_0_fun/while/body/eval_jaxpr/jit(cholesky)/cholesky | solution.py:87
  224.0 9.8 %custom-call.23 = f32[1,128,128]{1,2,0:T(8,128)S(1)} custom-call(f32[1,128,128]{2,1,0:T(8,128)S(1)} %fusion.43), custom_call_target="InvertDiagBlocksLowerTriangular" | custom-call | tf_op jit(solution)/shard_map/cond/branch_0_fun/while/body/eval_jaxpr/triangular_solve | solution.py:88
  234.6 11.8 %collective-permute-done.6 = f32[1024,128]{0,1:T(8,128)S(1)} collective-permute-done((f32[1024,128]{0,1:T(8,128)S(1)}, f32[1024,128]{0,1:T(8,128)S(1)}, u32[]{:S(2)}, u32[]{:S(2)}) %collective-permute-start.6) | collective-permute-done | bytes 524320 | tf_op jit(solution)/shard_map/cond/branch_0_fun/while/body/eval_jaxpr/ppermute | solution.py:34
  249.0 8.2 %collective-permute-done.7 = f32[1024,128]{0,1:T(8,128)S(1)} collective-permute-done((f32[1024,128]{0,1:T(8,128)S(1)}, f32[1024,128]{0,1:T(8,128)S(1)}, u32[]{:S(2)}, u32[]{:S(2)}) %collective-permute-start.7) | collective-permute-done | bytes 524320 | tf_op jit(solution)/shard_map/cond/branch_0_fun/while/body/eval_jaxpr/ppermute | solution.py:34
  320.2 11.7 %cholesky.58 = f32[128,128]{1,0:T(8,128)S(1)} custom-call(f32[128,128]{1,0:T(8,128)S(1)} %fusion.42), custom_call_target="Cholesky" | custom-call | tf_op jit(solution)/shard_map/cond/branch_0_fun/while/body/eval_jaxpr/jit(cholesky)/cholesky | solution.py:87
  333.3 9.8 %custom-call.23 = f32[1,128,128]{1,2,0:T(8,128)S(1)} custom-call(f32[1,128,128]{2,1,0:T(8,128)S(1)} %fusion.43), custom_call_target="InvertDiagBlocksLowerTriangular" | custom-call | tf_op jit(solution)/shard_map/cond/branch_0_fun/while/body/eval_jaxpr/triangular_solve | solution.py:88
  345.2 8.1 %collective-permute-done.6 = f32[1024,128]{0,1:T(8,128)S(1)} collective-permute-done((f32[1024,128]{0,1:T(8,128)S(1)}, f32[1024,128]{0,1:T(8,128)S(1)}, u32[]{:S(2)}, u32[]{:S(2)}) %collective-permute-start.6) | collective-permute-done | bytes 524320 | tf_op jit(solution)/shard_map/cond/branch_0_fun/while/body/eval_jaxpr/ppermute | solution.py:34
  353.3 9.6 %collective-permute-start.7 = (f32[1024,128]{0,1:T(8,128)S(1)}, f32[1024,128]{0,1:T(8,128)S(1)}, u32[]{:S(2)}, u32[]{:S(2)}) collective-permute-start(f32[1024,128]{0,1:T(8,128)S(1)} %add.232), channel_id=1, source_target_pairs={{0,2},{1,3},{2,0},{3,1},{4,6},{5,7},{6,4},{7,5},{8,10},{9,11},{10,... | collective-permute-start | bytes 1572872 | tf_op jit(solution)/shard_map/cond/branch_0_fun/while/body/eval_jaxpr/ppermute | solution.py:34
  362.9 7.2 %collective-permute-done.7 = f32[1024,128]{0,1:T(8,128)S(1)} collective-permute-done((f32[1024,128]{0,1:T(8,128)S(1)}, f32[1024,128]{0,1:T(8,128)S(1)}, u32[]{:S(2)}, u32[]{:S(2)}) %collective-permute-start.7) | collective-permute-done | bytes 524320 | tf_op jit(solution)/shard_map/cond/branch_0_fun/while/body/eval_jaxpr/ppermute | solution.py:34
  382.6 8.0 %collective-permute-done.11 = f32[128,128]{1,0:T(8,128)S(1)} collective-permute-done((f32[128,128]{1,0:T(8,128)S(1)}, f32[128,128]{1,0:T(8,128)S(1)}, u32[]{:S(2)}, u32[]{:S(2)}) %collective-permute-start.11) | collective-permute-done | bytes 65568 | tf_op jit(solution)/shard_map/cond/branch_0_fun/while/body/eval_jaxpr/ppermute | solution.py:34
  432.9 11.7 %cholesky.58 = f32[128,128]{1,0:T(8,128)S(1)} custom-call(f32[128,128]{1,0:T(8,128)S(1)} %fusion.42), custom_call_target="Cholesky" | custom-call | tf_op jit(solution)/shard_map/cond/branch_0_fun/while/body/eval_jaxpr/jit(cholesky)/cholesky | solution.py:87
  446.0 9.8 %custom-call.23 = f32[1,128,128]{1,2,0:T(8,128)S(1)} custom-call(f32[1,128,128]{2,1,0:T(8,128)S(1)} %fusion.43), custom_call_target="InvertDiagBlocksLowerTriangular" | custom-call | tf_op jit(solution)/shard_map/cond/branch_0_fun/while/body/eval_jaxpr/triangular_solve | solution.py:88
  457.6 8.1 %collective-permute-done.6 = f32[1024,128]{0,1:T(8,128)S(1)} collective-permute-done((f32[1024,128]{0,1:T(8,128)S(1)}, f32[1024,128]{0,1:T(8,128)S(1)}, u32[]{:S(2)}, u32[]{:S(2)}) %collective-permute-start.6) | collective-permute-done | bytes 524320 | tf_op jit(solution)/shard_map/cond/branch_0_fun/while/body/eval_jaxpr/ppermute | solution.py:34
  465.8 9.3 %collective-permute-start.7 = (f32[1024,128]{0,1:T(8,128)S(1)}, f32[1024,128]{0,1:T(8,128)S(1)}, u32[]{:S(2)}, u32[]{:S(2)}) collective-permute-start(f32[1024,128]{0,1:T(8,128)S(1)} %add.232), channel_id=1, source_target_pairs={{0,2},{1,3},{2,0},{3,1},{4,6},{5,7},{6,4},{7,5},{8,10},{9,11},{10,... | collective-permute-start | bytes 1572872 | tf_op jit(solution)/shard_map/cond/branch_0_fun/while/body/eval_jaxpr/ppermute | solution.py:34
  475.1 7.2 %collective-permute-done.7 = f32[1024,128]{0,1:T(8,128)S(1)} collective-permute-done((f32[1024,128]{0,1:T(8,128)S(1)}, f32[1024,128]{0,1:T(8,128)S(1)}, u32[]{:S(2)}, u32[]{:S(2)}) %collective-permute-start.7) | collective-permute-done | bytes 524320 | tf_op jit(solution)/shard_map/cond/branch_0_fun/while/body/eval_jaxpr/ppermute | solution.py:34
  495.4 7.8 %collective-permute-done.11 = f32[128,128]{1,0:T(8,128)S(1)} collective-permute-done((f32[128,128]{1,0:T(8,128)S(1)}, f32[128,128]{1,0:T(8,128)S(1)}, u32[]{:S(2)}, u32[]{:S(2)}) %collective-permute-start.11) | collective-permute-done | bytes 65568 | tf_op jit(solution)/shard_map/cond/branch_0_fun/while/body/eval_jaxpr/ppermute | solution.py:34
  (211 shorter events, 261.6 us)
Async XLA Ops:
  46.4 12.0 %collective-permute-start.14 = (f32[1024,128]{1,0:T(8,128)S(1)}, f32[1024,128]{1,0:T(8,128)S(1)}, u32[]{:S(2)}, u32[]{:S(2)}) collective-permute-start(f32[1024,128]{1,0:T(8,128)S(1)} %get-tuple-element.148), channel_id=1, source_target_pairs={{0,4},{4,8},{8,12},{12,16},{16,20},{20,24},{24,28},{28,32},{32,36}... | collective-permute-start | bytes 1572872 | tf_op jit(solution)/shard_map/cond/branch_0_fun/ppermute | solution.py:50
  47.5 10.9 %collective-permute-start.15 = (f32[1024,128]{1,0:T(8,128)S(1)}, f32[1024,128]{1,0:T(8,128)S(1)}, u32[]{:S(2)}, u32[]{:S(2)}) collective-permute-start(f32[1024,128]{1,0:T(8,128)S(1)} %get-tuple-element.148), channel_id=1, source_target_pairs={{4,0},{8,4},{12,8},{16,12},{20,16},{24,20},{28,24},{32,28},{36,32}... | collective-permute-start | bytes 1572872 | tf_op jit(solution)/shard_map/cond/branch_0_fun/ppermute | solution.py:52
  81.3 9.0 %collective-permute-start.3 = (f32[128,128]{0,1:T(8,128)S(1)}, f32[128,128]{0,1:T(8,128)S(1)}, u32[]{:S(2)}, u32[]{:S(2)}) collective-permute-start(f32[128,128]{0,1:T(8,128)S(1)} %add.228), channel_id=1, source_target_pairs={{0,32},{4,36},{8,40},{12,44},{16,48},{20,52},{24,56},{28,60},{32,0... | collective-permute-start | bytes 196616 | tf_op jit(solution)/shard_map/cond/branch_0_fun/while/body/eval_jaxpr/ppermute | solution.py:34
  94.6 5.9 %collective-permute-start.5 = (f32[128,128]{0,1:T(8,128)S(1)}, f32[128,128]{0,1:T(8,128)S(1)}, u32[]{:S(2)}, u32[]{:S(2)}) collective-permute-start(f32[128,128]{0,1:T(8,128)S(1)} %add.230), channel_id=1, source_target_pairs={{0,128},{4,132},{8,136},{12,140},{16,144},{20,148},{24,152},{28,15... | collective-permute-start | bytes 196616 | tf_op jit(solution)/shard_map/cond/branch_0_fun/while/body/eval_jaxpr/ppermute | solution.py:34
  124.2 11.9 %collective-permute-start.6 = (f32[1024,128]{0,1:T(8,128)S(1)}, f32[1024,128]{0,1:T(8,128)S(1)}, u32[]{:S(2)}, u32[]{:S(2)}) collective-permute-start(f32[1024,128]{0,1:T(8,128)S(1)} %fusion.44), channel_id=1, source_target_pairs={{0,1},{1,0},{2,3},{3,2},{4,5},{5,4},{6,7},{7,6},{8,9},{9,8},{10,11... | collective-permute-start | bytes 1572872 | tf_op jit(solution)/shard_map/cond/branch_0_fun/while/body/eval_jaxpr/ppermute | solution.py:34
  136.1 10.8 %collective-permute-start.7 = (f32[1024,128]{0,1:T(8,128)S(1)}, f32[1024,128]{0,1:T(8,128)S(1)}, u32[]{:S(2)}, u32[]{:S(2)}) collective-permute-start(f32[1024,128]{0,1:T(8,128)S(1)} %add.232), channel_id=1, source_target_pairs={{0,2},{1,3},{2,0},{3,1},{4,6},{5,7},{6,4},{7,5},{8,10},{9,11},{10,... | collective-permute-start | bytes 1572872 | tf_op jit(solution)/shard_map/cond/branch_0_fun/while/body/eval_jaxpr/ppermute | solution.py:34
  153.2 5.9 %collective-permute-start.10 = (f32[128,128]{1,0:T(8,128)S(1)}, f32[128,128]{1,0:T(8,128)S(1)}, u32[]{:S(2)}, u32[]{:S(2)}) collective-permute-start(f32[128,128]{1,0:T(8,128)S(1)} %add.235), channel_id=1, source_target_pairs={{0,16},{4,20},{8,24},{12,28},{16,0},{20,4},{24,8},{28,12},{32,48},... | collective-permute-start | bytes 196616 | tf_op jit(solution)/shard_map/cond/branch_0_fun/while/body/eval_jaxpr/ppermute | solution.py:34
  159.2 8.6 %collective-permute-start.11 = (f32[128,128]{1,0:T(8,128)S(1)}, f32[128,128]{1,0:T(8,128)S(1)}, u32[]{:S(2)}, u32[]{:S(2)}) collective-permute-start(f32[128,128]{1,0:T(8,128)S(1)} %add.236), channel_id=1, source_target_pairs={{0,32},{4,36},{8,40},{12,44},{16,48},{20,52},{24,56},{28,60},{32,0... | collective-permute-start | bytes 196616 | tf_op jit(solution)/shard_map/cond/branch_0_fun/while/body/eval_jaxpr/ppermute | solution.py:34
  173.2 5.9 %collective-permute-start.13 = (f32[128,128]{1,0:T(8,128)S(1)}, f32[128,128]{1,0:T(8,128)S(1)}, u32[]{:S(2)}, u32[]{:S(2)}) collective-permute-start(f32[128,128]{1,0:T(8,128)S(1)} %add.238), channel_id=1, source_target_pairs={{0,128},{4,132},{8,136},{12,140},{16,144},{20,148},{24,152},{28,15... | collective-permute-start | bytes 196616 | tf_op jit(solution)/shard_map/cond/branch_0_fun/while/body/eval_jaxpr/ppermute | solution.py:34
  191.7 8.3 %collective-permute-start.3 = (f32[128,128]{0,1:T(8,128)S(1)}, f32[128,128]{0,1:T(8,128)S(1)}, u32[]{:S(2)}, u32[]{:S(2)}) collective-permute-start(f32[128,128]{0,1:T(8,128)S(1)} %add.228), channel_id=1, source_target_pairs={{0,32},{4,36},{8,40},{12,44},{16,48},{20,52},{24,56},{28,60},{32,0... | collective-permute-start | bytes 196616 | tf_op jit(solution)/shard_map/cond/branch_0_fun/while/body/eval_jaxpr/ppermute | solution.py:34
  234.5 11.9 %collective-permute-start.6 = (f32[1024,128]{0,1:T(8,128)S(1)}, f32[1024,128]{0,1:T(8,128)S(1)}, u32[]{:S(2)}, u32[]{:S(2)}) collective-permute-start(f32[1024,128]{0,1:T(8,128)S(1)} %fusion.44), channel_id=1, source_target_pairs={{0,1},{1,0},{2,3},{3,2},{4,5},{5,4},{6,7},{7,6},{8,9},{9,8},{10,11... | collective-permute-start | bytes 1572872 | tf_op jit(solution)/shard_map/cond/branch_0_fun/while/body/eval_jaxpr/ppermute | solution.py:34
  246.4 10.8 %collective-permute-start.7 = (f32[1024,128]{0,1:T(8,128)S(1)}, f32[1024,128]{0,1:T(8,128)S(1)}, u32[]{:S(2)}, u32[]{:S(2)}) collective-permute-start(f32[1024,128]{0,1:T(8,128)S(1)} %add.232), channel_id=1, source_target_pairs={{0,2},{1,3},{2,0},{3,1},{4,6},{5,7},{6,4},{7,5},{8,10},{9,11},{10,... | collective-permute-start | bytes 1572872 | tf_op jit(solution)/shard_map/cond/branch_0_fun/while/body/eval_jaxpr/ppermute | solution.py:34
  268.9 8.3 %collective-permute-start.11 = (f32[128,128]{1,0:T(8,128)S(1)}, f32[128,128]{1,0:T(8,128)S(1)}, u32[]{:S(2)}, u32[]{:S(2)}) collective-permute-start(f32[128,128]{1,0:T(8,128)S(1)} %add.236), channel_id=1, source_target_pairs={{0,32},{4,36},{8,40},{12,44},{16,48},{20,52},{24,56},{28,60},{32,0... | collective-permute-start | bytes 196616 | tf_op jit(solution)/shard_map/cond/branch_0_fun/while/body/eval_jaxpr/ppermute | solution.py:34
  281.7 6.6 %collective-permute-start.13 = (f32[128,128]{1,0:T(8,128)S(1)}, f32[128,128]{1,0:T(8,128)S(1)}, u32[]{:S(2)}, u32[]{:S(2)}) collective-permute-start(f32[128,128]{1,0:T(8,128)S(1)} %add.238), channel_id=1, source_target_pairs={{0,128},{4,132},{8,136},{12,140},{16,144},{20,148},{24,152},{28,15... | collective-permute-start | bytes 196616 | tf_op jit(solution)/shard_map/cond/branch_0_fun/while/body/eval_jaxpr/ppermute | solution.py:34
  300.8 8.5 %collective-permute-start.3 = (f32[128,128]{0,1:T(8,128)S(1)}, f32[128,128]{0,1:T(8,128)S(1)}, u32[]{:S(2)}, u32[]{:S(2)}) collective-permute-start(f32[128,128]{0,1:T(8,128)S(1)} %add.228), channel_id=1, source_target_pairs={{0,32},{4,36},{8,40},{12,44},{16,48},{20,52},{24,56},{28,60},{32,0... | collective-permute-start | bytes 196616 | tf_op jit(solution)/shard_map/cond/branch_0_fun/while/body/eval_jaxpr/ppermute | solution.py:34
  313.7 6.4 %collective-permute-start.5 = (f32[128,128]{0,1:T(8,128)S(1)}, f32[128,128]{0,1:T(8,128)S(1)}, u32[]{:S(2)}, u32[]{:S(2)}) collective-permute-start(f32[128,128]{0,1:T(8,128)S(1)} %add.230), channel_id=1, source_target_pairs={{0,128},{4,132},{8,136},{12,140},{16,144},{20,148},{24,152},{28,15... | collective-permute-start | bytes 196616 | tf_op jit(solution)/shard_map/cond/branch_0_fun/while/body/eval_jaxpr/ppermute | solution.py:34
  343.8 9.5 %collective-permute-start.6 = (f32[1024,128]{0,1:T(8,128)S(1)}, f32[1024,128]{0,1:T(8,128)S(1)}, u32[]{:S(2)}, u32[]{:S(2)}) collective-permute-start(f32[1024,128]{0,1:T(8,128)S(1)} %fusion.44), channel_id=1, source_target_pairs={{0,1},{1,0},{2,3},{3,2},{4,5},{5,4},{6,7},{7,6},{8,9},{9,8},{10,11... | collective-permute-start | bytes 1572872 | tf_op jit(solution)/shard_map/cond/branch_0_fun/while/body/eval_jaxpr/ppermute | solution.py:34
  353.3 16.7 %collective-permute-start.7 = (f32[1024,128]{0,1:T(8,128)S(1)}, f32[1024,128]{0,1:T(8,128)S(1)}, u32[]{:S(2)}, u32[]{:S(2)}) collective-permute-start(f32[1024,128]{0,1:T(8,128)S(1)} %add.232), channel_id=1, source_target_pairs={{0,2},{1,3},{2,0},{3,1},{4,6},{5,7},{6,4},{7,5},{8,10},{9,11},{10,... | collective-permute-start | bytes 1572872 | tf_op jit(solution)/shard_map/cond/branch_0_fun/while/body/eval_jaxpr/ppermute | solution.py:34
  382.0 8.6 %collective-permute-start.11 = (f32[128,128]{1,0:T(8,128)S(1)}, f32[128,128]{1,0:T(8,128)S(1)}, u32[]{:S(2)}, u32[]{:S(2)}) collective-permute-start(f32[128,128]{1,0:T(8,128)S(1)} %add.236), channel_id=1, source_target_pairs={{0,32},{4,36},{8,40},{12,44},{16,48},{20,52},{24,56},{28,60},{32,0... | collective-permute-start | bytes 196616 | tf_op jit(solution)/shard_map/cond/branch_0_fun/while/body/eval_jaxpr/ppermute | solution.py:34
  413.6 9.0 %collective-permute-start.3 = (f32[128,128]{0,1:T(8,128)S(1)}, f32[128,128]{0,1:T(8,128)S(1)}, u32[]{:S(2)}, u32[]{:S(2)}) collective-permute-start(f32[128,128]{0,1:T(8,128)S(1)} %add.228), channel_id=1, source_target_pairs={{0,32},{4,36},{8,40},{12,44},{16,48},{20,52},{24,56},{28,60},{32,0... | collective-permute-start | bytes 196616 | tf_op jit(solution)/shard_map/cond/branch_0_fun/while/body/eval_jaxpr/ppermute | solution.py:34
  456.4 9.3 %collective-permute-start.6 = (f32[1024,128]{0,1:T(8,128)S(1)}, f32[1024,128]{0,1:T(8,128)S(1)}, u32[]{:S(2)}, u32[]{:S(2)}) collective-permute-start(f32[1024,128]{0,1:T(8,128)S(1)} %fusion.44), channel_id=1, source_target_pairs={{0,1},{1,0},{2,3},{3,2},{4,5},{5,4},{6,7},{7,6},{8,9},{9,8},{10,11... | collective-permute-start | bytes 1572872 | tf_op jit(solution)/shard_map/cond/branch_0_fun/while/body/eval_jaxpr/ppermute | solution.py:34
  465.8 16.4 %collective-permute-start.7 = (f32[1024,128]{0,1:T(8,128)S(1)}, f32[1024,128]{0,1:T(8,128)S(1)}, u32[]{:S(2)}, u32[]{:S(2)}) collective-permute-start(f32[1024,128]{0,1:T(8,128)S(1)} %add.232), channel_id=1, source_target_pairs={{0,2},{1,3},{2,0},{3,1},{4,6},{5,7},{6,4},{7,5},{8,10},{9,11},{10,... | collective-permute-start | bytes 1572872 | tf_op jit(solution)/shard_map/cond/branch_0_fun/while/body/eval_jaxpr/ppermute | solution.py:34
  488.6 6.4 %collective-permute-start.10 = (f32[128,128]{1,0:T(8,128)S(1)}, f32[128,128]{1,0:T(8,128)S(1)}, u32[]{:S(2)}, u32[]{:S(2)}) collective-permute-start(f32[128,128]{1,0:T(8,128)S(1)} %add.235), channel_id=1, source_target_pairs={{0,16},{4,20},{8,24},{12,28},{16,0},{20,4},{24,8},{28,12},{32,48},... | collective-permute-start | bytes 196616 | tf_op jit(solution)/shard_map/cond/branch_0_fun/while/body/eval_jaxpr/ppermute | solution.py:34
  495.0 8.3 %collective-permute-start.11 = (f32[128,128]{1,0:T(8,128)S(1)}, f32[128,128]{1,0:T(8,128)S(1)}, u32[]{:S(2)}, u32[]{:S(2)}) collective-permute-start(f32[128,128]{1,0:T(8,128)S(1)} %add.236), channel_id=1, source_target_pairs={{0,32},{4,36},{8,40},{12,44},{16,48},{20,52},{24,56},{28,60},{32,0... | collective-permute-start | bytes 196616 | tf_op jit(solution)/shard_map/cond/branch_0_fun/while/body/eval_jaxpr/ppermute | solution.py:34
  (37 other events, 277.5 us)

commit v7 on v6

--- a/solution.py
+++ b/solution.py
@@ -119,7 +119,7 @@
     start, cov, col_in, order_in, out, small,
     col_index, order,
     win, win_hl, covv, cov_hl, vall, vhl, acc, acc2, tb, r1, s1, r2, gb,
-    e0, w, b, u, mk, e0_h, e0_l, w_h, w2_h, w_l, b_h, b_l, u_h, w_by, u_by, x_hl, res, scol,
+    nat, e0, b, u, e0_h, e0_l, w_h, w2_h, b_h, b_l, u_h, w_by, u_by, inv, x_hl, res,
     word, i_sem, c_sem, l_sem,
     halo_s, halo_r, v_s, next_r, prev_r, rest_r,
     p1_s, p1_r, p2_s, p2_r, p4_s, p4_r, p5_s, p5_r, p6_s, p6_r,
@@ -199,19 +199,10 @@
         rank = jnp.int32(0)
         for t in range(1, GROUPS):
             rank += jnp.where(order[t] == a, t, 0)
-        ranks.append(rank)
+        ranks.append(lax.min(rank, GROUPS - 1))
     row_id = lax.broadcasted_iota(jnp.int32, (WIDTH, WIDTH), 0)
     col_id = lax.broadcasted_iota(jnp.int32, (WIDTH, WIDTH), 1)
     eye = (row_id == col_id).astype(F32)
-    upper = (row_id < col_id).astype(F32) + 0.5 * eye
-    for a in range(GROUPS):
-        for h in range(GROUPS):
-            rows, cols = slice(a * WIDTH, (a + 1) * WIDTH), slice(h * WIDTH, (h + 1) * WIDTH)
-            if a == h:
-                mk[rows, cols] = upper
-            else:
-                ahead = jnp.where(ranks[a] < ranks[h], 1.0, 0.0).astype(F32)
-                mk[rows, cols] = jnp.full((WIDTH, WIDTH), ahead, F32)
 
     cov_copy.wait()
 
@@ -477,22 +468,10 @@
     across = [lax.rsqrt(jnp.sum(d * eye, axis=0, keepdims=True)) for d in diag]
 
     def put(a, h, block):
-        rows, cols = slice(a * WIDTH, (a + 1) * WIDTH), slice(h * WIDTH, (h + 1) * WIDTH)
         block = block * down[a] * across[h]
-        if a == h:
-            block = block - eye
-        high, low = split(block)
-        e0[rows, cols] = block
-        e0_h[rows, cols] = high
-        e0_l[rows, cols] = low
-        block = -(mk[rows, cols] * block)
-        w[rows, cols] = block
-        high, low = split(block)
-        w_h[rows, cols] = high
-        w_l[rows, cols] = low
+        nat[a, h] = block - eye if a == h else block
 
     for a in range(GROUPS):
-        scol[a * WIDTH:(a + 1) * WIDTH, :] = jnp.broadcast_to(down[a], (WIDTH, WIDTH))
         put(a, a, diag[a])
         h = (a + 1) % GROUPS
         block = part(a, 0) + part(h, 1)
@@ -504,58 +483,84 @@
         put(a, h, block)
         put(h, a, block.T)
 
+    side = COLS // 2
+    first, second = slice(0, side), slice(side, COLS)
+    parts = ((first, first), (first, second), (second, second))
+    down_id = lax.broadcasted_iota(jnp.int32, (side, side), 0)
+    across_id = lax.broadcasted_iota(jnp.int32, (side, side), 1)
+    half_eye = jnp.where(down_id == across_id, 0.5, 0.0).astype(F32)
+    upper = jnp.where(down_id < across_id, 1.0, 0.0).astype(F32) + half_eye
+    w_h[second, first] = jnp.zeros((side, side), BF16)
+    for t in range(GROUPS):
+        for v in range(GROUPS):
+            block = nat[order[t], order[v]]
+            at = (slice(t * WIDTH, (t + 1) * WIDTH), slice(v * WIDTH, (v + 1) * WIDTH))
+            high, low = split(block)
+            e0_h[at] = high
+            e0_l[at] = low
+            e0[at] = block
+    for m, n in parts:
+        block = e0[m, n] if m != n else upper * e0[m, n]
+        w_h[m, n] = (-block).astype(BF16)
+
     def newton(w_h, next_h, fine):
-        for n in range(2):
-            cols = slice(n * COLS // 2, (n + 1) * COLS // 2)
-            prod = dot(e0_h[...], w_h[:, cols])
+        for m, n in parts:
+            depth = first if n == first else slice(0, COLS)
+            prod = dot(e0_h[m, depth], w_h[depth, n])
             if fine:
-                prod += dot(e0_l[...], w_h[:, cols]) + dot(e0_h[...], w_l[:, cols])
-            value = (e0[:, cols] + w[:, cols]) + prod
-            b[:, cols] = value
+                prod += dot(e0_l[m, depth], w_h[depth, n])
+            value = (e0[m, n] + w_h[m, n].astype(F32)) + prod
+            b[m, n] = value
             high, low = split(value)
-            b_h[:, cols] = high
+            b_h[m, n] = high
             if fine:
-                b_l[:, cols] = low
-        for n in range(2):
-            cols = slice(n * COLS // 2, (n + 1) * COLS // 2)
-            prod = dot_t(w_h[...], b_h[:, cols])
+                b_l[m, n] = low
+        for m, n in parts:
+            depth = first if m == first else slice(0, COLS)
+            prod = dot_t(w_h[depth, m], b_h[depth, n])
             if fine:
-                prod += dot_t(w_l[...], b_h[:, cols]) + dot_t(w_h[...], b_l[:, cols])
-            down_id = lax.broadcasted_iota(jnp.int32, (COLS, COLS // 2), 0)
-            across_id = lax.broadcasted_iota(jnp.int32, (COLS, COLS // 2), 1) + n * COLS // 2
-            own = jnp.where(down_id == across_id, w[:, cols], 0.0)
-            value = mk[:, cols] * ((b[:, cols] + own) + prod)
+                prod += dot_t(w_h[depth, m], b_l[depth, n])
+            value = b[m, n] + prod
+            if m == n:
+                value = upper * value + half_eye * w_h[m, n].astype(F32)
             if fine:
                 for k in range(2):
-                    u_by[2 * n + k] = value[:, k * WIDTH:(k + 1) * WIDTH]
+                    u_by[(2 if n == second else 0) + k, m] = value[:, k * WIDTH:(k + 1) * WIDTH]
+                res[...] += jnp.sum((value * value).reshape(side // 8, 8, side), axis=0)
             else:
-                u[:, cols] = value
-                u_h[:, cols] = value.astype(BF16)
-            if fine:
-                res[...] += jnp.sum((value * value).reshape(COLS // 8, 8, COLS // 2), axis=0)
+                u[m, n] = value
+                u_h[m, n] = value.astype(BF16)
         if fine:
             return
-        for n in range(2):
-            cols = slice(n * COLS // 2, (n + 1) * COLS // 2)
-            value = (w[:, cols] - u[:, cols]) - dot(w_h[...], u_h[:, cols])
-            w[:, cols] = value
+        next_h[second, first] = jnp.zeros((side, side), BF16)
+        for m, n in parts:
+            depth = slice(m.start, n.stop)
+            value = (w_h[m, n].astype(F32) - u[m, n]) - dot(w_h[m, depth], u_h[depth, n])
+            high = value.astype(BF16)
+            next_h[m, n] = high
             for k in range(2):
-                w_by[2 * n + k] = value[:, k * WIDTH:(k + 1) * WIDTH]
-            high, low = split(value)
-            next_h[:, cols] = high
-            w_l[:, cols] = low
+                w_by[(2 if n == second else 0) + k, m] = high[:, k * WIDTH:(k + 1) * WIDTH]
 
     res[...] = jnp.zeros_like(res)
+    for k in range(2):
+        u_by[k, second] = jnp.zeros((side, WIDTH), F32)
+        w_by[k, second] = jnp.zeros((side, WIDTH), BF16)
     newton(w_h, w2_h, False)
     newton(w2_h, None, True)
     small[0, 0] = jnp.where(jnp.sum(res[...]) < TOLERANCE, 1, 0).astype(jnp.int32)
 
-    step = u_by[g]
-    inverse = (w_by[g] - step) - dot(w2_h[...], step.astype(BF16))
+    rank = jnp.int32(0)
+    for t in range(1, GROUPS):
+        rank += jnp.where(order[t] == g, t, 0)
+    rank = lax.min(rank, GROUPS - 1)
+    step = u_by[rank]
+    inverse = (w_by[rank].astype(F32) - step) - dot(w2_h[...], step.astype(BF16))
+    for t in range(GROUPS):
+        inv[t] = inverse[t * WIDTH:(t + 1) * WIDTH]
     for a in range(GROUPS):
         rows_a = slice(a * WIDTH, (a + 1) * WIDTH)
         same = jnp.where(g == a, 1.0, 0.0).astype(F32)
-        high, low = split(scol[rows_a, :] * (inverse[rows_a] + same * eye))
+        high, low = split(down[a] * (inv[ranks[a]] + same * eye))
         x_hl[rows_a, :WIDTH] = high
         x_hl[rows_a, WIDTH:] = low
 
@@ -606,8 +611,7 @@
             pltpu.VMEM((TILES, 8, WIDTH), F32),
             pltpu.VMEM((PLANE, 8, WIDTH), F32),
             pltpu.VMEM((GROUPS, CORES, TILES, 8, WIDTH), F32),
-            pltpu.VMEM(square, F32),
-            pltpu.VMEM(square, F32),
+            pltpu.VMEM((GROUPS, GROUPS, WIDTH, WIDTH), F32),
             pltpu.VMEM(square, F32),
             pltpu.VMEM(square, F32),
             pltpu.VMEM(square, F32),
@@ -618,12 +622,11 @@
             pltpu.VMEM(square, BF16),
             pltpu.VMEM(square, BF16),
             pltpu.VMEM(square, BF16),
-            pltpu.VMEM(square, BF16),
+            pltpu.VMEM((GROUPS, COLS, WIDTH), BF16),
             pltpu.VMEM((GROUPS, COLS, WIDTH), F32),
-            pltpu.VMEM((GROUPS, COLS, WIDTH), F32),
+            pltpu.VMEM((GROUPS, WIDTH, WIDTH), F32),
             pltpu.VMEM((COLS, 2 * WIDTH), BF16),
             pltpu.VMEM((8, COLS // 2), F32),
-            pltpu.VMEM((COLS, WIDTH), F32),
             pltpu.SemaphoreType.REGULAR((5,)),
             dma((2,)),
             dma, dma,

time: 519 us -> 515 us (level)
  waiting for transfers between devices: 247 us -> 216 us
  starting transfers between devices: 95.8 us -> 124 us
    ppermute x56, waiting for transfers between devices: 240 us -> 210 us  [total(): value = value + lax.ppermute(value, axis, pairs)]
    ppermute x56, starting transfers between devices: 90.6 us -> 118 us  [total(): value = value + lax.ppermute(value, axis, pairs)]
where the time goes in v7:
time: 515 us; the launch traced here: 511 us
  waiting for transfers between devices  216 us (42%)
  starting transfers between devices  124 us (24%)
  other arithmetic  93.3 us (18%)
  Pallas kernels  45 us (9%)
  matrix products  18.2 us (4%)
  loops' own time  8.31 us (2%)
  local copies, waits for them, and re-layouts  6.85 us (1%)
    ppermute x56, waiting for transfers between devices, total(): value = value + lax.ppermute(value, axis, pairs)  210 us
    ppermute x56, starting transfers between devices, total(): value = value + lax.ppermute(value, axis, pairs)  118 us
    another operation x12, other arithmetic, step(): lower = jnp.linalg.cholesky(gram)  49.8 us
    pallas_call x1, Pallas kernels, fast(): pl.pallas_call(kernel, out_shape=(pltpu.VMEM((ROWS, WIDTH), F32), pltpu.S...  45 us
    another operation x8, other arithmetic, step(): lax.linalg.triangular_solve(lower, local, left_side=False, lower=True, tr...  41.8 us
  transfers between devices with their start and end apart: 58, of which 57 were waited for; matrix products, arithmetic and copies ran while one was open for 1% of the time, Pallas kernels for 0%

profile of v7, /device:TPU:6, one launch (start us, length us, event | category | flops | bytes accessed | tf_op | source)
XLA Modules:
  0.0 511.2 jit_solution(18241724747333013787)
XLA Ops:
  0.0 45.0 %shard_map.48 = (f32[1024,128]{1,0:T(8,128)S(1)}, s32[1,1]{1,0:T(1,128)S(4)}) custom-call(f32[1024,128]{1,0:T(8,128)} %start.1, f32[8,8,128,128]{3,2,1,0:T(8,128)} %cov.1, s32[8,8]{1,0:T(8,128)} %col_in.1, s32[4]{0:T(128)} %order_in.1), custom_call_target="tpu_custom_call" | custom-call | tf_op jit(solution)/shard_map/pallas_call | solution.py:590
  45.1 465.3 %conditional.1 = (f32[1024,128]{1,0:T(8,128)S(1)}) conditional(s32[]{:T(128)} %bitcast.11, (f32[1024,128]{1,0:T(8,128)S(1)}, s32[8,8]{1,0:T(8,128)S(1)}, f32[8,8,128,128]{3,2,1,0:T(8,128)}, s32[4]{0:T(128)S(1)}) %tuple.55, f32[1024,128]{1,0:T(8,128)S(1)} %get-tuple-element.156), branch_computations={%region_0.6_spmd, %region_6.7_spmd} | conditional | flops 2417838080 | bytes 44441020 | solution.py:649
  51.0 6.1 %collective-permute-done.14 = f32[1024,128]{1,0:T(8,128)S(1)} collective-permute-done((f32[1024,128]{1,0:T(8,128)S(1)}, f32[1024,128]{1,0:T(8,128)S(1)}, u32[]{:S(2)}, u32[]{:S(2)}) %collective-permute-start.14) | collective-permute-done | bytes 524320 | tf_op jit(solution)/shard_map/cond/branch_0_fun/ppermute | solution.py:50
  60.0 7.9 %fusion.10 = f32[8,128,128,1]{1,2,3,0:T(8,128)S(1)} fusion(f32[8,8,128,128]{3,2,1,0:T(8,128)} %bitcast.52, f32[8,8,128,128]{3,2,1,0:T(8,128)} %get-tuple-element.150), kind=kOutput, calls=%fused_computation.26 | convolution fusion | flops 1610612736 | bytes 8912896 | tf_op jit(solution)/shard_map/cond/branch_0_fun/rsab,rsbk->rak/dot_general | solution.py:80
  68.1 441.8 %while.14 = (s32[]{:T(128)}, f32[1024,128]{0,1:T(8,128)S(1)}, s32[]{:T(128)}, s32[4]{0:T(128)S(1)}, s32[]{:T(128)}, /*index=5*/s32[]{:T(128)}, u32[]{:T(128)}) while((s32[]{:T(128)}, f32[1024,128]{0,1:T(8,128)S(1)}, s32[]{:T(128)}, s32[4]{0:T(128)S(1)}, s32[]{:T(128)}, /*index=5*/s32[]{:T(128)}, u32[]{:T(128)}) %tuple.48), condition=%wide.region_5.5_spmd, body=%wide.region_2.4_spmd.sunk | while | flops 806436992 | bytes 17696444 | solution.py:98
  99.3 11.7 %cholesky.58 = f32[128,128]{1,0:T(8,128)S(1)} custom-call(f32[128,128]{1,0:T(8,128)S(1)} %fusion.42), custom_call_target="Cholesky" | custom-call | tf_op jit(solution)/shard_map/cond/branch_0_fun/while/body/eval_jaxpr/jit(cholesky)/cholesky | solution.py:87
  112.4 9.8 %custom-call.23 = f32[1,128,128]{1,2,0:T(8,128)S(1)} custom-call(f32[1,128,128]{2,1,0:T(8,128)S(1)} %fusion.43), custom_call_target="InvertDiagBlocksLowerTriangular" | custom-call | tf_op jit(solution)/shard_map/cond/branch_0_fun/while/body/eval_jaxpr/triangular_solve | solution.py:88
  123.7 11.0 %collective-permute-done.6 = f32[1024,128]{0,1:T(8,128)S(1)} collective-permute-done((f32[1024,128]{0,1:T(8,128)S(1)}, f32[1024,128]{0,1:T(8,128)S(1)}, u32[]{:S(2)}, u32[]{:S(2)}) %collective-permute-start.6) | collective-permute-done | bytes 524320 | tf_op jit(solution)/shard_map/cond/branch_0_fun/while/body/eval_jaxpr/ppermute | solution.py:34
  136.7 8.8 %collective-permute-done.7 = f32[1024,128]{0,1:T(8,128)S(1)} collective-permute-done((f32[1024,128]{0,1:T(8,128)S(1)}, f32[1024,128]{0,1:T(8,128)S(1)}, u32[]{:S(2)}, u32[]{:S(2)}) %collective-permute-start.7) | collective-permute-done | bytes 524320 | tf_op jit(solution)/shard_map/cond/branch_0_fun/while/body/eval_jaxpr/ppermute | solution.py:34
  209.7 11.7 %cholesky.58 = f32[128,128]{1,0:T(8,128)S(1)} custom-call(f32[128,128]{1,0:T(8,128)S(1)} %fusion.42), custom_call_target="Cholesky" | custom-call | tf_op jit(solution)/shard_map/cond/branch_0_fun/while/body/eval_jaxpr/jit(cholesky)/cholesky | solution.py:87
  222.8 9.8 %custom-call.23 = f32[1,128,128]{1,2,0:T(8,128)S(1)} custom-call(f32[1,128,128]{2,1,0:T(8,128)S(1)} %fusion.43), custom_call_target="InvertDiagBlocksLowerTriangular" | custom-call | tf_op jit(solution)/shard_map/cond/branch_0_fun/while/body/eval_jaxpr/triangular_solve | solution.py:88
  233.4 11.7 %collective-permute-done.6 = f32[1024,128]{0,1:T(8,128)S(1)} collective-permute-done((f32[1024,128]{0,1:T(8,128)S(1)}, f32[1024,128]{0,1:T(8,128)S(1)}, u32[]{:S(2)}, u32[]{:S(2)}) %collective-permute-start.6) | collective-permute-done | bytes 524320 | tf_op jit(solution)/shard_map/cond/branch_0_fun/while/body/eval_jaxpr/ppermute | solution.py:34
  247.9 8.1 %collective-permute-done.7 = f32[1024,128]{0,1:T(8,128)S(1)} collective-permute-done((f32[1024,128]{0,1:T(8,128)S(1)}, f32[1024,128]{0,1:T(8,128)S(1)}, u32[]{:S(2)}, u32[]{:S(2)}) %collective-permute-start.7) | collective-permute-done | bytes 524320 | tf_op jit(solution)/shard_map/cond/branch_0_fun/while/body/eval_jaxpr/ppermute | solution.py:34
  318.4 11.7 %cholesky.58 = f32[128,128]{1,0:T(8,128)S(1)} custom-call(f32[128,128]{1,0:T(8,128)S(1)} %fusion.42), custom_call_target="Cholesky" | custom-call | tf_op jit(solution)/shard_map/cond/branch_0_fun/while/body/eval_jaxpr/jit(cholesky)/cholesky | solution.py:87
  331.4 9.8 %custom-call.23 = f32[1,128,128]{1,2,0:T(8,128)S(1)} custom-call(f32[1,128,128]{2,1,0:T(8,128)S(1)} %fusion.43), custom_call_target="InvertDiagBlocksLowerTriangular" | custom-call | tf_op jit(solution)/shard_map/cond/branch_0_fun/while/body/eval_jaxpr/triangular_solve | solution.py:88
  343.9 7.3 %collective-permute-done.6 = f32[1024,128]{0,1:T(8,128)S(1)} collective-permute-done((f32[1024,128]{0,1:T(8,128)S(1)}, f32[1024,128]{0,1:T(8,128)S(1)}, u32[]{:S(2)}, u32[]{:S(2)}) %collective-permute-start.6) | collective-permute-done | bytes 524320 | tf_op jit(solution)/shard_map/cond/branch_0_fun/while/body/eval_jaxpr/ppermute | solution.py:34
  351.2 7.5 %collective-permute-start.7 = (f32[1024,128]{0,1:T(8,128)S(1)}, f32[1024,128]{0,1:T(8,128)S(1)}, u32[]{:S(2)}, u32[]{:S(2)}) collective-permute-start(f32[1024,128]{0,1:T(8,128)S(1)} %add.232), channel_id=1, source_target_pairs={{0,2},{1,3},{2,0},{3,1},{4,6},{5,7},{6,4},{7,5},{8,10},{9,11},{10,... | collective-permute-start | bytes 1572872 | tf_op jit(solution)/shard_map/cond/branch_0_fun/while/body/eval_jaxpr/ppermute | solution.py:34
  358.7 7.8 %collective-permute-done.7 = f32[1024,128]{0,1:T(8,128)S(1)} collective-permute-done((f32[1024,128]{0,1:T(8,128)S(1)}, f32[1024,128]{0,1:T(8,128)S(1)}, u32[]{:S(2)}, u32[]{:S(2)}) %collective-permute-start.7) | collective-permute-done | bytes 524320 | tf_op jit(solution)/shard_map/cond/branch_0_fun/while/body/eval_jaxpr/ppermute | solution.py:34
  429.5 11.7 %cholesky.58 = f32[128,128]{1,0:T(8,128)S(1)} custom-call(f32[128,128]{1,0:T(8,128)S(1)} %fusion.42), custom_call_target="Cholesky" | custom-call | tf_op jit(solution)/shard_map/cond/branch_0_fun/while/body/eval_jaxpr/jit(cholesky)/cholesky | solution.py:87
  442.6 9.8 %custom-call.23 = f32[1,128,128]{1,2,0:T(8,128)S(1)} custom-call(f32[1,128,128]{2,1,0:T(8,128)S(1)} %fusion.43), custom_call_target="InvertDiagBlocksLowerTriangular" | custom-call | tf_op jit(solution)/shard_map/cond/branch_0_fun/while/body/eval_jaxpr/triangular_solve | solution.py:88
  455.0 8.3 %collective-permute-done.6 = f32[1024,128]{0,1:T(8,128)S(1)} collective-permute-done((f32[1024,128]{0,1:T(8,128)S(1)}, f32[1024,128]{0,1:T(8,128)S(1)}, u32[]{:S(2)}, u32[]{:S(2)}) %collective-permute-start.6) | collective-permute-done | bytes 524320 | tf_op jit(solution)/shard_map/cond/branch_0_fun/while/body/eval_jaxpr/ppermute | solution.py:34
  463.3 6.7 %collective-permute-start.7 = (f32[1024,128]{0,1:T(8,128)S(1)}, f32[1024,128]{0,1:T(8,128)S(1)}, u32[]{:S(2)}, u32[]{:S(2)}) collective-permute-start(f32[1024,128]{0,1:T(8,128)S(1)} %add.232), channel_id=1, source_target_pairs={{0,2},{1,3},{2,0},{3,1},{4,6},{5,7},{6,4},{7,5},{8,10},{9,11},{10,... | collective-permute-start | bytes 1572872 | tf_op jit(solution)/shard_map/cond/branch_0_fun/while/body/eval_jaxpr/ppermute | solution.py:34
  470.1 7.2 %collective-permute-done.7 = f32[1024,128]{0,1:T(8,128)S(1)} collective-permute-done((f32[1024,128]{0,1:T(8,128)S(1)}, f32[1024,128]{0,1:T(8,128)S(1)}, u32[]{:S(2)}, u32[]{:S(2)}) %collective-permute-start.7) | collective-permute-done | bytes 524320 | tf_op jit(solution)/shard_map/cond/branch_0_fun/while/body/eval_jaxpr/ppermute | solution.py:34
  489.2 6.8 %collective-permute-start.11 = (f32[128,128]{1,0:T(8,128)S(1)}, f32[128,128]{1,0:T(8,128)S(1)}, u32[]{:S(2)}, u32[]{:S(2)}) collective-permute-start(f32[128,128]{1,0:T(8,128)S(1)} %add.236), channel_id=1, source_target_pairs={{0,32},{4,36},{8,40},{12,44},{16,48},{20,52},{24,56},{28,60},{32,0... | collective-permute-start | bytes 196616 | tf_op jit(solution)/shard_map/cond/branch_0_fun/while/body/eval_jaxpr/ppermute | solution.py:34
  (211 shorter events, 266.4 us)
Async XLA Ops:
  45.1 12.0 %collective-permute-start.14 = (f32[1024,128]{1,0:T(8,128)S(1)}, f32[1024,128]{1,0:T(8,128)S(1)}, u32[]{:S(2)}, u32[]{:S(2)}) collective-permute-start(f32[1024,128]{1,0:T(8,128)S(1)} %get-tuple-element.148), channel_id=1, source_target_pairs={{0,4},{4,8},{8,12},{12,16},{16,20},{20,24},{24,28},{28,32},{32,36}... | collective-permute-start | bytes 1572872 | tf_op jit(solution)/shard_map/cond/branch_0_fun/ppermute | solution.py:50
  46.2 10.9 %collective-permute-start.15 = (f32[1024,128]{1,0:T(8,128)S(1)}, f32[1024,128]{1,0:T(8,128)S(1)}, u32[]{:S(2)}, u32[]{:S(2)}) collective-permute-start(f32[1024,128]{1,0:T(8,128)S(1)} %get-tuple-element.148), channel_id=1, source_target_pairs={{4,0},{8,4},{12,8},{16,12},{20,16},{24,20},{28,24},{32,28},{36,32}... | collective-permute-start | bytes 1572872 | tf_op jit(solution)/shard_map/cond/branch_0_fun/ppermute | solution.py:52
  80.0 9.0 %collective-permute-start.3 = (f32[128,128]{0,1:T(8,128)S(1)}, f32[128,128]{0,1:T(8,128)S(1)}, u32[]{:S(2)}, u32[]{:S(2)}) collective-permute-start(f32[128,128]{0,1:T(8,128)S(1)} %add.228), channel_id=1, source_target_pairs={{0,32},{4,36},{8,40},{12,44},{16,48},{20,52},{24,56},{28,60},{32,0... | collective-permute-start | bytes 196616 | tf_op jit(solution)/shard_map/cond/branch_0_fun/while/body/eval_jaxpr/ppermute | solution.py:34
  122.9 11.8 %collective-permute-start.6 = (f32[1024,128]{0,1:T(8,128)S(1)}, f32[1024,128]{0,1:T(8,128)S(1)}, u32[]{:S(2)}, u32[]{:S(2)}) collective-permute-start(f32[1024,128]{0,1:T(8,128)S(1)} %fusion.44), channel_id=1, source_target_pairs={{0,1},{1,0},{2,3},{3,2},{4,5},{5,4},{6,7},{7,6},{8,9},{9,8},{10,11... | collective-permute-start | bytes 1572872 | tf_op jit(solution)/shard_map/cond/branch_0_fun/while/body/eval_jaxpr/ppermute | solution.py:34
  134.8 10.8 %collective-permute-start.7 = (f32[1024,128]{0,1:T(8,128)S(1)}, f32[1024,128]{0,1:T(8,128)S(1)}, u32[]{:S(2)}, u32[]{:S(2)}) collective-permute-start(f32[1024,128]{0,1:T(8,128)S(1)} %add.232), channel_id=1, source_target_pairs={{0,2},{1,3},{2,0},{3,1},{4,6},{5,7},{6,4},{7,5},{8,10},{9,11},{10,... | collective-permute-start | bytes 1572872 | tf_op jit(solution)/shard_map/cond/branch_0_fun/while/body/eval_jaxpr/ppermute | solution.py:34
  151.9 6.0 %collective-permute-start.10 = (f32[128,128]{1,0:T(8,128)S(1)}, f32[128,128]{1,0:T(8,128)S(1)}, u32[]{:S(2)}, u32[]{:S(2)}) collective-permute-start(f32[128,128]{1,0:T(8,128)S(1)} %add.235), channel_id=1, source_target_pairs={{0,16},{4,20},{8,24},{12,28},{16,0},{20,4},{24,8},{28,12},{32,48},... | collective-permute-start | bytes 196616 | tf_op jit(solution)/shard_map/cond/branch_0_fun/while/body/eval_jaxpr/ppermute | solution.py:34
  157.9 8.5 %collective-permute-start.11 = (f32[128,128]{1,0:T(8,128)S(1)}, f32[128,128]{1,0:T(8,128)S(1)}, u32[]{:S(2)}, u32[]{:S(2)}) collective-permute-start(f32[128,128]{1,0:T(8,128)S(1)} %add.236), channel_id=1, source_target_pairs={{0,32},{4,36},{8,40},{12,44},{16,48},{20,52},{24,56},{28,60},{32,0... | collective-permute-start | bytes 196616 | tf_op jit(solution)/shard_map/cond/branch_0_fun/while/body/eval_jaxpr/ppermute | solution.py:34
  190.4 8.3 %collective-permute-start.3 = (f32[128,128]{0,1:T(8,128)S(1)}, f32[128,128]{0,1:T(8,128)S(1)}, u32[]{:S(2)}, u32[]{:S(2)}) collective-permute-start(f32[128,128]{0,1:T(8,128)S(1)} %add.228), channel_id=1, source_target_pairs={{0,32},{4,36},{8,40},{12,44},{16,48},{20,52},{24,56},{28,60},{32,0... | collective-permute-start | bytes 196616 | tf_op jit(solution)/shard_map/cond/branch_0_fun/while/body/eval_jaxpr/ppermute | solution.py:34
  203.8 5.9 %collective-permute-start.5 = (f32[128,128]{0,1:T(8,128)S(1)}, f32[128,128]{0,1:T(8,128)S(1)}, u32[]{:S(2)}, u32[]{:S(2)}) collective-permute-start(f32[128,128]{0,1:T(8,128)S(1)} %add.230), channel_id=1, source_target_pairs={{0,128},{4,132},{8,136},{12,140},{16,144},{20,148},{24,152},{28,15... | collective-permute-start | bytes 196616 | tf_op jit(solution)/shard_map/cond/branch_0_fun/while/body/eval_jaxpr/ppermute | solution.py:34
  233.3 11.8 %collective-permute-start.6 = (f32[1024,128]{0,1:T(8,128)S(1)}, f32[1024,128]{0,1:T(8,128)S(1)}, u32[]{:S(2)}, u32[]{:S(2)}) collective-permute-start(f32[1024,128]{0,1:T(8,128)S(1)} %fusion.44), channel_id=1, source_target_pairs={{0,1},{1,0},{2,3},{3,2},{4,5},{5,4},{6,7},{7,6},{8,9},{9,8},{10,11... | collective-permute-start | bytes 1572872 | tf_op jit(solution)/shard_map/cond/branch_0_fun/while/body/eval_jaxpr/ppermute | solution.py:34
  245.2 10.8 %collective-permute-start.7 = (f32[1024,128]{0,1:T(8,128)S(1)}, f32[1024,128]{0,1:T(8,128)S(1)}, u32[]{:S(2)}, u32[]{:S(2)}) collective-permute-start(f32[1024,128]{0,1:T(8,128)S(1)} %add.232), channel_id=1, source_target_pairs={{0,2},{1,3},{2,0},{3,1},{4,6},{5,7},{6,4},{7,5},{8,10},{9,11},{10,... | collective-permute-start | bytes 1572872 | tf_op jit(solution)/shard_map/cond/branch_0_fun/while/body/eval_jaxpr/ppermute | solution.py:34
  267.6 8.3 %collective-permute-start.11 = (f32[128,128]{1,0:T(8,128)S(1)}, f32[128,128]{1,0:T(8,128)S(1)}, u32[]{:S(2)}, u32[]{:S(2)}) collective-permute-start(f32[128,128]{1,0:T(8,128)S(1)} %add.236), channel_id=1, source_target_pairs={{0,32},{4,36},{8,40},{12,44},{16,48},{20,52},{24,56},{28,60},{32,0... | collective-permute-start | bytes 196616 | tf_op jit(solution)/shard_map/cond/branch_0_fun/while/body/eval_jaxpr/ppermute | solution.py:34
  280.3 6.7 %collective-permute-start.13 = (f32[128,128]{1,0:T(8,128)S(1)}, f32[128,128]{1,0:T(8,128)S(1)}, u32[]{:S(2)}, u32[]{:S(2)}) collective-permute-start(f32[128,128]{1,0:T(8,128)S(1)} %add.238), channel_id=1, source_target_pairs={{0,128},{4,132},{8,136},{12,140},{16,144},{20,148},{24,152},{28,15... | collective-permute-start | bytes 196616 | tf_op jit(solution)/shard_map/cond/branch_0_fun/while/body/eval_jaxpr/ppermute | solution.py:34
  299.3 8.4 %collective-permute-start.3 = (f32[128,128]{0,1:T(8,128)S(1)}, f32[128,128]{0,1:T(8,128)S(1)}, u32[]{:S(2)}, u32[]{:S(2)}) collective-permute-start(f32[128,128]{0,1:T(8,128)S(1)} %add.228), channel_id=1, source_target_pairs={{0,32},{4,36},{8,40},{12,44},{16,48},{20,52},{24,56},{28,60},{32,0... | collective-permute-start | bytes 196616 | tf_op jit(solution)/shard_map/cond/branch_0_fun/while/body/eval_jaxpr/ppermute | solution.py:34
  312.1 6.1 %collective-permute-start.5 = (f32[128,128]{0,1:T(8,128)S(1)}, f32[128,128]{0,1:T(8,128)S(1)}, u32[]{:S(2)}, u32[]{:S(2)}) collective-permute-start(f32[128,128]{0,1:T(8,128)S(1)} %add.230), channel_id=1, source_target_pairs={{0,128},{4,132},{8,136},{12,140},{16,144},{20,148},{24,152},{28,15... | collective-permute-start | bytes 196616 | tf_op jit(solution)/shard_map/cond/branch_0_fun/while/body/eval_jaxpr/ppermute | solution.py:34
  341.9 9.3 %collective-permute-start.6 = (f32[1024,128]{0,1:T(8,128)S(1)}, f32[1024,128]{0,1:T(8,128)S(1)}, u32[]{:S(2)}, u32[]{:S(2)}) collective-permute-start(f32[1024,128]{0,1:T(8,128)S(1)} %fusion.44), channel_id=1, source_target_pairs={{0,1},{1,0},{2,3},{3,2},{4,5},{5,4},{6,7},{7,6},{8,9},{9,8},{10,11... | collective-permute-start | bytes 1572872 | tf_op jit(solution)/shard_map/cond/branch_0_fun/while/body/eval_jaxpr/ppermute | solution.py:34
  351.2 15.3 %collective-permute-start.7 = (f32[1024,128]{0,1:T(8,128)S(1)}, f32[1024,128]{0,1:T(8,128)S(1)}, u32[]{:S(2)}, u32[]{:S(2)}) collective-permute-start(f32[1024,128]{0,1:T(8,128)S(1)} %add.232), channel_id=1, source_target_pairs={{0,2},{1,3},{2,0},{3,1},{4,6},{5,7},{6,4},{7,5},{8,10},{9,11},{10,... | collective-permute-start | bytes 1572872 | tf_op jit(solution)/shard_map/cond/branch_0_fun/while/body/eval_jaxpr/ppermute | solution.py:34
  378.5 8.4 %collective-permute-start.11 = (f32[128,128]{1,0:T(8,128)S(1)}, f32[128,128]{1,0:T(8,128)S(1)}, u32[]{:S(2)}, u32[]{:S(2)}) collective-permute-start(f32[128,128]{1,0:T(8,128)S(1)} %add.236), channel_id=1, source_target_pairs={{0,32},{4,36},{8,40},{12,44},{16,48},{20,52},{24,56},{28,60},{32,0... | collective-permute-start | bytes 196616 | tf_op jit(solution)/shard_map/cond/branch_0_fun/while/body/eval_jaxpr/ppermute | solution.py:34
  391.2 6.3 %collective-permute-start.13 = (f32[128,128]{1,0:T(8,128)S(1)}, f32[128,128]{1,0:T(8,128)S(1)}, u32[]{:S(2)}, u32[]{:S(2)}) collective-permute-start(f32[128,128]{1,0:T(8,128)S(1)} %add.238), channel_id=1, source_target_pairs={{0,128},{4,132},{8,136},{12,140},{16,144},{20,148},{24,152},{28,15... | collective-permute-start | bytes 196616 | tf_op jit(solution)/shard_map/cond/branch_0_fun/while/body/eval_jaxpr/ppermute | solution.py:34
  410.3 8.4 %collective-permute-start.3 = (f32[128,128]{0,1:T(8,128)S(1)}, f32[128,128]{0,1:T(8,128)S(1)}, u32[]{:S(2)}, u32[]{:S(2)}) collective-permute-start(f32[128,128]{0,1:T(8,128)S(1)} %add.228), channel_id=1, source_target_pairs={{0,32},{4,36},{8,40},{12,44},{16,48},{20,52},{24,56},{28,60},{32,0... | collective-permute-start | bytes 196616 | tf_op jit(solution)/shard_map/cond/branch_0_fun/while/body/eval_jaxpr/ppermute | solution.py:34
  423.1 6.3 %collective-permute-start.5 = (f32[128,128]{0,1:T(8,128)S(1)}, f32[128,128]{0,1:T(8,128)S(1)}, u32[]{:S(2)}, u32[]{:S(2)}) collective-permute-start(f32[128,128]{0,1:T(8,128)S(1)} %add.230), channel_id=1, source_target_pairs={{0,128},{4,132},{8,136},{12,140},{16,144},{20,148},{24,152},{28,15... | collective-permute-start | bytes 196616 | tf_op jit(solution)/shard_map/cond/branch_0_fun/while/body/eval_jaxpr/ppermute | solution.py:34
  453.0 10.2 %collective-permute-start.6 = (f32[1024,128]{0,1:T(8,128)S(1)}, f32[1024,128]{0,1:T(8,128)S(1)}, u32[]{:S(2)}, u32[]{:S(2)}) collective-permute-start(f32[1024,128]{0,1:T(8,128)S(1)} %fusion.44), channel_id=1, source_target_pairs={{0,1},{1,0},{2,3},{3,2},{4,5},{5,4},{6,7},{7,6},{8,9},{9,8},{10,11... | collective-permute-start | bytes 1572872 | tf_op jit(solution)/shard_map/cond/branch_0_fun/while/body/eval_jaxpr/ppermute | solution.py:34
  463.3 13.9 %collective-permute-start.7 = (f32[1024,128]{0,1:T(8,128)S(1)}, f32[1024,128]{0,1:T(8,128)S(1)}, u32[]{:S(2)}, u32[]{:S(2)}) collective-permute-start(f32[1024,128]{0,1:T(8,128)S(1)} %add.232), channel_id=1, source_target_pairs={{0,2},{1,3},{2,0},{3,1},{4,6},{5,7},{6,4},{7,5},{8,10},{9,11},{10,... | collective-permute-start | bytes 1572872 | tf_op jit(solution)/shard_map/cond/branch_0_fun/while/body/eval_jaxpr/ppermute | solution.py:34
  489.2 9.4 %collective-permute-start.11 = (f32[128,128]{1,0:T(8,128)S(1)}, f32[128,128]{1,0:T(8,128)S(1)}, u32[]{:S(2)}, u32[]{:S(2)}) collective-permute-start(f32[128,128]{1,0:T(8,128)S(1)} %add.236), channel_id=1, source_target_pairs={{0,32},{4,36},{8,40},{12,44},{16,48},{20,52},{24,56},{28,60},{32,0... | collective-permute-start | bytes 196616 | tf_op jit(solution)/shard_map/cond/branch_0_fun/while/body/eval_jaxpr/ppermute | solution.py:34
  (37 other events, 273.8 us)

commit v8 on v7

--- a/solution.py
+++ b/solution.py
@@ -118,11 +118,11 @@
 def kernel(
     start, cov, col_in, order_in, out, small,
     col_index, order,
-    win, win_hl, covv, cov_hl, vall, vhl, acc, acc2, tb, r1, s1, r2, gb,
+    win, win_hl, covv, cov_hl, vall, vhl, acc, acc2, tb, r1, s1, r2, r3, gb,
     nat, e0, b, u, e0_h, e0_l, w_h, w2_h, b_h, b_l, u_h, w_by, u_by, inv, x_hl, res,
     word, i_sem, c_sem, l_sem,
-    halo_s, halo_r, v_s, next_r, prev_r, rest_r,
-    p1_s, p1_r, p2_s, p2_r, p4_s, p4_r, p5_s, p5_r, p6_s, p6_r,
+    halo_s, halo_r, n_s, n_r, v_s, next_r, prev_r, rest_r,
+    p1_s, p1_r, p2_s, p2_r, p3_r, p4_s, p4_r, p5_s, p5_r, p6_s, p6_r,
 ):
     p = lax.axis_index("pts")
     g = lax.axis_index("cols")
@@ -175,22 +175,24 @@
     tell(word.at[0], near_z)
     tell(word.at[1], near_x)
 
-    def halo_rows(side, k):
-        count = HALF + 1 if k == 0 else 1
-        low = HALF - 1 - k if side == 0 else (0 if k == 0 else HALF + k)
-        return slice(low * BLOCK, (low + count) * BLOCK)
-
-    def to_after(k):
-        rows = halo_rows(0, k)
-        return remote(start.at[rows, :], win.at[0, rows, :], halo_s.at[0], halo_r.at[0, k], pts=after)
-
-    def to_before(k):
-        rows = halo_rows(2, k)
-        return remote(start.at[rows, :], win.at[2, rows, :], halo_s.at[1], halo_r.at[1, k], pts=before)
-
-    for k in range(HALF):
-        to_after(k).start()
-        to_before(k).start()
+    def turn_row(j):
+        return ROW_BLOCKS - 1 - j + c * (2 * j - ROW_BLOCKS + 1)
+
+    def rows(r):
+        return pl.ds(pl.multiple_of(r * BLOCK, BLOCK), BLOCK)
+
+    far_side, near_side = 2 * c, 2 - 2 * c
+    far_device = before + c * (after - before)
+
+    def to_far(j):
+        block = rows(ROW_BLOCKS - 1 - turn_row(j))
+        return remote(start.at[block, :], win.at[near_side, block, :], halo_s, halo_r.at[j], pts=far_device)
+
+    to_near = remote(start, win.at[far_side], n_s, n_r, pts=sibling)
+    to_far(0).start()
+    to_near.start()
+    for j in range(1, ROW_BLOCKS):
+        to_far(j).start()
 
     col_copy.wait()
     order_copy.wait()
@@ -215,11 +217,8 @@
 
     lax.fori_loop(0, ROW_BLOCKS, split_cov, 0)
 
-    pl.semaphore_wait(word.at[0], 2)
-    tell(word.at[2], next_z)
     def split_window(side, k):
-        rows = pl.ds(k * BLOCK if isinstance(k, int) else pl.multiple_of(k * BLOCK, BLOCK), BLOCK)
-        high, low = split(win[side, rows, :])
+        high, low = split(win[side, rows(k), :])
         win_hl[side * ROW_BLOCKS + k, :, :WIDTH] = high
         win_hl[side * ROW_BLOCKS + k, :, WIDTH:] = low
 
@@ -227,24 +226,27 @@
         split_window(1, k)
         return carry
 
+    def split_near(k, carry):
+        split_window(near_side, k)
+        return carry
+
     own_copy.wait()
     lax.fori_loop(0, ROW_BLOCKS, split_own, 0)
+    to_near.wait_recv()
+    lax.fori_loop(0, ROW_BLOCKS, split_near, 0)
 
     base = p * ROW_BLOCKS - ROW_BLOCKS - NBLK
 
-    def rows(r):
-        return slice(r * BLOCK, (r + 1) * BLOCK)
-
     def turn(r):
-        return lax.rem(g + GROUPS - r % GROUPS, GROUPS)
+        return lax.rem(g + GROUPS - lax.rem(r, GROUPS), GROUPS)
 
     def goes_left(r):
         t = turn(r)
-        return (t >= 2) | (t == 0) if r < HALF else t >= 2
+        return (t >= 2) | ((t == 0) & (r < HALF))
 
     def goes_right(r):
         t = turn(r)
-        return t <= 1 if r < HALF else (t <= 1) | (t == 3)
+        return (t <= 1) | ((t == 3) & (r >= HALF))
 
     def between(r):
         t = turn(r)
@@ -252,15 +254,15 @@
 
     def has_next(r):
         t = turn(r)
-        return t >= 1 if r < HALF else (t == 1) | (t == 2)
+        return (t == 1) | (t == 2) | ((t == 3) & (r < HALF))
 
     def has_prev(r):
         t = turn(r)
-        return (t == 1) | (t == 2) if r < HALF else t <= 2
+        return (t == 1) | (t == 2) | ((t == 0) & (r >= HALF))
 
     def prev_pair(r):
         t = turn(r)
-        return t == 1 if r < HALF else t <= 1
+        return (t == 1) | ((t == 0) & (r >= HALF))
 
     def xcopy(src, r, recv, to):
         ref = vall.at[src, rows(r), :]
@@ -293,19 +295,16 @@
         def _():
             xcopy(g, r, prev_r.at[r], g_next).start()
 
-    for j in range(HALF):
-        to_after(j).wait_recv()
-        to_before(j).wait_recv()
+    for j in range(ROW_BLOCKS):
+        r = turn_row(j)
+        arrived(halo_r.at[j], win.at[0, pl.ds(0, BLOCK), :])
+        split_window(far_side, r)
+        image(r)
+        keep_split(g, r)
         if j == 0:
-            for k in range(HALF):
-                split_window(0, ROW_BLOCKS - 1 - k)
-                split_window(2, k)
-        split_window(0, HALF - 1 - j)
-        split_window(2, HALF + j)
-        for r in (HALF + j, HALF - 1 - j):
-            image(r)
-            keep_split(g, r)
-        if j == 0:
+            pl.semaphore_wait(word.at[0], 2)
+            tell(word.at[2], next_z)
+        if j == 3:
             pl.semaphore_wait(word.at[2], 2)
             tell(word.at[3], near_y)
 
@@ -334,10 +333,19 @@
         def _():
             scatter(y_to, 0).start()
 
+    def scatter_prev(z_to):
+        return remote(s1.at[TILES_G + z_to], r3.at[here], p2_s, p3_r, cols=g_prev, pts=device(z_to))
+
     def sum_tile():
         arrived(p2_r, r2.at[pl.ds(1, PLANE - 1)])
         r2[here] = s1[here]
         gb[g, c, here] = jnp.sum(r2[...], axis=0)
+
+        @pl.when(y == 0)
+        def _():
+            arrived(p3_r, r3)
+            gb[g, c, here] += jnp.sum(r3[...], axis=0)
+
         ref = gb.at[g, c, here]
         for over in (2, 1, 3, 0):
             for far in NEAR_LAST:
@@ -351,36 +359,37 @@
     own_core, own_part = core_sum(LATE, TILES_G, p1_s.at[0], p1_r.at[0])
     own_core.start()
 
-    for j in range(HALF):
-        for r in (HALF + j, HALF - 1 - j):
-            @pl.when(has_next(r))
-            def _():
-                arrived(next_r.at[r], several(1))
-                keep_split(g_next, r)
-
-            @pl.when(has_prev(r))
-            def _():
-                arrived(prev_r.at[r], several(1))
-                keep_split(g_prev, r)
-
-            @pl.when(between(r))
-            def _():
-                left = jnp.concatenate([vhl[g, rows(r), :], vhl[g_prev, rows(r), :]], axis=1)
-                acc[...] += dot_t(left, vhl[g_next, rows(r), :])
-
-            if r < HALF:
-                @pl.when(turn(r) == 3)
-                def _():
-                    acc[:2 * WIDTH] += dot_t(vhl[g, rows(r), :], vhl[g_next, rows(r), :])
-
-            @pl.when(prev_pair(r))
-            def _():
-                acc2[...] += dot_t(vhl[g_prev, rows(r), :], vhl[g, rows(r), :])
-
-        if j == 1:
+    for j in range(ROW_BLOCKS):
+        r = turn_row(j)
+
+        @pl.when(has_next(r))
+        def _():
+            arrived(next_r.at[r], several(1))
+            keep_split(g_next, r)
+
+        @pl.when(has_prev(r))
+        def _():
+            arrived(prev_r.at[r], several(1))
+            keep_split(g_prev, r)
+
+        @pl.when(between(r))
+        def _():
+            left = jnp.concatenate([vhl[g, rows(r), :], vhl[g_prev, rows(r), :]], axis=1)
+            acc[...] += dot_t(left, vhl[g_next, rows(r), :])
+
+        @pl.when((turn(r) == 3) & (r < HALF))
+        def _():
+            acc[:2 * WIDTH] += dot_t(vhl[g, rows(r), :], vhl[g_next, rows(r), :])
+
+        @pl.when(prev_pair(r))
+        def _():
+            acc2[...] += dot_t(vhl[g_prev, rows(r), :], vhl[g, rows(r), :])
+
+        if j == 2:
             own_core.wait_recv()
             s1[own_part] = tb[c, own_part] + r1[own_part]
             pl.semaphore_wait(word.at[4], 2)
+            tell(word.at[5], near_x)
             scatter_rows(YS - 1)
 
     place(0, quarters(acc[:2 * WIDTH], WIDTH, WIDTH))
@@ -392,8 +401,11 @@
     late_core.wait_recv()
     s1[late_part] = tb[c, late_part] + r1[late_part]
 
-    for y_to in range(YS - 1):
-        scatter_rows(y_to)
+    pl.semaphore_wait(word.at[5], 2)
+    for far in NEAR_LAST:
+        scatter_prev(lax.rem(z + far, ZS)).start()
+    scatter_rows(0)
+    scatter_rows(2)
 
     for r in range(ROW_BLOCKS):
         @pl.when(jnp.logical_not(goes_left(r)))
@@ -409,7 +421,9 @@
             xcopy(g_prev, r, rest_r.at[2], g_next).start()
             xcopy(g_next, r, rest_r.at[3], g_prev).start()
 
-    sum_tile()
+    @pl.when(y != 1)
+    def _():
+        sum_tile()
 
     pl.semaphore_wait(word.at[1], 2)
 
@@ -424,7 +438,7 @@
         ref = gb.at[lax.rem(g + k, GROUPS), c, of_set(n)]
         return remote(ref, ref, p6_s, p6_r, pts=sibling)
 
-    for n in (3, 0, 1, 2):
+    for n in (3, 0, 2):
         @pl.when(y == n)
         def _():
             arrived(p4_r.at[n], gb.at[g, c, pl.ds(0, TILES_G - 1)])
@@ -437,7 +451,7 @@
             x_share(k, n).start()
         core_share(0, n).start()
 
-    for n in (3, 0, 1, 2):
+    for n in (3, 0, 2):
         for k in (1, 3, 2):
             arrived(p5_r.at[k, n], gb.at[g, c, of_set(n)])
             core_share(k, n).start()
@@ -456,7 +470,7 @@
         def _():
             keep_split(g_prev, r)
 
-    arrived(p6_r, gb.at[:, 1 - c])
+    arrived(p6_r, gb.at[:, 1 - c, pl.ds(0, TILES - TILES_G)])
 
     def part(a, kind):
         return jnp.concatenate(
@@ -474,7 +488,7 @@
     for a in range(GROUPS):
         put(a, a, diag[a])
         h = (a + 1) % GROUPS
-        block = part(a, 0) + part(h, 1)
+        block = part(a, 0)
         put(a, h, block)
         put(h, a, block.T)
     for a in range(GROUPS // 2):
@@ -571,15 +585,23 @@
         q = dot(jnp.concatenate([high, low], axis=0), x_hl[...])
         out[rows_k, :] = quarters(q, 2 * BLOCK, WIDTH)
 
-    arrived(halo_s.at[0], win.at[0])
-    arrived(halo_s.at[1], win.at[2])
+    arrived(halo_s, win.at[0])
+    to_near.wait_send()
     arrived(v_s, vall.at[:3])
     own_core.wait_send()
     late_core.wait_send()
     arrived(p2_s, s1.at[pl.ds(0, TILES - 1)])
-    arrived(p4_s, r2.at[pl.ds(0, PLANE - 1)])
-    arrived(p5_s, gb.at[:3, 0])
-    arrived(p6_s, gb.at[:, 0])
+
+    @pl.when(y == 1)
+    def _():
+        arrived(p2_s, s1.at[pl.ds(0, 1)])
+
+    @pl.when(y != 1)
+    def _():
+        arrived(p4_s, r2.at[pl.ds(0, PLANE - 1)])
+
+    arrived(p5_s, gb.at[:3, 0, pl.ds(0, TILES - TILES_G)])
+    arrived(p6_s, gb.at[:, 0, pl.ds(0, TILES - TILES_G)])
 
 
 def fast(start, cov_blocks, col_index, order):
@@ -610,6 +632,7 @@
             pltpu.VMEM((TILES, 8, WIDTH), F32),
             pltpu.VMEM((TILES, 8, WIDTH), F32),
             pltpu.VMEM((PLANE, 8, WIDTH), F32),
+            pltpu.VMEM((PLANE, 8, WIDTH), F32),
             pltpu.VMEM((GROUPS, CORES, TILES, 8, WIDTH), F32),
             pltpu.VMEM((GROUPS, GROUPS, WIDTH, WIDTH), F32),
             pltpu.VMEM(square, F32),
@@ -627,13 +650,13 @@
             pltpu.VMEM((GROUPS, WIDTH, WIDTH), F32),
             pltpu.VMEM((COLS, 2 * WIDTH), BF16),
             pltpu.VMEM((8, COLS // 2), F32),
-            pltpu.SemaphoreType.REGULAR((5,)),
+            pltpu.SemaphoreType.REGULAR((6,)),
             dma((2,)),
             dma, dma,
-            dma((2,)), dma((2, HALF)),
+            dma, dma((ROW_BLOCKS,)), dma, dma,
             dma, dma((ROW_BLOCKS,)), dma((ROW_BLOCKS,)), dma((4,)),
             dma((2,)), dma((2,)),
-            dma, dma,
+            dma, dma, dma,
             dma, dma((KINDS,)),
             dma, dma((GROUPS, KINDS)),
             dma, dma,

time: 515 us -> 515 us (level)
  waiting for transfers between devices: 216 us -> 283 us
  starting transfers between devices: 124 us -> 61 us
    ppermute x56, waiting for transfers between devices: 210 us -> 277 us  [total(): value = value + lax.ppermute(value, axis, pairs)]
    ppermute x56, starting transfers between devices: 118 us -> 55.8 us  [total(): value = value + lax.ppermute(value, axis, pairs)]
where the time goes in v8:
time: 515 us
  waiting for transfers between devices  283 us (55%)
  other arithmetic  93.3 us (18%)
  starting transfers between devices  61 us (12%)
  Pallas kernels  44.4 us (9%)
  matrix products  18.2 us (4%)
  loops' own time  8.42 us (2%)
  local copies, waits for them, and re-layouts  6.85 us (1%)
    ppermute x56, waiting for transfers between devices, total(): value = value + lax.ppermute(value, axis, pairs)  277 us
    ppermute x56, starting transfers between devices, total(): value = value + lax.ppermute(value, axis, pairs)  55.8 us
    another operation x12, other arithmetic, step(): lower = jnp.linalg.cholesky(gram)  49.8 us
    pallas_call x1, Pallas kernels, fast(): pl.pallas_call(kernel, out_shape=(pltpu.VMEM((ROWS, WIDTH), F32), pltpu.S...  44.4 us
    another operation x8, other arithmetic, step(): lax.linalg.triangular_solve(lower, local, left_side=False, lower=True, tr...  41.8 us
  transfers between devices with their start and end apart: 58, of which 57 were waited for; matrix products, arithmetic and copies ran while one was open for 1% of the time, Pallas kernels for 0%

profile of v8, /device:TPU:6, one launch (start us, length us, event | category | flops | bytes accessed | tf_op | source)
XLA Modules:
  0.0 515.2 jit_solution(11954348042179515550)
XLA Ops:
  0.0 44.4 %shard_map.48 = (f32[1024,128]{1,0:T(8,128)S(1)}, s32[1,1]{1,0:T(1,128)S(4)}) custom-call(f32[1024,128]{1,0:T(8,128)} %start.1, f32[8,8,128,128]{3,2,1,0:T(8,128)} %cov.1, s32[8,8]{1,0:T(8,128)} %col_in.1, s32[4]{0:T(128)} %order_in.1), custom_call_target="tpu_custom_call" | custom-call | tf_op jit(solution)/shard_map/pallas_call | solution.py:612
  44.5 469.9 %conditional.1 = (f32[1024,128]{1,0:T(8,128)S(1)}) conditional(s32[]{:T(128)} %bitcast.11, (f32[1024,128]{1,0:T(8,128)S(1)}, s32[8,8]{1,0:T(8,128)S(1)}, f32[8,8,128,128]{3,2,1,0:T(8,128)}, s32[4]{0:T(128)S(1)}) %tuple.55, f32[1024,128]{1,0:T(8,128)S(1)} %get-tuple-element.156), branch_computations={%region_0.6_spmd, %region_6.7_spmd} | conditional | flops 2417838080 | bytes 44441020 | solution.py:672
  50.4 6.1 %collective-permute-done.14 = f32[1024,128]{1,0:T(8,128)S(1)} collective-permute-done((f32[1024,128]{1,0:T(8,128)S(1)}, f32[1024,128]{1,0:T(8,128)S(1)}, u32[]{:S(2)}, u32[]{:S(2)}) %collective-permute-start.14) | collective-permute-done | bytes 524320 | tf_op jit(solution)/shard_map/cond/branch_0_fun/ppermute | solution.py:50
  59.3 7.9 %fusion.10 = f32[8,128,128,1]{1,2,3,0:T(8,128)S(1)} fusion(f32[8,8,128,128]{3,2,1,0:T(8,128)} %bitcast.52, f32[8,8,128,128]{3,2,1,0:T(8,128)} %get-tuple-element.150), kind=kOutput, calls=%fused_computation.26 | convolution fusion | flops 1610612736 | bytes 8912896 | tf_op jit(solution)/shard_map/cond/branch_0_fun/rsab,rsbk->rak/dot_general | solution.py:80
  67.5 446.5 %while.14 = (s32[]{:T(128)}, f32[1024,128]{0,1:T(8,128)S(1)}, s32[]{:T(128)}, s32[4]{0:T(128)S(1)}, s32[]{:T(128)}, /*index=5*/s32[]{:T(128)}, u32[]{:T(128)}) while((s32[]{:T(128)}, f32[1024,128]{0,1:T(8,128)S(1)}, s32[]{:T(128)}, s32[4]{0:T(128)S(1)}, s32[]{:T(128)}, /*index=5*/s32[]{:T(128)}, u32[]{:T(128)}) %tuple.48), condition=%wide.region_5.5_spmd, body=%wide.region_2.4_spmd.sunk | while | flops 806436992 | bytes 17696444 | solution.py:98
  80.7 7.5 %collective-permute-done.3 = f32[128,128]{0,1:T(8,128)S(1)} collective-permute-done((f32[128,128]{0,1:T(8,128)S(1)}, f32[128,128]{0,1:T(8,128)S(1)}, u32[]{:S(2)}, u32[]{:S(2)}) %collective-permute-start.3) | collective-permute-done | bytes 65568 | tf_op jit(solution)/shard_map/cond/branch_0_fun/while/body/eval_jaxpr/ppermute | solution.py:34
  98.6 11.7 %cholesky.58 = f32[128,128]{1,0:T(8,128)S(1)} custom-call(f32[128,128]{1,0:T(8,128)S(1)} %fusion.42), custom_call_target="Cholesky" | custom-call | tf_op jit(solution)/shard_map/cond/branch_0_fun/while/body/eval_jaxpr/jit(cholesky)/cholesky | solution.py:87
  111.7 9.8 %custom-call.23 = f32[1,128,128]{1,2,0:T(8,128)S(1)} custom-call(f32[1,128,128]{2,1,0:T(8,128)S(1)} %fusion.43), custom_call_target="InvertDiagBlocksLowerTriangular" | custom-call | tf_op jit(solution)/shard_map/cond/branch_0_fun/while/body/eval_jaxpr/triangular_solve | solution.py:88
  122.2 13.2 %collective-permute-done.6 = f32[1024,128]{0,1:T(8,128)S(1)} collective-permute-done((f32[1024,128]{0,1:T(8,128)S(1)}, f32[1024,128]{0,1:T(8,128)S(1)}, u32[]{:S(2)}, u32[]{:S(2)}) %collective-permute-start.6) | collective-permute-done | bytes 524320 | tf_op jit(solution)/shard_map/cond/branch_0_fun/while/body/eval_jaxpr/ppermute | solution.py:34
  135.5 10.7 %collective-permute-done.7 = f32[1024,128]{0,1:T(8,128)S(1)} collective-permute-done((f32[1024,128]{0,1:T(8,128)S(1)}, f32[1024,128]{0,1:T(8,128)S(1)}, u32[]{:S(2)}, u32[]{:S(2)}) %collective-permute-start.7) | collective-permute-done | bytes 524320 | tf_op jit(solution)/shard_map/cond/branch_0_fun/while/body/eval_jaxpr/ppermute | solution.py:34
  159.6 6.8 %collective-permute-done.11 = f32[128,128]{1,0:T(8,128)S(1)} collective-permute-done((f32[128,128]{1,0:T(8,128)S(1)}, f32[128,128]{1,0:T(8,128)S(1)}, u32[]{:S(2)}, u32[]{:S(2)}) %collective-permute-start.11) | collective-permute-done | bytes 65568 | tf_op jit(solution)/shard_map/cond/branch_0_fun/while/body/eval_jaxpr/ppermute | solution.py:34
  208.9 11.7 %cholesky.58 = f32[128,128]{1,0:T(8,128)S(1)} custom-call(f32[128,128]{1,0:T(8,128)S(1)} %fusion.42), custom_call_target="Cholesky" | custom-call | tf_op jit(solution)/shard_map/cond/branch_0_fun/while/body/eval_jaxpr/jit(cholesky)/cholesky | solution.py:87
  222.0 9.8 %custom-call.23 = f32[1,128,128]{1,2,0:T(8,128)S(1)} custom-call(f32[1,128,128]{2,1,0:T(8,128)S(1)} %fusion.43), custom_call_target="InvertDiagBlocksLowerTriangular" | custom-call | tf_op jit(solution)/shard_map/cond/branch_0_fun/while/body/eval_jaxpr/triangular_solve | solution.py:88
  232.6 14.0 %collective-permute-done.6 = f32[1024,128]{0,1:T(8,128)S(1)} collective-permute-done((f32[1024,128]{0,1:T(8,128)S(1)}, f32[1024,128]{0,1:T(8,128)S(1)}, u32[]{:S(2)}, u32[]{:S(2)}) %collective-permute-start.6) | collective-permute-done | bytes 524320 | tf_op jit(solution)/shard_map/cond/branch_0_fun/while/body/eval_jaxpr/ppermute | solution.py:34
  246.8 10.7 %collective-permute-done.7 = f32[1024,128]{0,1:T(8,128)S(1)} collective-permute-done((f32[1024,128]{0,1:T(8,128)S(1)}, f32[1024,128]{0,1:T(8,128)S(1)}, u32[]{:S(2)}, u32[]{:S(2)}) %collective-permute-start.7) | collective-permute-done | bytes 524320 | tf_op jit(solution)/shard_map/cond/branch_0_fun/while/body/eval_jaxpr/ppermute | solution.py:34
  263.9 5.9 %collective-permute-done.10 = f32[128,128]{1,0:T(8,128)S(1)} collective-permute-done((f32[128,128]{1,0:T(8,128)S(1)}, f32[128,128]{1,0:T(8,128)S(1)}, u32[]{:S(2)}, u32[]{:S(2)}) %collective-permute-start.10) | collective-permute-done | bytes 65568 | tf_op jit(solution)/shard_map/cond/branch_0_fun/while/body/eval_jaxpr/ppermute | solution.py:34
  320.7 11.7 %cholesky.58 = f32[128,128]{1,0:T(8,128)S(1)} custom-call(f32[128,128]{1,0:T(8,128)S(1)} %fusion.42), custom_call_target="Cholesky" | custom-call | tf_op jit(solution)/shard_map/cond/branch_0_fun/while/body/eval_jaxpr/jit(cholesky)/cholesky | solution.py:87
  333.8 9.8 %custom-call.23 = f32[1,128,128]{1,2,0:T(8,128)S(1)} custom-call(f32[1,128,128]{2,1,0:T(8,128)S(1)} %fusion.43), custom_call_target="InvertDiagBlocksLowerTriangular" | custom-call | tf_op jit(solution)/shard_map/cond/branch_0_fun/while/body/eval_jaxpr/triangular_solve | solution.py:88
  344.4 14.5 %collective-permute-done.6 = f32[1024,128]{0,1:T(8,128)S(1)} collective-permute-done((f32[1024,128]{0,1:T(8,128)S(1)}, f32[1024,128]{0,1:T(8,128)S(1)}, u32[]{:S(2)}, u32[]{:S(2)}) %collective-permute-start.6) | collective-permute-done | bytes 524320 | tf_op jit(solution)/shard_map/cond/branch_0_fun/while/body/eval_jaxpr/ppermute | solution.py:34
  359.0 10.7 %collective-permute-done.7 = f32[1024,128]{0,1:T(8,128)S(1)} collective-permute-done((f32[1024,128]{0,1:T(8,128)S(1)}, f32[1024,128]{0,1:T(8,128)S(1)}, u32[]{:S(2)}, u32[]{:S(2)}) %collective-permute-start.7) | collective-permute-done | bytes 524320 | tf_op jit(solution)/shard_map/cond/branch_0_fun/while/body/eval_jaxpr/ppermute | solution.py:34
  433.0 11.7 %cholesky.58 = f32[128,128]{1,0:T(8,128)S(1)} custom-call(f32[128,128]{1,0:T(8,128)S(1)} %fusion.42), custom_call_target="Cholesky" | custom-call | tf_op jit(solution)/shard_map/cond/branch_0_fun/while/body/eval_jaxpr/jit(cholesky)/cholesky | solution.py:87
  446.1 9.8 %custom-call.23 = f32[1,128,128]{1,2,0:T(8,128)S(1)} custom-call(f32[1,128,128]{2,1,0:T(8,128)S(1)} %fusion.43), custom_call_target="InvertDiagBlocksLowerTriangular" | custom-call | tf_op jit(solution)/shard_map/cond/branch_0_fun/while/body/eval_jaxpr/triangular_solve | solution.py:88
  456.6 14.7 %collective-permute-done.6 = f32[1024,128]{0,1:T(8,128)S(1)} collective-permute-done((f32[1024,128]{0,1:T(8,128)S(1)}, f32[1024,128]{0,1:T(8,128)S(1)}, u32[]{:S(2)}, u32[]{:S(2)}) %collective-permute-start.6) | collective-permute-done | bytes 524320 | tf_op jit(solution)/shard_map/cond/branch_0_fun/while/body/eval_jaxpr/ppermute | solution.py:34
  471.5 10.7 %collective-permute-done.7 = f32[1024,128]{0,1:T(8,128)S(1)} collective-permute-done((f32[1024,128]{0,1:T(8,128)S(1)}, f32[1024,128]{0,1:T(8,128)S(1)}, u32[]{:S(2)}, u32[]{:S(2)}) %collective-permute-start.7) | collective-permute-done | bytes 524320 | tf_op jit(solution)/shard_map/cond/branch_0_fun/while/body/eval_jaxpr/ppermute | solution.py:34
  (211 shorter events, 243.0 us)
Async XLA Ops:
  44.5 12.0 %collective-permute-start.14 = (f32[1024,128]{1,0:T(8,128)S(1)}, f32[1024,128]{1,0:T(8,128)S(1)}, u32[]{:S(2)}, u32[]{:S(2)}) collective-permute-start(f32[1024,128]{1,0:T(8,128)S(1)} %get-tuple-element.148), channel_id=1, source_target_pairs={{0,4},{4,8},{8,12},{12,16},{16,20},{20,24},{24,28},{28,32},{32,36}... | collective-permute-start | bytes 1572872 | tf_op jit(solution)/shard_map/cond/branch_0_fun/ppermute | solution.py:50
  44.9 11.5 %collective-permute-start.15 = (f32[1024,128]{1,0:T(8,128)S(1)}, f32[1024,128]{1,0:T(8,128)S(1)}, u32[]{:S(2)}, u32[]{:S(2)}) collective-permute-start(f32[1024,128]{1,0:T(8,128)S(1)} %get-tuple-element.148), channel_id=1, source_target_pairs={{4,0},{8,4},{12,8},{16,12},{20,16},{24,20},{28,24},{32,28},{36,32}... | collective-permute-start | bytes 1572872 | tf_op jit(solution)/shard_map/cond/branch_0_fun/ppermute | solution.py:52
  79.4 8.8 %collective-permute-start.3 = (f32[128,128]{0,1:T(8,128)S(1)}, f32[128,128]{0,1:T(8,128)S(1)}, u32[]{:S(2)}, u32[]{:S(2)}) collective-permute-start(f32[128,128]{0,1:T(8,128)S(1)} %add.228), channel_id=1, source_target_pairs={{0,32},{4,36},{8,40},{12,44},{16,48},{20,52},{24,56},{28,60},{32,0... | collective-permute-start | bytes 196616 | tf_op jit(solution)/shard_map/cond/branch_0_fun/while/body/eval_jaxpr/ppermute | solution.py:34
  92.6 5.9 %collective-permute-start.5 = (f32[128,128]{0,1:T(8,128)S(1)}, f32[128,128]{0,1:T(8,128)S(1)}, u32[]{:S(2)}, u32[]{:S(2)}) collective-permute-start(f32[128,128]{0,1:T(8,128)S(1)} %add.230), channel_id=1, source_target_pairs={{0,128},{4,132},{8,136},{12,140},{16,144},{20,148},{24,152},{28,15... | collective-permute-start | bytes 196616 | tf_op jit(solution)/shard_map/cond/branch_0_fun/while/body/eval_jaxpr/ppermute | solution.py:34
  122.1 13.3 %collective-permute-start.6 = (f32[1024,128]{0,1:T(8,128)S(1)}, f32[1024,128]{0,1:T(8,128)S(1)}, u32[]{:S(2)}, u32[]{:S(2)}) collective-permute-start(f32[1024,128]{0,1:T(8,128)S(1)} %fusion.44), channel_id=1, source_target_pairs={{0,1},{1,0},{2,3},{3,2},{4,5},{5,4},{6,7},{7,6},{8,9},{9,8},{10,11... | collective-permute-start | bytes 1572872 | tf_op jit(solution)/shard_map/cond/branch_0_fun/while/body/eval_jaxpr/ppermute | solution.py:34
  135.4 10.8 %collective-permute-start.7 = (f32[1024,128]{0,1:T(8,128)S(1)}, f32[1024,128]{0,1:T(8,128)S(1)}, u32[]{:S(2)}, u32[]{:S(2)}) collective-permute-start(f32[1024,128]{0,1:T(8,128)S(1)} %add.232), channel_id=1, source_target_pairs={{0,2},{1,3},{2,0},{3,1},{4,6},{5,7},{6,4},{7,5},{8,10},{9,11},{10,... | collective-permute-start | bytes 1572872 | tf_op jit(solution)/shard_map/cond/branch_0_fun/while/body/eval_jaxpr/ppermute | solution.py:34
  158.2 8.3 %collective-permute-start.11 = (f32[128,128]{1,0:T(8,128)S(1)}, f32[128,128]{1,0:T(8,128)S(1)}, u32[]{:S(2)}, u32[]{:S(2)}) collective-permute-start(f32[128,128]{1,0:T(8,128)S(1)} %add.236), channel_id=1, source_target_pairs={{0,32},{4,36},{8,40},{12,44},{16,48},{20,52},{24,56},{28,60},{32,0... | collective-permute-start | bytes 196616 | tf_op jit(solution)/shard_map/cond/branch_0_fun/while/body/eval_jaxpr/ppermute | solution.py:34
  170.8 5.9 %collective-permute-start.13 = (f32[128,128]{1,0:T(8,128)S(1)}, f32[128,128]{1,0:T(8,128)S(1)}, u32[]{:S(2)}, u32[]{:S(2)}) collective-permute-start(f32[128,128]{1,0:T(8,128)S(1)} %add.238), channel_id=1, source_target_pairs={{0,128},{4,132},{8,136},{12,140},{16,144},{20,148},{24,152},{28,15... | collective-permute-start | bytes 196616 | tf_op jit(solution)/shard_map/cond/branch_0_fun/while/body/eval_jaxpr/ppermute | solution.py:34
  183.8 6.0 %collective-permute-start.2 = (f32[128,128]{0,1:T(8,128)S(1)}, f32[128,128]{0,1:T(8,128)S(1)}, u32[]{:S(2)}, u32[]{:S(2)}) collective-permute-start(f32[128,128]{0,1:T(8,128)S(1)} %add.227), channel_id=1, source_target_pairs={{0,16},{4,20},{8,24},{12,28},{16,0},{20,4},{24,8},{28,12},{32,48},... | collective-permute-start | bytes 196616 | tf_op jit(solution)/shard_map/cond/branch_0_fun/while/body/eval_jaxpr/ppermute | solution.py:34
  189.7 8.4 %collective-permute-start.3 = (f32[128,128]{0,1:T(8,128)S(1)}, f32[128,128]{0,1:T(8,128)S(1)}, u32[]{:S(2)}, u32[]{:S(2)}) collective-permute-start(f32[128,128]{0,1:T(8,128)S(1)} %add.228), channel_id=1, source_target_pairs={{0,32},{4,36},{8,40},{12,44},{16,48},{20,52},{24,56},{28,60},{32,0... | collective-permute-start | bytes 196616 | tf_op jit(solution)/shard_map/cond/branch_0_fun/while/body/eval_jaxpr/ppermute | solution.py:34
  202.9 5.9 %collective-permute-start.5 = (f32[128,128]{0,1:T(8,128)S(1)}, f32[128,128]{0,1:T(8,128)S(1)}, u32[]{:S(2)}, u32[]{:S(2)}) collective-permute-start(f32[128,128]{0,1:T(8,128)S(1)} %add.230), channel_id=1, source_target_pairs={{0,128},{4,132},{8,136},{12,140},{16,144},{20,148},{24,152},{28,15... | collective-permute-start | bytes 196616 | tf_op jit(solution)/shard_map/cond/branch_0_fun/while/body/eval_jaxpr/ppermute | solution.py:34
  232.5 14.1 %collective-permute-start.6 = (f32[1024,128]{0,1:T(8,128)S(1)}, f32[1024,128]{0,1:T(8,128)S(1)}, u32[]{:S(2)}, u32[]{:S(2)}) collective-permute-start(f32[1024,128]{0,1:T(8,128)S(1)} %fusion.44), channel_id=1, source_target_pairs={{0,1},{1,0},{2,3},{3,2},{4,5},{5,4},{6,7},{7,6},{8,9},{9,8},{10,11... | collective-permute-start | bytes 1572872 | tf_op jit(solution)/shard_map/cond/branch_0_fun/while/body/eval_jaxpr/ppermute | solution.py:34
  246.7 10.8 %collective-permute-start.7 = (f32[1024,128]{0,1:T(8,128)S(1)}, f32[1024,128]{0,1:T(8,128)S(1)}, u32[]{:S(2)}, u32[]{:S(2)}) collective-permute-start(f32[1024,128]{0,1:T(8,128)S(1)} %add.232), channel_id=1, source_target_pairs={{0,2},{1,3},{2,0},{3,1},{4,6},{5,7},{6,4},{7,5},{8,10},{9,11},{10,... | collective-permute-start | bytes 1572872 | tf_op jit(solution)/shard_map/cond/branch_0_fun/while/body/eval_jaxpr/ppermute | solution.py:34
  263.8 6.0 %collective-permute-start.10 = (f32[128,128]{1,0:T(8,128)S(1)}, f32[128,128]{1,0:T(8,128)S(1)}, u32[]{:S(2)}, u32[]{:S(2)}) collective-permute-start(f32[128,128]{1,0:T(8,128)S(1)} %add.235), channel_id=1, source_target_pairs={{0,16},{4,20},{8,24},{12,28},{16,0},{20,4},{24,8},{28,12},{32,48},... | collective-permute-start | bytes 196616 | tf_op jit(solution)/shard_map/cond/branch_0_fun/while/body/eval_jaxpr/ppermute | solution.py:34
  269.8 8.3 %collective-permute-start.11 = (f32[128,128]{1,0:T(8,128)S(1)}, f32[128,128]{1,0:T(8,128)S(1)}, u32[]{:S(2)}, u32[]{:S(2)}) collective-permute-start(f32[128,128]{1,0:T(8,128)S(1)} %add.236), channel_id=1, source_target_pairs={{0,32},{4,36},{8,40},{12,44},{16,48},{20,52},{24,56},{28,60},{32,0... | collective-permute-start | bytes 196616 | tf_op jit(solution)/shard_map/cond/branch_0_fun/while/body/eval_jaxpr/ppermute | solution.py:34
  283.1 5.9 %collective-permute-start.13 = (f32[128,128]{1,0:T(8,128)S(1)}, f32[128,128]{1,0:T(8,128)S(1)}, u32[]{:S(2)}, u32[]{:S(2)}) collective-permute-start(f32[128,128]{1,0:T(8,128)S(1)} %add.238), channel_id=1, source_target_pairs={{0,128},{4,132},{8,136},{12,140},{16,144},{20,148},{24,152},{28,15... | collective-permute-start | bytes 196616 | tf_op jit(solution)/shard_map/cond/branch_0_fun/while/body/eval_jaxpr/ppermute | solution.py:34
  301.7 8.6 %collective-permute-start.3 = (f32[128,128]{0,1:T(8,128)S(1)}, f32[128,128]{0,1:T(8,128)S(1)}, u32[]{:S(2)}, u32[]{:S(2)}) collective-permute-start(f32[128,128]{0,1:T(8,128)S(1)} %add.228), channel_id=1, source_target_pairs={{0,32},{4,36},{8,40},{12,44},{16,48},{20,52},{24,56},{28,60},{32,0... | collective-permute-start | bytes 196616 | tf_op jit(solution)/shard_map/cond/branch_0_fun/while/body/eval_jaxpr/ppermute | solution.py:34
  344.3 14.6 %collective-permute-start.6 = (f32[1024,128]{0,1:T(8,128)S(1)}, f32[1024,128]{0,1:T(8,128)S(1)}, u32[]{:S(2)}, u32[]{:S(2)}) collective-permute-start(f32[1024,128]{0,1:T(8,128)S(1)} %fusion.44), channel_id=1, source_target_pairs={{0,1},{1,0},{2,3},{3,2},{4,5},{5,4},{6,7},{7,6},{8,9},{9,8},{10,11... | collective-permute-start | bytes 1572872 | tf_op jit(solution)/shard_map/cond/branch_0_fun/while/body/eval_jaxpr/ppermute | solution.py:34
  358.9 10.8 %collective-permute-start.7 = (f32[1024,128]{0,1:T(8,128)S(1)}, f32[1024,128]{0,1:T(8,128)S(1)}, u32[]{:S(2)}, u32[]{:S(2)}) collective-permute-start(f32[1024,128]{0,1:T(8,128)S(1)} %add.232), channel_id=1, source_target_pairs={{0,2},{1,3},{2,0},{3,1},{4,6},{5,7},{6,4},{7,5},{8,10},{9,11},{10,... | collective-permute-start | bytes 1572872 | tf_op jit(solution)/shard_map/cond/branch_0_fun/while/body/eval_jaxpr/ppermute | solution.py:34
  381.7 8.3 %collective-permute-start.11 = (f32[128,128]{1,0:T(8,128)S(1)}, f32[128,128]{1,0:T(8,128)S(1)}, u32[]{:S(2)}, u32[]{:S(2)}) collective-permute-start(f32[128,128]{1,0:T(8,128)S(1)} %add.236), channel_id=1, source_target_pairs={{0,32},{4,36},{8,40},{12,44},{16,48},{20,52},{24,56},{28,60},{32,0... | collective-permute-start | bytes 196616 | tf_op jit(solution)/shard_map/cond/branch_0_fun/while/body/eval_jaxpr/ppermute | solution.py:34
  413.4 8.9 %collective-permute-start.3 = (f32[128,128]{0,1:T(8,128)S(1)}, f32[128,128]{0,1:T(8,128)S(1)}, u32[]{:S(2)}, u32[]{:S(2)}) collective-permute-start(f32[128,128]{0,1:T(8,128)S(1)} %add.228), channel_id=1, source_target_pairs={{0,32},{4,36},{8,40},{12,44},{16,48},{20,52},{24,56},{28,60},{32,0... | collective-permute-start | bytes 196616 | tf_op jit(solution)/shard_map/cond/branch_0_fun/while/body/eval_jaxpr/ppermute | solution.py:34
  456.5 14.8 %collective-permute-start.6 = (f32[1024,128]{0,1:T(8,128)S(1)}, f32[1024,128]{0,1:T(8,128)S(1)}, u32[]{:S(2)}, u32[]{:S(2)}) collective-permute-start(f32[1024,128]{0,1:T(8,128)S(1)} %fusion.44), channel_id=1, source_target_pairs={{0,1},{1,0},{2,3},{3,2},{4,5},{5,4},{6,7},{7,6},{8,9},{9,8},{10,11... | collective-permute-start | bytes 1572872 | tf_op jit(solution)/shard_map/cond/branch_0_fun/while/body/eval_jaxpr/ppermute | solution.py:34
  471.4 10.8 %collective-permute-start.7 = (f32[1024,128]{0,1:T(8,128)S(1)}, f32[1024,128]{0,1:T(8,128)S(1)}, u32[]{:S(2)}, u32[]{:S(2)}) collective-permute-start(f32[1024,128]{0,1:T(8,128)S(1)} %add.232), channel_id=1, source_target_pairs={{0,2},{1,3},{2,0},{3,1},{4,6},{5,7},{6,4},{7,5},{8,10},{9,11},{10,... | collective-permute-start | bytes 1572872 | tf_op jit(solution)/shard_map/cond/branch_0_fun/while/body/eval_jaxpr/ppermute | solution.py:34
  494.2 8.3 %collective-permute-start.11 = (f32[128,128]{1,0:T(8,128)S(1)}, f32[128,128]{1,0:T(8,128)S(1)}, u32[]{:S(2)}, u32[]{:S(2)}) collective-permute-start(f32[128,128]{1,0:T(8,128)S(1)} %add.236), channel_id=1, source_target_pairs={{0,32},{4,36},{8,40},{12,44},{16,48},{20,52},{24,56},{28,60},{32,0... | collective-permute-start | bytes 196616 | tf_op jit(solution)/shard_map/cond/branch_0_fun/while/body/eval_jaxpr/ppermute | solution.py:34
  (37 other events, 273.1 us)

commit v9 on v8

--- a/solution.py
+++ b/solution.py
@@ -22,7 +22,6 @@
 TILES_G = WIDTH // CORES // 8
 KINDS = 4
 TILES = KINDS * TILES_G
-LATE = TILES - TILES_G
 NEAR_LAST = (4, 3, 5, 2, 6, 1, 7, 0)
 TOLERANCE = 4e-4
 
@@ -149,6 +148,19 @@
             device_id=where, device_id_type=MESH,
         )
 
+    barrier = pltpu.get_barrier_semaphore()
+    near_x = [dict(cols=h) for h in (g_next, g_prev)]
+    near_z = [dict(pts=device(peer(k))) for k in (1, ZS - 1)]
+    near_y = [dict(pts=device(peer(k))) for k in (ZS, (YS - 1) * ZS)]
+    next_z = [dict(pts=device(peer(k))) for k in (2, ZS - 2)]
+    neighbours = [dict(pts=before), dict(pts=after)] + near_x + near_z + near_y
+
+    def tell(sem, devices):
+        for one in devices:
+            pl.semaphore_signal(sem, inc=1, device_id=one, device_id_type=MESH)
+
+    tell(barrier, neighbours)
+
     cov_copy = pltpu.make_async_copy(cov, covv, c_sem)
     own_copy = pltpu.make_async_copy(start, win.at[1], l_sem)
     own_copy.start()
@@ -159,18 +171,6 @@
 
     cov_copy.start()
 
-    barrier = pltpu.get_barrier_semaphore()
-    near_x = [dict(cols=h) for h in (g_next, g_prev)]
-    near_z = [dict(pts=device(peer(k))) for k in (1, ZS - 1)]
-    near_y = [dict(pts=device(peer(k))) for k in (ZS, (YS - 1) * ZS)]
-    next_z = [dict(pts=device(peer(k))) for k in (2, ZS - 2)]
-    neighbours = [dict(pts=before), dict(pts=after)] + near_x + near_z + near_y
-
-    def tell(sem, devices):
-        for one in devices:
-            pl.semaphore_signal(sem, inc=1, device_id=one, device_id_type=MESH)
-
-    tell(barrier, neighbours)
     pl.semaphore_wait(barrier, len(neighbours))
     tell(word.at[0], near_z)
     tell(word.at[1], near_x)
@@ -316,8 +316,9 @@
             part = block[core * WIDTH // CORES:(core + 1) * WIDTH // CORES]
             tb[core, kind * TILES_G:(kind + 1) * TILES_G] = part.reshape(TILES_G, 8, WIDTH)
 
-    def core_sum(first, count, send, recv):
-        part = pl.ds(first, count)
+    def core_sum(kind):
+        part = pl.ds(kind * TILES_G, TILES_G)
+        send, recv = p1_s.at[kind], p1_r.at[kind]
         copy = remote(tb.at[1 - c, part], r1.at[part], send, recv, pts=sibling)
         return copy, part
 
@@ -356,7 +357,7 @@
     acc[...] = jnp.zeros_like(acc)
     acc2[...] = jnp.zeros_like(acc2)
     place(3, quarters(dot_t(vhl[g], vhl[g]), WIDTH, WIDTH))
-    own_core, own_part = core_sum(LATE, TILES_G, p1_s.at[0], p1_r.at[0])
+    own_core, own_part = core_sum(3)
     own_core.start()
 
     for j in range(ROW_BLOCKS):
@@ -396,16 +397,18 @@
     place(1, quarters(acc2[...], WIDTH, WIDTH))
     place(2, quarters(acc[2 * WIDTH:], WIDTH, WIDTH))
 
-    late_core, late_part = core_sum(0, LATE, p1_s.at[1], p1_r.at[1])
-    late_core.start()
-    late_core.wait_recv()
-    s1[late_part] = tb[c, late_part] + r1[late_part]
-
+    late = [core_sum(kind) for kind in (1, 0, 2)]
+    for copy, _ in late:
+        copy.start()
     pl.semaphore_wait(word.at[5], 2)
-    for far in NEAR_LAST:
-        scatter_prev(lax.rem(z + far, ZS)).start()
-    scatter_rows(0)
-    scatter_rows(2)
+    for (copy, tiles_of), y_to in zip(late, (None, 0, 2)):
+        copy.wait_recv()
+        s1[tiles_of] = tb[c, tiles_of] + r1[tiles_of]
+        if y_to is None:
+            for far in NEAR_LAST:
+                scatter_prev(lax.rem(z + far, ZS)).start()
+        else:
+            scatter_rows(y_to)
 
     for r in range(ROW_BLOCKS):
         @pl.when(jnp.logical_not(goes_left(r)))
@@ -436,7 +439,7 @@
 
     def core_share(k, n):
         ref = gb.at[lax.rem(g + k, GROUPS), c, of_set(n)]
-        return remote(ref, ref, p6_s, p6_r, pts=sibling)
+        return remote(ref, ref, p6_s, p6_r.at[n], pts=sibling)
 
     for n in (3, 0, 2):
         @pl.when(y == n)
@@ -451,10 +454,21 @@
             x_share(k, n).start()
         core_share(0, n).start()
 
-    for n in (3, 0, 2):
+    def pass_to_core(n):
         for k in (1, 3, 2):
             arrived(p5_r.at[k, n], gb.at[g, c, of_set(n)])
             core_share(k, n).start()
+
+    def whole(n):
+        arrived(p6_r.at[n], gb.at[:, 1 - c, of_set(n)])
+
+    def part(a, kind):
+        return jnp.concatenate(
+            [gb[a, core, kind * TILES_G:(kind + 1) * TILES_G].reshape(WIDTH // CORES, WIDTH) for core in range(CORES)], axis=0
+        )
+
+    pass_to_core(3)
+    pass_to_core(0)
     arrived(rest_r.at[0], several(3))
     arrived(rest_r.at[1], several(3))
     arrived(rest_r.at[2], several(4))
@@ -470,13 +484,7 @@
         def _():
             keep_split(g_prev, r)
 
-    arrived(p6_r, gb.at[:, 1 - c, pl.ds(0, TILES - TILES_G)])
-
-    def part(a, kind):
-        return jnp.concatenate(
-            [gb[a, core, kind * TILES_G:(kind + 1) * TILES_G].reshape(WIDTH // CORES, WIDTH) for core in range(CORES)], axis=0
-        )
-
+    whole(3)
     diag = [part(a, 3) for a in range(GROUPS)]
     down = [lax.rsqrt(jnp.sum(d * eye, axis=1, keepdims=True)) for d in diag]
     across = [lax.rsqrt(jnp.sum(d * eye, axis=0, keepdims=True)) for d in diag]
@@ -487,10 +495,14 @@
 
     for a in range(GROUPS):
         put(a, a, diag[a])
+    pass_to_core(2)
+    whole(0)
+    for a in range(GROUPS):
         h = (a + 1) % GROUPS
         block = part(a, 0)
         put(a, h, block)
         put(h, a, block.T)
+    whole(2)
     for a in range(GROUPS // 2):
         h = a + GROUPS // 2
         block = part((a + 1) % GROUPS, 2) + part((a + 3) % GROUPS, 2).T
@@ -589,7 +601,8 @@
     to_near.wait_send()
     arrived(v_s, vall.at[:3])
     own_core.wait_send()
-    late_core.wait_send()
+    for copy, _ in late:
+        copy.wait_send()
     arrived(p2_s, s1.at[pl.ds(0, TILES - 1)])
 
     @pl.when(y == 1)
@@ -655,11 +668,11 @@
             dma, dma,
             dma, dma((ROW_BLOCKS,)), dma, dma,
             dma, dma((ROW_BLOCKS,)), dma((ROW_BLOCKS,)), dma((4,)),
-            dma((2,)), dma((2,)),
+            dma((KINDS,)), dma((KINDS,)),
             dma, dma, dma,
             dma, dma((KINDS,)),
             dma, dma((GROUPS, KINDS)),
-            dma, dma,
+            dma, dma((KINDS,)),
         ],
         compiler_params=pltpu.CompilerParams(
             collective_id=0, has_side_effects=True, vmem_limit_bytes=56 * 1024 * 1024

time: 515 us -> 513 us (level)
  waiting for transfers between devices: 283 us -> 276 us
    ppermute x56, waiting for transfers between devices: 277 us -> 270 us  [total(): value = value + lax.ppermute(value, axis, pairs)]
where the time goes in v9:
time: 513 us
  waiting for transfers between devices  276 us (54%)
  other arithmetic  93.3 us (18%)
  starting transfers between devices  65.8 us (13%)
  Pallas kernels  44.2 us (9%)
  matrix products  18.2 us (4%)
  loops' own time  8.38 us (2%)
  local copies, waits for them, and re-layouts  6.85 us (1%)
    ppermute x56, waiting for transfers between devices, total(): value = value + lax.ppermute(value, axis, pairs)  270 us
    ppermute x56, starting transfers between devices, total(): value = value + lax.ppermute(value, axis, pairs)  60.6 us
    another operation x12, other arithmetic, step(): lower = jnp.linalg.cholesky(gram)  49.8 us
    pallas_call x1, Pallas kernels, fast(): pl.pallas_call(kernel, out_shape=(pltpu.VMEM((ROWS, WIDTH), F32), pltpu.S...  44.2 us
    another operation x8, other arithmetic, step(): lax.linalg.triangular_solve(lower, local, left_side=False, lower=True, tr...  41.8 us
  transfers between devices with their start and end apart: 58, of which 57 were waited for; matrix products, arithmetic and copies ran while one was open for 1% of the time, Pallas kernels for 0%

profile of v9, /device:TPU:6, one launch (start us, length us, event | category | flops | bytes accessed | tf_op | source)
XLA Modules:
  0.0 513.2 jit_solution(9974315796333472475)
XLA Ops:
  0.0 44.2 %shard_map.48 = (f32[1024,128]{1,0:T(8,128)S(1)}, s32[1,1]{1,0:T(1,128)S(4)}) custom-call(f32[1024,128]{1,0:T(8,128)} %start.1, f32[8,8,128,128]{3,2,1,0:T(8,128)} %cov.1, s32[8,8]{1,0:T(8,128)} %col_in.1, s32[4]{0:T(128)} %order_in.1), custom_call_target="tpu_custom_call" | custom-call | tf_op jit(solution)/shard_map/pallas_call | solution.py:625
  44.3 468.2 %conditional.1 = (f32[1024,128]{1,0:T(8,128)S(1)}) conditional(s32[]{:T(128)} %bitcast.11, (f32[1024,128]{1,0:T(8,128)S(1)}, s32[8,8]{1,0:T(8,128)S(1)}, f32[8,8,128,128]{3,2,1,0:T(8,128)}, s32[4]{0:T(128)S(1)}) %tuple.55, f32[1024,128]{1,0:T(8,128)S(1)} %get-tuple-element.156), branch_computations={%region_0.6_spmd, %region_6.7_spmd} | conditional | flops 2417838080 | bytes 44441020 | solution.py:685
  50.2 6.1 %collective-permute-done.14 = f32[1024,128]{1,0:T(8,128)S(1)} collective-permute-done((f32[1024,128]{1,0:T(8,128)S(1)}, f32[1024,128]{1,0:T(8,128)S(1)}, u32[]{:S(2)}, u32[]{:S(2)}) %collective-permute-start.14) | collective-permute-done | bytes 524320 | tf_op jit(solution)/shard_map/cond/branch_0_fun/ppermute | solution.py:49
  59.1 7.9 %fusion.10 = f32[8,128,128,1]{1,2,3,0:T(8,128)S(1)} fusion(f32[8,8,128,128]{3,2,1,0:T(8,128)} %bitcast.52, f32[8,8,128,128]{3,2,1,0:T(8,128)} %get-tuple-element.150), kind=kOutput, calls=%fused_computation.26 | convolution fusion | flops 1610612736 | bytes 8912896 | tf_op jit(solution)/shard_map/cond/branch_0_fun/rsab,rsbk->rak/dot_general | solution.py:79
  67.3 444.7 %while.14 = (s32[]{:T(128)}, f32[1024,128]{0,1:T(8,128)S(1)}, s32[]{:T(128)}, s32[4]{0:T(128)S(1)}, s32[]{:T(128)}, /*index=5*/s32[]{:T(128)}, u32[]{:T(128)}) while((s32[]{:T(128)}, f32[1024,128]{0,1:T(8,128)S(1)}, s32[]{:T(128)}, s32[4]{0:T(128)S(1)}, s32[]{:T(128)}, /*index=5*/s32[]{:T(128)}, u32[]{:T(128)}) %tuple.48), condition=%wide.region_5.5_spmd, body=%wide.region_2.4_spmd.sunk | while | flops 806436992 | bytes 17696444 | solution.py:97
  80.7 7.4 %collective-permute-done.3 = f32[128,128]{0,1:T(8,128)S(1)} collective-permute-done((f32[128,128]{0,1:T(8,128)S(1)}, f32[128,128]{0,1:T(8,128)S(1)}, u32[]{:S(2)}, u32[]{:S(2)}) %collective-permute-start.3) | collective-permute-done | bytes 65568 | tf_op jit(solution)/shard_map/cond/branch_0_fun/while/body/eval_jaxpr/ppermute | solution.py:33
  98.5 11.7 %cholesky.58 = f32[128,128]{1,0:T(8,128)S(1)} custom-call(f32[128,128]{1,0:T(8,128)S(1)} %fusion.42), custom_call_target="Cholesky" | custom-call | tf_op jit(solution)/shard_map/cond/branch_0_fun/while/body/eval_jaxpr/jit(cholesky)/cholesky | solution.py:86
  111.6 9.8 %custom-call.23 = f32[1,128,128]{1,2,0:T(8,128)S(1)} custom-call(f32[1,128,128]{2,1,0:T(8,128)S(1)} %fusion.43), custom_call_target="InvertDiagBlocksLowerTriangular" | custom-call | tf_op jit(solution)/shard_map/cond/branch_0_fun/while/body/eval_jaxpr/triangular_solve | solution.py:87
  122.2 13.4 %collective-permute-done.6 = f32[1024,128]{0,1:T(8,128)S(1)} collective-permute-done((f32[1024,128]{0,1:T(8,128)S(1)}, f32[1024,128]{0,1:T(8,128)S(1)}, u32[]{:S(2)}, u32[]{:S(2)}) %collective-permute-start.6) | collective-permute-done | bytes 524320 | tf_op jit(solution)/shard_map/cond/branch_0_fun/while/body/eval_jaxpr/ppermute | solution.py:33
  135.7 10.7 %collective-permute-done.7 = f32[1024,128]{0,1:T(8,128)S(1)} collective-permute-done((f32[1024,128]{0,1:T(8,128)S(1)}, f32[1024,128]{0,1:T(8,128)S(1)}, u32[]{:S(2)}, u32[]{:S(2)}) %collective-permute-start.7) | collective-permute-done | bytes 524320 | tf_op jit(solution)/shard_map/cond/branch_0_fun/while/body/eval_jaxpr/ppermute | solution.py:33
  159.6 7.2 %collective-permute-done.11 = f32[128,128]{1,0:T(8,128)S(1)} collective-permute-done((f32[128,128]{1,0:T(8,128)S(1)}, f32[128,128]{1,0:T(8,128)S(1)}, u32[]{:S(2)}, u32[]{:S(2)}) %collective-permute-start.11) | collective-permute-done | bytes 65568 | tf_op jit(solution)/shard_map/cond/branch_0_fun/while/body/eval_jaxpr/ppermute | solution.py:33
  184.4 5.5 %collective-permute-done.2 = f32[128,128]{0,1:T(8,128)S(1)} collective-permute-done((f32[128,128]{0,1:T(8,128)S(1)}, f32[128,128]{0,1:T(8,128)S(1)}, u32[]{:S(2)}, u32[]{:S(2)}) %collective-permute-start.2) | collective-permute-done | bytes 65568 | tf_op jit(solution)/shard_map/cond/branch_0_fun/while/body/eval_jaxpr/ppermute | solution.py:33
  208.9 11.7 %cholesky.58 = f32[128,128]{1,0:T(8,128)S(1)} custom-call(f32[128,128]{1,0:T(8,128)S(1)} %fusion.42), custom_call_target="Cholesky" | custom-call | tf_op jit(solution)/shard_map/cond/branch_0_fun/while/body/eval_jaxpr/jit(cholesky)/cholesky | solution.py:86
  222.0 9.8 %custom-call.23 = f32[1,128,128]{1,2,0:T(8,128)S(1)} custom-call(f32[1,128,128]{2,1,0:T(8,128)S(1)} %fusion.43), custom_call_target="InvertDiagBlocksLowerTriangular" | custom-call | tf_op jit(solution)/shard_map/cond/branch_0_fun/while/body/eval_jaxpr/triangular_solve | solution.py:87
  232.5 14.1 %collective-permute-done.6 = f32[1024,128]{0,1:T(8,128)S(1)} collective-permute-done((f32[1024,128]{0,1:T(8,128)S(1)}, f32[1024,128]{0,1:T(8,128)S(1)}, u32[]{:S(2)}, u32[]{:S(2)}) %collective-permute-start.6) | collective-permute-done | bytes 524320 | tf_op jit(solution)/shard_map/cond/branch_0_fun/while/body/eval_jaxpr/ppermute | solution.py:33
  246.8 10.7 %collective-permute-done.7 = f32[1024,128]{0,1:T(8,128)S(1)} collective-permute-done((f32[1024,128]{0,1:T(8,128)S(1)}, f32[1024,128]{0,1:T(8,128)S(1)}, u32[]{:S(2)}, u32[]{:S(2)}) %collective-permute-start.7) | collective-permute-done | bytes 524320 | tf_op jit(solution)/shard_map/cond/branch_0_fun/while/body/eval_jaxpr/ppermute | solution.py:33
  319.7 11.7 %cholesky.58 = f32[128,128]{1,0:T(8,128)S(1)} custom-call(f32[128,128]{1,0:T(8,128)S(1)} %fusion.42), custom_call_target="Cholesky" | custom-call | tf_op jit(solution)/shard_map/cond/branch_0_fun/while/body/eval_jaxpr/jit(cholesky)/cholesky | solution.py:86
  332.8 9.8 %custom-call.23 = f32[1,128,128]{1,2,0:T(8,128)S(1)} custom-call(f32[1,128,128]{2,1,0:T(8,128)S(1)} %fusion.43), custom_call_target="InvertDiagBlocksLowerTriangular" | custom-call | tf_op jit(solution)/shard_map/cond/branch_0_fun/while/body/eval_jaxpr/triangular_solve | solution.py:87
  343.4 14.3 %collective-permute-done.6 = f32[1024,128]{0,1:T(8,128)S(1)} collective-permute-done((f32[1024,128]{0,1:T(8,128)S(1)}, f32[1024,128]{0,1:T(8,128)S(1)}, u32[]{:S(2)}, u32[]{:S(2)}) %collective-permute-start.6) | collective-permute-done | bytes 524320 | tf_op jit(solution)/shard_map/cond/branch_0_fun/while/body/eval_jaxpr/ppermute | solution.py:33
  357.9 10.7 %collective-permute-done.7 = f32[1024,128]{0,1:T(8,128)S(1)} collective-permute-done((f32[1024,128]{0,1:T(8,128)S(1)}, f32[1024,128]{0,1:T(8,128)S(1)}, u32[]{:S(2)}, u32[]{:S(2)}) %collective-permute-start.7) | collective-permute-done | bytes 524320 | tf_op jit(solution)/shard_map/cond/branch_0_fun/while/body/eval_jaxpr/ppermute | solution.py:33
  431.7 11.7 %cholesky.58 = f32[128,128]{1,0:T(8,128)S(1)} custom-call(f32[128,128]{1,0:T(8,128)S(1)} %fusion.42), custom_call_target="Cholesky" | custom-call | tf_op jit(solution)/shard_map/cond/branch_0_fun/while/body/eval_jaxpr/jit(cholesky)/cholesky | solution.py:86
  444.8 9.8 %custom-call.23 = f32[1,128,128]{1,2,0:T(8,128)S(1)} custom-call(f32[1,128,128]{2,1,0:T(8,128)S(1)} %fusion.43), custom_call_target="InvertDiagBlocksLowerTriangular" | custom-call | tf_op jit(solution)/shard_map/cond/branch_0_fun/while/body/eval_jaxpr/triangular_solve | solution.py:87
  455.3 14.6 %collective-permute-done.6 = f32[1024,128]{0,1:T(8,128)S(1)} collective-permute-done((f32[1024,128]{0,1:T(8,128)S(1)}, f32[1024,128]{0,1:T(8,128)S(1)}, u32[]{:S(2)}, u32[]{:S(2)}) %collective-permute-start.6) | collective-permute-done | bytes 524320 | tf_op jit(solution)/shard_map/cond/branch_0_fun/while/body/eval_jaxpr/ppermute | solution.py:33
  470.1 10.7 %collective-permute-done.7 = f32[1024,128]{0,1:T(8,128)S(1)} collective-permute-done((f32[1024,128]{0,1:T(8,128)S(1)}, f32[1024,128]{0,1:T(8,128)S(1)}, u32[]{:S(2)}, u32[]{:S(2)}) %collective-permute-start.7) | collective-permute-done | bytes 524320 | tf_op jit(solution)/shard_map/cond/branch_0_fun/while/body/eval_jaxpr/ppermute | solution.py:33
  (211 shorter events, 241.2 us)
Async XLA Ops:
  44.3 12.0 %collective-permute-start.14 = (f32[1024,128]{1,0:T(8,128)S(1)}, f32[1024,128]{1,0:T(8,128)S(1)}, u32[]{:S(2)}, u32[]{:S(2)}) collective-permute-start(f32[1024,128]{1,0:T(8,128)S(1)} %get-tuple-element.148), channel_id=1, source_target_pairs={{0,4},{4,8},{8,12},{12,16},{16,20},{20,24},{24,28},{28,32},{32,36}... | collective-permute-start | bytes 1572872 | tf_op jit(solution)/shard_map/cond/branch_0_fun/ppermute | solution.py:49
  44.7 11.5 %collective-permute-start.15 = (f32[1024,128]{1,0:T(8,128)S(1)}, f32[1024,128]{1,0:T(8,128)S(1)}, u32[]{:S(2)}, u32[]{:S(2)}) collective-permute-start(f32[1024,128]{1,0:T(8,128)S(1)} %get-tuple-element.148), channel_id=1, source_target_pairs={{4,0},{8,4},{12,8},{16,12},{20,16},{24,20},{28,24},{32,28},{36,32}... | collective-permute-start | bytes 1572872 | tf_op jit(solution)/shard_map/cond/branch_0_fun/ppermute | solution.py:51
  79.2 9.0 %collective-permute-start.3 = (f32[128,128]{0,1:T(8,128)S(1)}, f32[128,128]{0,1:T(8,128)S(1)}, u32[]{:S(2)}, u32[]{:S(2)}) collective-permute-start(f32[128,128]{0,1:T(8,128)S(1)} %add.228), channel_id=1, source_target_pairs={{0,32},{4,36},{8,40},{12,44},{16,48},{20,52},{24,56},{28,60},{32,0... | collective-permute-start | bytes 196616 | tf_op jit(solution)/shard_map/cond/branch_0_fun/while/body/eval_jaxpr/ppermute | solution.py:33
  92.5 5.9 %collective-permute-start.5 = (f32[128,128]{0,1:T(8,128)S(1)}, f32[128,128]{0,1:T(8,128)S(1)}, u32[]{:S(2)}, u32[]{:S(2)}) collective-permute-start(f32[128,128]{0,1:T(8,128)S(1)} %add.230), channel_id=1, source_target_pairs={{0,128},{4,132},{8,136},{12,140},{16,144},{20,148},{24,152},{28,15... | collective-permute-start | bytes 196616 | tf_op jit(solution)/shard_map/cond/branch_0_fun/while/body/eval_jaxpr/ppermute | solution.py:33
  122.1 13.5 %collective-permute-start.6 = (f32[1024,128]{0,1:T(8,128)S(1)}, f32[1024,128]{0,1:T(8,128)S(1)}, u32[]{:S(2)}, u32[]{:S(2)}) collective-permute-start(f32[1024,128]{0,1:T(8,128)S(1)} %fusion.44), channel_id=1, source_target_pairs={{0,1},{1,0},{2,3},{3,2},{4,5},{5,4},{6,7},{7,6},{8,9},{9,8},{10,11... | collective-permute-start | bytes 1572872 | tf_op jit(solution)/shard_map/cond/branch_0_fun/while/body/eval_jaxpr/ppermute | solution.py:33
  135.6 10.8 %collective-permute-start.7 = (f32[1024,128]{0,1:T(8,128)S(1)}, f32[1024,128]{0,1:T(8,128)S(1)}, u32[]{:S(2)}, u32[]{:S(2)}) collective-permute-start(f32[1024,128]{0,1:T(8,128)S(1)} %add.232), channel_id=1, source_target_pairs={{0,2},{1,3},{2,0},{3,1},{4,6},{5,7},{6,4},{7,5},{8,10},{9,11},{10,... | collective-permute-start | bytes 1572872 | tf_op jit(solution)/shard_map/cond/branch_0_fun/while/body/eval_jaxpr/ppermute | solution.py:33
  158.4 8.4 %collective-permute-start.11 = (f32[128,128]{1,0:T(8,128)S(1)}, f32[128,128]{1,0:T(8,128)S(1)}, u32[]{:S(2)}, u32[]{:S(2)}) collective-permute-start(f32[128,128]{1,0:T(8,128)S(1)} %add.236), channel_id=1, source_target_pairs={{0,32},{4,36},{8,40},{12,44},{16,48},{20,52},{24,56},{28,60},{32,0... | collective-permute-start | bytes 196616 | tf_op jit(solution)/shard_map/cond/branch_0_fun/while/body/eval_jaxpr/ppermute | solution.py:33
  171.1 5.9 %collective-permute-start.13 = (f32[128,128]{1,0:T(8,128)S(1)}, f32[128,128]{1,0:T(8,128)S(1)}, u32[]{:S(2)}, u32[]{:S(2)}) collective-permute-start(f32[128,128]{1,0:T(8,128)S(1)} %add.238), channel_id=1, source_target_pairs={{0,128},{4,132},{8,136},{12,140},{16,144},{20,148},{24,152},{28,15... | collective-permute-start | bytes 196616 | tf_op jit(solution)/shard_map/cond/branch_0_fun/while/body/eval_jaxpr/ppermute | solution.py:33
  189.9 8.3 %collective-permute-start.3 = (f32[128,128]{0,1:T(8,128)S(1)}, f32[128,128]{0,1:T(8,128)S(1)}, u32[]{:S(2)}, u32[]{:S(2)}) collective-permute-start(f32[128,128]{0,1:T(8,128)S(1)} %add.228), channel_id=1, source_target_pairs={{0,32},{4,36},{8,40},{12,44},{16,48},{20,52},{24,56},{28,60},{32,0... | collective-permute-start | bytes 196616 | tf_op jit(solution)/shard_map/cond/branch_0_fun/while/body/eval_jaxpr/ppermute | solution.py:33
  202.9 5.9 %collective-permute-start.5 = (f32[128,128]{0,1:T(8,128)S(1)}, f32[128,128]{0,1:T(8,128)S(1)}, u32[]{:S(2)}, u32[]{:S(2)}) collective-permute-start(f32[128,128]{0,1:T(8,128)S(1)} %add.230), channel_id=1, source_target_pairs={{0,128},{4,132},{8,136},{12,140},{16,144},{20,148},{24,152},{28,15... | collective-permute-start | bytes 196616 | tf_op jit(solution)/shard_map/cond/branch_0_fun/while/body/eval_jaxpr/ppermute | solution.py:33
  232.4 14.2 %collective-permute-start.6 = (f32[1024,128]{0,1:T(8,128)S(1)}, f32[1024,128]{0,1:T(8,128)S(1)}, u32[]{:S(2)}, u32[]{:S(2)}) collective-permute-start(f32[1024,128]{0,1:T(8,128)S(1)} %fusion.44), channel_id=1, source_target_pairs={{0,1},{1,0},{2,3},{3,2},{4,5},{5,4},{6,7},{7,6},{8,9},{9,8},{10,11... | collective-permute-start | bytes 1572872 | tf_op jit(solution)/shard_map/cond/branch_0_fun/while/body/eval_jaxpr/ppermute | solution.py:33
  246.7 10.8 %collective-permute-start.7 = (f32[1024,128]{0,1:T(8,128)S(1)}, f32[1024,128]{0,1:T(8,128)S(1)}, u32[]{:S(2)}, u32[]{:S(2)}) collective-permute-start(f32[1024,128]{0,1:T(8,128)S(1)} %add.232), channel_id=1, source_target_pairs={{0,2},{1,3},{2,0},{3,1},{4,6},{5,7},{6,4},{7,5},{8,10},{9,11},{10,... | collective-permute-start | bytes 1572872 | tf_op jit(solution)/shard_map/cond/branch_0_fun/while/body/eval_jaxpr/ppermute | solution.py:33
  269.4 8.3 %collective-permute-start.11 = (f32[128,128]{1,0:T(8,128)S(1)}, f32[128,128]{1,0:T(8,128)S(1)}, u32[]{:S(2)}, u32[]{:S(2)}) collective-permute-start(f32[128,128]{1,0:T(8,128)S(1)} %add.236), channel_id=1, source_target_pairs={{0,32},{4,36},{8,40},{12,44},{16,48},{20,52},{24,56},{28,60},{32,0... | collective-permute-start | bytes 196616 | tf_op jit(solution)/shard_map/cond/branch_0_fun/while/body/eval_jaxpr/ppermute | solution.py:33
  282.3 5.9 %collective-permute-start.13 = (f32[128,128]{1,0:T(8,128)S(1)}, f32[128,128]{1,0:T(8,128)S(1)}, u32[]{:S(2)}, u32[]{:S(2)}) collective-permute-start(f32[128,128]{1,0:T(8,128)S(1)} %add.238), channel_id=1, source_target_pairs={{0,128},{4,132},{8,136},{12,140},{16,144},{20,148},{24,152},{28,15... | collective-permute-start | bytes 196616 | tf_op jit(solution)/shard_map/cond/branch_0_fun/while/body/eval_jaxpr/ppermute | solution.py:33
  301.0 8.3 %collective-permute-start.3 = (f32[128,128]{0,1:T(8,128)S(1)}, f32[128,128]{0,1:T(8,128)S(1)}, u32[]{:S(2)}, u32[]{:S(2)}) collective-permute-start(f32[128,128]{0,1:T(8,128)S(1)} %add.228), channel_id=1, source_target_pairs={{0,32},{4,36},{8,40},{12,44},{16,48},{20,52},{24,56},{28,60},{32,0... | collective-permute-start | bytes 196616 | tf_op jit(solution)/shard_map/cond/branch_0_fun/while/body/eval_jaxpr/ppermute | solution.py:33
  313.8 5.9 %collective-permute-start.5 = (f32[128,128]{0,1:T(8,128)S(1)}, f32[128,128]{0,1:T(8,128)S(1)}, u32[]{:S(2)}, u32[]{:S(2)}) collective-permute-start(f32[128,128]{0,1:T(8,128)S(1)} %add.230), channel_id=1, source_target_pairs={{0,128},{4,132},{8,136},{12,140},{16,144},{20,148},{24,152},{28,15... | collective-permute-start | bytes 196616 | tf_op jit(solution)/shard_map/cond/branch_0_fun/while/body/eval_jaxpr/ppermute | solution.py:33
  343.3 14.4 %collective-permute-start.6 = (f32[1024,128]{0,1:T(8,128)S(1)}, f32[1024,128]{0,1:T(8,128)S(1)}, u32[]{:S(2)}, u32[]{:S(2)}) collective-permute-start(f32[1024,128]{0,1:T(8,128)S(1)} %fusion.44), channel_id=1, source_target_pairs={{0,1},{1,0},{2,3},{3,2},{4,5},{5,4},{6,7},{7,6},{8,9},{9,8},{10,11... | collective-permute-start | bytes 1572872 | tf_op jit(solution)/shard_map/cond/branch_0_fun/while/body/eval_jaxpr/ppermute | solution.py:33
  357.8 10.8 %collective-permute-start.7 = (f32[1024,128]{0,1:T(8,128)S(1)}, f32[1024,128]{0,1:T(8,128)S(1)}, u32[]{:S(2)}, u32[]{:S(2)}) collective-permute-start(f32[1024,128]{0,1:T(8,128)S(1)} %add.232), channel_id=1, source_target_pairs={{0,2},{1,3},{2,0},{3,1},{4,6},{5,7},{6,4},{7,5},{8,10},{9,11},{10,... | collective-permute-start | bytes 1572872 | tf_op jit(solution)/shard_map/cond/branch_0_fun/while/body/eval_jaxpr/ppermute | solution.py:33
  380.6 8.3 %collective-permute-start.11 = (f32[128,128]{1,0:T(8,128)S(1)}, f32[128,128]{1,0:T(8,128)S(1)}, u32[]{:S(2)}, u32[]{:S(2)}) collective-permute-start(f32[128,128]{1,0:T(8,128)S(1)} %add.236), channel_id=1, source_target_pairs={{0,32},{4,36},{8,40},{12,44},{16,48},{20,52},{24,56},{28,60},{32,0... | collective-permute-start | bytes 196616 | tf_op jit(solution)/shard_map/cond/branch_0_fun/while/body/eval_jaxpr/ppermute | solution.py:33
  406.4 6.0 %collective-permute-start.2 = (f32[128,128]{0,1:T(8,128)S(1)}, f32[128,128]{0,1:T(8,128)S(1)}, u32[]{:S(2)}, u32[]{:S(2)}) collective-permute-start(f32[128,128]{0,1:T(8,128)S(1)} %add.227), channel_id=1, source_target_pairs={{0,16},{4,20},{8,24},{12,28},{16,0},{20,4},{24,8},{28,12},{32,48},... | collective-permute-start | bytes 196616 | tf_op jit(solution)/shard_map/cond/branch_0_fun/while/body/eval_jaxpr/ppermute | solution.py:33
  412.4 8.3 %collective-permute-start.3 = (f32[128,128]{0,1:T(8,128)S(1)}, f32[128,128]{0,1:T(8,128)S(1)}, u32[]{:S(2)}, u32[]{:S(2)}) collective-permute-start(f32[128,128]{0,1:T(8,128)S(1)} %add.228), channel_id=1, source_target_pairs={{0,32},{4,36},{8,40},{12,44},{16,48},{20,52},{24,56},{28,60},{32,0... | collective-permute-start | bytes 196616 | tf_op jit(solution)/shard_map/cond/branch_0_fun/while/body/eval_jaxpr/ppermute | solution.py:33
  455.2 14.7 %collective-permute-start.6 = (f32[1024,128]{0,1:T(8,128)S(1)}, f32[1024,128]{0,1:T(8,128)S(1)}, u32[]{:S(2)}, u32[]{:S(2)}) collective-permute-start(f32[1024,128]{0,1:T(8,128)S(1)} %fusion.44), channel_id=1, source_target_pairs={{0,1},{1,0},{2,3},{3,2},{4,5},{5,4},{6,7},{7,6},{8,9},{9,8},{10,11... | collective-permute-start | bytes 1572872 | tf_op jit(solution)/shard_map/cond/branch_0_fun/while/body/eval_jaxpr/ppermute | solution.py:33
  470.0 10.8 %collective-permute-start.7 = (f32[1024,128]{0,1:T(8,128)S(1)}, f32[1024,128]{0,1:T(8,128)S(1)}, u32[]{:S(2)}, u32[]{:S(2)}) collective-permute-start(f32[1024,128]{0,1:T(8,128)S(1)} %add.232), channel_id=1, source_target_pairs={{0,2},{1,3},{2,0},{3,1},{4,6},{5,7},{6,4},{7,5},{8,10},{9,11},{10,... | collective-permute-start | bytes 1572872 | tf_op jit(solution)/shard_map/cond/branch_0_fun/while/body/eval_jaxpr/ppermute | solution.py:33
  492.7 8.3 %collective-permute-start.11 = (f32[128,128]{1,0:T(8,128)S(1)}, f32[128,128]{1,0:T(8,128)S(1)}, u32[]{:S(2)}, u32[]{:S(2)}) collective-permute-start(f32[128,128]{1,0:T(8,128)S(1)} %add.236), channel_id=1, source_target_pairs={{0,32},{4,36},{8,40},{12,44},{16,48},{20,52},{24,56},{28,60},{32,0... | collective-permute-start | bytes 196616 | tf_op jit(solution)/shard_map/cond/branch_0_fun/while/body/eval_jaxpr/ppermute | solution.py:33
  (37 other events, 271.7 us)

commit v10 on v9

--- a/solution.py
+++ b/solution.py
@@ -300,7 +300,6 @@
         arrived(halo_r.at[j], win.at[0, pl.ds(0, BLOCK), :])
         split_window(far_side, r)
         image(r)
-        keep_split(g, r)
         if j == 0:
             pl.semaphore_wait(word.at[0], 2)
             tell(word.at[2], next_z)
@@ -318,7 +317,7 @@
 
     def core_sum(kind):
         part = pl.ds(kind * TILES_G, TILES_G)
-        send, recv = p1_s.at[kind], p1_r.at[kind]
+        send, recv = p1_s, p1_r.at[kind]
         copy = remote(tb.at[1 - c, part], r1.at[part], send, recv, pts=sibling)
         return copy, part
 
@@ -356,6 +355,8 @@
 
     acc[...] = jnp.zeros_like(acc)
     acc2[...] = jnp.zeros_like(acc2)
+    for r in range(ROW_BLOCKS):
+        keep_split(g, r)
     place(3, quarters(dot_t(vhl[g], vhl[g]), WIDTH, WIDTH))
     own_core, own_part = core_sum(3)
     own_core.start()
@@ -435,7 +436,7 @@
 
     def x_share(k, n):
         ref = gb.at[g, c, of_set(n)]
-        return remote(ref, ref, p5_s, p5_r.at[GROUPS - k, n], cols=lax.rem(g + k, GROUPS))
+        return remote(ref, ref, p5_s, p5_r.at[GROUPS - 1 - k, {3: 0, 0: 1, 2: 2}[n]], cols=lax.rem(g + k, GROUPS))
 
     def core_share(k, n):
         ref = gb.at[lax.rem(g + k, GROUPS), c, of_set(n)]
@@ -456,7 +457,7 @@
 
     def pass_to_core(n):
         for k in (1, 3, 2):
-            arrived(p5_r.at[k, n], gb.at[g, c, of_set(n)])
+            arrived(p5_r.at[k - 1, {3: 0, 0: 1, 2: 2}[n]], gb.at[g, c, of_set(n)])
             core_share(k, n).start()
 
     def whole(n):
@@ -600,9 +601,7 @@
     arrived(halo_s, win.at[0])
     to_near.wait_send()
     arrived(v_s, vall.at[:3])
-    own_core.wait_send()
-    for copy, _ in late:
-        copy.wait_send()
+    arrived(p1_s, tb.at[0])
     arrived(p2_s, s1.at[pl.ds(0, TILES - 1)])
 
     @pl.when(y == 1)
@@ -668,10 +667,10 @@
             dma, dma,
             dma, dma((ROW_BLOCKS,)), dma, dma,
             dma, dma((ROW_BLOCKS,)), dma((ROW_BLOCKS,)), dma((4,)),
-            dma((KINDS,)), dma((KINDS,)),
+            dma, dma((KINDS,)),
             dma, dma, dma,
             dma, dma((KINDS,)),
-            dma, dma((GROUPS, KINDS)),
+            dma, dma((GROUPS - 1, KINDS - 1)),
             dma, dma((KINDS,)),
         ],
         compiler_params=pltpu.CompilerParams(

time: 513 us -> 513 us (level)
  waiting for transfers between devices: 276 us -> 308 us
  starting transfers between devices: 65.8 us -> 34.6 us
    ppermute x56, waiting for transfers between devices: 270 us -> 302 us  [total(): value = value + lax.ppermute(value, axis, pairs)]
    ppermute x56, starting transfers between devices: 60.6 us -> 29.4 us  [total(): value = value + lax.ppermute(value, axis, pairs)]
where the time goes in v10:
time: 513 us
  waiting for transfers between devices  308 us (60%)
  other arithmetic  93.3 us (18%)
  Pallas kernels  44 us (9%)
  starting transfers between devices  34.6 us (7%)
  matrix products  18.2 us (4%)
  loops' own time  8.4 us (2%)
  local copies, waits for them, and re-layouts  6.85 us (1%)
    ppermute x56, waiting for transfers between devices, total(): value = value + lax.ppermute(value, axis, pairs)  302 us
    another operation x12, other arithmetic, step(): lower = jnp.linalg.cholesky(gram)  49.8 us
    pallas_call x1, Pallas kernels, fast(): pl.pallas_call(kernel, out_shape=(pltpu.VMEM((ROWS, WIDTH), F32), pltpu.S...  44 us
    another operation x8, other arithmetic, step(): lax.linalg.triangular_solve(lower, local, left_side=False, lower=True, tr...  41.8 us
    ppermute x56, starting transfers between devices, total(): value = value + lax.ppermute(value, axis, pairs)  29.4 us
  transfers between devices with their start and end apart: 58, of which 57 were waited for; matrix products, arithmetic and copies ran while one was open for 1% of the time, Pallas kernels for 0%

profile of v10, /device:TPU:6, one launch (start us, length us, event | category | flops | bytes accessed | tf_op | source)
XLA Modules:
  0.0 513.5 jit_solution(15986976539320499377)
XLA Ops:
  0.0 44.0 %shard_map.48 = (f32[1024,128]{1,0:T(8,128)S(1)}, s32[1,1]{1,0:T(1,128)S(4)}) custom-call(f32[1024,128]{1,0:T(8,128)} %start.1, f32[8,8,128,128]{3,2,1,0:T(8,128)} %cov.1, s32[8,8]{1,0:T(8,128)} %col_in.1, s32[4]{0:T(128)} %order_in.1), custom_call_target="tpu_custom_call" | custom-call | tf_op jit(solution)/shard_map/pallas_call | solution.py:624
  44.1 468.6 %conditional.1 = (f32[1024,128]{1,0:T(8,128)S(1)}) conditional(s32[]{:T(128)} %bitcast.11, (f32[1024,128]{1,0:T(8,128)S(1)}, s32[8,8]{1,0:T(8,128)S(1)}, f32[8,8,128,128]{3,2,1,0:T(8,128)}, s32[4]{0:T(128)S(1)}) %tuple.55, f32[1024,128]{1,0:T(8,128)S(1)} %get-tuple-element.156), branch_computations={%region_0.6_spmd, %region_6.7_spmd} | conditional | flops 2417838080 | bytes 44441020 | solution.py:684
  59.0 7.9 %fusion.10 = f32[8,128,128,1]{1,2,3,0:T(8,128)S(1)} fusion(f32[8,8,128,128]{3,2,1,0:T(8,128)} %bitcast.52, f32[8,8,128,128]{3,2,1,0:T(8,128)} %get-tuple-element.150), kind=kOutput, calls=%fused_computation.26 | convolution fusion | flops 1610612736 | bytes 8912896 | tf_op jit(solution)/shard_map/cond/branch_0_fun/rsab,rsbk->rak/dot_general | solution.py:79
  67.1 445.1 %while.14 = (s32[]{:T(128)}, f32[1024,128]{0,1:T(8,128)S(1)}, s32[]{:T(128)}, s32[4]{0:T(128)S(1)}, s32[]{:T(128)}, /*index=5*/s32[]{:T(128)}, u32[]{:T(128)}) while((s32[]{:T(128)}, f32[1024,128]{0,1:T(8,128)S(1)}, s32[]{:T(128)}, s32[4]{0:T(128)S(1)}, s32[]{:T(128)}, /*index=5*/s32[]{:T(128)}, u32[]{:T(128)}) %tuple.48), condition=%wide.region_5.5_spmd, body=%wide.region_2.4_spmd.sunk | while | flops 806436992 | bytes 17696444 | solution.py:97
  80.6 7.4 %collective-permute-done.3 = f32[128,128]{0,1:T(8,128)S(1)} collective-permute-done((f32[128,128]{0,1:T(8,128)S(1)}, f32[128,128]{0,1:T(8,128)S(1)}, u32[]{:S(2)}, u32[]{:S(2)}) %collective-permute-start.3) | collective-permute-done | bytes 65568 | tf_op jit(solution)/shard_map/cond/branch_0_fun/while/body/eval_jaxpr/ppermute | solution.py:33
  98.3 11.7 %cholesky.58 = f32[128,128]{1,0:T(8,128)S(1)} custom-call(f32[128,128]{1,0:T(8,128)S(1)} %fusion.42), custom_call_target="Cholesky" | custom-call | tf_op jit(solution)/shard_map/cond/branch_0_fun/while/body/eval_jaxpr/jit(cholesky)/cholesky | solution.py:86
  111.4 9.8 %custom-call.23 = f32[1,128,128]{1,2,0:T(8,128)S(1)} custom-call(f32[1,128,128]{2,1,0:T(8,128)S(1)} %fusion.43), custom_call_target="InvertDiagBlocksLowerTriangular" | custom-call | tf_op jit(solution)/shard_map/cond/branch_0_fun/while/body/eval_jaxpr/triangular_solve | solution.py:87
  122.0 13.8 %collective-permute-done.6 = f32[1024,128]{0,1:T(8,128)S(1)} collective-permute-done((f32[1024,128]{0,1:T(8,128)S(1)}, f32[1024,128]{0,1:T(8,128)S(1)}, u32[]{:S(2)}, u32[]{:S(2)}) %collective-permute-start.6) | collective-permute-done | bytes 524320 | tf_op jit(solution)/shard_map/cond/branch_0_fun/while/body/eval_jaxpr/ppermute | solution.py:33
  136.0 10.7 %collective-permute-done.7 = f32[1024,128]{0,1:T(8,128)S(1)} collective-permute-done((f32[1024,128]{0,1:T(8,128)S(1)}, f32[1024,128]{0,1:T(8,128)S(1)}, u32[]{:S(2)}, u32[]{:S(2)}) %collective-permute-start.7) | collective-permute-done | bytes 524320 | tf_op jit(solution)/shard_map/cond/branch_0_fun/while/body/eval_jaxpr/ppermute | solution.py:33
  159.2 7.8 %collective-permute-done.11 = f32[128,128]{1,0:T(8,128)S(1)} collective-permute-done((f32[128,128]{1,0:T(8,128)S(1)}, f32[128,128]{1,0:T(8,128)S(1)}, u32[]{:S(2)}, u32[]{:S(2)}) %collective-permute-start.11) | collective-permute-done | bytes 65568 | tf_op jit(solution)/shard_map/cond/branch_0_fun/while/body/eval_jaxpr/ppermute | solution.py:33
  209.3 11.7 %cholesky.58 = f32[128,128]{1,0:T(8,128)S(1)} custom-call(f32[128,128]{1,0:T(8,128)S(1)} %fusion.42), custom_call_target="Cholesky" | custom-call | tf_op jit(solution)/shard_map/cond/branch_0_fun/while/body/eval_jaxpr/jit(cholesky)/cholesky | solution.py:86
  222.4 9.8 %custom-call.23 = f32[1,128,128]{1,2,0:T(8,128)S(1)} custom-call(f32[1,128,128]{2,1,0:T(8,128)S(1)} %fusion.43), custom_call_target="InvertDiagBlocksLowerTriangular" | custom-call | tf_op jit(solution)/shard_map/cond/branch_0_fun/while/body/eval_jaxpr/triangular_solve | solution.py:87
  233.0 14.6 %collective-permute-done.6 = f32[1024,128]{0,1:T(8,128)S(1)} collective-permute-done((f32[1024,128]{0,1:T(8,128)S(1)}, f32[1024,128]{0,1:T(8,128)S(1)}, u32[]{:S(2)}, u32[]{:S(2)}) %collective-permute-start.6) | collective-permute-done | bytes 524320 | tf_op jit(solution)/shard_map/cond/branch_0_fun/while/body/eval_jaxpr/ppermute | solution.py:33
  247.7 10.7 %collective-permute-done.7 = f32[1024,128]{0,1:T(8,128)S(1)} collective-permute-done((f32[1024,128]{0,1:T(8,128)S(1)}, f32[1024,128]{0,1:T(8,128)S(1)}, u32[]{:S(2)}, u32[]{:S(2)}) %collective-permute-start.7) | collective-permute-done | bytes 524320 | tf_op jit(solution)/shard_map/cond/branch_0_fun/while/body/eval_jaxpr/ppermute | solution.py:33
  320.5 11.7 %cholesky.58 = f32[128,128]{1,0:T(8,128)S(1)} custom-call(f32[128,128]{1,0:T(8,128)S(1)} %fusion.42), custom_call_target="Cholesky" | custom-call | tf_op jit(solution)/shard_map/cond/branch_0_fun/while/body/eval_jaxpr/jit(cholesky)/cholesky | solution.py:86
  333.6 9.8 %custom-call.23 = f32[1,128,128]{1,2,0:T(8,128)S(1)} custom-call(f32[1,128,128]{2,1,0:T(8,128)S(1)} %fusion.43), custom_call_target="InvertDiagBlocksLowerTriangular" | custom-call | tf_op jit(solution)/shard_map/cond/branch_0_fun/while/body/eval_jaxpr/triangular_solve | solution.py:87
  344.2 14.4 %collective-permute-done.6 = f32[1024,128]{0,1:T(8,128)S(1)} collective-permute-done((f32[1024,128]{0,1:T(8,128)S(1)}, f32[1024,128]{0,1:T(8,128)S(1)}, u32[]{:S(2)}, u32[]{:S(2)}) %collective-permute-start.6) | collective-permute-done | bytes 524320 | tf_op jit(solution)/shard_map/cond/branch_0_fun/while/body/eval_jaxpr/ppermute | solution.py:33
  358.7 10.7 %collective-permute-done.7 = f32[1024,128]{0,1:T(8,128)S(1)} collective-permute-done((f32[1024,128]{0,1:T(8,128)S(1)}, f32[1024,128]{0,1:T(8,128)S(1)}, u32[]{:S(2)}, u32[]{:S(2)}) %collective-permute-start.7) | collective-permute-done | bytes 524320 | tf_op jit(solution)/shard_map/cond/branch_0_fun/while/body/eval_jaxpr/ppermute | solution.py:33
  383.2 6.9 %collective-permute-done.11 = f32[128,128]{1,0:T(8,128)S(1)} collective-permute-done((f32[128,128]{1,0:T(8,128)S(1)}, f32[128,128]{1,0:T(8,128)S(1)}, u32[]{:S(2)}, u32[]{:S(2)}) %collective-permute-start.11) | collective-permute-done | bytes 65568 | tf_op jit(solution)/shard_map/cond/branch_0_fun/while/body/eval_jaxpr/ppermute | solution.py:33
  432.0 11.7 %cholesky.58 = f32[128,128]{1,0:T(8,128)S(1)} custom-call(f32[128,128]{1,0:T(8,128)S(1)} %fusion.42), custom_call_target="Cholesky" | custom-call | tf_op jit(solution)/shard_map/cond/branch_0_fun/while/body/eval_jaxpr/jit(cholesky)/cholesky | solution.py:86
  445.1 9.8 %custom-call.23 = f32[1,128,128]{1,2,0:T(8,128)S(1)} custom-call(f32[1,128,128]{2,1,0:T(8,128)S(1)} %fusion.43), custom_call_target="InvertDiagBlocksLowerTriangular" | custom-call | tf_op jit(solution)/shard_map/cond/branch_0_fun/while/body/eval_jaxpr/triangular_solve | solution.py:87
  455.6 14.5 %collective-permute-done.6 = f32[1024,128]{0,1:T(8,128)S(1)} collective-permute-done((f32[1024,128]{0,1:T(8,128)S(1)}, f32[1024,128]{0,1:T(8,128)S(1)}, u32[]{:S(2)}, u32[]{:S(2)}) %collective-permute-start.6) | collective-permute-done | bytes 524320 | tf_op jit(solution)/shard_map/cond/branch_0_fun/while/body/eval_jaxpr/ppermute | solution.py:33
  470.3 10.7 %collective-permute-done.7 = f32[1024,128]{0,1:T(8,128)S(1)} collective-permute-done((f32[1024,128]{0,1:T(8,128)S(1)}, f32[1024,128]{0,1:T(8,128)S(1)}, u32[]{:S(2)}, u32[]{:S(2)}) %collective-permute-start.7) | collective-permute-done | bytes 524320 | tf_op jit(solution)/shard_map/cond/branch_0_fun/while/body/eval_jaxpr/ppermute | solution.py:33
  494.1 7.2 %collective-permute-done.11 = f32[128,128]{1,0:T(8,128)S(1)} collective-permute-done((f32[128,128]{1,0:T(8,128)S(1)}, f32[128,128]{1,0:T(8,128)S(1)}, u32[]{:S(2)}, u32[]{:S(2)}) %collective-permute-start.11) | collective-permute-done | bytes 65568 | tf_op jit(solution)/shard_map/cond/branch_0_fun/while/body/eval_jaxpr/ppermute | solution.py:33
  (211 shorter events, 237.8 us)
Async XLA Ops:
  44.1 12.0 %collective-permute-start.14 = (f32[1024,128]{1,0:T(8,128)S(1)}, f32[1024,128]{1,0:T(8,128)S(1)}, u32[]{:S(2)}, u32[]{:S(2)}) collective-permute-start(f32[1024,128]{1,0:T(8,128)S(1)} %get-tuple-element.148), channel_id=1, source_target_pairs={{0,4},{4,8},{8,12},{12,16},{16,20},{20,24},{24,28},{28,32},{32,36}... | collective-permute-start | bytes 1572872 | tf_op jit(solution)/shard_map/cond/branch_0_fun/ppermute | solution.py:49
  44.6 11.5 %collective-permute-start.15 = (f32[1024,128]{1,0:T(8,128)S(1)}, f32[1024,128]{1,0:T(8,128)S(1)}, u32[]{:S(2)}, u32[]{:S(2)}) collective-permute-start(f32[1024,128]{1,0:T(8,128)S(1)} %get-tuple-element.148), channel_id=1, source_target_pairs={{4,0},{8,4},{12,8},{16,12},{20,16},{24,20},{28,24},{32,28},{36,32}... | collective-permute-start | bytes 1572872 | tf_op jit(solution)/shard_map/cond/branch_0_fun/ppermute | solution.py:51
  79.0 9.0 %collective-permute-start.3 = (f32[128,128]{0,1:T(8,128)S(1)}, f32[128,128]{0,1:T(8,128)S(1)}, u32[]{:S(2)}, u32[]{:S(2)}) collective-permute-start(f32[128,128]{0,1:T(8,128)S(1)} %add.228), channel_id=1, source_target_pairs={{0,32},{4,36},{8,40},{12,44},{16,48},{20,52},{24,56},{28,60},{32,0... | collective-permute-start | bytes 196616 | tf_op jit(solution)/shard_map/cond/branch_0_fun/while/body/eval_jaxpr/ppermute | solution.py:33
  92.4 5.9 %collective-permute-start.5 = (f32[128,128]{0,1:T(8,128)S(1)}, f32[128,128]{0,1:T(8,128)S(1)}, u32[]{:S(2)}, u32[]{:S(2)}) collective-permute-start(f32[128,128]{0,1:T(8,128)S(1)} %add.230), channel_id=1, source_target_pairs={{0,128},{4,132},{8,136},{12,140},{16,144},{20,148},{24,152},{28,15... | collective-permute-start | bytes 196616 | tf_op jit(solution)/shard_map/cond/branch_0_fun/while/body/eval_jaxpr/ppermute | solution.py:33
  121.9 13.9 %collective-permute-start.6 = (f32[1024,128]{0,1:T(8,128)S(1)}, f32[1024,128]{0,1:T(8,128)S(1)}, u32[]{:S(2)}, u32[]{:S(2)}) collective-permute-start(f32[1024,128]{0,1:T(8,128)S(1)} %fusion.44), channel_id=1, source_target_pairs={{0,1},{1,0},{2,3},{3,2},{4,5},{5,4},{6,7},{7,6},{8,9},{9,8},{10,11... | collective-permute-start | bytes 1572872 | tf_op jit(solution)/shard_map/cond/branch_0_fun/while/body/eval_jaxpr/ppermute | solution.py:33
  135.9 10.8 %collective-permute-start.7 = (f32[1024,128]{0,1:T(8,128)S(1)}, f32[1024,128]{0,1:T(8,128)S(1)}, u32[]{:S(2)}, u32[]{:S(2)}) collective-permute-start(f32[1024,128]{0,1:T(8,128)S(1)} %add.232), channel_id=1, source_target_pairs={{0,2},{1,3},{2,0},{3,1},{4,6},{5,7},{6,4},{7,5},{8,10},{9,11},{10,... | collective-permute-start | bytes 1572872 | tf_op jit(solution)/shard_map/cond/branch_0_fun/while/body/eval_jaxpr/ppermute | solution.py:33
  158.6 8.5 %collective-permute-start.11 = (f32[128,128]{1,0:T(8,128)S(1)}, f32[128,128]{1,0:T(8,128)S(1)}, u32[]{:S(2)}, u32[]{:S(2)}) collective-permute-start(f32[128,128]{1,0:T(8,128)S(1)} %add.236), channel_id=1, source_target_pairs={{0,32},{4,36},{8,40},{12,44},{16,48},{20,52},{24,56},{28,60},{32,0... | collective-permute-start | bytes 196616 | tf_op jit(solution)/shard_map/cond/branch_0_fun/while/body/eval_jaxpr/ppermute | solution.py:33
  171.4 5.9 %collective-permute-start.13 = (f32[128,128]{1,0:T(8,128)S(1)}, f32[128,128]{1,0:T(8,128)S(1)}, u32[]{:S(2)}, u32[]{:S(2)}) collective-permute-start(f32[128,128]{1,0:T(8,128)S(1)} %add.238), channel_id=1, source_target_pairs={{0,128},{4,132},{8,136},{12,140},{16,144},{20,148},{24,152},{28,15... | collective-permute-start | bytes 196616 | tf_op jit(solution)/shard_map/cond/branch_0_fun/while/body/eval_jaxpr/ppermute | solution.py:33
  190.0 9.0 %collective-permute-start.3 = (f32[128,128]{0,1:T(8,128)S(1)}, f32[128,128]{0,1:T(8,128)S(1)}, u32[]{:S(2)}, u32[]{:S(2)}) collective-permute-start(f32[128,128]{0,1:T(8,128)S(1)} %add.228), channel_id=1, source_target_pairs={{0,32},{4,36},{8,40},{12,44},{16,48},{20,52},{24,56},{28,60},{32,0... | collective-permute-start | bytes 196616 | tf_op jit(solution)/shard_map/cond/branch_0_fun/while/body/eval_jaxpr/ppermute | solution.py:33
  203.3 5.9 %collective-permute-start.5 = (f32[128,128]{0,1:T(8,128)S(1)}, f32[128,128]{0,1:T(8,128)S(1)}, u32[]{:S(2)}, u32[]{:S(2)}) collective-permute-start(f32[128,128]{0,1:T(8,128)S(1)} %add.230), channel_id=1, source_target_pairs={{0,128},{4,132},{8,136},{12,140},{16,144},{20,148},{24,152},{28,15... | collective-permute-start | bytes 196616 | tf_op jit(solution)/shard_map/cond/branch_0_fun/while/body/eval_jaxpr/ppermute | solution.py:33
  232.9 14.7 %collective-permute-start.6 = (f32[1024,128]{0,1:T(8,128)S(1)}, f32[1024,128]{0,1:T(8,128)S(1)}, u32[]{:S(2)}, u32[]{:S(2)}) collective-permute-start(f32[1024,128]{0,1:T(8,128)S(1)} %fusion.44), channel_id=1, source_target_pairs={{0,1},{1,0},{2,3},{3,2},{4,5},{5,4},{6,7},{7,6},{8,9},{9,8},{10,11... | collective-permute-start | bytes 1572872 | tf_op jit(solution)/shard_map/cond/branch_0_fun/while/body/eval_jaxpr/ppermute | solution.py:33
  247.6 10.8 %collective-permute-start.7 = (f32[1024,128]{0,1:T(8,128)S(1)}, f32[1024,128]{0,1:T(8,128)S(1)}, u32[]{:S(2)}, u32[]{:S(2)}) collective-permute-start(f32[1024,128]{0,1:T(8,128)S(1)} %add.232), channel_id=1, source_target_pairs={{0,2},{1,3},{2,0},{3,1},{4,6},{5,7},{6,4},{7,5},{8,10},{9,11},{10,... | collective-permute-start | bytes 1572872 | tf_op jit(solution)/shard_map/cond/branch_0_fun/while/body/eval_jaxpr/ppermute | solution.py:33
  270.3 8.4 %collective-permute-start.11 = (f32[128,128]{1,0:T(8,128)S(1)}, f32[128,128]{1,0:T(8,128)S(1)}, u32[]{:S(2)}, u32[]{:S(2)}) collective-permute-start(f32[128,128]{1,0:T(8,128)S(1)} %add.236), channel_id=1, source_target_pairs={{0,32},{4,36},{8,40},{12,44},{16,48},{20,52},{24,56},{28,60},{32,0... | collective-permute-start | bytes 196616 | tf_op jit(solution)/shard_map/cond/branch_0_fun/while/body/eval_jaxpr/ppermute | solution.py:33
  283.1 5.9 %collective-permute-start.13 = (f32[128,128]{1,0:T(8,128)S(1)}, f32[128,128]{1,0:T(8,128)S(1)}, u32[]{:S(2)}, u32[]{:S(2)}) collective-permute-start(f32[128,128]{1,0:T(8,128)S(1)} %add.238), channel_id=1, source_target_pairs={{0,128},{4,132},{8,136},{12,140},{16,144},{20,148},{24,152},{28,15... | collective-permute-start | bytes 196616 | tf_op jit(solution)/shard_map/cond/branch_0_fun/while/body/eval_jaxpr/ppermute | solution.py:33
  301.7 8.5 %collective-permute-start.3 = (f32[128,128]{0,1:T(8,128)S(1)}, f32[128,128]{0,1:T(8,128)S(1)}, u32[]{:S(2)}, u32[]{:S(2)}) collective-permute-start(f32[128,128]{0,1:T(8,128)S(1)} %add.228), channel_id=1, source_target_pairs={{0,32},{4,36},{8,40},{12,44},{16,48},{20,52},{24,56},{28,60},{32,0... | collective-permute-start | bytes 196616 | tf_op jit(solution)/shard_map/cond/branch_0_fun/while/body/eval_jaxpr/ppermute | solution.py:33
  314.5 5.9 %collective-permute-start.5 = (f32[128,128]{0,1:T(8,128)S(1)}, f32[128,128]{0,1:T(8,128)S(1)}, u32[]{:S(2)}, u32[]{:S(2)}) collective-permute-start(f32[128,128]{0,1:T(8,128)S(1)} %add.230), channel_id=1, source_target_pairs={{0,128},{4,132},{8,136},{12,140},{16,144},{20,148},{24,152},{28,15... | collective-permute-start | bytes 196616 | tf_op jit(solution)/shard_map/cond/branch_0_fun/while/body/eval_jaxpr/ppermute | solution.py:33
  344.1 14.5 %collective-permute-start.6 = (f32[1024,128]{0,1:T(8,128)S(1)}, f32[1024,128]{0,1:T(8,128)S(1)}, u32[]{:S(2)}, u32[]{:S(2)}) collective-permute-start(f32[1024,128]{0,1:T(8,128)S(1)} %fusion.44), channel_id=1, source_target_pairs={{0,1},{1,0},{2,3},{3,2},{4,5},{5,4},{6,7},{7,6},{8,9},{9,8},{10,11... | collective-permute-start | bytes 1572872 | tf_op jit(solution)/shard_map/cond/branch_0_fun/while/body/eval_jaxpr/ppermute | solution.py:33
  358.6 10.8 %collective-permute-start.7 = (f32[1024,128]{0,1:T(8,128)S(1)}, f32[1024,128]{0,1:T(8,128)S(1)}, u32[]{:S(2)}, u32[]{:S(2)}) collective-permute-start(f32[1024,128]{0,1:T(8,128)S(1)} %add.232), channel_id=1, source_target_pairs={{0,2},{1,3},{2,0},{3,1},{4,6},{5,7},{6,4},{7,5},{8,10},{9,11},{10,... | collective-permute-start | bytes 1572872 | tf_op jit(solution)/shard_map/cond/branch_0_fun/while/body/eval_jaxpr/ppermute | solution.py:33
  375.8 5.9 %collective-permute-start.10 = (f32[128,128]{1,0:T(8,128)S(1)}, f32[128,128]{1,0:T(8,128)S(1)}, u32[]{:S(2)}, u32[]{:S(2)}) collective-permute-start(f32[128,128]{1,0:T(8,128)S(1)} %add.235), channel_id=1, source_target_pairs={{0,16},{4,20},{8,24},{12,28},{16,0},{20,4},{24,8},{28,12},{32,48},... | collective-permute-start | bytes 196616 | tf_op jit(solution)/shard_map/cond/branch_0_fun/while/body/eval_jaxpr/ppermute | solution.py:33
  381.7 8.4 %collective-permute-start.11 = (f32[128,128]{1,0:T(8,128)S(1)}, f32[128,128]{1,0:T(8,128)S(1)}, u32[]{:S(2)}, u32[]{:S(2)}) collective-permute-start(f32[128,128]{1,0:T(8,128)S(1)} %add.236), channel_id=1, source_target_pairs={{0,32},{4,36},{8,40},{12,44},{16,48},{20,52},{24,56},{28,60},{32,0... | collective-permute-start | bytes 196616 | tf_op jit(solution)/shard_map/cond/branch_0_fun/while/body/eval_jaxpr/ppermute | solution.py:33
  413.0 8.6 %collective-permute-start.3 = (f32[128,128]{0,1:T(8,128)S(1)}, f32[128,128]{0,1:T(8,128)S(1)}, u32[]{:S(2)}, u32[]{:S(2)}) collective-permute-start(f32[128,128]{0,1:T(8,128)S(1)} %add.228), channel_id=1, source_target_pairs={{0,32},{4,36},{8,40},{12,44},{16,48},{20,52},{24,56},{28,60},{32,0... | collective-permute-start | bytes 196616 | tf_op jit(solution)/shard_map/cond/branch_0_fun/while/body/eval_jaxpr/ppermute | solution.py:33
  455.5 14.6 %collective-permute-start.6 = (f32[1024,128]{0,1:T(8,128)S(1)}, f32[1024,128]{0,1:T(8,128)S(1)}, u32[]{:S(2)}, u32[]{:S(2)}) collective-permute-start(f32[1024,128]{0,1:T(8,128)S(1)} %fusion.44), channel_id=1, source_target_pairs={{0,1},{1,0},{2,3},{3,2},{4,5},{5,4},{6,7},{7,6},{8,9},{9,8},{10,11... | collective-permute-start | bytes 1572872 | tf_op jit(solution)/shard_map/cond/branch_0_fun/while/body/eval_jaxpr/ppermute | solution.py:33
  470.2 10.8 %collective-permute-start.7 = (f32[1024,128]{0,1:T(8,128)S(1)}, f32[1024,128]{0,1:T(8,128)S(1)}, u32[]{:S(2)}, u32[]{:S(2)}) collective-permute-start(f32[1024,128]{0,1:T(8,128)S(1)} %add.232), channel_id=1, source_target_pairs={{0,2},{1,3},{2,0},{3,1},{4,6},{5,7},{6,4},{7,5},{8,10},{9,11},{10,... | collective-permute-start | bytes 1572872 | tf_op jit(solution)/shard_map/cond/branch_0_fun/while/body/eval_jaxpr/ppermute | solution.py:33
  493.0 8.3 %collective-permute-start.11 = (f32[128,128]{1,0:T(8,128)S(1)}, f32[128,128]{1,0:T(8,128)S(1)}, u32[]{:S(2)}, u32[]{:S(2)}) collective-permute-start(f32[128,128]{1,0:T(8,128)S(1)} %add.236), channel_id=1, source_target_pairs={{0,32},{4,36},{8,40},{12,44},{16,48},{20,52},{24,56},{28,60},{32,0... | collective-permute-start | bytes 196616 | tf_op jit(solution)/shard_map/cond/branch_0_fun/while/body/eval_jaxpr/ppermute | solution.py:33
  (37 other events, 269.2 us)

commit v11 on v10

--- a/solution.py
+++ b/solution.py
@@ -169,8 +169,6 @@
     order_copy = pltpu.make_async_copy(order_in, order, i_sem.at[1])
     order_copy.start()
 
-    cov_copy.start()
-
     pl.semaphore_wait(barrier, len(neighbours))
     tell(word.at[0], near_z)
     tell(word.at[1], near_x)
@@ -193,6 +191,7 @@
     to_near.start()
     for j in range(1, ROW_BLOCKS):
         to_far(j).start()
+    cov_copy.start()
 
     col_copy.wait()
     order_copy.wait()

time: 513 us -> 514 us (level)
  starting transfers between devices: 34.6 us -> 91.2 us
  waiting for transfers between devices: 308 us -> 252 us
    ppermute x56, starting transfers between devices: 29.4 us -> 86.1 us  [total(): value = value + lax.ppermute(value, axis, pairs)]
    ppermute x56, waiting for transfers between devices: 302 us -> 246 us  [total(): value = value + lax.ppermute(value, axis, pairs)]
where the time goes in v11:
time: 514 us; the launch traced here: 513 us
  waiting for transfers between devices  252 us (49%)
  other arithmetic  93.3 us (18%)
  starting transfers between devices  91.2 us (18%)
  Pallas kernels  43.7 us (9%)
  matrix products  18.2 us (4%)
  loops' own time  8.34 us (2%)
  local copies, waits for them, and re-layouts  6.85 us (1%)
    ppermute x56, waiting for transfers between devices, total(): value = value + lax.ppermute(value, axis, pairs)  246 us
    ppermute x56, starting transfers between devices, total(): value = value + lax.ppermute(value, axis, pairs)  86.1 us
    another operation x12, other arithmetic, step(): lower = jnp.linalg.cholesky(gram)  49.8 us
    pallas_call x1, Pallas kernels, fast(): pl.pallas_call(kernel, out_shape=(pltpu.VMEM((ROWS, WIDTH), F32), pltpu.S...  43.7 us
    another operation x8, other arithmetic, step(): lax.linalg.triangular_solve(lower, local, left_side=False, lower=True, tr...  41.8 us
  transfers between devices with their start and end apart: 58, of which 57 were waited for; matrix products, arithmetic and copies ran while one was open for 1% of the time, Pallas kernels for 0%

profile of v11, /device:TPU:6, one launch (start us, length us, event | category | flops | bytes accessed | tf_op | source)
XLA Modules:
  0.0 513.3 jit_solution(4829656246759266042)
XLA Ops:
  0.0 43.7 %shard_map.48 = (f32[1024,128]{1,0:T(8,128)S(1)}, s32[1,1]{1,0:T(1,128)S(4)}) custom-call(f32[1024,128]{1,0:T(8,128)} %start.1, f32[8,8,128,128]{3,2,1,0:T(8,128)} %cov.1, s32[8,8]{1,0:T(8,128)} %col_in.1, s32[4]{0:T(128)} %order_in.1), custom_call_target="tpu_custom_call" | custom-call | tf_op jit(solution)/shard_map/pallas_call | solution.py:623
  43.7 468.8 %conditional.1 = (f32[1024,128]{1,0:T(8,128)S(1)}) conditional(s32[]{:T(128)} %bitcast.11, (f32[1024,128]{1,0:T(8,128)S(1)}, s32[8,8]{1,0:T(8,128)S(1)}, f32[8,8,128,128]{3,2,1,0:T(8,128)}, s32[4]{0:T(128)S(1)}) %tuple.55, f32[1024,128]{1,0:T(8,128)S(1)} %get-tuple-element.156), branch_computations={%region_0.6_spmd, %region_6.7_spmd} | conditional | flops 2417838080 | bytes 44441020 | solution.py:683
  49.6 6.1 %collective-permute-done.14 = f32[1024,128]{1,0:T(8,128)S(1)} collective-permute-done((f32[1024,128]{1,0:T(8,128)S(1)}, f32[1024,128]{1,0:T(8,128)S(1)}, u32[]{:S(2)}, u32[]{:S(2)}) %collective-permute-start.14) | collective-permute-done | bytes 524320 | tf_op jit(solution)/shard_map/cond/branch_0_fun/ppermute | solution.py:49
  58.6 7.9 %fusion.10 = f32[8,128,128,1]{1,2,3,0:T(8,128)S(1)} fusion(f32[8,8,128,128]{3,2,1,0:T(8,128)} %bitcast.52, f32[8,8,128,128]{3,2,1,0:T(8,128)} %get-tuple-element.150), kind=kOutput, calls=%fused_computation.26 | convolution fusion | flops 1610612736 | bytes 8912896 | tf_op jit(solution)/shard_map/cond/branch_0_fun/rsab,rsbk->rak/dot_general | solution.py:79
  66.8 445.3 %while.14 = (s32[]{:T(128)}, f32[1024,128]{0,1:T(8,128)S(1)}, s32[]{:T(128)}, s32[4]{0:T(128)S(1)}, s32[]{:T(128)}, /*index=5*/s32[]{:T(128)}, u32[]{:T(128)}) while((s32[]{:T(128)}, f32[1024,128]{0,1:T(8,128)S(1)}, s32[]{:T(128)}, s32[4]{0:T(128)S(1)}, s32[]{:T(128)}, /*index=5*/s32[]{:T(128)}, u32[]{:T(128)}) %tuple.48), condition=%wide.region_5.5_spmd, body=%wide.region_2.4_spmd.sunk | while | flops 806436992 | bytes 17696444 | solution.py:97
  80.9 6.1 %collective-permute-done.3 = f32[128,128]{0,1:T(8,128)S(1)} collective-permute-done((f32[128,128]{0,1:T(8,128)S(1)}, f32[128,128]{0,1:T(8,128)S(1)}, u32[]{:S(2)}, u32[]{:S(2)}) %collective-permute-start.3) | collective-permute-done | bytes 65568 | tf_op jit(solution)/shard_map/cond/branch_0_fun/while/body/eval_jaxpr/ppermute | solution.py:33
  97.3 11.7 %cholesky.58 = f32[128,128]{1,0:T(8,128)S(1)} custom-call(f32[128,128]{1,0:T(8,128)S(1)} %fusion.42), custom_call_target="Cholesky" | custom-call | tf_op jit(solution)/shard_map/cond/branch_0_fun/while/body/eval_jaxpr/jit(cholesky)/cholesky | solution.py:86
  110.4 9.8 %custom-call.23 = f32[1,128,128]{1,2,0:T(8,128)S(1)} custom-call(f32[1,128,128]{2,1,0:T(8,128)S(1)} %fusion.43), custom_call_target="InvertDiagBlocksLowerTriangular" | custom-call | tf_op jit(solution)/shard_map/cond/branch_0_fun/while/body/eval_jaxpr/triangular_solve | solution.py:87
  121.6 11.8 %collective-permute-done.6 = f32[1024,128]{0,1:T(8,128)S(1)} collective-permute-done((f32[1024,128]{0,1:T(8,128)S(1)}, f32[1024,128]{0,1:T(8,128)S(1)}, u32[]{:S(2)}, u32[]{:S(2)}) %collective-permute-start.6) | collective-permute-done | bytes 524320 | tf_op jit(solution)/shard_map/cond/branch_0_fun/while/body/eval_jaxpr/ppermute | solution.py:33
  134.0 10.2 %collective-permute-done.7 = f32[1024,128]{0,1:T(8,128)S(1)} collective-permute-done((f32[1024,128]{0,1:T(8,128)S(1)}, f32[1024,128]{0,1:T(8,128)S(1)}, u32[]{:S(2)}, u32[]{:S(2)}) %collective-permute-start.7) | collective-permute-done | bytes 524320 | tf_op jit(solution)/shard_map/cond/branch_0_fun/while/body/eval_jaxpr/ppermute | solution.py:33
  207.7 11.7 %cholesky.58 = f32[128,128]{1,0:T(8,128)S(1)} custom-call(f32[128,128]{1,0:T(8,128)S(1)} %fusion.42), custom_call_target="Cholesky" | custom-call | tf_op jit(solution)/shard_map/cond/branch_0_fun/while/body/eval_jaxpr/jit(cholesky)/cholesky | solution.py:86
  220.8 9.8 %custom-call.23 = f32[1,128,128]{1,2,0:T(8,128)S(1)} custom-call(f32[1,128,128]{2,1,0:T(8,128)S(1)} %fusion.43), custom_call_target="InvertDiagBlocksLowerTriangular" | custom-call | tf_op jit(solution)/shard_map/cond/branch_0_fun/while/body/eval_jaxpr/triangular_solve | solution.py:87
  231.4 14.6 %collective-permute-done.6 = f32[1024,128]{0,1:T(8,128)S(1)} collective-permute-done((f32[1024,128]{0,1:T(8,128)S(1)}, f32[1024,128]{0,1:T(8,128)S(1)}, u32[]{:S(2)}, u32[]{:S(2)}) %collective-permute-start.6) | collective-permute-done | bytes 524320 | tf_op jit(solution)/shard_map/cond/branch_0_fun/while/body/eval_jaxpr/ppermute | solution.py:33
  246.1 10.7 %collective-permute-done.7 = f32[1024,128]{0,1:T(8,128)S(1)} collective-permute-done((f32[1024,128]{0,1:T(8,128)S(1)}, f32[1024,128]{0,1:T(8,128)S(1)}, u32[]{:S(2)}, u32[]{:S(2)}) %collective-permute-start.7) | collective-permute-done | bytes 524320 | tf_op jit(solution)/shard_map/cond/branch_0_fun/while/body/eval_jaxpr/ppermute | solution.py:33
  319.1 11.7 %cholesky.58 = f32[128,128]{1,0:T(8,128)S(1)} custom-call(f32[128,128]{1,0:T(8,128)S(1)} %fusion.42), custom_call_target="Cholesky" | custom-call | tf_op jit(solution)/shard_map/cond/branch_0_fun/while/body/eval_jaxpr/jit(cholesky)/cholesky | solution.py:86
  332.2 9.8 %custom-call.23 = f32[1,128,128]{1,2,0:T(8,128)S(1)} custom-call(f32[1,128,128]{2,1,0:T(8,128)S(1)} %fusion.43), custom_call_target="InvertDiagBlocksLowerTriangular" | custom-call | tf_op jit(solution)/shard_map/cond/branch_0_fun/while/body/eval_jaxpr/triangular_solve | solution.py:87
  342.7 14.2 %collective-permute-done.6 = f32[1024,128]{0,1:T(8,128)S(1)} collective-permute-done((f32[1024,128]{0,1:T(8,128)S(1)}, f32[1024,128]{0,1:T(8,128)S(1)}, u32[]{:S(2)}, u32[]{:S(2)}) %collective-permute-start.6) | collective-permute-done | bytes 524320 | tf_op jit(solution)/shard_map/cond/branch_0_fun/while/body/eval_jaxpr/ppermute | solution.py:33
  357.1 10.7 %collective-permute-done.7 = f32[1024,128]{0,1:T(8,128)S(1)} collective-permute-done((f32[1024,128]{0,1:T(8,128)S(1)}, f32[1024,128]{0,1:T(8,128)S(1)}, u32[]{:S(2)}, u32[]{:S(2)}) %collective-permute-start.7) | collective-permute-done | bytes 524320 | tf_op jit(solution)/shard_map/cond/branch_0_fun/while/body/eval_jaxpr/ppermute | solution.py:33
  379.4 6.0 %collective-permute-start.11 = (f32[128,128]{1,0:T(8,128)S(1)}, f32[128,128]{1,0:T(8,128)S(1)}, u32[]{:S(2)}, u32[]{:S(2)}) collective-permute-start(f32[128,128]{1,0:T(8,128)S(1)} %add.236), channel_id=1, source_target_pairs={{0,32},{4,36},{8,40},{12,44},{16,48},{20,52},{24,56},{28,60},{32,0... | collective-permute-start | bytes 196616 | tf_op jit(solution)/shard_map/cond/branch_0_fun/while/body/eval_jaxpr/ppermute | solution.py:33
  431.0 11.7 %cholesky.58 = f32[128,128]{1,0:T(8,128)S(1)} custom-call(f32[128,128]{1,0:T(8,128)S(1)} %fusion.42), custom_call_target="Cholesky" | custom-call | tf_op jit(solution)/shard_map/cond/branch_0_fun/while/body/eval_jaxpr/jit(cholesky)/cholesky | solution.py:86
  444.1 9.8 %custom-call.23 = f32[1,128,128]{1,2,0:T(8,128)S(1)} custom-call(f32[1,128,128]{2,1,0:T(8,128)S(1)} %fusion.43), custom_call_target="InvertDiagBlocksLowerTriangular" | custom-call | tf_op jit(solution)/shard_map/cond/branch_0_fun/while/body/eval_jaxpr/triangular_solve | solution.py:87
  454.6 13.5 %collective-permute-done.6 = f32[1024,128]{0,1:T(8,128)S(1)} collective-permute-done((f32[1024,128]{0,1:T(8,128)S(1)}, f32[1024,128]{0,1:T(8,128)S(1)}, u32[]{:S(2)}, u32[]{:S(2)}) %collective-permute-start.6) | collective-permute-done | bytes 524320 | tf_op jit(solution)/shard_map/cond/branch_0_fun/while/body/eval_jaxpr/ppermute | solution.py:33
  468.3 10.7 %collective-permute-done.7 = f32[1024,128]{0,1:T(8,128)S(1)} collective-permute-done((f32[1024,128]{0,1:T(8,128)S(1)}, f32[1024,128]{0,1:T(8,128)S(1)}, u32[]{:S(2)}, u32[]{:S(2)}) %collective-permute-start.7) | collective-permute-done | bytes 524320 | tf_op jit(solution)/shard_map/cond/branch_0_fun/while/body/eval_jaxpr/ppermute | solution.py:33
  490.8 8.0 %collective-permute-start.11 = (f32[128,128]{1,0:T(8,128)S(1)}, f32[128,128]{1,0:T(8,128)S(1)}, u32[]{:S(2)}, u32[]{:S(2)}) collective-permute-start(f32[128,128]{1,0:T(8,128)S(1)} %add.236), channel_id=1, source_target_pairs={{0,32},{4,36},{8,40},{12,44},{16,48},{20,52},{24,56},{28,60},{32,0... | collective-permute-start | bytes 196616 | tf_op jit(solution)/shard_map/cond/branch_0_fun/while/body/eval_jaxpr/ppermute | solution.py:33
  (211 shorter events, 244.6 us)
Async XLA Ops:
  43.8 12.0 %collective-permute-start.14 = (f32[1024,128]{1,0:T(8,128)S(1)}, f32[1024,128]{1,0:T(8,128)S(1)}, u32[]{:S(2)}, u32[]{:S(2)}) collective-permute-start(f32[1024,128]{1,0:T(8,128)S(1)} %get-tuple-element.148), channel_id=1, source_target_pairs={{0,4},{4,8},{8,12},{12,16},{16,20},{20,24},{24,28},{28,32},{32,36}... | collective-permute-start | bytes 1572872 | tf_op jit(solution)/shard_map/cond/branch_0_fun/ppermute | solution.py:49
  44.8 11.0 %collective-permute-start.15 = (f32[1024,128]{1,0:T(8,128)S(1)}, f32[1024,128]{1,0:T(8,128)S(1)}, u32[]{:S(2)}, u32[]{:S(2)}) collective-permute-start(f32[1024,128]{1,0:T(8,128)S(1)} %get-tuple-element.148), channel_id=1, source_target_pairs={{4,0},{8,4},{12,8},{16,12},{20,16},{24,20},{28,24},{32,28},{36,32}... | collective-permute-start | bytes 1572872 | tf_op jit(solution)/shard_map/cond/branch_0_fun/ppermute | solution.py:51
  78.7 8.3 %collective-permute-start.3 = (f32[128,128]{0,1:T(8,128)S(1)}, f32[128,128]{0,1:T(8,128)S(1)}, u32[]{:S(2)}, u32[]{:S(2)}) collective-permute-start(f32[128,128]{0,1:T(8,128)S(1)} %add.228), channel_id=1, source_target_pairs={{0,32},{4,36},{8,40},{12,44},{16,48},{20,52},{24,56},{28,60},{32,0... | collective-permute-start | bytes 196616 | tf_op jit(solution)/shard_map/cond/branch_0_fun/while/body/eval_jaxpr/ppermute | solution.py:33
  91.3 5.9 %collective-permute-start.5 = (f32[128,128]{0,1:T(8,128)S(1)}, f32[128,128]{0,1:T(8,128)S(1)}, u32[]{:S(2)}, u32[]{:S(2)}) collective-permute-start(f32[128,128]{0,1:T(8,128)S(1)} %add.230), channel_id=1, source_target_pairs={{0,128},{4,132},{8,136},{12,140},{16,144},{20,148},{24,152},{28,15... | collective-permute-start | bytes 196616 | tf_op jit(solution)/shard_map/cond/branch_0_fun/while/body/eval_jaxpr/ppermute | solution.py:33
  120.9 12.5 %collective-permute-start.6 = (f32[1024,128]{0,1:T(8,128)S(1)}, f32[1024,128]{0,1:T(8,128)S(1)}, u32[]{:S(2)}, u32[]{:S(2)}) collective-permute-start(f32[1024,128]{0,1:T(8,128)S(1)} %fusion.44), channel_id=1, source_target_pairs={{0,1},{1,0},{2,3},{3,2},{4,5},{5,4},{6,7},{7,6},{8,9},{9,8},{10,11... | collective-permute-start | bytes 1572872 | tf_op jit(solution)/shard_map/cond/branch_0_fun/while/body/eval_jaxpr/ppermute | solution.py:33
  133.4 10.8 %collective-permute-start.7 = (f32[1024,128]{0,1:T(8,128)S(1)}, f32[1024,128]{0,1:T(8,128)S(1)}, u32[]{:S(2)}, u32[]{:S(2)}) collective-permute-start(f32[1024,128]{0,1:T(8,128)S(1)} %add.232), channel_id=1, source_target_pairs={{0,2},{1,3},{2,0},{3,1},{4,6},{5,7},{6,4},{7,5},{8,10},{9,11},{10,... | collective-permute-start | bytes 1572872 | tf_op jit(solution)/shard_map/cond/branch_0_fun/while/body/eval_jaxpr/ppermute | solution.py:33
  150.6 6.0 %collective-permute-start.10 = (f32[128,128]{1,0:T(8,128)S(1)}, f32[128,128]{1,0:T(8,128)S(1)}, u32[]{:S(2)}, u32[]{:S(2)}) collective-permute-start(f32[128,128]{1,0:T(8,128)S(1)} %add.235), channel_id=1, source_target_pairs={{0,16},{4,20},{8,24},{12,28},{16,0},{20,4},{24,8},{28,12},{32,48},... | collective-permute-start | bytes 196616 | tf_op jit(solution)/shard_map/cond/branch_0_fun/while/body/eval_jaxpr/ppermute | solution.py:33
  156.6 8.3 %collective-permute-start.11 = (f32[128,128]{1,0:T(8,128)S(1)}, f32[128,128]{1,0:T(8,128)S(1)}, u32[]{:S(2)}, u32[]{:S(2)}) collective-permute-start(f32[128,128]{1,0:T(8,128)S(1)} %add.236), channel_id=1, source_target_pairs={{0,32},{4,36},{8,40},{12,44},{16,48},{20,52},{24,56},{28,60},{32,0... | collective-permute-start | bytes 196616 | tf_op jit(solution)/shard_map/cond/branch_0_fun/while/body/eval_jaxpr/ppermute | solution.py:33
  169.6 5.9 %collective-permute-start.13 = (f32[128,128]{1,0:T(8,128)S(1)}, f32[128,128]{1,0:T(8,128)S(1)}, u32[]{:S(2)}, u32[]{:S(2)}) collective-permute-start(f32[128,128]{1,0:T(8,128)S(1)} %add.238), channel_id=1, source_target_pairs={{0,128},{4,132},{8,136},{12,140},{16,144},{20,148},{24,152},{28,15... | collective-permute-start | bytes 196616 | tf_op jit(solution)/shard_map/cond/branch_0_fun/while/body/eval_jaxpr/ppermute | solution.py:33
  188.4 8.3 %collective-permute-start.3 = (f32[128,128]{0,1:T(8,128)S(1)}, f32[128,128]{0,1:T(8,128)S(1)}, u32[]{:S(2)}, u32[]{:S(2)}) collective-permute-start(f32[128,128]{0,1:T(8,128)S(1)} %add.228), channel_id=1, source_target_pairs={{0,32},{4,36},{8,40},{12,44},{16,48},{20,52},{24,56},{28,60},{32,0... | collective-permute-start | bytes 196616 | tf_op jit(solution)/shard_map/cond/branch_0_fun/while/body/eval_jaxpr/ppermute | solution.py:33
  231.3 14.7 %collective-permute-start.6 = (f32[1024,128]{0,1:T(8,128)S(1)}, f32[1024,128]{0,1:T(8,128)S(1)}, u32[]{:S(2)}, u32[]{:S(2)}) collective-permute-start(f32[1024,128]{0,1:T(8,128)S(1)} %fusion.44), channel_id=1, source_target_pairs={{0,1},{1,0},{2,3},{3,2},{4,5},{5,4},{6,7},{7,6},{8,9},{9,8},{10,11... | collective-permute-start | bytes 1572872 | tf_op jit(solution)/shard_map/cond/branch_0_fun/while/body/eval_jaxpr/ppermute | solution.py:33
  246.0 10.8 %collective-permute-start.7 = (f32[1024,128]{0,1:T(8,128)S(1)}, f32[1024,128]{0,1:T(8,128)S(1)}, u32[]{:S(2)}, u32[]{:S(2)}) collective-permute-start(f32[1024,128]{0,1:T(8,128)S(1)} %add.232), channel_id=1, source_target_pairs={{0,2},{1,3},{2,0},{3,1},{4,6},{5,7},{6,4},{7,5},{8,10},{9,11},{10,... | collective-permute-start | bytes 1572872 | tf_op jit(solution)/shard_map/cond/branch_0_fun/while/body/eval_jaxpr/ppermute | solution.py:33
  268.8 8.3 %collective-permute-start.11 = (f32[128,128]{1,0:T(8,128)S(1)}, f32[128,128]{1,0:T(8,128)S(1)}, u32[]{:S(2)}, u32[]{:S(2)}) collective-permute-start(f32[128,128]{1,0:T(8,128)S(1)} %add.236), channel_id=1, source_target_pairs={{0,32},{4,36},{8,40},{12,44},{16,48},{20,52},{24,56},{28,60},{32,0... | collective-permute-start | bytes 196616 | tf_op jit(solution)/shard_map/cond/branch_0_fun/while/body/eval_jaxpr/ppermute | solution.py:33
  294.4 6.0 %collective-permute-start.2 = (f32[128,128]{0,1:T(8,128)S(1)}, f32[128,128]{0,1:T(8,128)S(1)}, u32[]{:S(2)}, u32[]{:S(2)}) collective-permute-start(f32[128,128]{0,1:T(8,128)S(1)} %add.227), channel_id=1, source_target_pairs={{0,16},{4,20},{8,24},{12,28},{16,0},{20,4},{24,8},{28,12},{32,48},... | collective-permute-start | bytes 196616 | tf_op jit(solution)/shard_map/cond/branch_0_fun/while/body/eval_jaxpr/ppermute | solution.py:33
  300.3 8.3 %collective-permute-start.3 = (f32[128,128]{0,1:T(8,128)S(1)}, f32[128,128]{0,1:T(8,128)S(1)}, u32[]{:S(2)}, u32[]{:S(2)}) collective-permute-start(f32[128,128]{0,1:T(8,128)S(1)} %add.228), channel_id=1, source_target_pairs={{0,32},{4,36},{8,40},{12,44},{16,48},{20,52},{24,56},{28,60},{32,0... | collective-permute-start | bytes 196616 | tf_op jit(solution)/shard_map/cond/branch_0_fun/while/body/eval_jaxpr/ppermute | solution.py:33
  342.6 14.3 %collective-permute-start.6 = (f32[1024,128]{0,1:T(8,128)S(1)}, f32[1024,128]{0,1:T(8,128)S(1)}, u32[]{:S(2)}, u32[]{:S(2)}) collective-permute-start(f32[1024,128]{0,1:T(8,128)S(1)} %fusion.44), channel_id=1, source_target_pairs={{0,1},{1,0},{2,3},{3,2},{4,5},{5,4},{6,7},{7,6},{8,9},{9,8},{10,11... | collective-permute-start | bytes 1572872 | tf_op jit(solution)/shard_map/cond/branch_0_fun/while/body/eval_jaxpr/ppermute | solution.py:33
  357.0 10.8 %collective-permute-start.7 = (f32[1024,128]{0,1:T(8,128)S(1)}, f32[1024,128]{0,1:T(8,128)S(1)}, u32[]{:S(2)}, u32[]{:S(2)}) collective-permute-start(f32[1024,128]{0,1:T(8,128)S(1)} %add.232), channel_id=1, source_target_pairs={{0,2},{1,3},{2,0},{3,1},{4,6},{5,7},{6,4},{7,5},{8,10},{9,11},{10,... | collective-permute-start | bytes 1572872 | tf_op jit(solution)/shard_map/cond/branch_0_fun/while/body/eval_jaxpr/ppermute | solution.py:33
  379.4 9.0 %collective-permute-start.11 = (f32[128,128]{1,0:T(8,128)S(1)}, f32[128,128]{1,0:T(8,128)S(1)}, u32[]{:S(2)}, u32[]{:S(2)}) collective-permute-start(f32[128,128]{1,0:T(8,128)S(1)} %add.236), channel_id=1, source_target_pairs={{0,32},{4,36},{8,40},{12,44},{16,48},{20,52},{24,56},{28,60},{32,0... | collective-permute-start | bytes 196616 | tf_op jit(solution)/shard_map/cond/branch_0_fun/while/body/eval_jaxpr/ppermute | solution.py:33
  406.0 6.0 %collective-permute-start.2 = (f32[128,128]{0,1:T(8,128)S(1)}, f32[128,128]{0,1:T(8,128)S(1)}, u32[]{:S(2)}, u32[]{:S(2)}) collective-permute-start(f32[128,128]{0,1:T(8,128)S(1)} %add.227), channel_id=1, source_target_pairs={{0,16},{4,20},{8,24},{12,28},{16,0},{20,4},{24,8},{28,12},{32,48},... | collective-permute-start | bytes 196616 | tf_op jit(solution)/shard_map/cond/branch_0_fun/while/body/eval_jaxpr/ppermute | solution.py:33
  412.0 8.5 %collective-permute-start.3 = (f32[128,128]{0,1:T(8,128)S(1)}, f32[128,128]{0,1:T(8,128)S(1)}, u32[]{:S(2)}, u32[]{:S(2)}) collective-permute-start(f32[128,128]{0,1:T(8,128)S(1)} %add.228), channel_id=1, source_target_pairs={{0,32},{4,36},{8,40},{12,44},{16,48},{20,52},{24,56},{28,60},{32,0... | collective-permute-start | bytes 196616 | tf_op jit(solution)/shard_map/cond/branch_0_fun/while/body/eval_jaxpr/ppermute | solution.py:33
  425.0 5.9 %collective-permute-start.5 = (f32[128,128]{0,1:T(8,128)S(1)}, f32[128,128]{0,1:T(8,128)S(1)}, u32[]{:S(2)}, u32[]{:S(2)}) collective-permute-start(f32[128,128]{0,1:T(8,128)S(1)} %add.230), channel_id=1, source_target_pairs={{0,128},{4,132},{8,136},{12,140},{16,144},{20,148},{24,152},{28,15... | collective-permute-start | bytes 196616 | tf_op jit(solution)/shard_map/cond/branch_0_fun/while/body/eval_jaxpr/ppermute | solution.py:33
  454.5 13.6 %collective-permute-start.6 = (f32[1024,128]{0,1:T(8,128)S(1)}, f32[1024,128]{0,1:T(8,128)S(1)}, u32[]{:S(2)}, u32[]{:S(2)}) collective-permute-start(f32[1024,128]{0,1:T(8,128)S(1)} %fusion.44), channel_id=1, source_target_pairs={{0,1},{1,0},{2,3},{3,2},{4,5},{5,4},{6,7},{7,6},{8,9},{9,8},{10,11... | collective-permute-start | bytes 1572872 | tf_op jit(solution)/shard_map/cond/branch_0_fun/while/body/eval_jaxpr/ppermute | solution.py:33
  468.2 10.8 %collective-permute-start.7 = (f32[1024,128]{0,1:T(8,128)S(1)}, f32[1024,128]{0,1:T(8,128)S(1)}, u32[]{:S(2)}, u32[]{:S(2)}) collective-permute-start(f32[1024,128]{0,1:T(8,128)S(1)} %add.232), channel_id=1, source_target_pairs={{0,2},{1,3},{2,0},{3,1},{4,6},{5,7},{6,4},{7,5},{8,10},{9,11},{10,... | collective-permute-start | bytes 1572872 | tf_op jit(solution)/shard_map/cond/branch_0_fun/while/body/eval_jaxpr/ppermute | solution.py:33
  490.8 10.3 %collective-permute-start.11 = (f32[128,128]{1,0:T(8,128)S(1)}, f32[128,128]{1,0:T(8,128)S(1)}, u32[]{:S(2)}, u32[]{:S(2)}) collective-permute-start(f32[128,128]{1,0:T(8,128)S(1)} %add.236), channel_id=1, source_target_pairs={{0,32},{4,36},{8,40},{12,44},{16,48},{20,52},{24,56},{28,60},{32,0... | collective-permute-start | bytes 196616 | tf_op jit(solution)/shard_map/cond/branch_0_fun/while/body/eval_jaxpr/ppermute | solution.py:33
  (37 other events, 270.0 us)
